TPU v7x, 32 devices: a whole 2x2x4 slice. The times are simulated.
32 devices in a mesh: groups: 2 (over y), tensor: 16 (over z, x, core).
Axes of the slice: x: 2, y: 2, z: 4, core: 2. Of those that a mesh axis runs over, the one named last changes fastest.
Arguments:
- tokens: bfloat16 [32, 8192], P(('groups', 'tensor')), parts along dimension 0, may hold values from -6 to 6
- norm_gain: bfloat16 [8192], replicated, may hold values from 0.5 to 1.5
- w_gate: bfloat16 [8192, 28672], P(None, 'tensor'), may hold values from -0.0625 to 0.0625
- w_up: bfloat16 [8192, 28672], P(None, 'tensor'), may hold values from -0.0625 to 0.0625
- w_down: bfloat16 [28672, 8192], P('tensor'), may hold values from -0.03125 to 0.03125
- lengths: int32 [16], P('groups'), parts along dimension 0, may hold values from 1 to 4, 16 in all
- hit_lengths: int32 [16], P('groups'), parts along dimension 0, may hold values from 0 to 4095, as said below
- start_positions: int32 [16], P('groups'), parts along dimension 0, may hold values from 0 to 4093
Outputs:
- block_out: bfloat16 [32, 8192], P(('groups', 'tensor')), parts along dimension 0
There are 2 independent parts, one for each index of `groups`. A program takes and returns all parts, laid end to end along the dimension named above; an argument that names none is the same for every part. Nothing has to cross between parts.
Inputs may be any that keep to these rules, and one draw needn't show every extreme that they name: start_positions[r] <= hit_lengths[r] <= start_positions[r] + 2.
All inputs are finite; a program needn't handle non-finite values.
Results may differ from a plain program's by a relative error of at most 0.0071.
Values may be sent and summed in bfloat16 or wider, within the bound.
No kernel may reach another device: no remote copies, remote signals or barrier semaphores. Data moves between devices by JAX's collectives and lax.ppermute only.
A program may use at most 192 MiB of HBM per device.

v0:
```python
import jax
import jax.numpy as jnp
from jax import lax
from jax.sharding import PartitionSpec as P


def normalize(tokens, norm_gain):
    values = tokens.astype(jnp.float32)
    mean_sq = jnp.mean(values * values, axis=-1, keepdims=True)
    return (values * lax.rsqrt(mean_sq + 1e-05) * norm_gain.astype(jnp.float32)).astype(
        jnp.bfloat16
    )


def live_rows(lengths, hit_lengths, start_positions, token_index):
    ends = jnp.cumsum(lengths)
    begins = ends - lengths
    member = (token_index[:, None] >= begins[None, :]) & (token_index[:, None] < ends[None, :])
    member_int = member.astype(jnp.int32)
    offsets = token_index - jnp.sum(member_int * begins[None, :], axis=1)
    position = jnp.sum(member_int * start_positions[None, :], axis=1) + offsets
    covered = jnp.sum(member_int * hit_lengths[None, :], axis=1)
    return position >= covered


def local(tokens, norm_gain, w_gate, w_up, w_down, lengths, hit_lengths, start_positions):
    row_count = tokens.shape[0]
    normed = normalize(tokens, norm_gain)
    piece_rows = lax.all_gather(normed, "tensor", axis=0, tiled=True)
    gate_out = jnp.dot(piece_rows, w_gate, preferred_element_type=jnp.float32)
    up_out = jnp.dot(piece_rows, w_up, preferred_element_type=jnp.float32)
    hidden = (jax.nn.silu(gate_out) * up_out).astype(jnp.bfloat16)
    partial_value = jnp.dot(hidden, w_down, preferred_element_type=jnp.float32)
    rounded = partial_value.astype(jnp.bfloat16)
    totals = jnp.sum(
        lax.all_to_all(rounded[None], "tensor", split_axis=1, concat_axis=0, tiled=True).astype(
            jnp.float32
        ),
        axis=0,
    )
    token_index = lax.axis_index("tensor") * row_count + jnp.arange(row_count, dtype=jnp.int32)
    live = live_rows(lengths, hit_lengths, start_positions, token_index)
    return jnp.where(live[:, None], totals, jnp.zeros_like(totals)).astype(jnp.bfloat16)


def solution(mesh):
    placed = (
        P(("groups", "tensor"), None),
        P(),
        P(None, "tensor"),
        P(None, "tensor"),
        P("tensor", None),
        P("groups"),
        P("groups"),
        P("groups"),
    )
    return jax.shard_map(
        local, mesh=mesh, in_specs=placed, out_specs=P(("groups", "tensor"), None), check_vma=False
    )
```

profile of v0, /device:TPU:0, one launch (start us, length us, event | category | flops | bytes accessed | tf_op | source)
XLA Modules:
  0.0 79.9 jit_solution(14068949305238477064)
XLA Ops:
  0.0 0.7 broadcast_in_dim.32
  0.7 1.4 %multiply_reduce_fusion = f32[]{:T(128)} fusion(bf16[1,8192]{1,0:T(2,128)(2,1)} %param.8), kind=kLoop, calls=%fused_computation.18 | loop fusion | flops 24575 | bytes 16388 | tf_op jit(solution)/shard_map/reduce_sum | solution.py:9
  2.8 0.8 %convert_bitcast_fusion = bf16[1,1,8192]{2,1,0:T(2,128)(2,1)S(1)} fusion(f32[1,8192]{1,0:T(1,128)S(1)} %bitcast.28, bf16[1,8192]{1,0:T(2,128)(2,1)} %param.8, f32[]{:T(128)S(6)} %rsqrt.4), kind=kLoop, calls=%fused_computation.17 | loop fusion | flops 32768 | bytes 65540
  3.7 24.6 %all-gather = bf16[16,1,8192]{2,1,0:T(2,128)(2,1)S(1)} all-gather(bf16[1,1,8192]{2,1,0:T(2,128)(2,1)S(1)} %convert_bitcast_fusion), channel_id=1, replica_groups=mesh['groups'=2,'tensor'=16] {'tensor'}, dimensions={0}, use_global_device_ids=true | all-gather | bytes 278528 | tf_op jit(solution)/shard_map/all_gather | solution.py:29
  28.2 11.4 %fusion.4 = f32[16,1792]{1,0:T(8,128)S(1)} fusion(bf16[8192,1792]{1,0:T(8,128)(2,1)} %param.10, bf16[16,1,8192]{2,1,0:T(2,128)(2,1)S(1)} %all-gather), kind=kOutput, calls=%fused_computation.6 | convolution fusion | flops 469762048 | bytes 29736960 | tf_op jit(solution)/shard_map/dot_general | solution.py:30
  39.7 0.0 copy-start.1
  39.7 0.0 copy-start
  39.7 0.0 copy-start.2
  39.7 21.1 %fusion = bf16[1,16,8192]{2,1,0:T(8,128)(2,1)S(1)} fusion(bf16[1792,8192]{1,0:T(8,128)(2,1)} %param.12, bf16[8192,1792]{1,0:T(8,128)(2,1)} %param.11, f32[16,1792]{1,0:T(8,128)S(1)} %fusion.4, bf16[16,1,8192]{2,1,0:T(2,128)(2,1)S(1)} %all-gather), kind=kOutput, calls=%fused_computation.1 | convolution fusion | flops 939827200 | bytes 59359232 | tf_op jit(solution)/shard_map/dot_general | solution.py:33
  60.8 0.5 copy.21
  61.3 0.5 broadcast.42
  61.8 2.2 %reduce.9 = bf16[16,8192]{1,0:T(8,128)(2,1)S(1)} reduce(bf16[16,1,8192]{2,1,0:T(2,128)(2,1)S(1)} %bitcast.27, bf16[]{:T(256)} %broadcast.42), dimensions={1}, to_apply=%bitcast.26.reduce_sub_computation | reduce | bytes 524290
  64.0 0.9 %reshape.90 = bf16[16,2,4096]{2,1,0:T(2,128)(2,1)} reshape(bf16[16,8192]{1,0:T(8,128)(2,1)S(1)} %reduce.9) | data formatting | bytes 524288
  64.9 3.5 %all-to-all-start = ((bf16[16,2,4096]{2,1,0:T(2,128)(2,1)}), bf16[16,2,4096]{2,1,0:T(2,128)(2,1)S(1)}, u32[]{:S(2)}, u32[]{:S(2)}) async-start(bf16[16,2,4096]{2,1,0:T(2,128)(2,1)} %reshape.90), calls=%async_computation | async-start | bytes 524288 | tf_op jit(solution)/shard_map/all_to_all | solution.py:36
  68.4 0.0 copy-done.1
  68.4 0.2 reduce-window.8
  68.6 0.0 copy-done
  68.6 0.0 copy-done.2
  68.6 0.7 select_reduce_fusion
  71.2 7.2 %all-to-all-done = bf16[16,2,4096]{2,1,0:T(2,128)(2,1)S(1)} async-done(((bf16[16,2,4096]{2,1,0:T(2,128)(2,1)}), bf16[16,2,4096]{2,1,0:T(2,128)(2,1)S(1)}, u32[]{:S(2)}, u32[]{:S(2)}) %all-to-all-start) | async-done | bytes 262176 | tf_op jit(solution)/shard_map/all_to_all | solution.py:36
  78.4 0.3 reshape.91
  78.7 0.6 convert_reduce_fusion
  79.3 0.6 convert_element_type.46
  (1 shorter events, 0.0 us)
Async XLA Ops:
  39.7 28.7 %copy-start.1 = (s32[8]{0:T(128)S(1)}, s32[8]{0:T(128)}, u32[]{:S(2)}) copy-start(s32[8]{0:T(128)} %param.13) | copy-start | bytes 100
  39.7 28.9 %copy-start = (s32[8]{0:T(128)S(1)}, s32[8]{0:T(128)}, u32[]{:S(2)}) copy-start(s32[8]{0:T(128)} %param.14) | copy-start | bytes 100
  39.7 28.9 %copy-start.2 = (s32[8]{0:T(128)S(1)}, s32[8]{0:T(128)}, u32[]{:S(2)}) copy-start(s32[8]{0:T(128)} %param.15) | copy-start | bytes 100
  64.9 13.5 %all-to-all-start = ((bf16[16,2,4096]{2,1,0:T(2,128)(2,1)}), bf16[16,2,4096]{2,1,0:T(2,128)(2,1)S(1)}, u32[]{:S(2)}, u32[]{:S(2)}) async-start(bf16[16,2,4096]{2,1,0:T(2,128)(2,1)} %reshape.90), calls=%async_computation | async-start | bytes 524288 | tf_op jit(solution)/shard_map/all_to_all | solution.py:36
where the time goes:
time: 80.4 us; the launch traced here: 79.9 us
  matrix products  32.5 us (40%)
  blocking collectives  24.6 us (31%)
  waiting for transfers between devices  7.19 us (9%)
  other arithmetic  6.62 us (8%)
  starting transfers between devices  3.53 us (4%)
  local copies, waits for them, and re-layouts  2.81 us (3%)
  between operations  2.69 us (3%)
    all_gather x1, blocking collectives, local(): piece_rows = lax.all_gather(normed, 'tensor', axis=0, tiled=True)  24.6 us
    dot_general x1, matrix products, local(): partial_value = jnp.dot(hidden, w_down, preferred_element_type=jnp.float32)  21.1 us
    dot_general x1, matrix products, local(): gate_out = jnp.dot(piece_rows, w_gate, preferred_element_type=jnp.float32)  11.4 us
    all_to_all x1, waiting for transfers between devices, local(): lax.all_to_all(rounded[None], 'tensor', split_axis=1, concat_axis=0, tile...  7.19 us
    all_to_all x1, starting transfers between devices, local(): lax.all_to_all(rounded[None], 'tensor', split_axis=1, concat_axis=0, tile...  3.53 us
    unnamed x2, other arithmetic  2.98 us
    unnamed x9, local copies, waits for them, and re-layouts  1.67 us
  transfers between devices with their start and end apart: 1, of which 1 were waited for; matrix products, arithmetic and copies ran while one was open for 1% of the time, Pallas kernels for 0%

commit v1 on v0

--- a/solution.py
+++ b/solution.py
@@ -1,7 +1,14 @@
+import functools
+
 import jax
 import jax.numpy as jnp
 from jax import lax
+from jax.experimental import pallas as pl
+from jax.experimental.pallas import tpu as pltpu
 from jax.sharding import PartitionSpec as P
+
+LANES = 128
+BOTH = ("groups", "tensor")
 
 
 def normalize(tokens, norm_gain):
@@ -43,6 +50,135 @@
     return jnp.where(live[:, None], totals, jnp.zeros_like(totals)).astype(jnp.bfloat16)
 
 
+def load_kernel(half, gate_hbm, up_hbm, down_hbm, both_vmem, down_vmem, sems):
+    own = pl.multiple_of(lax.axis_index("groups") * half, LANES)
+    copies = [
+        pltpu.make_async_copy(
+            gate_hbm.at[:, pl.ds(own, half)], both_vmem.at[:, pl.ds(0, half)], sems.at[0]
+        ),
+        pltpu.make_async_copy(
+            up_hbm.at[:, pl.ds(own, half)], both_vmem.at[:, pl.ds(half, half)], sems.at[1]
+        ),
+        pltpu.make_async_copy(down_hbm.at[pl.ds(own, half), :], down_vmem, sems.at[2]),
+    ]
+    for copy in copies:
+        copy.start()
+    for copy in copies:
+        copy.wait()
+
+
+def load_weights(w_gate, w_up, w_down, half):
+    depth = w_gate.shape[0]
+    width = w_down.shape[1]
+    return pl.pallas_call(
+        functools.partial(load_kernel, half),
+        out_shape=(
+            pltpu.VMEM((depth, 2 * half), w_gate.dtype),
+            pltpu.VMEM((half, width), w_down.dtype),
+        ),
+        in_specs=[pl.BlockSpec(memory_space=pl.ANY)] * 3,
+        out_specs=(
+            pl.BlockSpec(memory_space=pltpu.VMEM),
+            pl.BlockSpec(memory_space=pltpu.VMEM),
+        ),
+        scratch_shapes=[pltpu.SemaphoreType.DMA((3,))],
+        compiler_params=pltpu.CompilerParams(vmem_limit_bytes=1 << 20),
+        cost_estimate=pl.CostEstimate(
+            flops=0, bytes_accessed=3 * depth * half * 2, transcendentals=0
+        ),
+        name="load_weights",
+    )(w_gate, w_up, w_down)
+
+
+def block_kernel(
+    half, tokens_ref, gain_ref, both_ref, down_ref, out_ref, wide_ref, normed_ref, hidden_ref
+):
+    rows, lines, lanes = tokens_ref.shape
+    depth = lines * lanes
+    wide_ref[...] = tokens_ref[...].astype(jnp.float32)
+    squares = wide_ref[:, 0, :] * wide_ref[:, 0, :]
+    for line in range(1, lines):
+        value = wide_ref[:, line, :]
+        squares = squares + value * value
+    scale = lax.rsqrt(jnp.sum(squares, axis=-1, keepdims=True) * (1.0 / depth) + 1e-05)
+    for line in range(lines):
+        columns = pl.ds(line * lanes, lanes)
+        normed_ref[:, columns] = (
+            wide_ref[:, line, :] * scale * gain_ref[:, columns].astype(jnp.float32)
+        ).astype(jnp.bfloat16)
+    tile = 256
+    parts = []
+    for at in range(0, 2 * half, tile):
+        parts.append(
+            jnp.dot(
+                normed_ref[...], both_ref[:, pl.ds(at, tile)], preferred_element_type=jnp.float32
+            )
+        )
+    product = jnp.concatenate(parts, axis=1)
+    gate_out = product[:, :half]
+    up_out = product[:, half:]
+    hidden_ref[...] = (gate_out / (1.0 + jnp.exp(-gate_out)) * up_out).astype(jnp.bfloat16)
+    for at in range(0, depth, tile):
+        result = jnp.dot(
+            hidden_ref[...], down_ref[:, pl.ds(at, tile)], preferred_element_type=jnp.float32
+        )
+        for step in range(tile // lanes):
+            wide_ref[:, at // lanes + step, :] = result[:, step * lanes : (step + 1) * lanes]
+    out_ref[...] = wide_ref[...].astype(jnp.bfloat16)
+
+
+def block(tokens, gain, both, down, half):
+    rows, lines, lanes = tokens.shape
+    depth = lines * lanes
+    vmem = pl.BlockSpec(memory_space=pltpu.VMEM)
+    return pl.pallas_call(
+        functools.partial(block_kernel, half),
+        out_shape=jax.ShapeDtypeStruct(tokens.shape, jnp.bfloat16),
+        in_specs=[vmem] * 4,
+        out_specs=vmem,
+        scratch_shapes=[
+            pltpu.VMEM(tokens.shape, jnp.float32),
+            pltpu.VMEM((rows, depth), jnp.bfloat16),
+            pltpu.VMEM((rows, half), jnp.bfloat16),
+        ],
+        compiler_params=pltpu.CompilerParams(vmem_limit_bytes=12 << 20),
+        cost_estimate=pl.CostEstimate(
+            flops=6 * rows * depth * half, bytes_accessed=2 * rows * depth * 2, transcendentals=0
+        ),
+        name="block",
+    )(
+        tokens,
+        gain,
+        pltpu.with_memory_space_constraint(both, pltpu.VMEM),
+        pltpu.with_memory_space_constraint(down, pltpu.VMEM),
+    )
+
+
+def shared(tokens, norm_gain, w_gate, w_up, w_down, lengths, hit_lengths, start_positions):
+    row_count, depth = tokens.shape
+    members = lax.axis_size("groups") * lax.axis_size("tensor")
+    half = w_gate.shape[1] // lax.axis_size("groups")
+    mine = tokens.reshape(1, row_count, depth // LANES, LANES)
+    everywhere = jnp.broadcast_to(mine, (members,) + mine.shape[1:])
+    gathered = lax.all_to_all(everywhere, BOTH, split_axis=0, concat_axis=0, tiled=True)
+    both, down = load_weights(w_gate, w_up, w_down, half)
+    partials = block(
+        gathered.reshape(members * row_count, depth // LANES, LANES),
+        norm_gain.reshape(1, depth),
+        both,
+        down,
+        half,
+    )
+    arrived = lax.all_to_all(
+        partials.reshape((members,) + mine.shape[1:]), BOTH, split_axis=0, concat_axis=0, tiled=True
+    )
+    totals = jnp.sum(arrived.astype(jnp.float32), axis=0)
+    token_index = lax.axis_index("tensor") * row_count + jnp.arange(row_count, dtype=jnp.int32)
+    live = live_rows(lengths, hit_lengths, start_positions, token_index)
+    kept = jnp.where(live[:, None, None], totals, jnp.zeros_like(totals)).astype(jnp.bfloat16)
+    return kept.reshape(row_count, depth)
+
+
 def solution(mesh):
     placed = (
         P(("groups", "tensor"), None),
@@ -54,6 +190,17 @@
         P("groups"),
         P("groups"),
     )
-    return jax.shard_map(
-        local, mesh=mesh, in_specs=placed, out_specs=P(("groups", "tensor"), None), check_vma=False
-    )
+
+    def run(*arrays):
+        units = arrays[2].shape[1] // mesh.shape["tensor"]
+        halves = units % (LANES * mesh.shape["groups"]) == 0
+        body = shared if halves else local
+        return jax.shard_map(
+            body,
+            mesh=mesh,
+            in_specs=placed,
+            out_specs=P(("groups", "tensor"), None),
+            check_vma=False,
+        )(*arrays)
+
+    return run

time: 80.4 us -> 89.1 us (1.11)
  matrix products: 32.5 us -> 0 us
  local copies, waits for them, and re-layouts: 2.81 us -> 33.1 us
  Pallas kernels: 0 us -> 25.2 us
  blocking collectives: 24.6 us -> 0 us
  starting transfers between devices: 3.53 us -> 13.4 us
  waiting for transfers between devices: 7.19 us -> 13.1 us
  other arithmetic: 6.62 us -> 1.84 us
    dot_general x2 -> x0, matrix products: 32.5 us -> none  [the longest x1 21.1 us: local(): partial_value = jnp.dot(hidden, w_down, preferred_element_type=jnp.float32)]
    unnamed x9 -> x17, local copies, waits for them, and re-layouts: 1.67 us -> 30.9 us
    pallas_call x0 -> x2, Pallas kernels: none -> 25.2 us  [the longest x1 13.9 us: load_weights(): pl.pallas_call(functools.partial(load_kernel, half), out_shape=(pltpu.VME...]
    all_gather x1 -> x0, blocking collectives: 24.6 us -> none  [local(): piece_rows = lax.all_gather(normed, 'tensor', axis=0, tiled=True)]
    all_to_all x1 -> x2, starting transfers between devices: 3.53 us -> 13.4 us  [the longest x1 7.3 us: shared(): lax.all_to_all(everywhere, BOTH, split_axis=0, concat_axis=0, tiled=True)]
    all_to_all x1 -> x2, waiting for transfers between devices: 7.19 us -> 13.1 us  [the longest x1 13.1 us: shared(): lax.all_to_all(partials.reshape((members,) + mine.shape[1:]), BOTH, split...]
    unnamed x2, other arithmetic: 2.98 us -> 0.86 us
    reduce_sum x2 -> x1, other arithmetic: 2.03 us -> 0.08 us  [shared(): totals = jnp.sum(arrived.astype(jnp.float32), axis=0)]
  transfers between devices with their start and end apart: 1 -> 2, of which waited for: 1 -> 1; matrix products, arithmetic and copies ran while one was open for 1% -> 3% of each run, Pallas kernels for 0% -> 16%
where the time goes in v1:
time: 89.1 us; the launch traced here: 88.6 us
  local copies, waits for them, and re-layouts  33.1 us (37%)
  Pallas kernels  25.2 us (28%)
  starting transfers between devices  13.4 us (15%)
  waiting for transfers between devices  13.1 us (15%)
  between operations  1.98 us (2%)
  other arithmetic  1.84 us (2%)
    unnamed x17, local copies, waits for them, and re-layouts  30.9 us
    pallas_call x1, Pallas kernels, load_weights(): pl.pallas_call(functools.partial(load_kernel, half), out_shape=(pltpu.VME...  13.9 us
    all_to_all x1, waiting for transfers between devices, shared(): lax.all_to_all(partials.reshape((members,) + mine.shape[1:]), BOTH, split...  13.1 us
    pallas_call x1, Pallas kernels, block(): pl.pallas_call(functools.partial(block_kernel, half), out_shape=jax.Shape...  11.4 us
    all_to_all x1, starting transfers between devices, shared(): lax.all_to_all(everywhere, BOTH, split_axis=0, concat_axis=0, tiled=True)  7.3 us
    all_to_all x1, starting transfers between devices, shared(): lax.all_to_all(partials.reshape((members,) + mine.shape[1:]), BOTH, split...  6.08 us
  transfers between devices with their start and end apart: 2, of which 1 were waited for; matrix products, arithmetic and copies ran while one was open for 3% of the time, Pallas kernels for 16%

profile of v1, /device:TPU:0, one launch (start us, length us, event | category | flops | bytes accessed | tf_op | source)
XLA Modules:
  0.0 88.6 jit_solution(38010731459069514)
XLA Ops:
  0.0 0.8 reduce.7
  0.8 0.9 %broadcast_in_dim.26 = bf16[32,1,64,128]{3,2,1,0:T(8,128)(2,1)} broadcast(bf16[64,128]{1,0:T(8,128)(2,1)S(1)} %bitcast.21), dimensions={2,3} | broadcast | bytes 540672 | tf_op jit(solution)/shard_map/broadcast_in_dim | solution.py:162
  1.8 7.3 %all-to-all-start = ((bf16[32,1,64,128]{3,2,1,0:T(8,128)(2,1)}), bf16[32,1,64,128]{3,2,1,0:T(8,128)(2,1)S(1)}, u32[]{:S(2)}, u32[]{:S(2)}) async-start(bf16[32,1,64,128]{3,2,1,0:T(8,128)(2,1)} %broadcast_in_dim.26), calls=%async_computation | async-start | bytes 1048576 | tf_op jit(solution)/shard_map/all_to_all | solution.py:163
  9.1 1.4 %reshape.81.gain_ref = bf16[1,8192]{1,0:T(2,128)(2,1)} reshape(bf16[8192]{0:T(1024)(128)(2,1)} %param.9) | data formatting | bytes 32768 | tf_op jit(solution)/shard_map/reshape | solution.py:167
  10.4 13.9 %load_weights.1 = (bf16[8192,1792]{1,0:T(8,128)(2,1)S(1)}, bf16[896,8192]{1,0:T(8,128)(2,1)S(1)}) custom-call(bf16[8192,1792]{1,0:T(8,128)(2,1)} %gate_hbm.1, bf16[8192,1792]{1,0:T(8,128)(2,1)} %up_hbm.1, bf16[1792,8192]{1,0:T(8,128)(2,1)} %down_hbm.1), custom_call_target="tpu_custom_call" | custom-call | bytes 44040192 | tf_op jit(solution)/shard_map/load_weights/pallas_call | solution.py:73
  24.3 0.0 copy-start
  24.3 9.7 %copy-done = bf16[8192,1792]{1,0:T(8,128)(2,1)} copy-done((bf16[8192,1792]{1,0:T(8,128)(2,1)}, bf16[8192,1792]{1,0:T(8,128)(2,1)S(1)}, u32[]{:S(2)}) %copy-start) | copy-done | bytes 29360152
  34.0 0.0 copy-start.2
  34.0 5.2 %copy-done.2 = bf16[896,8192]{1,0:T(8,128)(2,1)} copy-done((bf16[896,8192]{1,0:T(8,128)(2,1)}, bf16[896,8192]{1,0:T(8,128)(2,1)S(1)}, u32[]{:S(2)}) %copy-start.2) | copy-done | bytes 14680088
  39.2 0.0 copy-start.6
  39.2 0.0 copy-start.5
  39.2 0.0 copy-start.7
  39.2 0.0 all-to-all-done
  39.2 0.0 copy-start.4
  39.2 0.8 copy-done.4
  40.0 0.0 copy-start.1
  40.0 9.3 %copy-done.1 = bf16[8192,1792]{1,0:T(8,128)(2,1)S(1)} copy-done((bf16[8192,1792]{1,0:T(8,128)(2,1)S(1)}, bf16[8192,1792]{1,0:T(8,128)(2,1)}, u32[]{:S(2)}) %copy-start.1) | copy-done | bytes 29360152
  49.4 0.0 copy-start.3
  49.4 5.2 %copy-done.3 = bf16[896,8192]{1,0:T(8,128)(2,1)S(1)} copy-done((bf16[896,8192]{1,0:T(8,128)(2,1)S(1)}, bf16[896,8192]{1,0:T(8,128)(2,1)}, u32[]{:S(2)}) %copy-start.3) | copy-done | bytes 14680088
  54.5 11.4 %block.1 = bf16[32,64,128]{2,1,0:T(8,128)(2,1)} custom-call(bf16[32,64,128]{2,1,0:T(8,128)(2,1)} %bitcast.20, bf16[1,8192]{1,0:T(2,128)(2,1)} %reshape.81.gain_ref, bf16[8192,1792]{1,0:T(8,128)(2,1)S(1)} %copy-done.1, bf16[896,8192]{1,0:T(8,128)(2,1)S(1)} %copy-done.3), custom_call_target="tpu_custom_call" | custom-call | flops 1409286144 | bytes 1048576 | tf_op jit(solution)/shard_map/block/pallas_call | solution.py:134
  65.9 6.1 %all-to-all-start.1 = ((bf16[32,1,64,128]{3,2,1,0:T(8,128)(2,1)}), bf16[32,1,64,128]{3,2,1,0:T(8,128)(2,1)S(1)}, u32[]{:S(2)}, u32[]{:S(2)}) async-start(bf16[32,1,64,128]{3,2,1,0:T(8,128)(2,1)} %bitcast.19), calls=%async_computation.1 | async-start | bytes 1048576 | tf_op jit(solution)/shard_map/all_to_all | solution.py:172
  72.0 0.0 copy-done.6
  72.0 0.2 reduce-window.8
  72.2 0.0 copy-done.5
  72.2 0.0 copy-done.7
  72.2 0.7 select_reduce_fusion
  74.8 13.1 %all-to-all-done.1 = bf16[32,1,64,128]{3,2,1,0:T(8,128)(2,1)S(1)} async-done(((bf16[32,1,64,128]{3,2,1,0:T(8,128)(2,1)}), bf16[32,1,64,128]{3,2,1,0:T(8,128)(2,1)S(1)}, u32[]{:S(2)}, u32[]{:S(2)}) %all-to-all-start.1) | async-done | bytes 524320 | tf_op jit(solution)/shard_map/all_to_all | solution.py:172
  87.9 0.1 convert_reduce_fusion
  88.0 0.6 copy.12
  (1 shorter events, 0.0 us)
Async XLA Ops:
  1.8 37.4 %all-to-all-start = ((bf16[32,1,64,128]{3,2,1,0:T(8,128)(2,1)}), bf16[32,1,64,128]{3,2,1,0:T(8,128)(2,1)S(1)}, u32[]{:S(2)}, u32[]{:S(2)}) async-start(bf16[32,1,64,128]{3,2,1,0:T(8,128)(2,1)} %broadcast_in_dim.26), calls=%async_computation | async-start | bytes 1048576 | tf_op jit(solution)/shard_map/all_to_all | solution.py:163
  24.3 9.7 %copy-start = (bf16[8192,1792]{1,0:T(8,128)(2,1)}, bf16[8192,1792]{1,0:T(8,128)(2,1)S(1)}, u32[]{:S(2)}) copy-start(bf16[8192,1792]{1,0:T(8,128)(2,1)S(1)} %get-tuple-element.7.both_ref) | copy-start | bytes 88080384
  34.0 5.2 %copy-start.2 = (bf16[896,8192]{1,0:T(8,128)(2,1)}, bf16[896,8192]{1,0:T(8,128)(2,1)S(1)}, u32[]{:S(2)}) copy-start(bf16[896,8192]{1,0:T(8,128)(2,1)S(1)} %get-tuple-element.8.down_ref) | copy-start | bytes 44040196
  39.2 32.8 %copy-start.6 = (s32[8]{0:T(128)S(1)}, s32[8]{0:T(128)}, u32[]{:S(2)}) copy-start(s32[8]{0:T(128)} %param.13) | copy-start | bytes 100
  39.2 33.0 %copy-start.5 = (s32[8]{0:T(128)S(1)}, s32[8]{0:T(128)}, u32[]{:S(2)}) copy-start(s32[8]{0:T(128)} %param.14) | copy-start | bytes 100
  39.2 33.0 %copy-start.7 = (s32[8]{0:T(128)S(1)}, s32[8]{0:T(128)}, u32[]{:S(2)}) copy-start(s32[8]{0:T(128)} %param.15) | copy-start | bytes 100
  39.2 0.8 copy-start.4
  40.0 9.4 %copy-start.1 = (bf16[8192,1792]{1,0:T(8,128)(2,1)S(1)}, bf16[8192,1792]{1,0:T(8,128)(2,1)}, u32[]{:S(2)}) copy-start(bf16[8192,1792]{1,0:T(8,128)(2,1)} %copy-done) | copy-start | bytes 88080384
  49.4 5.2 %copy-start.3 = (bf16[896,8192]{1,0:T(8,128)(2,1)S(1)}, bf16[896,8192]{1,0:T(8,128)(2,1)}, u32[]{:S(2)}) copy-start(bf16[896,8192]{1,0:T(8,128)(2,1)} %copy-done.2) | copy-start | bytes 44040196
  65.9 22.0 %all-to-all-start.1 = ((bf16[32,1,64,128]{3,2,1,0:T(8,128)(2,1)}), bf16[32,1,64,128]{3,2,1,0:T(8,128)(2,1)S(1)}, u32[]{:S(2)}, u32[]{:S(2)}) async-start(bf16[32,1,64,128]{3,2,1,0:T(8,128)(2,1)} %bitcast.19), calls=%async_computation.1 | async-start | bytes 1048576 | tf_op jit(solution)/shard_map/all_to_all | solution.py:172

commit v2 on v0

--- a/solution.py
+++ b/solution.py
@@ -1,7 +1,14 @@
+import functools
+
 import jax
 import jax.numpy as jnp
 from jax import lax
+from jax.experimental import pallas as pl
+from jax.experimental.pallas import tpu as pltpu
 from jax.sharding import PartitionSpec as P
+
+LANES = 128
+BOTH = ("groups", "tensor")
 
 
 def normalize(tokens, norm_gain):
@@ -43,6 +50,225 @@
     return jnp.where(live[:, None], totals, jnp.zeros_like(totals)).astype(jnp.bfloat16)
 
 
+def columns_of(tile, ref):
+    return [pl.ds(at, tile) for at in range(0, ref.shape[1], tile)]
+
+
+def load_kernel(half, gate_hbm, up_hbm, both_vmem, sems):
+    own = pl.multiple_of(lax.axis_index("groups") * half, LANES)
+    depth = both_vmem.shape[0]
+    copies = [
+        pltpu.make_async_copy(
+            weight.at[pl.ds(0, depth), pl.ds(own, half)],
+            both_vmem.at[:, pl.ds(at * half, half)],
+            sems.at[at],
+        )
+        for at, weight in enumerate((gate_hbm, up_hbm))
+    ]
+    for copy in copies:
+        copy.start()
+    for copy in copies:
+        copy.wait()
+
+
+def load_weights(w_gate, w_up, half, depth):
+    return pl.pallas_call(
+        functools.partial(load_kernel, half),
+        out_shape=pltpu.VMEM((depth, 2 * half), w_gate.dtype),
+        in_specs=[pl.BlockSpec(memory_space=pltpu.HBM)] * 2,
+        out_specs=pl.BlockSpec(memory_space=pltpu.VMEM),
+        scratch_shapes=[pltpu.SemaphoreType.DMA((2,))],
+        compiler_params=pltpu.CompilerParams(vmem_limit_bytes=1 << 20),
+        cost_estimate=pl.CostEstimate(
+            flops=0, bytes_accessed=2 * depth * half * 2, transcendentals=0
+        ),
+        name="load_weights",
+    )(w_gate, w_up)
+
+
+def block_kernel(
+    half,
+    chunk,
+    near_ref,
+    far_ref,
+    gain_ref,
+    first_ref,
+    gate_hbm,
+    up_hbm,
+    down_hbm,
+    out_ref,
+    wide_ref,
+    normed_ref,
+    product_ref,
+    hidden_ref,
+    rest_ref,
+    down_ref,
+    both_sems,
+    down_sems,
+):
+    tile = 256
+    rows, lines, lanes = out_ref.shape
+    depth = lines * lanes
+    loaded = first_ref.shape[0]
+    own = pl.multiple_of(lax.axis_index("groups") * half, LANES)
+    both_copies = []
+    for step, at in enumerate(range(0, depth - loaded, chunk)):
+        both_copies.append(
+            [
+                pltpu.make_async_copy(
+                    weight.at[pl.ds(loaded + at, chunk), pl.ds(own, half)],
+                    rest_ref.at[pl.ds(at, chunk), pl.ds(side * half, half)],
+                    both_sems.at[step, side],
+                )
+                for side, weight in enumerate((gate_hbm, up_hbm))
+            ]
+        )
+    down_copies = [
+        pltpu.make_async_copy(
+            down_hbm.at[pl.ds(own, half), pl.ds(at, chunk)],
+            down_ref.at[:, pl.ds(at, chunk)],
+            down_sems.at[step],
+        )
+        for step, at in enumerate(range(0, depth, chunk))
+    ]
+    for pair in both_copies:
+        for copy in pair:
+            copy.start()
+    for copy in down_copies:
+        copy.start()
+
+    wide_ref[: rows // 2] = near_ref[...].astype(jnp.float32)
+    wide_ref[rows // 2 :] = far_ref[...].astype(jnp.float32)
+    squares = wide_ref[:, 0, :] * wide_ref[:, 0, :]
+    for line in range(1, lines):
+        value = wide_ref[:, line, :]
+        squares = squares + value * value
+    scale = lax.rsqrt(jnp.sum(squares, axis=-1, keepdims=True) * (1.0 / depth) + 1e-05)
+    for line in range(lines):
+        columns = pl.ds(line * lanes, lanes)
+        normed_ref[:, columns] = (
+            wide_ref[:, line, :] * scale * gain_ref[:, columns].astype(jnp.float32)
+        ).astype(jnp.bfloat16)
+
+    for columns in columns_of(tile, product_ref):
+        product_ref[:, columns] = jnp.dot(
+            normed_ref[:, :loaded], first_ref[:, columns], preferred_element_type=jnp.float32
+        )
+    for step, pair in enumerate(both_copies):
+        for copy in pair:
+            copy.wait()
+        at = step * chunk
+        for columns in columns_of(tile, product_ref):
+            product_ref[:, columns] += jnp.dot(
+                normed_ref[:, loaded + at : loaded + at + chunk],
+                rest_ref[at : at + chunk, columns],
+                preferred_element_type=jnp.float32,
+            )
+    gate_out = product_ref[:, :half]
+    up_out = product_ref[:, half:]
+    hidden_ref[...] = (gate_out / (1.0 + jnp.exp(-gate_out)) * up_out).astype(jnp.bfloat16)
+    for step, copy in enumerate(down_copies):
+        copy.wait()
+        for at in range(step * chunk, (step + 1) * chunk, tile):
+            result = jnp.dot(
+                hidden_ref[...], down_ref[:, pl.ds(at, tile)], preferred_element_type=jnp.float32
+            )
+            for line in range(tile // lanes):
+                wide_ref[:, at // lanes + line, :] = result[:, line * lanes : (line + 1) * lanes]
+        lines_done = pl.ds(step * chunk // lanes, chunk // lanes)
+        out_ref[:, lines_done, :] = wide_ref[:, lines_done, :].astype(jnp.bfloat16)
+
+
+def block(near, far, gain, first, w_gate, w_up, w_down, half):
+    rows, lines, lanes = near.shape
+    rows = 2 * rows
+    depth = lines * lanes
+    chunk = 1024
+    rest = depth - first.shape[0]
+    vmem = pl.BlockSpec(memory_space=pltpu.VMEM)
+    hbm = pl.BlockSpec(memory_space=pltpu.HBM)
+    return pl.pallas_call(
+        functools.partial(block_kernel, half, chunk),
+        out_shape=jax.ShapeDtypeStruct((rows, lines, lanes), jnp.bfloat16),
+        in_specs=[vmem] * 4 + [hbm] * 3,
+        out_specs=vmem,
+        scratch_shapes=[
+            pltpu.VMEM((rows, lines, lanes), jnp.float32),
+            pltpu.VMEM((rows, depth), jnp.bfloat16),
+            pltpu.VMEM((rows, 2 * half), jnp.float32),
+            pltpu.VMEM((rows, half), jnp.bfloat16),
+            pltpu.VMEM((rest, 2 * half), jnp.bfloat16),
+            pltpu.VMEM((half, depth), jnp.bfloat16),
+            pltpu.SemaphoreType.DMA((rest // chunk, 2)),
+            pltpu.SemaphoreType.DMA((depth // chunk,)),
+        ],
+        compiler_params=pltpu.CompilerParams(
+            vmem_limit_bytes=(rest * 2 + depth) * half * 2 + (6 << 20)
+        ),
+        cost_estimate=pl.CostEstimate(
+            flops=6 * rows * depth * half,
+            bytes_accessed=(rest * 2 + depth) * half * 2,
+            transcendentals=0,
+        ),
+        name="block",
+    )(near, far, gain, pltpu.with_memory_space_constraint(first, pltpu.VMEM), w_gate, w_up, w_down)
+
+
+def swap(value, offset):
+    members = lax.axis_size("groups") * lax.axis_size("tensor")
+    return lax.ppermute(value, BOTH, [(place, place ^ offset) for place in range(members)])
+
+
+def stages(members):
+    bits = members.bit_length() - 1
+    core, column, group = (0,), (1, bits - 1), tuple(range(2, bits - 1))
+    return [[1 << bit for bit in stage] for stage in (group, column, core)]
+
+
+def offsets(steps):
+    found = [0]
+    for step in steps:
+        found = found + [at + step for at in found]
+    return found
+
+
+def gather(value, members):
+    early, late, last = stages(members)
+    for steps in (early, late):
+        value = jnp.concatenate(
+            [swap(value, at) if at else value for at in offsets(steps)], axis=0
+        )
+    return value, swap(value, last[0])
+
+
+def scatter_sum(value, members):
+    for steps in reversed(stages(members)):
+        reach = offsets(steps)
+        pieces = jnp.split(value, len(reach), axis=0)
+        total = pieces[0].astype(jnp.float32)
+        for at, piece in zip(reach[1:], pieces[1:]):
+            total = total + swap(piece.astype(jnp.bfloat16), at).astype(jnp.float32)
+        value = total.astype(jnp.bfloat16)
+    return total
+
+
+def shared(tokens, norm_gain, w_gate, w_up, w_down, lengths, hit_lengths, start_positions):
+    row_count, depth = tokens.shape
+    members = lax.axis_size("groups") * lax.axis_size("tensor")
+    half = w_gate.shape[1] // lax.axis_size("groups")
+    token_index = lax.axis_index("tensor") * row_count + jnp.arange(row_count, dtype=jnp.int32)
+    live = live_rows(lengths, hit_lengths, start_positions, token_index)
+    near, far = gather(tokens.reshape(row_count, depth // LANES, LANES), members)
+    w_gate, w_up, w_down = (
+        pltpu.with_memory_space_constraint(weight, pltpu.HBM) for weight in (w_gate, w_up, w_down)
+    )
+    first = load_weights(w_gate, w_up, half, depth // 2)
+    partials = block(near, far, norm_gain.reshape(1, depth), first, w_gate, w_up, w_down, half)
+    totals = scatter_sum(partials, members)
+    kept = jnp.where(live[:, None, None], totals, jnp.zeros_like(totals)).astype(jnp.bfloat16)
+    return kept.reshape(row_count, depth)
+
+
 def solution(mesh):
     placed = (
         P(("groups", "tensor"), None),
@@ -54,6 +280,24 @@
         P("groups"),
         P("groups"),
     )
-    return jax.shard_map(
-        local, mesh=mesh, in_specs=placed, out_specs=P(("groups", "tensor"), None), check_vma=False
-    )
+
+    def run(*arrays):
+        units = arrays[2].shape[1] // mesh.shape["tensor"]
+        members = mesh.shape["groups"] * mesh.shape["tensor"]
+        halves = (
+            units % (LANES * mesh.shape["groups"]) == 0
+            and arrays[0].shape[0] == members
+            and mesh.shape["groups"] == 2
+            and members & (members - 1) == 0
+            and members >= 8
+        )
+        body = shared if halves else local
+        return jax.shard_map(
+            body,
+            mesh=mesh,
+            in_specs=placed,
+            out_specs=P(("groups", "tensor"), None),
+            check_vma=False,
+        )(*arrays)
+
+    return run

time: 80.4 us -> 59 us (0.73)
  matrix products: 32.5 us -> 0 us
  blocking collectives: 24.6 us -> 0 us
  Pallas kernels: 0 us -> 21.1 us
  starting transfers between devices: 3.53 us -> 17.9 us
  waiting for transfers between devices: 7.19 us -> 14.3 us
  other arithmetic: 6.62 us -> 1.92 us
  local copies, waits for them, and re-layouts: 2.81 us -> 1.5 us
    dot_general x2 -> x0, matrix products: 32.5 us -> none  [the longest x1 21.1 us: local(): partial_value = jnp.dot(hidden, w_down, preferred_element_type=jnp.float32)]
    all_gather x1 -> x0, blocking collectives: 24.6 us -> none  [local(): piece_rows = lax.all_gather(normed, 'tensor', axis=0, tiled=True)]
    pallas_call x0 -> x2, Pallas kernels: none -> 21.1 us  [the longest x1 15.7 us: block(): pl.pallas_call(functools.partial(block_kernel, half, chunk), out_shape=ja...]
    ppermute x0 -> x14, starting transfers between devices: none -> 17.9 us  [swap(): lax.ppermute(value, BOTH, [(place, place ^ offset) for place in range(mem...]
    ppermute x0 -> x14, waiting for transfers between devices: none -> 14.3 us  [swap(): lax.ppermute(value, BOTH, [(place, place ^ offset) for place in range(mem...]
    all_to_all x1 -> x0, waiting for transfers between devices: 7.19 us -> none  [local(): lax.all_to_all(rounded[None], 'tensor', split_axis=1, concat_axis=0, tile...]
    all_to_all x1 -> x0, starting transfers between devices: 3.53 us -> none  [local(): lax.all_to_all(rounded[None], 'tensor', split_axis=1, concat_axis=0, tile...]
    unnamed x2, other arithmetic: 2.98 us -> 0.86 us
  transfers between devices with their start and end apart: 1 -> 14, of which waited for: 1 -> 8; matrix products, arithmetic and copies ran while one was open for 1% -> 3% of each run, Pallas kernels for 0% -> 9%
where the time goes in v2:
time: 59 us; the launch traced here: 58.8 us
  Pallas kernels  21.1 us (36%)
  starting transfers between devices  17.9 us (30%)
  waiting for transfers between devices  14.3 us (24%)
  between operations  2.05 us (3%)
  other arithmetic  1.92 us (3%)
  local copies, waits for them, and re-layouts  1.5 us (3%)
    ppermute x14, starting transfers between devices, swap(): lax.ppermute(value, BOTH, [(place, place ^ offset) for place in range(mem...  17.9 us
    pallas_call x1, Pallas kernels, block(): pl.pallas_call(functools.partial(block_kernel, half, chunk), out_shape=ja...  15.7 us
    ppermute x14, waiting for transfers between devices, swap(): lax.ppermute(value, BOTH, [(place, place ^ offset) for place in range(mem...  14.3 us
    pallas_call x1, Pallas kernels, load_weights(): pl.pallas_call(functools.partial(load_kernel, half), out_shape=pltpu.VMEM...  5.44 us
  transfers between devices with their start and end apart: 14, of which 8 were waited for; matrix products, arithmetic and copies ran while one was open for 3% of the time, Pallas kernels for 9%

profile of v2, /device:TPU:0, one launch (start us, length us, event | category | flops | bytes accessed | tf_op | source)
XLA Modules:
  0.0 58.8 jit_solution(1181543857302843875)
XLA Ops:
  0.0 0.8 %reduce.6 = bf16[8192]{0:T(1024)(128)(2,1)S(1)} reduce(bf16[1,8192]{1,0:T(2,128)(2,1)} %param.8, bf16[]{:T(256)} %constant.15), dimensions={0}, to_apply=%param.8.reduce_sub_computation | reduce | bytes 32770 | tf_op args[0]
  0.8 3.1 %collective-permute-start = (bf16[1,64,128]{2,1,0:T(8,128)(2,1)S(1)}, bf16[1,64,128]{2,1,0:T(8,128)(2,1)S(1)}, u32[]{:S(2)}, u32[]{:S(2)}) collective-permute-start(bf16[1,64,128]{2,1,0:T(8,128)(2,1)S(1)} %bitcast.15), channel_id=1, source_target_pairs={{0,4},{1,5},{2,6},{3,7},{4,0},{5,1},{6,2},{7,3},{8,12},{9,13},{10,... | collective-permute-start | bytes 49160 | tf_op jit(solution)/shard_map/ppermute | solution.py:219
  3.9 2.6 %collective-permute-start.1 = (bf16[1,64,128]{2,1,0:T(8,128)(2,1)S(1)}, bf16[1,64,128]{2,1,0:T(8,128)(2,1)S(1)}, u32[]{:S(2)}, u32[]{:S(2)}) collective-permute-start(bf16[1,64,128]{2,1,0:T(8,128)(2,1)S(1)} %bitcast.16), channel_id=1, source_target_pairs={{0,8},{1,9},{2,10},{3,11},{4,12},{5,13},{6,14},{7,15},{8,0},{9,1},... | collective-permute-start | bytes 49160 | tf_op jit(solution)/shard_map/ppermute | solution.py:219
  6.5 0.0 collective-permute-start.2
  6.5 0.0 collective-permute-done
  6.5 2.1 %collective-permute-done.1 = bf16[1,64,128]{2,1,0:T(8,128)(2,1)S(1)} collective-permute-done((bf16[1,64,128]{2,1,0:T(8,128)(2,1)S(1)}, bf16[1,64,128]{2,1,0:T(8,128)(2,1)S(1)}, u32[]{:S(2)}, u32[]{:S(2)}) %collective-permute-start.1) | collective-permute-done | bytes 16416 | tf_op jit(solution)/shard_map/ppermute | solution.py:219
  8.7 3.4 %collective-permute-done.2 = bf16[1,64,128]{2,1,0:T(8,128)(2,1)S(1)} collective-permute-done((bf16[1,64,128]{2,1,0:T(8,128)(2,1)S(1)}, bf16[1,64,128]{2,1,0:T(8,128)(2,1)S(1)}, u32[]{:S(2)}, u32[]{:S(2)}) %collective-permute-start.2) | collective-permute-done | bytes 16416 | tf_op jit(solution)/shard_map/ppermute | solution.py:219
  12.1 1.6 %collective-permute-start.3 = (bf16[4,64,128]{2,1,0:T(8,128)(2,1)S(1)}, bf16[4,64,128]{2,1,0:T(8,128)(2,1)S(1)}, u32[]{:S(2)}, u32[]{:S(2)}) collective-permute-start(bf16[4,64,128]{2,1,0:T(8,128)(2,1)S(1)} %pad_maximum_fusion), channel_id=1, source_target_pairs={{0,2},{1,3},{2,0},{3,1},{4,6},{5,7},{6,4},{7,5},{8,10},{9,11},{10,... | collective-permute-start | bytes 196616 | tf_op jit(solution)/shard_map/ppermute | solution.py:219
  13.6 1.5 %collective-permute-start.4 = (bf16[4,64,128]{2,1,0:T(8,128)(2,1)S(1)}, bf16[4,64,128]{2,1,0:T(8,128)(2,1)S(1)}, u32[]{:S(2)}, u32[]{:S(2)}) collective-permute-start(bf16[4,64,128]{2,1,0:T(8,128)(2,1)S(1)} %pad_maximum_fusion), channel_id=1, source_target_pairs={{0,16},{1,17},{2,18},{3,19},{4,20},{5,21},{6,22},{7,23},{8,24},{9,... | collective-permute-start | bytes 196616 | tf_op jit(solution)/shard_map/ppermute | solution.py:219
  15.2 0.5 collective-permute-start.5
  15.7 1.0 %collective-permute-done.3 = bf16[4,64,128]{2,1,0:T(8,128)(2,1)S(1)} collective-permute-done((bf16[4,64,128]{2,1,0:T(8,128)(2,1)S(1)}, bf16[4,64,128]{2,1,0:T(8,128)(2,1)S(1)}, u32[]{:S(2)}, u32[]{:S(2)}) %collective-permute-start.3) | collective-permute-done | bytes 65568 | tf_op jit(solution)/shard_map/ppermute | solution.py:219
  16.7 1.2 %collective-permute-done.4 = bf16[4,64,128]{2,1,0:T(8,128)(2,1)S(1)} collective-permute-done((bf16[4,64,128]{2,1,0:T(8,128)(2,1)S(1)}, bf16[4,64,128]{2,1,0:T(8,128)(2,1)S(1)}, u32[]{:S(2)}, u32[]{:S(2)}) %collective-permute-start.4) | collective-permute-done | bytes 65568 | tf_op jit(solution)/shard_map/ppermute | solution.py:219
  17.9 2.4 %collective-permute-done.5 = bf16[4,64,128]{2,1,0:T(8,128)(2,1)S(1)} collective-permute-done((bf16[4,64,128]{2,1,0:T(8,128)(2,1)S(1)}, bf16[4,64,128]{2,1,0:T(8,128)(2,1)S(1)}, u32[]{:S(2)}, u32[]{:S(2)}) %collective-permute-start.5) | collective-permute-done | bytes 65568 | tf_op jit(solution)/shard_map/ppermute | solution.py:219
  20.3 0.1 collective-permute-start.6
  20.4 0.7 %reshape.54.gain_ref = bf16[1,8192]{1,0:T(2,128)(2,1)S(1)} reshape(bf16[8192]{0:T(1024)(128)(2,1)} %param.9) | data formatting | bytes 32768 | tf_op jit(solution)/shard_map/reshape | solution.py:266
  21.2 5.4 %load_weights.1.first_ref = bf16[4096,1792]{1,0:T(8,128)(2,1)S(1)} custom-call(bf16[8192,1792]{1,0:T(8,128)(2,1)} %gate_hbm.3, bf16[8192,1792]{1,0:T(8,128)(2,1)} %up_hbm.3), custom_call_target="tpu_custom_call" | custom-call | bytes 14680064 | tf_op jit(solution)/shard_map/load_weights/pallas_call | solution.py:75
  26.6 0.0 copy-start.1
  26.6 0.0 copy-start
  26.6 0.0 copy-start.2
  26.6 0.0 collective-permute-done.6.far_ref
  26.6 15.7 %block.1 = bf16[32,64,128]{2,1,0:T(8,128)(2,1)S(1)} custom-call(bf16[16,64,128]{2,1,0:T(8,128)(2,1)S(1)} %constant_dynamic-update-slice_fusion.near_ref, bf16[16,64,128]{2,1,0:T(8,128)(2,1)S(1)} %collective-permute-done.6.far_ref, bf16[1,8192]{1,0:T(2,128)(2,1)S(1)} %reshape.54.gain_ref, bf16[4096,1792]{1,0:T(8,128)(2,1)S(1)} %load_weights.1.first_ref, ...), custom_call_target="tpu_custom_call" | custom-call | flops 1409286144 | bytes 29360128 | tf_op jit(solution)/shard_map/block/pallas_call | solution.py:190
  42.4 0.6 collective-permute-start.7
  42.9 1.2 %collective-permute-done.7 = bf16[16,64,128]{2,1,0:T(8,128)(2,1)S(1)} collective-permute-done((bf16[16,64,128]{2,1,0:T(8,128)(2,1)S(1)}, bf16[16,64,128]{2,1,0:T(8,128)(2,1)S(1)}, u32[]{:S(2)}, u32[]{:S(2)}) %collective-permute-start.7) | collective-permute-done | bytes 262176 | tf_op jit(solution)/shard_map/ppermute | solution.py:219
  44.1 0.1 add_convert_fusion
  44.2 0.5 collective-permute-start.10
  44.7 1.5 %collective-permute-start.8 = (bf16[4,64,128]{2,1,0:T(8,128)(2,1)S(1)}, bf16[4,64,128]{2,1,0:T(8,128)(2,1)S(1)}, u32[]{:S(2)}, u32[]{:S(2)}) collective-permute-start(bf16[4,64,128]{2,1,0:T(8,128)(2,1)S(1)} %get-tuple-element.8), channel_id=1, source_target_pairs={{0,2},{1,3},{2,0},{3,1},{4,6},{5,7},{6,4},{7,5},{8,10},{9,11},{10,... | collective-permute-start | bytes 196616 | tf_op jit(solution)/shard_map/ppermute | solution.py:219
  46.2 1.5 %collective-permute-start.9 = (bf16[4,64,128]{2,1,0:T(8,128)(2,1)S(1)}, bf16[4,64,128]{2,1,0:T(8,128)(2,1)S(1)}, u32[]{:S(2)}, u32[]{:S(2)}) collective-permute-start(bf16[4,64,128]{2,1,0:T(8,128)(2,1)S(1)} %get-tuple-element.10), channel_id=1, source_target_pairs={{0,16},{1,17},{2,18},{3,19},{4,20},{5,21},{6,22},{7,23},{8,24},{9,... | collective-permute-start | bytes 196616 | tf_op jit(solution)/shard_map/ppermute | solution.py:219
  47.8 0.0 copy-done.1
  47.8 0.2 reduce-window.8
  47.9 2.1 %collective-permute-done.10 = bf16[4,64,128]{2,1,0:T(8,128)(2,1)S(1)} collective-permute-done((bf16[4,64,128]{2,1,0:T(8,128)(2,1)S(1)}, bf16[4,64,128]{2,1,0:T(8,128)(2,1)S(1)}, u32[]{:S(2)}, u32[]{:S(2)}) %collective-permute-start.10) | collective-permute-done | bytes 65568 | tf_op jit(solution)/shard_map/ppermute | solution.py:219
  50.1 0.0 collective-permute-done.8
  50.1 0.8 %collective-permute-done.9 = bf16[4,64,128]{2,1,0:T(8,128)(2,1)S(1)} collective-permute-done((bf16[4,64,128]{2,1,0:T(8,128)(2,1)S(1)}, bf16[4,64,128]{2,1,0:T(8,128)(2,1)S(1)}, u32[]{:S(2)}, u32[]{:S(2)}) %collective-permute-start.9) | collective-permute-done | bytes 65568 | tf_op jit(solution)/shard_map/ppermute | solution.py:219
  51.0 0.1 collective-permute-start.11
  51.1 0.8 %collective-permute-start.12 = (bf16[1,64,128]{2,1,0:T(8,128)(2,1)S(1)}, bf16[1,64,128]{2,1,0:T(8,128)(2,1)S(1)}, u32[]{:S(2)}, u32[]{:S(2)}) collective-permute-start(bf16[1,64,128]{2,1,0:T(8,128)(2,1)S(1)} %get-tuple-element.13), channel_id=1, source_target_pairs={{0,8},{1,9},{2,10},{3,11},{4,12},{5,13},{6,14},{7,15},{8,0},{9,1},... | collective-permute-start | bytes 49160 | tf_op jit(solution)/shard_map/ppermute | solution.py:219
  51.8 3.6 %collective-permute-start.13 = (bf16[1,64,128]{2,1,0:T(8,128)(2,1)S(1)}, bf16[1,64,128]{2,1,0:T(8,128)(2,1)S(1)}, u32[]{:S(2)}, u32[]{:S(2)}) collective-permute-start(bf16[1,64,128]{2,1,0:T(8,128)(2,1)S(1)} %get-tuple-element.12), channel_id=1, source_target_pairs={{0,12},{1,13},{2,14},{3,15},{4,8},{5,9},{6,10},{7,11},{8,4},{9,5},... | collective-permute-start | bytes 49160 | tf_op jit(solution)/shard_map/ppermute | solution.py:219
  55.4 0.0 copy-done
  55.4 0.0 copy-done.2
  55.4 0.7 %select_reduce_fusion = (s32[]{:T(128)}, s32[]{:T(128)}, s32[]{:T(128)}) fusion(s32[8]{0:T(128)S(1)} %copy-done, s32[8]{0:T(128)S(1)} %copy-done.1, s32[8,1]{0,1:T(1,128)S(1)} %reduce-window.8, s32[8]{0:T(128)S(1)} %copy-done.2, s32[]{:T(128)S(6)} %axis_index.12), kind=kLoop, calls=%fused_computation.15 | loop fusion | flops 77 | bytes 144 | tf_op jit(solution)/shard_map/reduce_sum | solution.py:29
  58.1 0.0 collective-permute-done.11
  58.1 0.0 collective-permute-done.12
  58.1 0.0 collective-permute-done.13
  58.1 0.6 %copy.11 = bf16[1,1,64,128]{3,1,2,0:T(2,128)(2,1)} copy(bf16[1,1,64,128]{3,2,1,0:T(8,128)(2,1)S(1)} %fusion) | data formatting | bytes 32768
  (13 shorter events, 0.2 us)
Async XLA Ops:
  0.8 5.7 %collective-permute-start = (bf16[1,64,128]{2,1,0:T(8,128)(2,1)S(1)}, bf16[1,64,128]{2,1,0:T(8,128)(2,1)S(1)}, u32[]{:S(2)}, u32[]{:S(2)}) collective-permute-start(bf16[1,64,128]{2,1,0:T(8,128)(2,1)S(1)} %bitcast.15), channel_id=1, source_target_pairs={{0,4},{1,5},{2,6},{3,7},{4,0},{5,1},{6,2},{7,3},{8,12},{9,13},{10,... | collective-permute-start | bytes 49160 | tf_op jit(solution)/shard_map/ppermute | solution.py:219
  3.9 4.7 %collective-permute-start.1 = (bf16[1,64,128]{2,1,0:T(8,128)(2,1)S(1)}, bf16[1,64,128]{2,1,0:T(8,128)(2,1)S(1)}, u32[]{:S(2)}, u32[]{:S(2)}) collective-permute-start(bf16[1,64,128]{2,1,0:T(8,128)(2,1)S(1)} %bitcast.16), channel_id=1, source_target_pairs={{0,8},{1,9},{2,10},{3,11},{4,12},{5,13},{6,14},{7,15},{8,0},{9,1},... | collective-permute-start | bytes 49160 | tf_op jit(solution)/shard_map/ppermute | solution.py:219
  6.5 5.5 %collective-permute-start.2 = (bf16[1,64,128]{2,1,0:T(8,128)(2,1)S(1)}, bf16[1,64,128]{2,1,0:T(8,128)(2,1)S(1)}, u32[]{:S(2)}, u32[]{:S(2)}) collective-permute-start(bf16[1,64,128]{2,1,0:T(8,128)(2,1)S(1)} %bitcast.17), channel_id=1, source_target_pairs={{0,12},{1,13},{2,14},{3,15},{4,8},{5,9},{6,10},{7,11},{8,4},{9,5},... | collective-permute-start | bytes 49160 | tf_op jit(solution)/shard_map/ppermute | solution.py:219
  12.1 4.6 %collective-permute-start.3 = (bf16[4,64,128]{2,1,0:T(8,128)(2,1)S(1)}, bf16[4,64,128]{2,1,0:T(8,128)(2,1)S(1)}, u32[]{:S(2)}, u32[]{:S(2)}) collective-permute-start(bf16[4,64,128]{2,1,0:T(8,128)(2,1)S(1)} %pad_maximum_fusion), channel_id=1, source_target_pairs={{0,2},{1,3},{2,0},{3,1},{4,6},{5,7},{6,4},{7,5},{8,10},{9,11},{10,... | collective-permute-start | bytes 196616 | tf_op jit(solution)/shard_map/ppermute | solution.py:219
  13.6 4.3 %collective-permute-start.4 = (bf16[4,64,128]{2,1,0:T(8,128)(2,1)S(1)}, bf16[4,64,128]{2,1,0:T(8,128)(2,1)S(1)}, u32[]{:S(2)}, u32[]{:S(2)}) collective-permute-start(bf16[4,64,128]{2,1,0:T(8,128)(2,1)S(1)} %pad_maximum_fusion), channel_id=1, source_target_pairs={{0,16},{1,17},{2,18},{3,19},{4,20},{5,21},{6,22},{7,23},{8,24},{9,... | collective-permute-start | bytes 196616 | tf_op jit(solution)/shard_map/ppermute | solution.py:219
  15.2 5.2 %collective-permute-start.5 = (bf16[4,64,128]{2,1,0:T(8,128)(2,1)S(1)}, bf16[4,64,128]{2,1,0:T(8,128)(2,1)S(1)}, u32[]{:S(2)}, u32[]{:S(2)}) collective-permute-start(bf16[4,64,128]{2,1,0:T(8,128)(2,1)S(1)} %pad_maximum_fusion), channel_id=1, source_target_pairs={{0,18},{1,19},{2,16},{3,17},{4,22},{5,23},{6,20},{7,21},{8,26},{9,... | collective-permute-start | bytes 196616 | tf_op jit(solution)/shard_map/ppermute | solution.py:219
  20.3 6.3 %collective-permute-start.6 = (bf16[16,64,128]{2,1,0:T(8,128)(2,1)S(1)}, bf16[16,64,128]{2,1,0:T(8,128)(2,1)S(1)}, u32[]{:S(2)}, u32[]{:S(2)}) collective-permute-start(bf16[16,64,128]{2,1,0:T(8,128)(2,1)S(1)} %constant_dynamic-update-slice_fusion.near_ref), channel_id=1, source_target_pairs={{0,1},{1,0},{2,3},{3,2},{4,5},{5,4},{6,7},{7,6},{8,9},{9,8},{10,11... | collective-permute-start | bytes 786440 | tf_op jit(solution)/shard_map/ppermute | solution.py:219
  26.6 21.1 %copy-start.1 = (s32[8]{0:T(128)S(1)}, s32[8]{0:T(128)}, u32[]{:S(2)}) copy-start(s32[8]{0:T(128)} %param.13) | copy-start | bytes 100
  26.6 28.8 %copy-start = (s32[8]{0:T(128)S(1)}, s32[8]{0:T(128)}, u32[]{:S(2)}) copy-start(s32[8]{0:T(128)} %param.14) | copy-start | bytes 100
  26.6 28.8 %copy-start.2 = (s32[8]{0:T(128)S(1)}, s32[8]{0:T(128)}, u32[]{:S(2)}) copy-start(s32[8]{0:T(128)} %param.15) | copy-start | bytes 100
  42.4 1.7 %collective-permute-start.7 = (bf16[16,64,128]{2,1,0:T(8,128)(2,1)S(1)}, bf16[16,64,128]{2,1,0:T(8,128)(2,1)S(1)}, u32[]{:S(2)}, u32[]{:S(2)}) collective-permute-start(bf16[16,64,128]{2,1,0:T(8,128)(2,1)S(1)} %split.41), channel_id=1, source_target_pairs={{0,1},{1,0},{2,3},{3,2},{4,5},{5,4},{6,7},{7,6},{8,9},{9,8},{10,11... | collective-permute-start | bytes 786440 | tf_op jit(solution)/shard_map/ppermute | solution.py:219
  44.2 5.9 %collective-permute-start.10 = (bf16[4,64,128]{2,1,0:T(8,128)(2,1)S(1)}, bf16[4,64,128]{2,1,0:T(8,128)(2,1)S(1)}, u32[]{:S(2)}, u32[]{:S(2)}) collective-permute-start(bf16[4,64,128]{2,1,0:T(8,128)(2,1)S(1)} %get-tuple-element.9), channel_id=1, source_target_pairs={{0,18},{1,19},{2,16},{3,17},{4,22},{5,23},{6,20},{7,21},{8,26},{9,... | collective-permute-start | bytes 196616 | tf_op jit(solution)/shard_map/ppermute | solution.py:219
  44.7 5.3 %collective-permute-start.8 = (bf16[4,64,128]{2,1,0:T(8,128)(2,1)S(1)}, bf16[4,64,128]{2,1,0:T(8,128)(2,1)S(1)}, u32[]{:S(2)}, u32[]{:S(2)}) collective-permute-start(bf16[4,64,128]{2,1,0:T(8,128)(2,1)S(1)} %get-tuple-element.8), channel_id=1, source_target_pairs={{0,2},{1,3},{2,0},{3,1},{4,6},{5,7},{6,4},{7,5},{8,10},{9,11},{10,... | collective-permute-start | bytes 196616 | tf_op jit(solution)/shard_map/ppermute | solution.py:219
  46.2 4.7 %collective-permute-start.9 = (bf16[4,64,128]{2,1,0:T(8,128)(2,1)S(1)}, bf16[4,64,128]{2,1,0:T(8,128)(2,1)S(1)}, u32[]{:S(2)}, u32[]{:S(2)}) collective-permute-start(bf16[4,64,128]{2,1,0:T(8,128)(2,1)S(1)} %get-tuple-element.10), channel_id=1, source_target_pairs={{0,16},{1,17},{2,18},{3,19},{4,20},{5,21},{6,22},{7,23},{8,24},{9,... | collective-permute-start | bytes 196616 | tf_op jit(solution)/shard_map/ppermute | solution.py:219
  51.0 7.1 %collective-permute-start.11 = (bf16[1,64,128]{2,1,0:T(8,128)(2,1)S(1)}, bf16[1,64,128]{2,1,0:T(8,128)(2,1)S(1)}, u32[]{:S(2)}, u32[]{:S(2)}) collective-permute-start(bf16[1,64,128]{2,1,0:T(8,128)(2,1)S(1)} %get-tuple-element.11), channel_id=1, source_target_pairs={{0,4},{1,5},{2,6},{3,7},{4,0},{5,1},{6,2},{7,3},{8,12},{9,13},{10,... | collective-permute-start | bytes 49160 | tf_op jit(solution)/shard_map/ppermute | solution.py:219
  51.1 7.0 %collective-permute-start.12 = (bf16[1,64,128]{2,1,0:T(8,128)(2,1)S(1)}, bf16[1,64,128]{2,1,0:T(8,128)(2,1)S(1)}, u32[]{:S(2)}, u32[]{:S(2)}) collective-permute-start(bf16[1,64,128]{2,1,0:T(8,128)(2,1)S(1)} %get-tuple-element.13), channel_id=1, source_target_pairs={{0,8},{1,9},{2,10},{3,11},{4,12},{5,13},{6,14},{7,15},{8,0},{9,1},... | collective-permute-start | bytes 49160 | tf_op jit(solution)/shard_map/ppermute | solution.py:219
  51.8 6.3 %collective-permute-start.13 = (bf16[1,64,128]{2,1,0:T(8,128)(2,1)S(1)}, bf16[1,64,128]{2,1,0:T(8,128)(2,1)S(1)}, u32[]{:S(2)}, u32[]{:S(2)}) collective-permute-start(bf16[1,64,128]{2,1,0:T(8,128)(2,1)S(1)} %get-tuple-element.12), channel_id=1, source_target_pairs={{0,12},{1,13},{2,14},{3,15},{4,8},{5,9},{6,10},{7,11},{8,4},{9,5},... | collective-permute-start | bytes 49160 | tf_op jit(solution)/shard_map/ppermute | solution.py:219

commit v3 on v2

v3 whole, which is shorter than its diff:
```python
import functools

import jax
import jax.numpy as jnp
from jax import lax
from jax.experimental import pallas as pl
from jax.experimental.pallas import tpu as pltpu
from jax.sharding import PartitionSpec as P

LANES = 128
ROW_LINES = ("groups", "z", "x", "core")


def normalize(tokens, norm_gain):
    values = tokens.astype(jnp.float32)
    mean_sq = jnp.mean(values * values, axis=-1, keepdims=True)
    return (values * lax.rsqrt(mean_sq + 1e-05) * norm_gain.astype(jnp.float32)).astype(
        jnp.bfloat16
    )


def live_rows(lengths, hit_lengths, start_positions, token_index):
    ends = jnp.cumsum(lengths)
    begins = ends - lengths
    member = (token_index[:, None] >= begins[None, :]) & (token_index[:, None] < ends[None, :])
    member_int = member.astype(jnp.int32)
    offsets = token_index - jnp.sum(member_int * begins[None, :], axis=1)
    position = jnp.sum(member_int * start_positions[None, :], axis=1) + offsets
    covered = jnp.sum(member_int * hit_lengths[None, :], axis=1)
    return position >= covered


def local(tokens, norm_gain, w_gate, w_up, w_down, lengths, hit_lengths, start_positions):
    row_count = tokens.shape[0]
    normed = normalize(tokens, norm_gain)
    piece_rows = lax.all_gather(normed, "tensor", axis=0, tiled=True)
    gate_out = jnp.dot(piece_rows, w_gate, preferred_element_type=jnp.float32)
    up_out = jnp.dot(piece_rows, w_up, preferred_element_type=jnp.float32)
    hidden = (jax.nn.silu(gate_out) * up_out).astype(jnp.bfloat16)
    partial_value = jnp.dot(hidden, w_down, preferred_element_type=jnp.float32)
    rounded = partial_value.astype(jnp.bfloat16)
    totals = jnp.sum(
        lax.all_to_all(rounded[None], "tensor", split_axis=1, concat_axis=0, tiled=True).astype(
            jnp.float32
        ),
        axis=0,
    )
    token_index = lax.axis_index("tensor") * row_count + jnp.arange(row_count, dtype=jnp.int32)
    live = live_rows(lengths, hit_lengths, start_positions, token_index)
    return jnp.where(live[:, None], totals, jnp.zeros_like(totals)).astype(jnp.bfloat16)


def live_flag(lengths, hit_lengths, start_positions, token):
    begin = 0
    live = False
    for request in range(lengths.shape[0]):
        end = begin + lengths[request]
        position = start_positions[request] + token - begin
        inside = (token >= begin) & (token < end)
        live = live | (inside & (position >= hit_lengths[request]))
        begin = end
    return live


def load_kernel(
    half, place, lengths, hit_lengths, start_positions, gate_hbm, up_hbm, both_vmem, keep_vmem, sems
):
    own = pl.multiple_of(lax.axis_index("groups") * half, LANES)
    depth = both_vmem.shape[0]
    copies = [
        pltpu.make_async_copy(
            weight.at[pl.ds(0, depth), pl.ds(own, half)],
            both_vmem.at[:, pl.ds(at * half, half)],
            sems.at[at],
        )
        for at, weight in enumerate((gate_hbm, up_hbm))
    ]
    for copy in copies:
        copy.start()
    live = live_flag(lengths, hit_lengths, start_positions, place())
    keep_vmem[...] = jnp.full(keep_vmem.shape, live.astype(jnp.float32), jnp.float32)
    for copy in copies:
        copy.wait()


def load_weights(requests, w_gate, w_up, half, depth, place):
    smem = pl.BlockSpec(memory_space=pltpu.SMEM)
    vmem = pl.BlockSpec(memory_space=pltpu.VMEM)
    hbm = pl.BlockSpec(memory_space=pltpu.HBM)
    return pl.pallas_call(
        functools.partial(load_kernel, half, place),
        out_shape=(
            pltpu.VMEM((depth, 2 * half), w_gate.dtype),
            jax.ShapeDtypeStruct((8, LANES), jnp.float32),
        ),
        in_specs=[smem] * 3 + [hbm] * 2,
        out_specs=(vmem, vmem),
        scratch_shapes=[pltpu.SemaphoreType.DMA((2,))],
        compiler_params=pltpu.CompilerParams(vmem_limit_bytes=1 << 20),
        cost_estimate=pl.CostEstimate(
            flops=0, bytes_accessed=2 * depth * half * 2, transcendentals=0
        ),
        name="load_weights",
    )(*requests, w_gate, w_up)


def block_kernel(
    half,
    chunk,
    near_ref,
    far_ref,
    gain_ref,
    first_ref,
    gate_hbm,
    up_hbm,
    down_hbm,
    keep_ref,
    send_ref,
    wide_ref,
    normed_ref,
    product_ref,
    hidden_ref,
    rest_ref,
    down_ref,
    both_sems,
    down_sems,
):
    tile = 256
    ahead = 3
    rows, lines, lanes = wide_ref.shape
    depth = lines * lanes
    loaded = first_ref.shape[0]
    own = pl.multiple_of(lax.axis_index("groups") * half, LANES)
    loads = []
    for step, at in enumerate(range(0, depth - loaded, chunk)):
        loads.append(
            [
                pltpu.make_async_copy(
                    weight.at[pl.ds(loaded + at, chunk), pl.ds(own, half)],
                    rest_ref.at[pl.ds(at, chunk), pl.ds(side * half, half)],
                    both_sems.at[step, side],
                )
                for side, weight in enumerate((gate_hbm, up_hbm))
            ]
        )
    pairs = len(loads)
    for step, at in enumerate(range(0, depth, chunk)):
        loads.append(
            [
                pltpu.make_async_copy(
                    down_hbm.at[pl.ds(own, half), pl.ds(at, chunk)],
                    down_ref.at[:, pl.ds(at, chunk)],
                    down_sems.at[step],
                )
            ]
        )

    def start(number):
        if number < len(loads):
            for copy in loads[number]:
                copy.start()

    def wait(number):
        for copy in loads[number]:
            copy.wait()

    for number in range(ahead):
        start(number)

    wide_ref[: rows // 2] = near_ref[...].astype(jnp.float32)
    wide_ref[rows // 2 :] = far_ref[...].astype(jnp.float32)
    squares = wide_ref[:, 0, :] * wide_ref[:, 0, :]
    for line in range(1, lines):
        value = wide_ref[:, line, :]
        squares = squares + value * value
    scale = lax.rsqrt(jnp.sum(squares, axis=-1, keepdims=True) * (1.0 / depth) + 1e-05)
    for line in range(lines):
        columns = pl.ds(line * lanes, lanes)
        normed_ref[:, columns] = (
            wide_ref[:, line, :] * scale * gain_ref[:, columns].astype(jnp.float32)
        ).astype(jnp.bfloat16)

    started = ahead
    for at in range(0, depth, chunk):
        if at >= loaded:
            wait((at - loaded) // chunk)
        for column in range(0, 2 * half, tile):
            columns = pl.ds(column, tile)
            weight = (
                first_ref[at : at + chunk, columns]
                if at < loaded
                else rest_ref[at - loaded : at - loaded + chunk, columns]
            )
            value = jnp.dot(
                normed_ref[:, at : at + chunk], weight, preferred_element_type=jnp.float32
            )
            if at == 0:
                product_ref[:, columns] = value
            else:
                product_ref[:, columns] += value
        start(started)
        started += 1
    gate_out = product_ref[:, :half]
    up_out = product_ref[:, half:]
    hidden_ref[...] = (gate_out / (1.0 + jnp.exp(-gate_out)) * up_out).astype(jnp.bfloat16)
    for step in range(depth // chunk):
        wait(pairs + step)
        for at in range(step * chunk, (step + 1) * chunk, tile):
            result = jnp.dot(
                hidden_ref[...], down_ref[:, pl.ds(at, tile)], preferred_element_type=jnp.float32
            )
            for line in range(tile // lanes):
                wide_ref[:, at // lanes + line, :] = result[:, line * lanes : (line + 1) * lanes]
        start(started)
        started += 1
        done = pl.ds(step * chunk // lanes, chunk // lanes)
        keep_ref[:, done, :] = wide_ref[: rows // 2, done, :]
        send_ref[:, done, :] = wide_ref[rows // 2 :, done, :].astype(jnp.bfloat16)


def block(near, far, gain, first, w_gate, w_up, w_down, half):
    rows, lines, lanes = near.shape
    depth = lines * lanes
    chunk = 1024
    rest = depth - first.shape[0]
    vmem = pl.BlockSpec(memory_space=pltpu.VMEM)
    hbm = pl.BlockSpec(memory_space=pltpu.HBM)
    return pl.pallas_call(
        functools.partial(block_kernel, half, chunk),
        out_shape=(
            jax.ShapeDtypeStruct(near.shape, jnp.float32),
            jax.ShapeDtypeStruct(near.shape, jnp.bfloat16),
        ),
        in_specs=[vmem] * 4 + [hbm] * 3,
        out_specs=(vmem, vmem),
        scratch_shapes=[
            pltpu.VMEM((2 * rows, lines, lanes), jnp.float32),
            pltpu.VMEM((2 * rows, depth), jnp.bfloat16),
            pltpu.VMEM((2 * rows, 2 * half), jnp.float32),
            pltpu.VMEM((2 * rows, half), jnp.bfloat16),
            pltpu.VMEM((rest, 2 * half), jnp.bfloat16),
            pltpu.VMEM((half, depth), jnp.bfloat16),
            pltpu.SemaphoreType.DMA((rest // chunk, 2)),
            pltpu.SemaphoreType.DMA((depth // chunk,)),
        ],
        compiler_params=pltpu.CompilerParams(
            vmem_limit_bytes=(rest * 2 + depth) * half * 2 + (6 << 20)
        ),
        cost_estimate=pl.CostEstimate(
            flops=12 * rows * depth * half,
            bytes_accessed=(rest * 2 + depth) * half * 2,
            transcendentals=0,
        ),
        name="block",
    )(near, far, gain, pltpu.with_memory_space_constraint(first, pltpu.VMEM), w_gate, w_up, w_down)


def deal(pieces, axes):
    return lax.all_to_all(pieces, axes, split_axis=0, concat_axis=0, tiled=True)


def other_core(value):
    return lax.ppermute(value, "core", [(0, 1), (1, 0)])


def shared(tokens, norm_gain, w_gate, w_up, w_down, lengths, hit_lengths, start_positions):
    depth = tokens.shape[1]
    lines = depth // LANES
    half = w_gate.shape[1] // lax.axis_size("groups")
    deep = lax.axis_size("z")
    square = lax.axis_size("groups") * lax.axis_size("x")
    w_gate, w_up, w_down = (
        pltpu.with_memory_space_constraint(weight, pltpu.HBM) for weight in (w_gate, w_up, w_down)
    )

    def place():
        return (lax.axis_index("z") * lax.axis_size("x") + lax.axis_index("x")) * lax.axis_size(
            "core"
        ) + lax.axis_index("core")

    first, keep = load_weights(
        (lengths, hit_lengths, start_positions), w_gate, w_up, half, depth // 2, place
    )
    column = deal(jnp.broadcast_to(tokens.reshape(1, lines, LANES), (deep, lines, LANES)), "z")
    plane = deal(jnp.broadcast_to(column, (square,) + column.shape), ("groups", "x"))
    near = plane.reshape(square * deep, lines, LANES)
    far = other_core(near)
    kept, sent = block(near, far, norm_gain.reshape(1, depth), first, w_gate, w_up, w_down, half)
    plane = (kept + other_core(sent).astype(jnp.float32)).astype(jnp.bfloat16)
    column = jnp.sum(
        deal(plane.reshape(square, deep, lines, LANES), ("groups", "x")).astype(jnp.float32), axis=0
    ).astype(jnp.bfloat16)
    totals = jnp.sum(deal(column, "z").astype(jnp.float32), axis=0)
    return jnp.where(keep[:1] > 0, totals, jnp.zeros_like(totals)).astype(jnp.bfloat16).reshape(1, depth)


def solution(mesh):
    groups, members = mesh.shape["groups"], mesh.shape["tensor"]

    def placed(axes, whole):
        return (
            P(whole, None),
            P(),
            P(None, axes),
            P(None, axes),
            P(axes, None),
            P("groups"),
            P("groups"),
            P("groups"),
        )

    def run(*arrays):
        units = arrays[2].shape[1] // members
        if (
            units % (LANES * groups) == 0
            and arrays[0].shape[0] == groups * members
            and groups == 2
            and members % 8 == 0
        ):
            body, axes, whole = shared, ("z", "x", "core"), ROW_LINES
            over = jax.sharding.Mesh(mesh.devices.reshape(groups, members // 4, 2, 2), ROW_LINES)
        else:
            body, axes, whole, over = local, "tensor", ("groups", "tensor"), mesh
        return jax.shard_map(
            body,
            mesh=over,
            in_specs=placed(axes, whole),
            out_specs=P(whole, None),
            check_vma=False,
        )(*arrays)

    return run
```

time: 59 us -> 64.7 us (1.097)
  blocking collectives: 0 us -> 30 us
  starting transfers between devices: 17.9 us -> 3.86 us
  waiting for transfers between devices: 14.3 us -> 6.86 us
  Pallas kernels: 21.1 us -> 18.4 us
  between operations: 2.05 us -> 0.09 us
  local copies, waits for them, and re-layouts: 1.5 us -> 3.39 us
    all_to_all x0 -> x3, blocking collectives: none -> 30 us  [deal(): return lax.all_to_all(pieces, axes, split_axis=0, concat_axis=0, tiled=True)]
    ppermute x14 -> x2, starting transfers between devices: 17.9 us -> 0.57 us  [other_core(): return lax.ppermute(value, 'core', [(0, 1), (1, 0)])]
    ppermute x14 -> x2, waiting for transfers between devices: 14.3 us -> 1.16 us  [other_core(): return lax.ppermute(value, 'core', [(0, 1), (1, 0)])]
    all_to_all x0 -> x1, waiting for transfers between devices: none -> 5.7 us  [deal(): return lax.all_to_all(pieces, axes, split_axis=0, concat_axis=0, tiled=True)]
    all_to_all x0 -> x1, starting transfers between devices: none -> 3.28 us  [deal(): return lax.all_to_all(pieces, axes, split_axis=0, concat_axis=0, tiled=True)]
    pallas_call x2, Pallas kernels: 21.1 us -> 18.4 us  [the longest x1 12.5 us: block(): pl.pallas_call(functools.partial(block_kernel, half, chunk), out_shape=(j...]
    unnamed x13 -> x7, local copies, waits for them, and re-layouts: 0.71 us -> 2.6 us
  transfers between devices with their start and end apart: 14 -> 3, of which waited for: 8 -> 2; matrix products, arithmetic and copies ran while one was open for 3% -> 1% of each run, Pallas kernels for 9% -> 9%
where the time goes in v3:
time: 64.7 us; the launch traced here: 64.3 us
  blocking collectives  30 us (46%)
  Pallas kernels  18.4 us (28%)
  waiting for transfers between devices  6.86 us (11%)
  starting transfers between devices  3.86 us (6%)
  local copies, waits for them, and re-layouts  3.39 us (5%)
  other arithmetic  1.6 us (2%)
    all_to_all x3, blocking collectives, deal(): return lax.all_to_all(pieces, axes, split_axis=0, concat_axis=0, tiled=True)  30 us
    pallas_call x1, Pallas kernels, block(): pl.pallas_call(functools.partial(block_kernel, half, chunk), out_shape=(j...  12.5 us
    pallas_call x1, Pallas kernels, load_weights(): pl.pallas_call(functools.partial(load_kernel, half, place), out_shape=(pl...  5.99 us
    all_to_all x1, waiting for transfers between devices, deal(): return lax.all_to_all(pieces, axes, split_axis=0, concat_axis=0, tiled=True)  5.7 us
    all_to_all x1, starting transfers between devices, deal(): return lax.all_to_all(pieces, axes, split_axis=0, concat_axis=0, tiled=True)  3.28 us
    unnamed x7, local copies, waits for them, and re-layouts  2.6 us
  transfers between devices with their start and end apart: 3, of which 2 were waited for; matrix products, arithmetic and copies ran while one was open for 1% of the time, Pallas kernels for 9%

profile of v3, /device:TPU:0, one launch (start us, length us, event | category | flops | bytes accessed | tf_op | source)
XLA Modules:
  0.0 64.3 jit_solution(16991309107684504343)
XLA Ops:
  0.0 0.8 %reduce.1 = bf16[8192]{0:T(1024)(128)(2,1)S(1)} reduce(bf16[1,8192]{1,0:T(2,128)(2,1)} %param.8, bf16[]{:T(256)} %constant.7), dimensions={0}, to_apply=%param.8.reduce_sub_computation | reduce | bytes 32770 | tf_op args[0]
  0.9 11.9 %all_to_all.20 = bf16[4,64,128]{2,1,0:T(8,128)(2,1)S(1)} all-to-all(bf16[4,64,128]{2,1,0:T(8,128)(2,1)S(1)} %broadcast_in_dim.26), channel_id=1, replica_groups=mesh['groups'=2,'z'=4,'x'=2,'core'=2] {'z'}, dimensions={0} | all-to-all | bytes 131072 | tf_op jit(solution)/shard_map/all_to_all | solution.py:259
  12.8 9.2 %all_to_all.21 = bf16[4,4,64,128]{3,2,1,0:T(8,128)(2,1)S(1)} all-to-all(bf16[4,4,64,128]{3,2,1,0:T(8,128)(2,1)S(1)} %broadcast_in_dim.27), channel_id=1, replica_groups=mesh['groups'=2,'z'=4,'x'=2,'core'=2] {'groups','x'}, dimensions={0} | all-to-all | bytes 524288 | tf_op jit(solution)/shard_map/all_to_all | solution.py:259
  22.0 0.0 collective-permute-start
  22.0 0.7 %reshape.38.gain_ref = bf16[1,8192]{1,0:T(2,128)(2,1)S(1)} reshape(bf16[8192]{0:T(1024)(128)(2,1)} %param.9) | data formatting | bytes 32768 | tf_op jit(solution)/shard_map/reshape | solution.py:288
  22.8 0.0 copy-start
  22.8 0.6 %copy-done = s32[8]{0:T(128)S(1)} copy-done((s32[8]{0:T(128)S(1)}, s32[8]{0:T(128)}, u32[]{:S(2)}) %copy-start) | copy-done | bytes 56
  23.4 0.0 copy-start.1
  23.4 0.7 %copy-done.1 = s32[8]{0:T(128)S(1)} copy-done((s32[8]{0:T(128)S(1)}, s32[8]{0:T(128)}, u32[]{:S(2)}) %copy-start.1) | copy-done | bytes 56
  24.1 0.0 copy-start.2
  24.1 0.7 %copy-done.2 = s32[8]{0:T(128)S(1)} copy-done((s32[8]{0:T(128)S(1)}, s32[8]{0:T(128)}, u32[]{:S(2)}) %copy-start.2) | copy-done | bytes 56
  24.7 6.0 %load_weights.1 = (bf16[4096,1792]{1,0:T(8,128)(2,1)S(1)}, f32[8,128]{1,0:T(8,128)S(1)}) custom-call(s32[8]{0:T(128)S(1)} %copy-done, s32[8]{0:T(128)S(1)} %copy-done.1, s32[8]{0:T(128)S(1)} %copy-done.2, bf16[8192,1792]{1,0:T(8,128)(2,1)} %gate_hbm.3, bf16[8192,1792]{1,0:T(8,128)(2,1)} %up_hbm.3), custom_call_target="tpu_custom_call" | custom-call | bytes 14680064 | tf_op jit(solution)/shard_map/load_weights/pallas_call | solution.py:90
  30.7 0.0 collective-permute-done.far_ref
  30.7 12.5 %block.1 = (f32[16,64,128]{2,1,0:T(8,128)S(1)}, bf16[16,64,128]{2,1,0:T(8,128)(2,1)S(1)}) custom-call(bf16[16,64,128]{2,1,0:T(8,128)(2,1)S(1)} %bitcast.12, bf16[16,64,128]{2,1,0:T(8,128)(2,1)S(1)} %collective-permute-done.far_ref, bf16[1,8192]{1,0:T(2,128)(2,1)S(1)} %reshape.38.gain_ref, bf16[4096,1792]{1,0:T(8,128)(2,1)S(1)} %get-tuple-element.10.first_ref, ...), custom_call_target="tpu_custom_call" | custom-call | flops 1409286144 | bytes 29360128 | tf_op jit(solution)/shard_map/block/pallas_call | solution.py:228
  43.2 0.6 collective-permute-start.1
  43.8 1.2 %collective-permute-done.1 = bf16[16,64,128]{2,1,0:T(8,128)(2,1)S(1)} collective-permute-done((bf16[16,64,128]{2,1,0:T(8,128)(2,1)S(1)}, bf16[16,64,128]{2,1,0:T(8,128)(2,1)S(1)}, u32[]{:S(2)}, u32[]{:S(2)}) %collective-permute-start.1) | collective-permute-done | bytes 262176 | tf_op jit(solution)/shard_map/ppermute | solution.py:263
  44.9 0.1 add_convert_fusion
  45.0 8.9 %all_to_all.22 = bf16[4,4,64,128]{3,2,1,0:T(8,128)(2,1)S(1)} all-to-all(bf16[4,4,64,128]{3,2,1,0:T(8,128)(2,1)S(1)} %bitcast.13), channel_id=1, replica_groups=mesh['groups'=2,'z'=4,'x'=2,'core'=2] {'groups','x'}, dimensions={0} | all-to-all | bytes 524288 | tf_op jit(solution)/shard_map/all_to_all | solution.py:259
  53.9 0.7 %reduce_sum.21 = bf16[4,64,128]{2,1,0:T(8,128)(2,1)} reduce(bf16[4,4,64,128]{3,2,1,0:T(8,128)(2,1)S(1)} %all_to_all.22, bf16[]{:T(256)} %constant.1.clone.1), dimensions={0}, to_apply=%region_0.0 | reduce | flops 98304 | bytes 327682 | tf_op jit(solution)/shard_map/reduce_sum | solution.py:290
  54.6 3.3 %all-to-all-start.3 = ((bf16[4,64,128]{2,1,0:T(8,128)(2,1)}), bf16[4,64,128]{2,1,0:T(8,128)(2,1)S(1)}, u32[]{:S(2)}, u32[]{:S(2)}) async-start(bf16[4,64,128]{2,1,0:T(8,128)(2,1)} %reduce_sum.21), calls=%async_computation.3 | async-start | bytes 131072 | tf_op jit(solution)/shard_map/all_to_all | solution.py:259
  57.9 5.7 %all-to-all-done.3 = bf16[4,64,128]{2,1,0:T(8,128)(2,1)S(1)} async-done(((bf16[4,64,128]{2,1,0:T(8,128)(2,1)}), bf16[4,64,128]{2,1,0:T(8,128)(2,1)S(1)}, u32[]{:S(2)}, u32[]{:S(2)}) %all-to-all-start.3) | async-done | bytes 65568 | tf_op jit(solution)/shard_map/all_to_all | solution.py:259
  63.6 0.6 copy.11
  (5 shorter events, 0.1 us)
Async XLA Ops:
  22.0 8.7 %collective-permute-start = (bf16[16,64,128]{2,1,0:T(8,128)(2,1)S(1)}, bf16[16,64,128]{2,1,0:T(8,128)(2,1)S(1)}, u32[]{:S(2)}, u32[]{:S(2)}) collective-permute-start(bf16[16,64,128]{2,1,0:T(8,128)(2,1)S(1)} %bitcast.11), channel_id=1, source_target_pairs={{0,1},{1,0},{2,3},{3,2},{4,5},{5,4},{6,7},{7,6},{8,9},{9,8},{10,11... | collective-permute-start | bytes 786440 | tf_op jit(solution)/shard_map/ppermute | solution.py:263
  22.8 0.7 %copy-start = (s32[8]{0:T(128)S(1)}, s32[8]{0:T(128)}, u32[]{:S(2)}) copy-start(s32[8]{0:T(128)} %lengths.1) | copy-start | bytes 100
  23.4 0.7 %copy-start.1 = (s32[8]{0:T(128)S(1)}, s32[8]{0:T(128)}, u32[]{:S(2)}) copy-start(s32[8]{0:T(128)} %hit_lengths.1) | copy-start | bytes 100
  24.1 0.7 %copy-start.2 = (s32[8]{0:T(128)S(1)}, s32[8]{0:T(128)}, u32[]{:S(2)}) copy-start(s32[8]{0:T(128)} %start_positions.1) | copy-start | bytes 100
  43.2 1.7 %collective-permute-start.1 = (bf16[16,64,128]{2,1,0:T(8,128)(2,1)S(1)}, bf16[16,64,128]{2,1,0:T(8,128)(2,1)S(1)}, u32[]{:S(2)}, u32[]{:S(2)}) collective-permute-start(bf16[16,64,128]{2,1,0:T(8,128)(2,1)S(1)} %get-tuple-element.12), channel_id=1, source_target_pairs={{0,1},{1,0},{2,3},{3,2},{4,5},{5,4},{6,7},{7,6},{8,9},{9,8},{10,11... | collective-permute-start | bytes 786440 | tf_op jit(solution)/shard_map/ppermute | solution.py:263
  54.6 9.0 %all-to-all-start.3 = ((bf16[4,64,128]{2,1,0:T(8,128)(2,1)}), bf16[4,64,128]{2,1,0:T(8,128)(2,1)S(1)}, u32[]{:S(2)}, u32[]{:S(2)}) async-start(bf16[4,64,128]{2,1,0:T(8,128)(2,1)} %reduce_sum.21), calls=%async_computation.3 | async-start | bytes 131072 | tf_op jit(solution)/shard_map/all_to_all | solution.py:259

commit v4 on v3

--- a/solution.py
+++ b/solution.py
@@ -50,6 +50,11 @@
     return jnp.where(live[:, None], totals, jnp.zeros_like(totals)).astype(jnp.bfloat16)
 
 
+VMEM = pl.BlockSpec(memory_space=pltpu.VMEM)
+HBM = pl.BlockSpec(memory_space=pltpu.HBM)
+CHUNK = 1024
+
+
 def live_flag(lengths, hit_lengths, start_positions, token):
     begin = 0
     live = False
@@ -62,14 +67,63 @@
     return live
 
 
-def load_kernel(
-    half, place, lengths, hit_lengths, start_positions, gate_hbm, up_hbm, both_vmem, keep_vmem, sems
-):
+def norm_kernel(tokens_hbm, gain_hbm, out_ref, tokens_ref, gain_ref, sems):
+    copies = [
+        pltpu.make_async_copy(tokens_hbm, tokens_ref, sems.at[0]),
+        pltpu.make_async_copy(gain_hbm, gain_ref, sems.at[1]),
+    ]
+    for copy in copies:
+        copy.start()
+    for copy in copies:
+        copy.wait()
+    values = tokens_ref[...].astype(jnp.float32)
+    mean_sq = jnp.mean(values * values, axis=-1, keepdims=True)
+    scaled = values * lax.rsqrt(mean_sq + 1e-05)
+    lines = out_ref.shape[1]
+    rows = [scaled[:, line * LANES : (line + 1) * LANES] for line in range(lines)]
+    stacked = jnp.concatenate(rows, axis=0)
+    out_ref[0] = (stacked * gain_ref[...].astype(jnp.float32)).astype(jnp.bfloat16)
+
+
+def norm(tokens, gain):
+    lines = tokens.shape[1] // LANES
+    gain = gain.reshape(lines, LANES)
+    return pl.pallas_call(
+        norm_kernel,
+        out_shape=jax.ShapeDtypeStruct((1, lines, LANES), jnp.bfloat16),
+        in_specs=[HBM, HBM],
+        out_specs=VMEM,
+        scratch_shapes=[
+            pltpu.VMEM(tokens.shape, tokens.dtype),
+            pltpu.VMEM(gain.shape, gain.dtype),
+            pltpu.SemaphoreType.DMA((2,)),
+        ],
+        compiler_params=pltpu.CompilerParams(vmem_limit_bytes=1 << 20),
+        name="norm",
+    )(*(pltpu.with_memory_space_constraint(array, pltpu.HBM) for array in (tokens, gain)))
+
+
+def stack_kernel(*refs):
+    for at, piece in enumerate(refs[:-2]):
+        refs[-1][at : at + 1] = piece[...]
+
+
+def stack(pieces, mark):
+    return pl.pallas_call(
+        stack_kernel,
+        out_shape=jax.ShapeDtypeStruct((len(pieces),) + pieces[0].shape[1:], pieces[0].dtype),
+        in_specs=[VMEM] * len(pieces) + [pl.BlockSpec(memory_space=pl.ANY)],
+        out_specs=VMEM,
+        compiler_params=pltpu.CompilerParams(vmem_limit_bytes=1 << 20),
+        name="stack",
+    )(*pieces, mark)
+
+
+def load_kernel(half, row, gate_hbm, up_hbm, both_vmem, mark_vmem, sems):
     own = pl.multiple_of(lax.axis_index("groups") * half, LANES)
-    depth = both_vmem.shape[0]
     copies = [
         pltpu.make_async_copy(
-            weight.at[pl.ds(0, depth), pl.ds(own, half)],
+            weight.at[pl.ds(row, both_vmem.shape[0]), pl.ds(own, half)],
             both_vmem.at[:, pl.ds(at * half, half)],
             sems.at[at],
         )
@@ -77,31 +131,97 @@
     ]
     for copy in copies:
         copy.start()
-    live = live_flag(lengths, hit_lengths, start_positions, place())
-    keep_vmem[...] = jnp.full(keep_vmem.shape, live.astype(jnp.float32), jnp.float32)
+    mark_vmem[...] = jnp.ones(mark_vmem.shape, mark_vmem.dtype)
     for copy in copies:
         copy.wait()
 
 
-def load_weights(requests, w_gate, w_up, half, depth, place):
-    smem = pl.BlockSpec(memory_space=pltpu.SMEM)
-    vmem = pl.BlockSpec(memory_space=pltpu.VMEM)
-    hbm = pl.BlockSpec(memory_space=pltpu.HBM)
-    return pl.pallas_call(
-        functools.partial(load_kernel, half, place),
+def load_live_kernel(
+    half,
+    row,
+    place,
+    lengths,
+    hit_lengths,
+    start_positions,
+    gate_hbm,
+    up_hbm,
+    both_vmem,
+    mark_vmem,
+    lengths_smem,
+    hit_smem,
+    start_smem,
+    sems,
+):
+    own = pl.multiple_of(lax.axis_index("groups") * half, LANES)
+    small = [
+        pltpu.make_async_copy(source, target, sems.at[2 + at])
+        for at, (source, target) in enumerate(
+            ((lengths, lengths_smem), (hit_lengths, hit_smem), (start_positions, start_smem))
+        )
+    ]
+    copies = [
+        pltpu.make_async_copy(
+            weight.at[pl.ds(row, both_vmem.shape[0]), pl.ds(own, half)],
+            both_vmem.at[:, pl.ds(at * half, half)],
+            sems.at[at],
+        )
+        for at, weight in enumerate((gate_hbm, up_hbm))
+    ]
+    for copy in small + copies:
+        copy.start()
+    for copy in small:
+        copy.wait()
+    live = live_flag(lengths_smem, hit_smem, start_smem, place())
+    mark_vmem[...] = jnp.full(mark_vmem.shape, live.astype(jnp.float32), jnp.float32)
+    for copy in copies:
+        copy.wait()
+
+
+def load_weights(w_gate, w_up, half, row, count, requests=(), place=None):
+    if requests:
+        body = functools.partial(load_live_kernel, half, row, place)
+        small = [pltpu.SMEM(array.shape, array.dtype) for array in requests]
+    else:
+        body, small = functools.partial(load_kernel, half, row), []
+    return pl.pallas_call(
+        body,
         out_shape=(
-            pltpu.VMEM((depth, 2 * half), w_gate.dtype),
+            pltpu.VMEM((count, 2 * half), w_gate.dtype),
             jax.ShapeDtypeStruct((8, LANES), jnp.float32),
         ),
-        in_specs=[smem] * 3 + [hbm] * 2,
-        out_specs=(vmem, vmem),
-        scratch_shapes=[pltpu.SemaphoreType.DMA((2,))],
+        in_specs=[HBM] * (2 + len(requests)),
+        out_specs=(VMEM, VMEM),
+        scratch_shapes=small + [pltpu.SemaphoreType.DMA((5,))],
         compiler_params=pltpu.CompilerParams(vmem_limit_bytes=1 << 20),
         cost_estimate=pl.CostEstimate(
-            flops=0, bytes_accessed=2 * depth * half * 2, transcendentals=0
+            flops=0, bytes_accessed=2 * count * half * 2, transcendentals=0
         ),
         name="load_weights",
     )(*requests, w_gate, w_up)
+
+
+def pack_kernel(*refs):
+    pieces, out_ref, wide_ref = refs[:-3], refs[-2], refs[-1]
+    at = 0
+    for piece in pieces:
+        wide_ref[at : at + piece.shape[0]] = piece[...].astype(jnp.float32)
+        at += piece.shape[0]
+    for line in range(wide_ref.shape[1]):
+        out_ref[:, line * LANES : (line + 1) * LANES] = wide_ref[:, line, :].astype(jnp.bfloat16)
+
+
+def pack(pieces, mark):
+    rows = sum(piece.shape[0] for piece in pieces)
+    lines = pieces[0].shape[1]
+    return pl.pallas_call(
+        pack_kernel,
+        out_shape=jax.ShapeDtypeStruct((rows, lines * LANES), jnp.bfloat16),
+        in_specs=[VMEM] * len(pieces) + [pl.BlockSpec(memory_space=pl.ANY)],
+        out_specs=VMEM,
+        scratch_shapes=[pltpu.VMEM((rows, lines, LANES), jnp.float32)],
+        compiler_params=pltpu.CompilerParams(vmem_limit_bytes=4 << 20),
+        name="pack",
+    )(*pieces, mark)
 
 
 def block_kernel(
@@ -109,15 +229,14 @@
     chunk,
     near_ref,
     far_ref,
-    gain_ref,
-    first_ref,
+    first_refs,
     gate_hbm,
     up_hbm,
     down_hbm,
     keep_ref,
     send_ref,
     wide_ref,
-    normed_ref,
+    rows_ref,
     product_ref,
     hidden_ref,
     rest_ref,
@@ -129,7 +248,8 @@
     ahead = 3
     rows, lines, lanes = wide_ref.shape
     depth = lines * lanes
-    loaded = first_ref.shape[0]
+    held = [(ref, at) for ref in first_refs for at in range(0, ref.shape[0], chunk)]
+    loaded = len(held) * chunk
     own = pl.multiple_of(lax.axis_index("groups") * half, LANES)
     loads = []
     for step, at in enumerate(range(0, depth - loaded, chunk)):
@@ -167,32 +287,19 @@
     for number in range(ahead):
         start(number)
 
-    wide_ref[: rows // 2] = near_ref[...].astype(jnp.float32)
-    wide_ref[rows // 2 :] = far_ref[...].astype(jnp.float32)
-    squares = wide_ref[:, 0, :] * wide_ref[:, 0, :]
-    for line in range(1, lines):
-        value = wide_ref[:, line, :]
-        squares = squares + value * value
-    scale = lax.rsqrt(jnp.sum(squares, axis=-1, keepdims=True) * (1.0 / depth) + 1e-05)
-    for line in range(lines):
-        columns = pl.ds(line * lanes, lanes)
-        normed_ref[:, columns] = (
-            wide_ref[:, line, :] * scale * gain_ref[:, columns].astype(jnp.float32)
-        ).astype(jnp.bfloat16)
-
+    rows_ref[: rows // 2] = near_ref[...]
+    rows_ref[rows // 2 :] = far_ref[...]
     started = ahead
     for at in range(0, depth, chunk):
         if at >= loaded:
             wait((at - loaded) // chunk)
         for column in range(0, 2 * half, tile):
             columns = pl.ds(column, tile)
-            weight = (
-                first_ref[at : at + chunk, columns]
-                if at < loaded
-                else rest_ref[at - loaded : at - loaded + chunk, columns]
-            )
+            ref, row = held[at // chunk] if at < loaded else (rest_ref, at - loaded)
             value = jnp.dot(
-                normed_ref[:, at : at + chunk], weight, preferred_element_type=jnp.float32
+                rows_ref[:, at : at + chunk],
+                ref[row : row + chunk, columns],
+                preferred_element_type=jnp.float32,
             )
             if at == 0:
                 product_ref[:, columns] = value
@@ -218,30 +325,32 @@
         send_ref[:, done, :] = wide_ref[rows // 2 :, done, :].astype(jnp.bfloat16)
 
 
-def block(near, far, gain, first, w_gate, w_up, w_down, half):
-    rows, lines, lanes = near.shape
-    depth = lines * lanes
-    chunk = 1024
-    rest = depth - first.shape[0]
-    vmem = pl.BlockSpec(memory_space=pltpu.VMEM)
-    hbm = pl.BlockSpec(memory_space=pltpu.HBM)
-    return pl.pallas_call(
-        functools.partial(block_kernel, half, chunk),
+def block(near, far, firsts, w_gate, w_up, w_down, half):
+    rows, depth = near.shape
+    lines = depth // LANES
+    rest = depth - sum(first.shape[0] for first in firsts)
+
+    def body(near_ref, far_ref, *refs):
+        count = len(firsts)
+        block_kernel(half, CHUNK, near_ref, far_ref, refs[:count], *refs[count:])
+
+    return pl.pallas_call(
+        body,
         out_shape=(
-            jax.ShapeDtypeStruct(near.shape, jnp.float32),
-            jax.ShapeDtypeStruct(near.shape, jnp.bfloat16),
-        ),
-        in_specs=[vmem] * 4 + [hbm] * 3,
-        out_specs=(vmem, vmem),
+            jax.ShapeDtypeStruct((rows, lines, LANES), jnp.float32),
+            jax.ShapeDtypeStruct((rows, lines, LANES), jnp.bfloat16),
+        ),
+        in_specs=[VMEM] * (2 + len(firsts)) + [HBM] * 3,
+        out_specs=(VMEM, VMEM),
         scratch_shapes=[
-            pltpu.VMEM((2 * rows, lines, lanes), jnp.float32),
+            pltpu.VMEM((2 * rows, lines, LANES), jnp.float32),
             pltpu.VMEM((2 * rows, depth), jnp.bfloat16),
             pltpu.VMEM((2 * rows, 2 * half), jnp.float32),
             pltpu.VMEM((2 * rows, half), jnp.bfloat16),
             pltpu.VMEM((rest, 2 * half), jnp.bfloat16),
             pltpu.VMEM((half, depth), jnp.bfloat16),
-            pltpu.SemaphoreType.DMA((rest // chunk, 2)),
-            pltpu.SemaphoreType.DMA((depth // chunk,)),
+            pltpu.SemaphoreType.DMA((rest // CHUNK, 2)),
+            pltpu.SemaphoreType.DMA((depth // CHUNK,)),
         ],
         compiler_params=pltpu.CompilerParams(
             vmem_limit_bytes=(rest * 2 + depth) * half * 2 + (6 << 20)
@@ -252,25 +361,52 @@
             transcendentals=0,
         ),
         name="block",
-    )(near, far, gain, pltpu.with_memory_space_constraint(first, pltpu.VMEM), w_gate, w_up, w_down)
-
-
-def deal(pieces, axes):
-    return lax.all_to_all(pieces, axes, split_axis=0, concat_axis=0, tiled=True)
-
-
-def other_core(value):
-    return lax.ppermute(value, "core", [(0, 1), (1, 0)])
+    )(
+        near,
+        far,
+        *(pltpu.with_memory_space_constraint(first, pltpu.VMEM) for first in firsts),
+        w_gate,
+        w_up,
+        w_down,
+    )
+
+
+def finish_kernel(*refs):
+    pieces, live_ref, out_ref = refs[:-2], refs[-2], refs[-1]
+    totals = pieces[0][...].astype(jnp.float32)
+    for piece in pieces[1:]:
+        totals = totals + piece[...].astype(jnp.float32)
+    totals = jnp.where(live_ref[:1] > 0, totals[0], jnp.zeros_like(totals[0]))
+    for line in range(totals.shape[0]):
+        out_ref[:, line * LANES : (line + 1) * LANES] = totals[line : line + 1].astype(jnp.bfloat16)
+
+
+def finish(pieces, live):
+    lines = pieces[0].shape[1]
+    return pl.pallas_call(
+        finish_kernel,
+        out_shape=jax.ShapeDtypeStruct((1, lines * LANES), jnp.bfloat16),
+        in_specs=[VMEM] * (len(pieces) + 1),
+        out_specs=VMEM,
+        compiler_params=pltpu.CompilerParams(vmem_limit_bytes=1 << 20),
+        name="finish",
+    )(*pieces, live)
+
+
+def swap(value, axes, offset):
+    places = range(lax.axis_size(axes))
+    return lax.ppermute(value, axes, [(place, place ^ offset) for place in places])
 
 
 def shared(tokens, norm_gain, w_gate, w_up, w_down, lengths, hit_lengths, start_positions):
-    depth = tokens.shape[1]
-    lines = depth // LANES
+    square = ("groups", "x")
     half = w_gate.shape[1] // lax.axis_size("groups")
-    deep = lax.axis_size("z")
-    square = lax.axis_size("groups") * lax.axis_size("x")
     w_gate, w_up, w_down = (
-        pltpu.with_memory_space_constraint(weight, pltpu.HBM) for weight in (w_gate, w_up, w_down)
+        pltpu.with_memory_space_constraint(array, pltpu.HBM) for array in (w_gate, w_up, w_down)
+    )
+    requests = tuple(
+        pltpu.with_memory_space_constraint(array, pltpu.HBM)
+        for array in (lengths, hit_lengths, start_positions)
     )
 
     def place():
@@ -278,20 +414,26 @@
             "core"
         ) + lax.axis_index("core")
 
-    first, keep = load_weights(
-        (lengths, hit_lengths, start_positions), w_gate, w_up, half, depth // 2, place
-    )
-    column = deal(jnp.broadcast_to(tokens.reshape(1, lines, LANES), (deep, lines, LANES)), "z")
-    plane = deal(jnp.broadcast_to(column, (square,) + column.shape), ("groups", "x"))
-    near = plane.reshape(square * deep, lines, LANES)
-    far = other_core(near)
-    kept, sent = block(near, far, norm_gain.reshape(1, depth), first, w_gate, w_up, w_down, half)
-    plane = (kept + other_core(sent).astype(jnp.float32)).astype(jnp.bfloat16)
-    column = jnp.sum(
-        deal(plane.reshape(square, deep, lines, LANES), ("groups", "x")).astype(jnp.float32), axis=0
-    ).astype(jnp.bfloat16)
-    totals = jnp.sum(deal(column, "z").astype(jnp.float32), axis=0)
-    return jnp.where(keep[:1] > 0, totals, jnp.zeros_like(totals)).astype(jnp.bfloat16).reshape(1, depth)
+    own = norm(tokens, norm_gain)
+    column = [own] + [swap(own, "z", at) for at in range(1, lax.axis_size("z"))]
+    first, mark = load_weights(w_gate, w_up, half, 0, CHUNK)
+    column = stack(column, mark)
+    plane = [column] + [swap(column, square, at) for at in range(1, lax.axis_size(square))]
+    second, live = load_weights(w_gate, w_up, half, CHUNK, 2 * CHUNK, requests, place)
+    near = pack(plane, live)
+    far = swap(near, "core", 1)
+    third, mark = load_weights(w_gate, w_up, half, 3 * CHUNK, CHUNK)
+    kept, sent = block(near, far, (first, second, third), w_gate, w_up, w_down, half)
+    plane = (kept + swap(sent, "core", 1).astype(jnp.float32)).astype(jnp.bfloat16)
+    pieces = jnp.split(plane, lax.axis_size(square), axis=0)
+    column = pieces[0].astype(jnp.float32)
+    for at, piece in enumerate(pieces[1:]):
+        column = column + swap(piece, square, at + 1).astype(jnp.float32)
+    column = column.astype(jnp.bfloat16)
+    pieces = jnp.split(column, lax.axis_size("z"), axis=0)
+    return finish(
+        pieces[:1] + [swap(piece, "z", at + 1) for at, piece in enumerate(pieces[1:])], live
+    )
 
 
 def solution(mesh):
@@ -315,7 +457,8 @@
             units % (LANES * groups) == 0
             and arrays[0].shape[0] == groups * members
             and groups == 2
-            and members % 8 == 0
+            and members >= 8
+            and members & (members - 1) == 0
         ):
             body, axes, whole = shared, ("z", "x", "core"), ROW_LINES
             over = jax.sharding.Mesh(mesh.devices.reshape(groups, members // 4, 2, 2), ROW_LINES)

time: 64.7 us -> 52.5 us (0.81)
  blocking collectives: 30 us -> 0 us
  starting transfers between devices: 3.86 us -> 17.9 us
  Pallas kernels: 18.4 us -> 23.8 us
  waiting for transfers between devices: 6.86 us -> 10.3 us
  local copies, waits for them, and re-layouts: 3.39 us -> 0.02 us
  other arithmetic: 1.6 us -> 0.11 us
    all_to_all x3 -> x0, blocking collectives: 30 us -> none  [deal(): return lax.all_to_all(pieces, axes, split_axis=0, concat_axis=0, tiled=True)]
    ppermute x2 -> x14, starting transfers between devices: 0.57 us -> 17.9 us  [swap(): lax.ppermute(value, axes, [(place, place ^ offset) for place in places])]
    ppermute x2 -> x14, waiting for transfers between devices: 1.16 us -> 10.3 us  [swap(): lax.ppermute(value, axes, [(place, place ^ offset) for place in places])]
    all_to_all x1 -> x0, waiting for transfers between devices: 5.7 us -> none  [deal(): return lax.all_to_all(pieces, axes, split_axis=0, concat_axis=0, tiled=True)]
    pallas_call x2 -> x8, Pallas kernels: 18.4 us -> 23.8 us  [the longest x1 13.6 us: block(): pl.pallas_call(body, out_shape=(jax.ShapeDtypeStruct((rows, lines, LANES)...]
    all_to_all x1 -> x0, starting transfers between devices: 3.28 us -> none  [deal(): return lax.all_to_all(pieces, axes, split_axis=0, concat_axis=0, tiled=True)]
    unnamed x7 -> x0, local copies, waits for them, and re-layouts: 2.6 us -> none
    unnamed x2 -> x0, other arithmetic: 0.86 us -> none
  transfers between devices with their start and end apart: 3 -> 14, of which waited for: 2 -> 8; matrix products, arithmetic and copies ran while one was open for 1% -> 0% of each run, Pallas kernels for 9% -> 15%
where the time goes in v4:
time: 52.5 us; the launch traced here: 52.3 us
  Pallas kernels  23.8 us (45%)
  starting transfers between devices  17.9 us (34%)
  waiting for transfers between devices  10.3 us (20%)
    ppermute x14, starting transfers between devices, swap(): lax.ppermute(value, axes, [(place, place ^ offset) for place in places])  17.9 us
    pallas_call x1, Pallas kernels, block(): pl.pallas_call(body, out_shape=(jax.ShapeDtypeStruct((rows, lines, LANES)...  13.6 us
    ppermute x14, waiting for transfers between devices, swap(): lax.ppermute(value, axes, [(place, place ^ offset) for place in places])  10.3 us
    pallas_call x3, Pallas kernels, load_weights(): pl.pallas_call(body, out_shape=(pltpu.VMEM((count, 2 * half), w_gate.dtyp...  8 us
  transfers between devices with their start and end apart: 14, of which 8 were waited for; matrix products, arithmetic and copies ran while one was open for 0% of the time, Pallas kernels for 15%

profile of v4, /device:TPU:0, one launch (start us, length us, event | category | flops | bytes accessed | tf_op | source)
XLA Modules:
  0.0 52.3 jit_solution(3836911687341770395)
XLA Ops:
  0.0 1.0 %norm.1.refs_0_ = bf16[1,64,128]{2,1,0:T(8,128)(2,1)S(1)} custom-call(bf16[1,8192]{1,0:T(2,128)(2,1)} %tokens_hbm.1, bf16[64,128]{1,0:T(8,128)(2,1)} %bitcast.1), custom_call_target="tpu_custom_call" | custom-call | tf_op jit(solution)/shard_map/norm/pallas_call | solution.py:91
  1.0 5.1 %collective-permute-start.2 = (bf16[1,64,128]{2,1,0:T(8,128)(2,1)S(1)}, bf16[1,64,128]{2,1,0:T(8,128)(2,1)S(1)}, u32[]{:S(2)}, u32[]{:S(2)}) collective-permute-start(bf16[1,64,128]{2,1,0:T(8,128)(2,1)S(1)} %norm.1.refs_0_), channel_id=1, source_target_pairs={{0,12},{4,8},{8,4},{12,0},{1,13},{5,9},{9,5},{13,1},{2,14},{6,10},... | collective-permute-start | bytes 49160 | tf_op jit(solution)/shard_map/ppermute | solution.py:398
  6.1 0.0 collective-permute-start.1
  6.1 0.6 %collective-permute-start = (bf16[1,64,128]{2,1,0:T(8,128)(2,1)S(1)}, bf16[1,64,128]{2,1,0:T(8,128)(2,1)S(1)}, u32[]{:S(2)}, u32[]{:S(2)}) collective-permute-start(bf16[1,64,128]{2,1,0:T(8,128)(2,1)S(1)} %norm.1.refs_0_), channel_id=1, source_target_pairs={{0,4},{4,0},{8,12},{12,8},{1,5},{5,1},{9,13},{13,9},{2,6},{6,2},{1... | collective-permute-start | bytes 49160 | tf_op jit(solution)/shard_map/ppermute | solution.py:398
  6.7 2.1 %load_weights.3 = (bf16[1024,1792]{1,0:T(8,128)(2,1)S(1)}, f32[8,128]{1,0:T(8,128)S(1)}) custom-call(bf16[8192,1792]{1,0:T(8,128)(2,1)} %refs_3_.1, bf16[8192,1792]{1,0:T(8,128)(2,1)} %refs_4_.1), custom_call_target="tpu_custom_call" | custom-call | bytes 3670016 | tf_op jit(solution)/shard_map/load_weights/pallas_call | solution.py:186
  8.8 0.0 collective-permute-done.2.refs_3_
  8.8 1.9 %collective-permute-done.1.refs_2_ = bf16[1,64,128]{2,1,0:T(8,128)(2,1)S(1)} collective-permute-done((bf16[1,64,128]{2,1,0:T(8,128)(2,1)S(1)}, bf16[1,64,128]{2,1,0:T(8,128)(2,1)S(1)}, u32[]{:S(2)}, u32[]{:S(2)}) %collective-permute-start.1) | collective-permute-done | bytes 16416 | tf_op jit(solution)/shard_map/ppermute | solution.py:398
  10.7 0.0 collective-permute-done.refs_1_
  10.7 2.5 %collective-permute-start.5 = (bf16[4,64,128]{2,1,0:T(8,128)(2,1)S(1)}, bf16[4,64,128]{2,1,0:T(8,128)(2,1)S(1)}, u32[]{:S(2)}, u32[]{:S(2)}) collective-permute-start(bf16[4,64,128]{2,1,0:T(8,128)(2,1)S(1)} %stack.1.refs_0_), channel_id=1, source_target_pairs={{0,18},{2,16},{16,2},{18,0},{1,19},{3,17},{17,3},{19,1},{4,22},{6,... | collective-permute-start | bytes 196616 | tf_op jit(solution)/shard_map/ppermute | solution.py:398
  13.2 0.5 collective-permute-start.4
  13.7 0.5 %collective-permute-start.3 = (bf16[4,64,128]{2,1,0:T(8,128)(2,1)S(1)}, bf16[4,64,128]{2,1,0:T(8,128)(2,1)S(1)}, u32[]{:S(2)}, u32[]{:S(2)}) collective-permute-start(bf16[4,64,128]{2,1,0:T(8,128)(2,1)S(1)} %stack.1.refs_0_), channel_id=1, source_target_pairs={{0,2},{2,0},{16,18},{18,16},{1,3},{3,1},{17,19},{19,17},{4,6},{6,4... | collective-permute-start | bytes 196616 | tf_op jit(solution)/shard_map/ppermute | solution.py:398
  14.3 3.2 %load_weights.4 = (bf16[2048,1792]{1,0:T(8,128)(2,1)S(1)}, f32[8,128]{1,0:T(8,128)S(1)}) custom-call(s32[8]{0:T(128)} %lengths.1, s32[8]{0:T(128)} %hit_lengths.1, s32[8]{0:T(128)} %start_positions.1, bf16[8192,1792]{1,0:T(8,128)(2,1)} %refs_3_.1, bf16[8192,1792]{1,0:T(8,128)(2,1)} %refs_4_.1), custom_call_target="tpu_custom_call" | custom-call | bytes 7340032 | tf_op jit(solution)/shard_map/load_weights/pallas_call | solution.py:186
  17.5 0.0 collective-permute-done.5.refs_3_
  17.5 0.0 collective-permute-done.4.refs_2_
  17.5 0.5 collective-permute-done.3.refs_1_
  18.0 0.6 %pack.1.near_ref = bf16[16,8192]{1,0:T(8,128)(2,1)S(1)} custom-call(bf16[4,64,128]{2,1,0:T(8,128)(2,1)S(1)} %stack.1.refs_0_, bf16[4,64,128]{2,1,0:T(8,128)(2,1)S(1)} %collective-permute-done.3.refs_1_, bf16[4,64,128]{2,1,0:T(8,128)(2,1)S(1)} %collective-permute-done.4.refs_2_, bf16[4,64,128]{2,1,0:T(8,128)(2,1)S(1)} %collective-permute-done.5.refs_3_, ...), custom_call_target="tpu_custom_call" | custom-call | tf_op jit(solution)/shard_map/pack/pallas_call | solution.py:216
  18.6 0.1 collective-permute-start.6
  18.7 2.7 %load_weights.5 = (bf16[1024,1792]{1,0:T(8,128)(2,1)S(1)}, f32[8,128]{1,0:T(8,128)}) custom-call(bf16[8192,1792]{1,0:T(8,128)(2,1)} %refs_3_.1, bf16[8192,1792]{1,0:T(8,128)(2,1)} %refs_4_.1), custom_call_target="tpu_custom_call" | custom-call | bytes 3670016 | tf_op jit(solution)/shard_map/load_weights/pallas_call | solution.py:186
  21.4 0.0 collective-permute-done.6.far_ref
  21.4 13.6 %block.1 = (f32[16,64,128]{2,1,0:T(8,128)S(1)}, bf16[16,64,128]{2,1,0:T(8,128)(2,1)S(1)}) custom-call(bf16[16,8192]{1,0:T(8,128)(2,1)S(1)} %pack.1.near_ref, bf16[16,8192]{1,0:T(8,128)(2,1)S(1)} %collective-permute-done.6.far_ref, bf16[1024,1792]{1,0:T(8,128)(2,1)S(1)} %get-tuple-element.14.refs_0_, bf16[2048,1792]{1,0:T(8,128)(2,1)S(1)} %get-tuple-element.15.refs_1_, ...), custom_call_target="tpu_custom_call" | custom-call | flops 1409286144 | bytes 29360128 | tf_op jit(solution)/shard_map/block/pallas_call | solution.py:337
  35.0 0.5 %collective-permute-start.7 = (bf16[16,64,128]{2,1,0:T(8,128)(2,1)S(1)}, bf16[16,64,128]{2,1,0:T(8,128)(2,1)S(1)}, u32[]{:S(2)}, u32[]{:S(2)}) collective-permute-start(bf16[16,64,128]{2,1,0:T(8,128)(2,1)S(1)} %get-tuple-element.18), channel_id=1, source_target_pairs={{0,1},{1,0},{2,3},{3,2},{4,5},{5,4},{6,7},{7,6},{8,9},{9,8},{10,11... | collective-permute-start | bytes 786440 | tf_op jit(solution)/shard_map/ppermute | solution.py:398
  35.6 1.2 %collective-permute-done.7 = bf16[16,64,128]{2,1,0:T(8,128)(2,1)S(1)} collective-permute-done((bf16[16,64,128]{2,1,0:T(8,128)(2,1)S(1)}, bf16[16,64,128]{2,1,0:T(8,128)(2,1)S(1)}, u32[]{:S(2)}, u32[]{:S(2)}) %collective-permute-start.7) | collective-permute-done | bytes 262176 | tf_op jit(solution)/shard_map/ppermute | solution.py:398
  36.7 0.1 add_convert_fusion
  36.8 1.1 %collective-permute-start.8 = (bf16[4,64,128]{2,1,0:T(8,128)(2,1)S(1)}, bf16[4,64,128]{2,1,0:T(8,128)(2,1)S(1)}, u32[]{:S(2)}, u32[]{:S(2)}) collective-permute-start(bf16[4,64,128]{2,1,0:T(8,128)(2,1)S(1)} %get-tuple-element.19), channel_id=1, source_target_pairs={{0,2},{2,0},{16,18},{18,16},{1,3},{3,1},{17,19},{19,17},{4,6},{6,4... | collective-permute-start | bytes 196616 | tf_op jit(solution)/shard_map/ppermute | solution.py:398
  37.9 2.0 %collective-permute-start.10 = (bf16[4,64,128]{2,1,0:T(8,128)(2,1)S(1)}, bf16[4,64,128]{2,1,0:T(8,128)(2,1)S(1)}, u32[]{:S(2)}, u32[]{:S(2)}) collective-permute-start(bf16[4,64,128]{2,1,0:T(8,128)(2,1)S(1)} %get-tuple-element.20), channel_id=1, source_target_pairs={{0,18},{2,16},{16,2},{18,0},{1,19},{3,17},{17,3},{19,1},{4,22},{6,... | collective-permute-start | bytes 196616 | tf_op jit(solution)/shard_map/ppermute | solution.py:398
  39.9 0.5 collective-permute-start.9
  40.4 0.9 %collective-permute-done.8 = bf16[4,64,128]{2,1,0:T(8,128)(2,1)S(1)} collective-permute-done((bf16[4,64,128]{2,1,0:T(8,128)(2,1)S(1)}, bf16[4,64,128]{2,1,0:T(8,128)(2,1)S(1)}, u32[]{:S(2)}, u32[]{:S(2)}) %collective-permute-start.8) | collective-permute-done | bytes 65568 | tf_op jit(solution)/shard_map/ppermute | solution.py:398
  41.3 2.5 %collective-permute-done.10 = bf16[4,64,128]{2,1,0:T(8,128)(2,1)S(1)} collective-permute-done((bf16[4,64,128]{2,1,0:T(8,128)(2,1)S(1)}, bf16[4,64,128]{2,1,0:T(8,128)(2,1)S(1)}, u32[]{:S(2)}, u32[]{:S(2)}) %collective-permute-start.10) | collective-permute-done | bytes 65568 | tf_op jit(solution)/shard_map/ppermute | solution.py:398
  43.7 1.1 %collective-permute-done.9 = bf16[4,64,128]{2,1,0:T(8,128)(2,1)S(1)} collective-permute-done((bf16[4,64,128]{2,1,0:T(8,128)(2,1)S(1)}, bf16[4,64,128]{2,1,0:T(8,128)(2,1)S(1)}, u32[]{:S(2)}, u32[]{:S(2)}) %collective-permute-start.9) | collective-permute-done | bytes 65568 | tf_op jit(solution)/shard_map/ppermute | solution.py:398
  44.9 2.0 %collective-permute-start.13 = (bf16[1,64,128]{2,1,0:T(8,128)(2,1)S(1)}, bf16[1,64,128]{2,1,0:T(8,128)(2,1)S(1)}, u32[]{:S(2)}, u32[]{:S(2)}) collective-permute-start(bf16[1,64,128]{2,1,0:T(8,128)(2,1)S(1)} %get-tuple-element.22), channel_id=1, source_target_pairs={{0,12},{4,8},{8,4},{12,0},{1,13},{5,9},{9,5},{13,1},{2,14},{6,10},... | collective-permute-start | bytes 49160 | tf_op jit(solution)/shard_map/ppermute | solution.py:398
  46.8 0.1 collective-permute-start.12
  47.0 2.4 %collective-permute-start.11 = (bf16[1,64,128]{2,1,0:T(8,128)(2,1)S(1)}, bf16[1,64,128]{2,1,0:T(8,128)(2,1)S(1)}, u32[]{:S(2)}, u32[]{:S(2)}) collective-permute-start(bf16[1,64,128]{2,1,0:T(8,128)(2,1)S(1)} %get-tuple-element.24), channel_id=1, source_target_pairs={{0,4},{4,0},{8,12},{12,8},{1,5},{5,1},{9,13},{13,9},{2,6},{6,2},{1... | collective-permute-start | bytes 49160 | tf_op jit(solution)/shard_map/ppermute | solution.py:398
  49.3 1.1 %collective-permute-done.13.refs_3_ = bf16[1,64,128]{2,1,0:T(8,128)(2,1)S(1)} collective-permute-done((bf16[1,64,128]{2,1,0:T(8,128)(2,1)S(1)}, bf16[1,64,128]{2,1,0:T(8,128)(2,1)S(1)}, u32[]{:S(2)}, u32[]{:S(2)}) %collective-permute-start.13) | collective-permute-done | bytes 16416 | tf_op jit(solution)/shard_map/ppermute | solution.py:398
  50.5 1.2 %collective-permute-done.12.refs_2_ = bf16[1,64,128]{2,1,0:T(8,128)(2,1)S(1)} collective-permute-done((bf16[1,64,128]{2,1,0:T(8,128)(2,1)S(1)}, bf16[1,64,128]{2,1,0:T(8,128)(2,1)S(1)}, u32[]{:S(2)}, u32[]{:S(2)}) %collective-permute-start.12) | collective-permute-done | bytes 16416 | tf_op jit(solution)/shard_map/ppermute | solution.py:398
  51.6 0.0 collective-permute-done.11.refs_1_
  51.6 0.7 %finish.1 = bf16[1,8192]{1,0:T(2,128)(2,1)} custom-call(bf16[1,64,128]{2,1,0:T(8,128)(2,1)S(1)} %get-tuple-element.25.refs_0_, bf16[1,64,128]{2,1,0:T(8,128)(2,1)S(1)} %collective-permute-done.11.refs_1_, bf16[1,64,128]{2,1,0:T(8,128)(2,1)S(1)} %collective-permute-done.12.refs_2_, bf16[1,64,128]{2,1,0:T(8,128)(2,1)S(1)} %collective-permute-done.13.refs_3_, ...), custom_call_target="tpu_custom_call" | custom-call | tf_op jit(solution)/shard_map/finish/pallas_call | solution.py:386
  (4 shorter events, 0.1 us)
Async XLA Ops:
  1.0 7.9 %collective-permute-start.2 = (bf16[1,64,128]{2,1,0:T(8,128)(2,1)S(1)}, bf16[1,64,128]{2,1,0:T(8,128)(2,1)S(1)}, u32[]{:S(2)}, u32[]{:S(2)}) collective-permute-start(bf16[1,64,128]{2,1,0:T(8,128)(2,1)S(1)} %norm.1.refs_0_), channel_id=1, source_target_pairs={{0,12},{4,8},{8,4},{12,0},{1,13},{5,9},{9,5},{13,1},{2,14},{6,10},... | collective-permute-start | bytes 49160 | tf_op jit(solution)/shard_map/ppermute | solution.py:398
  6.1 4.6 %collective-permute-start.1 = (bf16[1,64,128]{2,1,0:T(8,128)(2,1)S(1)}, bf16[1,64,128]{2,1,0:T(8,128)(2,1)S(1)}, u32[]{:S(2)}, u32[]{:S(2)}) collective-permute-start(bf16[1,64,128]{2,1,0:T(8,128)(2,1)S(1)} %norm.1.refs_0_), channel_id=1, source_target_pairs={{0,8},{4,12},{8,0},{12,4},{1,9},{5,13},{9,1},{13,5},{2,10},{6,14},... | collective-permute-start | bytes 49160 | tf_op jit(solution)/shard_map/ppermute | solution.py:398
  6.1 4.6 %collective-permute-start = (bf16[1,64,128]{2,1,0:T(8,128)(2,1)S(1)}, bf16[1,64,128]{2,1,0:T(8,128)(2,1)S(1)}, u32[]{:S(2)}, u32[]{:S(2)}) collective-permute-start(bf16[1,64,128]{2,1,0:T(8,128)(2,1)S(1)} %norm.1.refs_0_), channel_id=1, source_target_pairs={{0,4},{4,0},{8,12},{12,8},{1,5},{5,1},{9,13},{13,9},{2,6},{6,2},{1... | collective-permute-start | bytes 49160 | tf_op jit(solution)/shard_map/ppermute | solution.py:398
  10.7 6.8 %collective-permute-start.5 = (bf16[4,64,128]{2,1,0:T(8,128)(2,1)S(1)}, bf16[4,64,128]{2,1,0:T(8,128)(2,1)S(1)}, u32[]{:S(2)}, u32[]{:S(2)}) collective-permute-start(bf16[4,64,128]{2,1,0:T(8,128)(2,1)S(1)} %stack.1.refs_0_), channel_id=1, source_target_pairs={{0,18},{2,16},{16,2},{18,0},{1,19},{3,17},{17,3},{19,1},{4,22},{6,... | collective-permute-start | bytes 196616 | tf_op jit(solution)/shard_map/ppermute | solution.py:398
  13.2 4.3 %collective-permute-start.4 = (bf16[4,64,128]{2,1,0:T(8,128)(2,1)S(1)}, bf16[4,64,128]{2,1,0:T(8,128)(2,1)S(1)}, u32[]{:S(2)}, u32[]{:S(2)}) collective-permute-start(bf16[4,64,128]{2,1,0:T(8,128)(2,1)S(1)} %stack.1.refs_0_), channel_id=1, source_target_pairs={{0,16},{2,18},{16,0},{18,2},{1,17},{3,19},{17,1},{19,3},{4,20},{6,... | collective-permute-start | bytes 196616 | tf_op jit(solution)/shard_map/ppermute | solution.py:398
  13.7 4.3 %collective-permute-start.3 = (bf16[4,64,128]{2,1,0:T(8,128)(2,1)S(1)}, bf16[4,64,128]{2,1,0:T(8,128)(2,1)S(1)}, u32[]{:S(2)}, u32[]{:S(2)}) collective-permute-start(bf16[4,64,128]{2,1,0:T(8,128)(2,1)S(1)} %stack.1.refs_0_), channel_id=1, source_target_pairs={{0,2},{2,0},{16,18},{18,16},{1,3},{3,1},{17,19},{19,17},{4,6},{6,4... | collective-permute-start | bytes 196616 | tf_op jit(solution)/shard_map/ppermute | solution.py:398
  18.6 2.8 %collective-permute-start.6 = (bf16[16,8192]{1,0:T(8,128)(2,1)S(1)}, bf16[16,8192]{1,0:T(8,128)(2,1)S(1)}, u32[]{:S(2)}, u32[]{:S(2)}) collective-permute-start(bf16[16,8192]{1,0:T(8,128)(2,1)S(1)} %pack.1.near_ref), channel_id=1, source_target_pairs={{0,1},{1,0},{2,3},{3,2},{4,5},{5,4},{6,7},{7,6},{8,9},{9,8},{10,11... | collective-permute-start | bytes 786440 | tf_op jit(solution)/shard_map/ppermute | solution.py:398
  35.0 1.7 %collective-permute-start.7 = (bf16[16,64,128]{2,1,0:T(8,128)(2,1)S(1)}, bf16[16,64,128]{2,1,0:T(8,128)(2,1)S(1)}, u32[]{:S(2)}, u32[]{:S(2)}) collective-permute-start(bf16[16,64,128]{2,1,0:T(8,128)(2,1)S(1)} %get-tuple-element.18), channel_id=1, source_target_pairs={{0,1},{1,0},{2,3},{3,2},{4,5},{5,4},{6,7},{7,6},{8,9},{9,8},{10,11... | collective-permute-start | bytes 786440 | tf_op jit(solution)/shard_map/ppermute | solution.py:398
  36.8 4.4 %collective-permute-start.8 = (bf16[4,64,128]{2,1,0:T(8,128)(2,1)S(1)}, bf16[4,64,128]{2,1,0:T(8,128)(2,1)S(1)}, u32[]{:S(2)}, u32[]{:S(2)}) collective-permute-start(bf16[4,64,128]{2,1,0:T(8,128)(2,1)S(1)} %get-tuple-element.19), channel_id=1, source_target_pairs={{0,2},{2,0},{16,18},{18,16},{1,3},{3,1},{17,19},{19,17},{4,6},{6,4... | collective-permute-start | bytes 196616 | tf_op jit(solution)/shard_map/ppermute | solution.py:398
  37.9 5.8 %collective-permute-start.10 = (bf16[4,64,128]{2,1,0:T(8,128)(2,1)S(1)}, bf16[4,64,128]{2,1,0:T(8,128)(2,1)S(1)}, u32[]{:S(2)}, u32[]{:S(2)}) collective-permute-start(bf16[4,64,128]{2,1,0:T(8,128)(2,1)S(1)} %get-tuple-element.20), channel_id=1, source_target_pairs={{0,18},{2,16},{16,2},{18,0},{1,19},{3,17},{17,3},{19,1},{4,22},{6,... | collective-permute-start | bytes 196616 | tf_op jit(solution)/shard_map/ppermute | solution.py:398
  39.9 4.9 %collective-permute-start.9 = (bf16[4,64,128]{2,1,0:T(8,128)(2,1)S(1)}, bf16[4,64,128]{2,1,0:T(8,128)(2,1)S(1)}, u32[]{:S(2)}, u32[]{:S(2)}) collective-permute-start(bf16[4,64,128]{2,1,0:T(8,128)(2,1)S(1)} %get-tuple-element.21), channel_id=1, source_target_pairs={{0,16},{2,18},{16,0},{18,2},{1,17},{3,19},{17,1},{19,3},{4,20},{6,... | collective-permute-start | bytes 196616 | tf_op jit(solution)/shard_map/ppermute | solution.py:398
  44.9 5.6 %collective-permute-start.13 = (bf16[1,64,128]{2,1,0:T(8,128)(2,1)S(1)}, bf16[1,64,128]{2,1,0:T(8,128)(2,1)S(1)}, u32[]{:S(2)}, u32[]{:S(2)}) collective-permute-start(bf16[1,64,128]{2,1,0:T(8,128)(2,1)S(1)} %get-tuple-element.22), channel_id=1, source_target_pairs={{0,12},{4,8},{8,4},{12,0},{1,13},{5,9},{9,5},{13,1},{2,14},{6,10},... | collective-permute-start | bytes 49160 | tf_op jit(solution)/shard_map/ppermute | solution.py:398
  46.8 4.8 %collective-permute-start.12 = (bf16[1,64,128]{2,1,0:T(8,128)(2,1)S(1)}, bf16[1,64,128]{2,1,0:T(8,128)(2,1)S(1)}, u32[]{:S(2)}, u32[]{:S(2)}) collective-permute-start(bf16[1,64,128]{2,1,0:T(8,128)(2,1)S(1)} %get-tuple-element.23), channel_id=1, source_target_pairs={{0,8},{4,12},{8,0},{12,4},{1,9},{5,13},{9,1},{13,5},{2,10},{6,14},... | collective-permute-start | bytes 49160 | tf_op jit(solution)/shard_map/ppermute | solution.py:398
  47.0 4.7 %collective-permute-start.11 = (bf16[1,64,128]{2,1,0:T(8,128)(2,1)S(1)}, bf16[1,64,128]{2,1,0:T(8,128)(2,1)S(1)}, u32[]{:S(2)}, u32[]{:S(2)}) collective-permute-start(bf16[1,64,128]{2,1,0:T(8,128)(2,1)S(1)} %get-tuple-element.24), channel_id=1, source_target_pairs={{0,4},{4,0},{8,12},{12,8},{1,5},{5,1},{9,13},{13,9},{2,6},{6,2},{1... | collective-permute-start | bytes 49160 | tf_op jit(solution)/shard_map/ppermute | solution.py:398

commit v5 on v4

--- a/solution.py
+++ b/solution.py
@@ -202,12 +202,18 @@
 
 def pack_kernel(*refs):
     pieces, out_ref, wide_ref = refs[:-3], refs[-2], refs[-1]
-    at = 0
+    rows = out_ref.shape[0]
+    lines = out_ref.shape[1] // LANES
+    stride = wide_ref.shape[0] // rows
+    row = 0
     for piece in pieces:
-        wide_ref[at : at + piece.shape[0]] = piece[...].astype(jnp.float32)
-        at += piece.shape[0]
-    for line in range(wide_ref.shape[1]):
-        out_ref[:, line * LANES : (line + 1) * LANES] = wide_ref[:, line, :].astype(jnp.bfloat16)
+        for at in range(piece.shape[0]):
+            wide_ref[row * stride : row * stride + lines] = piece[at].astype(jnp.float32)
+            row += 1
+    for line in range(lines):
+        out_ref[:, line * LANES : (line + 1) * LANES] = wide_ref[
+            pl.ds(line, rows, stride=stride), :
+        ].astype(jnp.bfloat16)
 
 
 def pack(pieces, mark):
@@ -218,7 +224,7 @@
         out_shape=jax.ShapeDtypeStruct((rows, lines * LANES), jnp.bfloat16),
         in_specs=[VMEM] * len(pieces) + [pl.BlockSpec(memory_space=pl.ANY)],
         out_specs=VMEM,
-        scratch_shapes=[pltpu.VMEM((rows, lines, LANES), jnp.float32)],
+        scratch_shapes=[pltpu.VMEM((rows * (lines + 1), LANES), jnp.float32)],
         compiler_params=pltpu.CompilerParams(vmem_limit_bytes=4 << 20),
         name="pack",
     )(*pieces, mark)
@@ -245,9 +251,10 @@
     down_sems,
 ):
     tile = 256
-    ahead = 3
-    rows, lines, lanes = wide_ref.shape
-    depth = lines * lanes
+    rows, depth = rows_ref.shape
+    lanes = LANES
+    lines = depth // lanes
+    stride = wide_ref.shape[0] // rows
     held = [(ref, at) for ref in first_refs for at in range(0, ref.shape[0], chunk)]
     loaded = len(held) * chunk
     own = pl.multiple_of(lax.axis_index("groups") * half, LANES)
@@ -275,8 +282,16 @@
             ]
         )
 
-    def start(number):
-        if number < len(loads):
+    steps = depth // chunk
+    early = min(3, pairs)
+    due = [[] for _ in range(2 * steps)]
+    for number in range(early, pairs):
+        due[number - early].append(number)
+    for number in range(pairs, len(loads)):
+        due[pairs - 1 + (number - pairs) // 2].append(number)
+
+    def start(numbers):
+        for number in numbers:
             for copy in loads[number]:
                 copy.start()
 
@@ -284,12 +299,9 @@
         for copy in loads[number]:
             copy.wait()
 
-    for number in range(ahead):
-        start(number)
-
+    start(range(early))
     rows_ref[: rows // 2] = near_ref[...]
     rows_ref[rows // 2 :] = far_ref[...]
-    started = ahead
     for at in range(0, depth, chunk):
         if at >= loaded:
             wait((at - loaded) // chunk)
@@ -305,24 +317,29 @@
                 product_ref[:, columns] = value
             else:
                 product_ref[:, columns] += value
-        start(started)
-        started += 1
+        start(due[at // chunk])
     gate_out = product_ref[:, :half]
     up_out = product_ref[:, half:]
     hidden_ref[...] = (gate_out / (1.0 + jnp.exp(-gate_out)) * up_out).astype(jnp.bfloat16)
-    for step in range(depth // chunk):
+    for step in range(steps):
         wait(pairs + step)
         for at in range(step * chunk, (step + 1) * chunk, tile):
             result = jnp.dot(
                 hidden_ref[...], down_ref[:, pl.ds(at, tile)], preferred_element_type=jnp.float32
             )
             for line in range(tile // lanes):
-                wide_ref[:, at // lanes + line, :] = result[:, line * lanes : (line + 1) * lanes]
-        start(started)
-        started += 1
-        done = pl.ds(step * chunk // lanes, chunk // lanes)
-        keep_ref[:, done, :] = wide_ref[: rows // 2, done, :]
-        send_ref[:, done, :] = wide_ref[rows // 2 :, done, :].astype(jnp.bfloat16)
+                wide_ref[pl.ds(at // lanes + line, rows, stride=stride), :] = result[
+                    :, line * lanes : (line + 1) * lanes
+                ]
+        start(due[steps + step])
+        done = step * chunk // lanes
+        count = chunk // lanes
+        for row in range(rows):
+            ready = wide_ref[row * stride + done : row * stride + done + count]
+            if row < rows // 2:
+                keep_ref[row, done : done + count] = ready
+            else:
+                send_ref[row - rows // 2, done : done + count] = ready.astype(jnp.bfloat16)
 
 
 def block(near, far, firsts, w_gate, w_up, w_down, half):
@@ -343,7 +360,7 @@
         in_specs=[VMEM] * (2 + len(firsts)) + [HBM] * 3,
         out_specs=(VMEM, VMEM),
         scratch_shapes=[
-            pltpu.VMEM((2 * rows, lines, LANES), jnp.float32),
+            pltpu.VMEM((2 * rows * (lines + 1), LANES), jnp.float32),
             pltpu.VMEM((2 * rows, depth), jnp.bfloat16),
             pltpu.VMEM((2 * rows, 2 * half), jnp.float32),
             pltpu.VMEM((2 * rows, half), jnp.bfloat16),
@@ -398,6 +415,15 @@
     return lax.ppermute(value, axes, [(place, place ^ offset) for place in places])
 
 
+def halving(count):
+    order = [0]
+    bit = count // 2
+    while bit:
+        order = order + [at + bit for at in order]
+        bit //= 2
+    return order
+
+
 def shared(tokens, norm_gain, w_gate, w_up, w_down, lengths, hit_lengths, start_positions):
     square = ("groups", "x")
     half = w_gate.shape[1] // lax.axis_size("groups")
@@ -414,26 +440,34 @@
             "core"
         ) + lax.axis_index("core")
 
+    deep = lax.axis_size("z")
+    far_first = [3, 1, 2]
+    rest = [0] + far_first
     own = norm(tokens, norm_gain)
-    column = [own] + [swap(own, "z", at) for at in range(1, lax.axis_size("z"))]
-    first, mark = load_weights(w_gate, w_up, half, 0, CHUNK)
+    column = [own] + [swap(own, "z", at) for at in halving(deep)[1:]]
+    first, mark = load_weights(w_gate, w_up, half, 0, 2 * CHUNK)
     column = stack(column, mark)
-    plane = [column] + [swap(column, square, at) for at in range(1, lax.axis_size(square))]
-    second, live = load_weights(w_gate, w_up, half, CHUNK, 2 * CHUNK, requests, place)
+    plane = [column] + [swap(column, square, at) for at in far_first]
+    second, live = load_weights(w_gate, w_up, half, 2 * CHUNK, 2 * CHUNK, requests, place)
     near = pack(plane, live)
     far = swap(near, "core", 1)
-    third, mark = load_weights(w_gate, w_up, half, 3 * CHUNK, CHUNK)
-    kept, sent = block(near, far, (first, second, third), w_gate, w_up, w_down, half)
+    kept, sent = block(near, far, (first, second), w_gate, w_up, w_down, half)
     plane = (kept + swap(sent, "core", 1).astype(jnp.float32)).astype(jnp.bfloat16)
-    pieces = jnp.split(plane, lax.axis_size(square), axis=0)
+    pieces = jnp.split(plane, len(rest), axis=0)
+    arrived = [swap(piece, square, at) for at, piece in zip(far_first, pieces[1:])]
     column = pieces[0].astype(jnp.float32)
-    for at, piece in enumerate(pieces[1:]):
-        column = column + swap(piece, square, at + 1).astype(jnp.float32)
+    for piece in arrived:
+        column = column + piece.astype(jnp.float32)
     column = column.astype(jnp.bfloat16)
-    pieces = jnp.split(column, lax.axis_size("z"), axis=0)
-    return finish(
-        pieces[:1] + [swap(piece, "z", at + 1) for at, piece in enumerate(pieces[1:])], live
-    )
+    distance = 1
+    while distance < deep // 2:
+        kept, sent = jnp.split(column, 2, axis=0)
+        column = (kept.astype(jnp.float32) + swap(sent, "z", distance).astype(jnp.float32)).astype(
+            jnp.bfloat16
+        )
+        distance *= 2
+    kept, sent = jnp.split(column, 2, axis=0)
+    return finish([kept, swap(sent, "z", distance)], live)
 
 
 def solution(mesh):

time: 52.5 us -> 50.6 us (0.964)
  Pallas kernels: 23.8 us -> 20.4 us
  waiting for transfers between devices: 10.3 us -> 12.8 us
  starting transfers between devices: 17.9 us -> 16.8 us
    ppermute x14 -> x13, waiting for transfers between devices: 10.3 us -> 12.8 us  [swap(): lax.ppermute(value, axes, [(place, place ^ offset) for place in places])]
    pallas_call x3 -> x2, Pallas kernels: 8 us -> 6.42 us  [load_weights(): pl.pallas_call(body, out_shape=(pltpu.VMEM((count, 2 * half), w_gate.dtyp...]
    pallas_call x1, Pallas kernels: 13.6 us -> 12.3 us  [block(): pl.pallas_call(body, out_shape=(jax.ShapeDtypeStruct((rows, lines, LANES)...]
    ppermute x14 -> x13, starting transfers between devices: 17.9 us -> 16.8 us  [swap(): lax.ppermute(value, axes, [(place, place ^ offset) for place in places])]
  transfers between devices with their start and end apart: 14 -> 13, of which waited for: 8 -> 8; matrix products, arithmetic and copies ran while one was open for 0% -> 0% of each run, Pallas kernels for 15% -> 13%
where the time goes in v5:
time: 50.6 us; the launch traced here: 50.4 us
  Pallas kernels  20.4 us (40%)
  starting transfers between devices  16.8 us (33%)
  waiting for transfers between devices  12.8 us (25%)
    ppermute x13, starting transfers between devices, swap(): lax.ppermute(value, axes, [(place, place ^ offset) for place in places])  16.8 us
    ppermute x13, waiting for transfers between devices, swap(): lax.ppermute(value, axes, [(place, place ^ offset) for place in places])  12.8 us
    pallas_call x1, Pallas kernels, block(): pl.pallas_call(body, out_shape=(jax.ShapeDtypeStruct((rows, lines, LANES)...  12.3 us
    pallas_call x2, Pallas kernels, load_weights(): pl.pallas_call(body, out_shape=(pltpu.VMEM((count, 2 * half), w_gate.dtyp...  6.42 us
  transfers between devices with their start and end apart: 13, of which 8 were waited for; matrix products, arithmetic and copies ran while one was open for 0% of the time, Pallas kernels for 13%

profile of v5, /device:TPU:0, one launch (start us, length us, event | category | flops | bytes accessed | tf_op | source)
XLA Modules:
  0.0 50.4 jit_solution(6739210406175049105)
XLA Ops:
  0.0 1.0 %norm.1.refs_0_ = bf16[1,64,128]{2,1,0:T(8,128)(2,1)S(1)} custom-call(bf16[1,8192]{1,0:T(2,128)(2,1)} %tokens_hbm.1, bf16[64,128]{1,0:T(8,128)(2,1)} %bitcast.1), custom_call_target="tpu_custom_call" | custom-call | tf_op jit(solution)/shard_map/norm/pallas_call | solution.py:91
  1.0 5.1 %collective-permute-start.2 = (bf16[1,64,128]{2,1,0:T(8,128)(2,1)S(1)}, bf16[1,64,128]{2,1,0:T(8,128)(2,1)S(1)}, u32[]{:S(2)}, u32[]{:S(2)}) collective-permute-start(bf16[1,64,128]{2,1,0:T(8,128)(2,1)S(1)} %norm.1.refs_0_), channel_id=1, source_target_pairs={{0,12},{4,8},{8,4},{12,0},{1,13},{5,9},{9,5},{13,1},{2,14},{6,10},... | collective-permute-start | bytes 49160 | tf_op jit(solution)/shard_map/ppermute | solution.py:415
  6.1 0.0 collective-permute-start.1
  6.1 0.6 %collective-permute-start = (bf16[1,64,128]{2,1,0:T(8,128)(2,1)S(1)}, bf16[1,64,128]{2,1,0:T(8,128)(2,1)S(1)}, u32[]{:S(2)}, u32[]{:S(2)}) collective-permute-start(bf16[1,64,128]{2,1,0:T(8,128)(2,1)S(1)} %norm.1.refs_0_), channel_id=1, source_target_pairs={{0,8},{4,12},{8,0},{12,4},{1,9},{5,13},{9,1},{13,5},{2,10},{6,14},... | collective-permute-start | bytes 49160 | tf_op jit(solution)/shard_map/ppermute | solution.py:415
  6.7 3.2 %load_weights.2 = (bf16[2048,1792]{1,0:T(8,128)(2,1)S(1)}, f32[8,128]{1,0:T(8,128)S(1)}) custom-call(bf16[8192,1792]{1,0:T(8,128)(2,1)} %refs_2_.1, bf16[8192,1792]{1,0:T(8,128)(2,1)} %refs_3_.1), custom_call_target="tpu_custom_call" | custom-call | bytes 7340032 | tf_op jit(solution)/shard_map/load_weights/pallas_call | solution.py:186
  9.9 0.0 collective-permute-done.2.refs_3_
  10.0 0.0 collective-permute-done.1.refs_2_
  10.0 0.7 %collective-permute-done.refs_1_ = bf16[1,64,128]{2,1,0:T(8,128)(2,1)S(1)} collective-permute-done((bf16[1,64,128]{2,1,0:T(8,128)(2,1)S(1)}, bf16[1,64,128]{2,1,0:T(8,128)(2,1)S(1)}, u32[]{:S(2)}, u32[]{:S(2)}) %collective-permute-start) | collective-permute-done | bytes 16416 | tf_op jit(solution)/shard_map/ppermute | solution.py:415
  10.7 1.5 %collective-permute-start.5 = (bf16[4,64,128]{2,1,0:T(8,128)(2,1)S(1)}, bf16[4,64,128]{2,1,0:T(8,128)(2,1)S(1)}, u32[]{:S(2)}, u32[]{:S(2)}) collective-permute-start(bf16[4,64,128]{2,1,0:T(8,128)(2,1)S(1)} %stack.1.refs_0_), channel_id=1, source_target_pairs={{0,16},{2,18},{16,0},{18,2},{1,17},{3,19},{17,1},{19,3},{4,20},{6,... | collective-permute-start | bytes 196616 | tf_op jit(solution)/shard_map/ppermute | solution.py:415
  12.2 1.5 %collective-permute-start.4 = (bf16[4,64,128]{2,1,0:T(8,128)(2,1)S(1)}, bf16[4,64,128]{2,1,0:T(8,128)(2,1)S(1)}, u32[]{:S(2)}, u32[]{:S(2)}) collective-permute-start(bf16[4,64,128]{2,1,0:T(8,128)(2,1)S(1)} %stack.1.refs_0_), channel_id=1, source_target_pairs={{0,2},{2,0},{16,18},{18,16},{1,3},{3,1},{17,19},{19,17},{4,6},{6,4... | collective-permute-start | bytes 196616 | tf_op jit(solution)/shard_map/ppermute | solution.py:415
  13.7 0.5 collective-permute-start.3
  14.2 3.2 %load_weights.3 = (bf16[2048,1792]{1,0:T(8,128)(2,1)S(1)}, f32[8,128]{1,0:T(8,128)S(1)}) custom-call(s32[8]{0:T(128)} %lengths.1, s32[8]{0:T(128)} %hit_lengths.1, s32[8]{0:T(128)} %start_positions.1, bf16[8192,1792]{1,0:T(8,128)(2,1)} %refs_2_.1, bf16[8192,1792]{1,0:T(8,128)(2,1)} %refs_3_.1), custom_call_target="tpu_custom_call" | custom-call | bytes 7340032 | tf_op jit(solution)/shard_map/load_weights/pallas_call | solution.py:186
  17.4 0.0 collective-permute-done.5.refs_3_
  17.4 0.0 collective-permute-done.4.refs_2_
  17.4 1.5 %collective-permute-done.3.refs_1_ = bf16[4,64,128]{2,1,0:T(8,128)(2,1)S(1)} collective-permute-done((bf16[4,64,128]{2,1,0:T(8,128)(2,1)S(1)}, bf16[4,64,128]{2,1,0:T(8,128)(2,1)S(1)}, u32[]{:S(2)}, u32[]{:S(2)}) %collective-permute-start.3) | collective-permute-done | bytes 65568 | tf_op jit(solution)/shard_map/ppermute | solution.py:415
  18.9 0.1 pack.1.near_ref
  19.0 0.1 collective-permute-start.6
  19.1 1.5 %collective-permute-done.6.far_ref = bf16[16,8192]{1,0:T(8,128)(2,1)S(1)} collective-permute-done((bf16[16,8192]{1,0:T(8,128)(2,1)S(1)}, bf16[16,8192]{1,0:T(8,128)(2,1)S(1)}, u32[]{:S(2)}, u32[]{:S(2)}) %collective-permute-start.6) | collective-permute-done | bytes 262176 | tf_op jit(solution)/shard_map/ppermute | solution.py:415
  20.6 12.3 %block.1 = (f32[16,64,128]{2,1,0:T(8,128)S(1)}, bf16[16,64,128]{2,1,0:T(8,128)(2,1)S(1)}) custom-call(bf16[16,8192]{1,0:T(8,128)(2,1)S(1)} %pack.1.near_ref, bf16[16,8192]{1,0:T(8,128)(2,1)S(1)} %collective-permute-done.6.far_ref, bf16[2048,1792]{1,0:T(8,128)(2,1)S(1)} %get-tuple-element.13.refs_0_, bf16[2048,1792]{1,0:T(8,128)(2,1)S(1)} %get-tuple-element.14.refs_1_, ...), custom_call_target="tpu_custom_call" | custom-call | flops 1409286144 | bytes 29360128 | tf_op jit(solution)/shard_map/block/pallas_call | solution.py:354
  32.9 0.2 collective-permute-start.7
  33.1 1.4 %collective-permute-done.7 = bf16[16,64,128]{2,1,0:T(8,128)(2,1)S(1)} collective-permute-done((bf16[16,64,128]{2,1,0:T(8,128)(2,1)S(1)}, bf16[16,64,128]{2,1,0:T(8,128)(2,1)S(1)}, u32[]{:S(2)}, u32[]{:S(2)}) %collective-permute-start.7) | collective-permute-done | bytes 262176 | tf_op jit(solution)/shard_map/ppermute | solution.py:415
  34.5 0.1 add_convert_fusion
  34.6 1.1 %collective-permute-start.8 = (bf16[4,64,128]{2,1,0:T(8,128)(2,1)S(1)}, bf16[4,64,128]{2,1,0:T(8,128)(2,1)S(1)}, u32[]{:S(2)}, u32[]{:S(2)}) collective-permute-start(bf16[4,64,128]{2,1,0:T(8,128)(2,1)S(1)} %get-tuple-element.17), channel_id=1, source_target_pairs={{0,18},{2,16},{16,2},{18,0},{1,19},{3,17},{17,3},{19,1},{4,22},{6,... | collective-permute-start | bytes 196616 | tf_op jit(solution)/shard_map/ppermute | solution.py:415
  35.7 1.0 %collective-permute-start.10 = (bf16[4,64,128]{2,1,0:T(8,128)(2,1)S(1)}, bf16[4,64,128]{2,1,0:T(8,128)(2,1)S(1)}, u32[]{:S(2)}, u32[]{:S(2)}) collective-permute-start(bf16[4,64,128]{2,1,0:T(8,128)(2,1)S(1)} %get-tuple-element.18), channel_id=1, source_target_pairs={{0,16},{2,18},{16,0},{18,2},{1,17},{3,19},{17,1},{19,3},{4,20},{6,... | collective-permute-start | bytes 196616 | tf_op jit(solution)/shard_map/ppermute | solution.py:415
  36.7 1.5 %collective-permute-start.9 = (bf16[4,64,128]{2,1,0:T(8,128)(2,1)S(1)}, bf16[4,64,128]{2,1,0:T(8,128)(2,1)S(1)}, u32[]{:S(2)}, u32[]{:S(2)}) collective-permute-start(bf16[4,64,128]{2,1,0:T(8,128)(2,1)S(1)} %get-tuple-element.19), channel_id=1, source_target_pairs={{0,2},{2,0},{16,18},{18,16},{1,3},{3,1},{17,19},{19,17},{4,6},{6,4... | collective-permute-start | bytes 196616 | tf_op jit(solution)/shard_map/ppermute | solution.py:415
  38.2 2.2 %collective-permute-done.8 = bf16[4,64,128]{2,1,0:T(8,128)(2,1)S(1)} collective-permute-done((bf16[4,64,128]{2,1,0:T(8,128)(2,1)S(1)}, bf16[4,64,128]{2,1,0:T(8,128)(2,1)S(1)}, u32[]{:S(2)}, u32[]{:S(2)}) %collective-permute-start.8) | collective-permute-done | bytes 65568 | tf_op jit(solution)/shard_map/ppermute | solution.py:415
  40.4 0.6 %collective-permute-done.10 = bf16[4,64,128]{2,1,0:T(8,128)(2,1)S(1)} collective-permute-done((bf16[4,64,128]{2,1,0:T(8,128)(2,1)S(1)}, bf16[4,64,128]{2,1,0:T(8,128)(2,1)S(1)}, u32[]{:S(2)}, u32[]{:S(2)}) %collective-permute-start.10) | collective-permute-done | bytes 65568 | tf_op jit(solution)/shard_map/ppermute | solution.py:415
  41.0 0.0 collective-permute-done.9
  41.0 2.1 %collective-permute-start.11 = (bf16[2,64,128]{2,1,0:T(8,128)(2,1)S(1)}, bf16[2,64,128]{2,1,0:T(8,128)(2,1)S(1)}, u32[]{:S(2)}, u32[]{:S(2)}) collective-permute-start(bf16[2,64,128]{2,1,0:T(8,128)(2,1)S(1)} %split.37), channel_id=1, source_target_pairs={{0,4},{4,0},{8,12},{12,8},{1,5},{5,1},{9,13},{13,9},{2,6},{6,2},{1... | collective-permute-start | bytes 98312 | tf_op jit(solution)/shard_map/ppermute | solution.py:415
  43.1 1.9 %collective-permute-done.11 = bf16[2,64,128]{2,1,0:T(8,128)(2,1)S(1)} collective-permute-done((bf16[2,64,128]{2,1,0:T(8,128)(2,1)S(1)}, bf16[2,64,128]{2,1,0:T(8,128)(2,1)S(1)}, u32[]{:S(2)}, u32[]{:S(2)}) %collective-permute-start.11) | collective-permute-done | bytes 32800 | tf_op jit(solution)/shard_map/ppermute | solution.py:415
  45.0 1.7 %collective-permute-start.12 = (bf16[1,64,128]{2,1,0:T(8,128)(2,1)S(1)}, bf16[1,64,128]{2,1,0:T(8,128)(2,1)S(1)}, u32[]{:S(2)}, u32[]{:S(2)}) collective-permute-start(bf16[1,64,128]{2,1,0:T(8,128)(2,1)S(1)} %get-tuple-element.20), channel_id=1, source_target_pairs={{0,8},{4,12},{8,0},{12,4},{1,9},{5,13},{9,1},{13,5},{2,10},{6,14},... | collective-permute-start | bytes 49160 | tf_op jit(solution)/shard_map/ppermute | solution.py:415
  46.7 3.0 %collective-permute-done.12.refs_1_ = bf16[1,64,128]{2,1,0:T(8,128)(2,1)S(1)} collective-permute-done((bf16[1,64,128]{2,1,0:T(8,128)(2,1)S(1)}, bf16[1,64,128]{2,1,0:T(8,128)(2,1)S(1)}, u32[]{:S(2)}, u32[]{:S(2)}) %collective-permute-start.12) | collective-permute-done | bytes 16416 | tf_op jit(solution)/shard_map/ppermute | solution.py:415
  49.7 0.6 %finish.1 = bf16[1,8192]{1,0:T(2,128)(2,1)} custom-call(bf16[1,64,128]{2,1,0:T(8,128)(2,1)S(1)} %get-tuple-element.21.refs_0_, bf16[1,64,128]{2,1,0:T(8,128)(2,1)S(1)} %collective-permute-done.12.refs_1_, f32[8,128]{1,0:T(8,128)S(1)} %get-tuple-element.12.refs_4_.refs_2_), custom_call_target="tpu_custom_call" | custom-call | tf_op jit(solution)/shard_map/finish/pallas_call | solution.py:403
  (6 shorter events, 0.1 us)
Async XLA Ops:
  1.0 9.0 %collective-permute-start.2 = (bf16[1,64,128]{2,1,0:T(8,128)(2,1)S(1)}, bf16[1,64,128]{2,1,0:T(8,128)(2,1)S(1)}, u32[]{:S(2)}, u32[]{:S(2)}) collective-permute-start(bf16[1,64,128]{2,1,0:T(8,128)(2,1)S(1)} %norm.1.refs_0_), channel_id=1, source_target_pairs={{0,12},{4,8},{8,4},{12,0},{1,13},{5,9},{9,5},{13,1},{2,14},{6,10},... | collective-permute-start | bytes 49160 | tf_op jit(solution)/shard_map/ppermute | solution.py:415
  6.1 3.9 %collective-permute-start.1 = (bf16[1,64,128]{2,1,0:T(8,128)(2,1)S(1)}, bf16[1,64,128]{2,1,0:T(8,128)(2,1)S(1)}, u32[]{:S(2)}, u32[]{:S(2)}) collective-permute-start(bf16[1,64,128]{2,1,0:T(8,128)(2,1)S(1)} %norm.1.refs_0_), channel_id=1, source_target_pairs={{0,4},{4,0},{8,12},{12,8},{1,5},{5,1},{9,13},{13,9},{2,6},{6,2},{1... | collective-permute-start | bytes 49160 | tf_op jit(solution)/shard_map/ppermute | solution.py:415
  6.1 4.6 %collective-permute-start = (bf16[1,64,128]{2,1,0:T(8,128)(2,1)S(1)}, bf16[1,64,128]{2,1,0:T(8,128)(2,1)S(1)}, u32[]{:S(2)}, u32[]{:S(2)}) collective-permute-start(bf16[1,64,128]{2,1,0:T(8,128)(2,1)S(1)} %norm.1.refs_0_), channel_id=1, source_target_pairs={{0,8},{4,12},{8,0},{12,4},{1,9},{5,13},{9,1},{13,5},{2,10},{6,14},... | collective-permute-start | bytes 49160 | tf_op jit(solution)/shard_map/ppermute | solution.py:415
  10.7 6.7 %collective-permute-start.5 = (bf16[4,64,128]{2,1,0:T(8,128)(2,1)S(1)}, bf16[4,64,128]{2,1,0:T(8,128)(2,1)S(1)}, u32[]{:S(2)}, u32[]{:S(2)}) collective-permute-start(bf16[4,64,128]{2,1,0:T(8,128)(2,1)S(1)} %stack.1.refs_0_), channel_id=1, source_target_pairs={{0,16},{2,18},{16,0},{18,2},{1,17},{3,19},{17,1},{19,3},{4,20},{6,... | collective-permute-start | bytes 196616 | tf_op jit(solution)/shard_map/ppermute | solution.py:415
  12.2 5.2 %collective-permute-start.4 = (bf16[4,64,128]{2,1,0:T(8,128)(2,1)S(1)}, bf16[4,64,128]{2,1,0:T(8,128)(2,1)S(1)}, u32[]{:S(2)}, u32[]{:S(2)}) collective-permute-start(bf16[4,64,128]{2,1,0:T(8,128)(2,1)S(1)} %stack.1.refs_0_), channel_id=1, source_target_pairs={{0,2},{2,0},{16,18},{18,16},{1,3},{3,1},{17,19},{19,17},{4,6},{6,4... | collective-permute-start | bytes 196616 | tf_op jit(solution)/shard_map/ppermute | solution.py:415
  13.7 5.2 %collective-permute-start.3 = (bf16[4,64,128]{2,1,0:T(8,128)(2,1)S(1)}, bf16[4,64,128]{2,1,0:T(8,128)(2,1)S(1)}, u32[]{:S(2)}, u32[]{:S(2)}) collective-permute-start(bf16[4,64,128]{2,1,0:T(8,128)(2,1)S(1)} %stack.1.refs_0_), channel_id=1, source_target_pairs={{0,18},{2,16},{16,2},{18,0},{1,19},{3,17},{17,3},{19,1},{4,22},{6,... | collective-permute-start | bytes 196616 | tf_op jit(solution)/shard_map/ppermute | solution.py:415
  19.0 1.6 %collective-permute-start.6 = (bf16[16,8192]{1,0:T(8,128)(2,1)S(1)}, bf16[16,8192]{1,0:T(8,128)(2,1)S(1)}, u32[]{:S(2)}, u32[]{:S(2)}) collective-permute-start(bf16[16,8192]{1,0:T(8,128)(2,1)S(1)} %pack.1.near_ref), channel_id=1, source_target_pairs={{0,1},{1,0},{2,3},{3,2},{4,5},{5,4},{6,7},{7,6},{8,9},{9,8},{10,11... | collective-permute-start | bytes 786440 | tf_op jit(solution)/shard_map/ppermute | solution.py:415
  32.9 1.6 %collective-permute-start.7 = (bf16[16,64,128]{2,1,0:T(8,128)(2,1)S(1)}, bf16[16,64,128]{2,1,0:T(8,128)(2,1)S(1)}, u32[]{:S(2)}, u32[]{:S(2)}) collective-permute-start(bf16[16,64,128]{2,1,0:T(8,128)(2,1)S(1)} %get-tuple-element.16), channel_id=1, source_target_pairs={{0,1},{1,0},{2,3},{3,2},{4,5},{5,4},{6,7},{7,6},{8,9},{9,8},{10,11... | collective-permute-start | bytes 786440 | tf_op jit(solution)/shard_map/ppermute | solution.py:415
  34.6 5.8 %collective-permute-start.8 = (bf16[4,64,128]{2,1,0:T(8,128)(2,1)S(1)}, bf16[4,64,128]{2,1,0:T(8,128)(2,1)S(1)}, u32[]{:S(2)}, u32[]{:S(2)}) collective-permute-start(bf16[4,64,128]{2,1,0:T(8,128)(2,1)S(1)} %get-tuple-element.17), channel_id=1, source_target_pairs={{0,18},{2,16},{16,2},{18,0},{1,19},{3,17},{17,3},{19,1},{4,22},{6,... | collective-permute-start | bytes 196616 | tf_op jit(solution)/shard_map/ppermute | solution.py:415
  35.7 5.3 %collective-permute-start.10 = (bf16[4,64,128]{2,1,0:T(8,128)(2,1)S(1)}, bf16[4,64,128]{2,1,0:T(8,128)(2,1)S(1)}, u32[]{:S(2)}, u32[]{:S(2)}) collective-permute-start(bf16[4,64,128]{2,1,0:T(8,128)(2,1)S(1)} %get-tuple-element.18), channel_id=1, source_target_pairs={{0,16},{2,18},{16,0},{18,2},{1,17},{3,19},{17,1},{19,3},{4,20},{6,... | collective-permute-start | bytes 196616 | tf_op jit(solution)/shard_map/ppermute | solution.py:415
  36.7 4.3 %collective-permute-start.9 = (bf16[4,64,128]{2,1,0:T(8,128)(2,1)S(1)}, bf16[4,64,128]{2,1,0:T(8,128)(2,1)S(1)}, u32[]{:S(2)}, u32[]{:S(2)}) collective-permute-start(bf16[4,64,128]{2,1,0:T(8,128)(2,1)S(1)} %get-tuple-element.19), channel_id=1, source_target_pairs={{0,2},{2,0},{16,18},{18,16},{1,3},{3,1},{17,19},{19,17},{4,6},{6,4... | collective-permute-start | bytes 196616 | tf_op jit(solution)/shard_map/ppermute | solution.py:415
  41.0 4.0 %collective-permute-start.11 = (bf16[2,64,128]{2,1,0:T(8,128)(2,1)S(1)}, bf16[2,64,128]{2,1,0:T(8,128)(2,1)S(1)}, u32[]{:S(2)}, u32[]{:S(2)}) collective-permute-start(bf16[2,64,128]{2,1,0:T(8,128)(2,1)S(1)} %split.37), channel_id=1, source_target_pairs={{0,4},{4,0},{8,12},{12,8},{1,5},{5,1},{9,13},{13,9},{2,6},{6,2},{1... | collective-permute-start | bytes 98312 | tf_op jit(solution)/shard_map/ppermute | solution.py:415
  45.0 4.7 %collective-permute-start.12 = (bf16[1,64,128]{2,1,0:T(8,128)(2,1)S(1)}, bf16[1,64,128]{2,1,0:T(8,128)(2,1)S(1)}, u32[]{:S(2)}, u32[]{:S(2)}) collective-permute-start(bf16[1,64,128]{2,1,0:T(8,128)(2,1)S(1)} %get-tuple-element.20), channel_id=1, source_target_pairs={{0,8},{4,12},{8,0},{12,4},{1,9},{5,13},{9,1},{13,5},{2,10},{6,14},... | collective-permute-start | bytes 49160 | tf_op jit(solution)/shard_map/ppermute | solution.py:415

commit v6 on v5

--- a/solution.py
+++ b/solution.py
@@ -67,76 +67,64 @@
     return live
 
 
-def norm_kernel(tokens_hbm, gain_hbm, out_ref, tokens_ref, gain_ref, sems):
-    copies = [
-        pltpu.make_async_copy(tokens_hbm, tokens_ref, sems.at[0]),
-        pltpu.make_async_copy(gain_hbm, gain_ref, sems.at[1]),
+def stack_kernel(*refs):
+    pieces, out_ref, wide_ref = refs[:-3], refs[-2], refs[-1]
+    lines = out_ref.shape[1]
+    for at, piece in enumerate(pieces):
+        values = piece[...].astype(jnp.float32)
+        for line in range(lines):
+            wide_ref[at, line : line + 1] = values[:, line * LANES : (line + 1) * LANES]
+    out_ref[...] = wide_ref[...].astype(out_ref.dtype)
+
+
+def stack(pieces, gain):
+    shape = (len(pieces), pieces[0].shape[1] // LANES, LANES)
+    return pl.pallas_call(
+        stack_kernel,
+        out_shape=jax.ShapeDtypeStruct(shape, pieces[0].dtype),
+        in_specs=[VMEM] * len(pieces) + [pl.BlockSpec(memory_space=pl.ANY)],
+        out_specs=VMEM,
+        scratch_shapes=[pltpu.VMEM(shape, jnp.float32)],
+        compiler_params=pltpu.CompilerParams(vmem_limit_bytes=2 << 20),
+        name="stack",
+    )(*pieces, gain)
+
+
+def load_gain_kernel(half, gate_hbm, up_hbm, gain_hbm, both_vmem, gain_vmem, sems):
+    own = pl.multiple_of(lax.axis_index("groups") * half, LANES)
+    copies = [pltpu.make_async_copy(gain_hbm, gain_vmem, sems.at[2])] + [
+        pltpu.make_async_copy(
+            weight.at[pl.ds(0, both_vmem.shape[0]), pl.ds(own, half)],
+            both_vmem.at[:, pl.ds(at * half, half)],
+            sems.at[at],
+        )
+        for at, weight in enumerate((gate_hbm, up_hbm))
     ]
     for copy in copies:
         copy.start()
     for copy in copies:
         copy.wait()
-    values = tokens_ref[...].astype(jnp.float32)
-    mean_sq = jnp.mean(values * values, axis=-1, keepdims=True)
-    scaled = values * lax.rsqrt(mean_sq + 1e-05)
-    lines = out_ref.shape[1]
-    rows = [scaled[:, line * LANES : (line + 1) * LANES] for line in range(lines)]
-    stacked = jnp.concatenate(rows, axis=0)
-    out_ref[0] = (stacked * gain_ref[...].astype(jnp.float32)).astype(jnp.bfloat16)
-
-
-def norm(tokens, gain):
-    lines = tokens.shape[1] // LANES
-    gain = gain.reshape(lines, LANES)
-    return pl.pallas_call(
-        norm_kernel,
-        out_shape=jax.ShapeDtypeStruct((1, lines, LANES), jnp.bfloat16),
-        in_specs=[HBM, HBM],
-        out_specs=VMEM,
-        scratch_shapes=[
-            pltpu.VMEM(tokens.shape, tokens.dtype),
+
+
+def load_first(w_gate, w_up, gain, half, count):
+    return pl.pallas_call(
+        functools.partial(load_gain_kernel, half),
+        out_shape=(
+            pltpu.VMEM((count, 2 * half), w_gate.dtype),
             pltpu.VMEM(gain.shape, gain.dtype),
-            pltpu.SemaphoreType.DMA((2,)),
-        ],
+        ),
+        in_specs=[HBM] * 3,
+        out_specs=(VMEM, VMEM),
+        scratch_shapes=[pltpu.SemaphoreType.DMA((3,))],
         compiler_params=pltpu.CompilerParams(vmem_limit_bytes=1 << 20),
-        name="norm",
-    )(*(pltpu.with_memory_space_constraint(array, pltpu.HBM) for array in (tokens, gain)))
-
-
-def stack_kernel(*refs):
-    for at, piece in enumerate(refs[:-2]):
-        refs[-1][at : at + 1] = piece[...]
-
-
-def stack(pieces, mark):
-    return pl.pallas_call(
-        stack_kernel,
-        out_shape=jax.ShapeDtypeStruct((len(pieces),) + pieces[0].shape[1:], pieces[0].dtype),
-        in_specs=[VMEM] * len(pieces) + [pl.BlockSpec(memory_space=pl.ANY)],
-        out_specs=VMEM,
-        compiler_params=pltpu.CompilerParams(vmem_limit_bytes=1 << 20),
-        name="stack",
-    )(*pieces, mark)
-
-
-def load_kernel(half, row, gate_hbm, up_hbm, both_vmem, mark_vmem, sems):
-    own = pl.multiple_of(lax.axis_index("groups") * half, LANES)
-    copies = [
-        pltpu.make_async_copy(
-            weight.at[pl.ds(row, both_vmem.shape[0]), pl.ds(own, half)],
-            both_vmem.at[:, pl.ds(at * half, half)],
-            sems.at[at],
-        )
-        for at, weight in enumerate((gate_hbm, up_hbm))
-    ]
-    for copy in copies:
-        copy.start()
-    mark_vmem[...] = jnp.ones(mark_vmem.shape, mark_vmem.dtype)
-    for copy in copies:
-        copy.wait()
-
-
-def load_live_kernel(
+        cost_estimate=pl.CostEstimate(
+            flops=0, bytes_accessed=2 * count * half * 2, transcendentals=0
+        ),
+        name="load_first",
+    )(w_gate, w_up, pltpu.with_memory_space_constraint(gain, pltpu.HBM))
+
+
+def load_second_kernel(
     half,
     row,
     place,
@@ -177,38 +165,38 @@
         copy.wait()
 
 
-def load_weights(w_gate, w_up, half, row, count, requests=(), place=None):
-    if requests:
-        body = functools.partial(load_live_kernel, half, row, place)
-        small = [pltpu.SMEM(array.shape, array.dtype) for array in requests]
-    else:
-        body, small = functools.partial(load_kernel, half, row), []
-    return pl.pallas_call(
-        body,
+def load_second(w_gate, w_up, half, row, count, requests, place):
+    return pl.pallas_call(
+        functools.partial(load_second_kernel, half, row, place),
         out_shape=(
             pltpu.VMEM((count, 2 * half), w_gate.dtype),
             jax.ShapeDtypeStruct((8, LANES), jnp.float32),
         ),
         in_specs=[HBM] * (2 + len(requests)),
         out_specs=(VMEM, VMEM),
-        scratch_shapes=small + [pltpu.SemaphoreType.DMA((5,))],
+        scratch_shapes=[pltpu.SMEM(array.shape, array.dtype) for array in requests]
+        + [pltpu.SemaphoreType.DMA((5,))],
         compiler_params=pltpu.CompilerParams(vmem_limit_bytes=1 << 20),
         cost_estimate=pl.CostEstimate(
             flops=0, bytes_accessed=2 * count * half * 2, transcendentals=0
         ),
-        name="load_weights",
+        name="load_second",
     )(*requests, w_gate, w_up)
 
 
 def pack_kernel(*refs):
-    pieces, out_ref, wide_ref = refs[:-3], refs[-2], refs[-1]
+    pieces, gain_ref, out_ref, wide_ref = refs[:-4], refs[-4], refs[-2], refs[-1]
     rows = out_ref.shape[0]
     lines = out_ref.shape[1] // LANES
     stride = wide_ref.shape[0] // rows
+    gain = gain_ref[...].astype(jnp.float32)
     row = 0
     for piece in pieces:
+        values = piece[...].astype(jnp.float32)
+        mean_sq = jnp.sum(values * values, axis=(1, 2), keepdims=True) * (1.0 / (lines * LANES))
+        scaled = values * lax.rsqrt(mean_sq + 1e-05) * gain[None]
         for at in range(piece.shape[0]):
-            wide_ref[row * stride : row * stride + lines] = piece[at].astype(jnp.float32)
+            wide_ref[row * stride : row * stride + lines] = scaled[at]
             row += 1
     for line in range(lines):
         out_ref[:, line * LANES : (line + 1) * LANES] = wide_ref[
@@ -216,18 +204,18 @@
         ].astype(jnp.bfloat16)
 
 
-def pack(pieces, mark):
+def pack(pieces, gain, mark):
     rows = sum(piece.shape[0] for piece in pieces)
     lines = pieces[0].shape[1]
     return pl.pallas_call(
         pack_kernel,
         out_shape=jax.ShapeDtypeStruct((rows, lines * LANES), jnp.bfloat16),
-        in_specs=[VMEM] * len(pieces) + [pl.BlockSpec(memory_space=pl.ANY)],
+        in_specs=[VMEM] * (len(pieces) + 1) + [pl.BlockSpec(memory_space=pl.ANY)],
         out_specs=VMEM,
         scratch_shapes=[pltpu.VMEM((rows * (lines + 1), LANES), jnp.float32)],
         compiler_params=pltpu.CompilerParams(vmem_limit_bytes=4 << 20),
         name="pack",
-    )(*pieces, mark)
+    )(*pieces, pltpu.with_memory_space_constraint(gain, pltpu.VMEM), mark)
 
 
 def block_kernel(
@@ -255,8 +243,7 @@
     lanes = LANES
     lines = depth // lanes
     stride = wide_ref.shape[0] // rows
-    held = [(ref, at) for ref in first_refs for at in range(0, ref.shape[0], chunk)]
-    loaded = len(held) * chunk
+    loaded = sum(ref.shape[0] for ref in first_refs)
     own = pl.multiple_of(lax.axis_index("groups") * half, LANES)
     loads = []
     for step, at in enumerate(range(0, depth - loaded, chunk)):
@@ -282,14 +269,6 @@
             ]
         )
 
-    steps = depth // chunk
-    early = min(3, pairs)
-    due = [[] for _ in range(2 * steps)]
-    for number in range(early, pairs):
-        due[number - early].append(number)
-    for number in range(pairs, len(loads)):
-        due[pairs - 1 + (number - pairs) // 2].append(number)
-
     def start(numbers):
         for number in numbers:
             for copy in loads[number]:
@@ -299,29 +278,44 @@
         for copy in loads[number]:
             copy.wait()
 
-    start(range(early))
+    waiting = list(range(len(loads)))
+
+    def start_next(count):
+        start(waiting[:count])
+        del waiting[:count]
+
+    start_next(1)
     rows_ref[: rows // 2] = near_ref[...]
     rows_ref[rows // 2 :] = far_ref[...]
-    for at in range(0, depth, chunk):
-        if at >= loaded:
-            wait((at - loaded) // chunk)
-        for column in range(0, 2 * half, tile):
+
+    def multiply(at, count, ref, row, paced):
+        for number, column in enumerate(range(0, 2 * half, tile)):
             columns = pl.ds(column, tile)
-            ref, row = held[at // chunk] if at < loaded else (rest_ref, at - loaded)
             value = jnp.dot(
-                rows_ref[:, at : at + chunk],
-                ref[row : row + chunk, columns],
+                rows_ref[:, at : at + count],
+                ref[row : row + count, columns],
                 preferred_element_type=jnp.float32,
             )
             if at == 0:
                 product_ref[:, columns] = value
             else:
                 product_ref[:, columns] += value
-        start(due[at // chunk])
+            if number in paced:
+                start_next(1)
+
+    at = 0
+    for ref in first_refs:
+        multiply(at, ref.shape[0], ref, 0, (1, 6) if at == 0 else (3, 5, 6))
+        at += ref.shape[0]
+    for step in range(pairs):
+        wait(step)
+        multiply(at, chunk, rest_ref, step * chunk, (3, 6))
+        at += chunk
     gate_out = product_ref[:, :half]
     up_out = product_ref[:, half:]
     hidden_ref[...] = (gate_out / (1.0 + jnp.exp(-gate_out)) * up_out).astype(jnp.bfloat16)
-    for step in range(steps):
+    start_next(len(waiting))
+    for step in range(depth // chunk):
         wait(pairs + step)
         for at in range(step * chunk, (step + 1) * chunk, tile):
             result = jnp.dot(
@@ -331,7 +325,6 @@
                 wide_ref[pl.ds(at // lanes + line, rows, stride=stride), :] = result[
                     :, line * lanes : (line + 1) * lanes
                 ]
-        start(due[steps + step])
         done = step * chunk // lanes
         count = chunk // lanes
         for row in range(rows):
@@ -415,15 +408,6 @@
     return lax.ppermute(value, axes, [(place, place ^ offset) for place in places])
 
 
-def halving(count):
-    order = [0]
-    bit = count // 2
-    while bit:
-        order = order + [at + bit for at in order]
-        bit //= 2
-    return order
-
-
 def shared(tokens, norm_gain, w_gate, w_up, w_down, lengths, hit_lengths, start_positions):
     square = ("groups", "x")
     half = w_gate.shape[1] // lax.axis_size("groups")
@@ -443,13 +427,12 @@
     deep = lax.axis_size("z")
     far_first = [3, 1, 2]
     rest = [0] + far_first
-    own = norm(tokens, norm_gain)
-    column = [own] + [swap(own, "z", at) for at in halving(deep)[1:]]
-    first, mark = load_weights(w_gate, w_up, half, 0, 2 * CHUNK)
-    column = stack(column, mark)
+    column = [tokens] + [swap(tokens, "z", at) for at in range(1, deep)]
+    first, gain = load_first(w_gate, w_up, norm_gain.reshape(-1, LANES), half, 2 * CHUNK)
+    column = stack(column, gain)
     plane = [column] + [swap(column, square, at) for at in far_first]
-    second, live = load_weights(w_gate, w_up, half, 2 * CHUNK, 2 * CHUNK, requests, place)
-    near = pack(plane, live)
+    second, live = load_second(w_gate, w_up, half, 2 * CHUNK, 2 * CHUNK, requests, place)
+    near = pack(plane, gain, live)
     far = swap(near, "core", 1)
     kept, sent = block(near, far, (first, second), w_gate, w_up, w_down, half)
     plane = (kept + swap(sent, "core", 1).astype(jnp.float32)).astype(jnp.bfloat16)
@@ -459,15 +442,10 @@
     for piece in arrived:
         column = column + piece.astype(jnp.float32)
     column = column.astype(jnp.bfloat16)
-    distance = 1
-    while distance < deep // 2:
-        kept, sent = jnp.split(column, 2, axis=0)
-        column = (kept.astype(jnp.float32) + swap(sent, "z", distance).astype(jnp.float32)).astype(
-            jnp.bfloat16
-        )
-        distance *= 2
-    kept, sent = jnp.split(column, 2, axis=0)
-    return finish([kept, swap(sent, "z", distance)], live)
+    pieces = jnp.split(column, deep, axis=0)
+    return finish(
+        pieces[:1] + [swap(piece, "z", at + 1) for at, piece in enumerate(pieces[1:])], live
+    )
 
 
 def solution(mesh):

time: 50.6 us -> 49 us (0.968)
  waiting for transfers between devices: 12.8 us -> 11.6 us
  Pallas kernels: 20.4 us -> 19.6 us
  starting transfers between devices: 16.8 us -> 17.4 us
    ppermute x13 -> x14, waiting for transfers between devices: 12.8 us -> 11.6 us  [swap(): lax.ppermute(value, axes, [(place, place ^ offset) for place in places])]
    pallas_call x4 -> x3, Pallas kernels: 7.38 us -> 6.5 us  [the longest x1 3.22 us: load_first(): pl.pallas_call(functools.partial(load_gain_kernel, half), out_shape=(pltp...]
    ppermute x13 -> x14, starting transfers between devices: 16.8 us -> 17.4 us  [swap(): lax.ppermute(value, axes, [(place, place ^ offset) for place in places])]
  transfers between devices with their start and end apart: 13 -> 14, of which waited for: 8 -> 8; matrix products, arithmetic and copies ran while one was open for 0% -> 0% of each run, Pallas kernels for 13% -> 13%
where the time goes in v6:
time: 49 us; the launch traced here: 48.9 us
  Pallas kernels  19.6 us (40%)
  starting transfers between devices  17.4 us (36%)
  waiting for transfers between devices  11.6 us (24%)
    ppermute x14, starting transfers between devices, swap(): lax.ppermute(value, axes, [(place, place ^ offset) for place in places])  17.4 us
    pallas_call x1, Pallas kernels, block(): pl.pallas_call(body, out_shape=(jax.ShapeDtypeStruct((rows, lines, LANES)...  12.2 us
    ppermute x14, waiting for transfers between devices, swap(): lax.ppermute(value, axes, [(place, place ^ offset) for place in places])  11.6 us
    pallas_call x1, Pallas kernels, load_first(): pl.pallas_call(functools.partial(load_gain_kernel, half), out_shape=(pltp...  3.22 us
    pallas_call x1, Pallas kernels, load_second(): pl.pallas_call(functools.partial(load_second_kernel, half, row, place), o...  3.2 us
  transfers between devices with their start and end apart: 14, of which 8 were waited for; matrix products, arithmetic and copies ran while one was open for 0% of the time, Pallas kernels for 13%

profile of v6, /device:TPU:0, one launch (start us, length us, event | category | flops | bytes accessed | tf_op | source)
XLA Modules:
  0.0 48.9 jit_solution(4557107318485689651)
XLA Ops:
  0.0 4.0 %collective-permute-start.1 = (bf16[1,8192]{1,0:T(2,128)(2,1)}, bf16[1,8192]{1,0:T(2,128)(2,1)S(1)}, u32[]{:S(2)}, u32[]{:S(2)}) collective-permute-start(bf16[1,8192]{1,0:T(2,128)(2,1)} %refs_0_.1), channel_id=1, source_target_pairs={{0,8},{4,12},{8,0},{12,4},{1,9},{5,13},{9,1},{13,5},{2,10},{6,14},... | collective-permute-start | bytes 49160 | tf_op jit(solution)/shard_map/ppermute | solution.py:408
  4.0 1.6 %collective-permute-start = (bf16[1,8192]{1,0:T(2,128)(2,1)}, bf16[1,8192]{1,0:T(2,128)(2,1)S(1)}, u32[]{:S(2)}, u32[]{:S(2)}) collective-permute-start(bf16[1,8192]{1,0:T(2,128)(2,1)} %refs_0_.1), channel_id=1, source_target_pairs={{0,4},{4,0},{8,12},{12,8},{1,5},{5,1},{9,13},{13,9},{2,6},{6,2},{1... | collective-permute-start | bytes 49160 | tf_op jit(solution)/shard_map/ppermute | solution.py:408
  5.6 0.0 collective-permute-start.2
  5.6 0.0 copy-start
  5.6 3.2 %load_first.1 = (bf16[2048,1792]{1,0:T(8,128)(2,1)S(1)}, bf16[64,128]{1,0:T(8,128)(2,1)S(1)}) custom-call(bf16[8192,1792]{1,0:T(8,128)(2,1)} %refs_2_.1, bf16[8192,1792]{1,0:T(8,128)(2,1)} %refs_3_.1, bf16[64,128]{1,0:T(8,128)(2,1)} %bitcast.1), custom_call_target="tpu_custom_call" | custom-call | bytes 7340032 | tf_op jit(solution)/shard_map/load_first/pallas_call | solution.py:110
  8.8 0.0 collective-permute-done.1.refs_2_
  8.9 0.0 collective-permute-done.refs_1_
  8.9 2.7 %collective-permute-done.2.refs_3_ = bf16[1,8192]{1,0:T(2,128)(2,1)S(1)} collective-permute-done((bf16[1,8192]{1,0:T(2,128)(2,1)}, bf16[1,8192]{1,0:T(2,128)(2,1)S(1)}, u32[]{:S(2)}, u32[]{:S(2)}) %collective-permute-start.2) | collective-permute-done | bytes 16416 | tf_op jit(solution)/shard_map/ppermute | solution.py:408
  11.5 0.0 copy-done
  11.5 0.1 stack.1.refs_0_
  11.6 1.6 %collective-permute-start.5 = (bf16[4,64,128]{2,1,0:T(8,128)(2,1)S(1)}, bf16[4,64,128]{2,1,0:T(8,128)(2,1)S(1)}, u32[]{:S(2)}, u32[]{:S(2)}) collective-permute-start(bf16[4,64,128]{2,1,0:T(8,128)(2,1)S(1)} %stack.1.refs_0_), channel_id=1, source_target_pairs={{0,16},{2,18},{16,0},{18,2},{1,17},{3,19},{17,1},{19,3},{4,20},{6,... | collective-permute-start | bytes 196616 | tf_op jit(solution)/shard_map/ppermute | solution.py:408
  13.2 1.5 %collective-permute-start.4 = (bf16[4,64,128]{2,1,0:T(8,128)(2,1)S(1)}, bf16[4,64,128]{2,1,0:T(8,128)(2,1)S(1)}, u32[]{:S(2)}, u32[]{:S(2)}) collective-permute-start(bf16[4,64,128]{2,1,0:T(8,128)(2,1)S(1)} %stack.1.refs_0_), channel_id=1, source_target_pairs={{0,2},{2,0},{16,18},{18,16},{1,3},{3,1},{17,19},{19,17},{4,6},{6,4... | collective-permute-start | bytes 196616 | tf_op jit(solution)/shard_map/ppermute | solution.py:408
  14.7 0.5 collective-permute-start.3
  15.2 3.2 %load_second.1 = (bf16[2048,1792]{1,0:T(8,128)(2,1)S(1)}, f32[8,128]{1,0:T(8,128)S(1)}) custom-call(s32[8]{0:T(128)} %lengths.1, s32[8]{0:T(128)} %hit_lengths.1, s32[8]{0:T(128)} %start_positions.1, bf16[8192,1792]{1,0:T(8,128)(2,1)} %refs_2_.1, bf16[8192,1792]{1,0:T(8,128)(2,1)} %refs_3_.1), custom_call_target="tpu_custom_call" | custom-call | bytes 7340032 | tf_op jit(solution)/shard_map/load_second/pallas_call | solution.py:169
  18.4 0.0 collective-permute-done.5.refs_3_
  18.4 0.0 collective-permute-done.4.refs_2_
  18.4 1.5 %collective-permute-done.3.refs_1_ = bf16[4,64,128]{2,1,0:T(8,128)(2,1)S(1)} collective-permute-done((bf16[4,64,128]{2,1,0:T(8,128)(2,1)S(1)}, bf16[4,64,128]{2,1,0:T(8,128)(2,1)S(1)}, u32[]{:S(2)}, u32[]{:S(2)}) %collective-permute-start.3) | collective-permute-done | bytes 65568 | tf_op jit(solution)/shard_map/ppermute | solution.py:408
  19.9 0.2 pack.1.near_ref
  20.1 0.1 collective-permute-start.6
  20.2 1.5 %collective-permute-done.6.far_ref = bf16[16,8192]{1,0:T(8,128)(2,1)S(1)} collective-permute-done((bf16[16,8192]{1,0:T(8,128)(2,1)S(1)}, bf16[16,8192]{1,0:T(8,128)(2,1)S(1)}, u32[]{:S(2)}, u32[]{:S(2)}) %collective-permute-start.6) | collective-permute-done | bytes 262176 | tf_op jit(solution)/shard_map/ppermute | solution.py:408
  21.7 12.2 %block.1 = (f32[16,64,128]{2,1,0:T(8,128)S(1)}, bf16[16,64,128]{2,1,0:T(8,128)(2,1)S(1)}) custom-call(bf16[16,8192]{1,0:T(8,128)(2,1)S(1)} %pack.1.near_ref, bf16[16,8192]{1,0:T(8,128)(2,1)S(1)} %collective-permute-done.6.far_ref, bf16[2048,1792]{1,0:T(8,128)(2,1)S(1)} %get-tuple-element.13.refs_0_, bf16[2048,1792]{1,0:T(8,128)(2,1)S(1)} %get-tuple-element.14.refs_1_, ...), custom_call_target="tpu_custom_call" | custom-call | flops 1409286144 | bytes 29360128 | tf_op jit(solution)/shard_map/block/pallas_call | solution.py:347
  33.9 0.2 collective-permute-start.7
  34.1 1.4 %collective-permute-done.7 = bf16[16,64,128]{2,1,0:T(8,128)(2,1)S(1)} collective-permute-done((bf16[16,64,128]{2,1,0:T(8,128)(2,1)S(1)}, bf16[16,64,128]{2,1,0:T(8,128)(2,1)S(1)}, u32[]{:S(2)}, u32[]{:S(2)}) %collective-permute-start.7) | collective-permute-done | bytes 262176 | tf_op jit(solution)/shard_map/ppermute | solution.py:408
  35.5 0.1 add_convert_fusion
  35.6 1.1 %collective-permute-start.8 = (bf16[4,64,128]{2,1,0:T(8,128)(2,1)S(1)}, bf16[4,64,128]{2,1,0:T(8,128)(2,1)S(1)}, u32[]{:S(2)}, u32[]{:S(2)}) collective-permute-start(bf16[4,64,128]{2,1,0:T(8,128)(2,1)S(1)} %get-tuple-element.17), channel_id=1, source_target_pairs={{0,18},{2,16},{16,2},{18,0},{1,19},{3,17},{17,3},{19,1},{4,22},{6,... | collective-permute-start | bytes 196616 | tf_op jit(solution)/shard_map/ppermute | solution.py:408
  36.7 1.0 %collective-permute-start.10 = (bf16[4,64,128]{2,1,0:T(8,128)(2,1)S(1)}, bf16[4,64,128]{2,1,0:T(8,128)(2,1)S(1)}, u32[]{:S(2)}, u32[]{:S(2)}) collective-permute-start(bf16[4,64,128]{2,1,0:T(8,128)(2,1)S(1)} %get-tuple-element.18), channel_id=1, source_target_pairs={{0,16},{2,18},{16,0},{18,2},{1,17},{3,19},{17,1},{19,3},{4,20},{6,... | collective-permute-start | bytes 196616 | tf_op jit(solution)/shard_map/ppermute | solution.py:408
  37.7 1.5 %collective-permute-start.9 = (bf16[4,64,128]{2,1,0:T(8,128)(2,1)S(1)}, bf16[4,64,128]{2,1,0:T(8,128)(2,1)S(1)}, u32[]{:S(2)}, u32[]{:S(2)}) collective-permute-start(bf16[4,64,128]{2,1,0:T(8,128)(2,1)S(1)} %get-tuple-element.19), channel_id=1, source_target_pairs={{0,2},{2,0},{16,18},{18,16},{1,3},{3,1},{17,19},{19,17},{4,6},{6,4... | collective-permute-start | bytes 196616 | tf_op jit(solution)/shard_map/ppermute | solution.py:408
  39.2 2.2 %collective-permute-done.8 = bf16[4,64,128]{2,1,0:T(8,128)(2,1)S(1)} collective-permute-done((bf16[4,64,128]{2,1,0:T(8,128)(2,1)S(1)}, bf16[4,64,128]{2,1,0:T(8,128)(2,1)S(1)}, u32[]{:S(2)}, u32[]{:S(2)}) %collective-permute-start.8) | collective-permute-done | bytes 65568 | tf_op jit(solution)/shard_map/ppermute | solution.py:408
  41.4 0.6 %collective-permute-done.10 = bf16[4,64,128]{2,1,0:T(8,128)(2,1)S(1)} collective-permute-done((bf16[4,64,128]{2,1,0:T(8,128)(2,1)S(1)}, bf16[4,64,128]{2,1,0:T(8,128)(2,1)S(1)}, u32[]{:S(2)}, u32[]{:S(2)}) %collective-permute-start.10) | collective-permute-done | bytes 65568 | tf_op jit(solution)/shard_map/ppermute | solution.py:408
  41.9 0.0 collective-permute-done.9
  42.0 1.2 %collective-permute-start.13 = (bf16[1,64,128]{2,1,0:T(8,128)(2,1)S(1)}, bf16[1,64,128]{2,1,0:T(8,128)(2,1)S(1)}, u32[]{:S(2)}, u32[]{:S(2)}) collective-permute-start(bf16[1,64,128]{2,1,0:T(8,128)(2,1)S(1)} %get-tuple-element.20), channel_id=1, source_target_pairs={{0,12},{4,8},{8,4},{12,0},{1,13},{5,9},{9,5},{13,1},{2,14},{6,10},... | collective-permute-start | bytes 49160 | tf_op jit(solution)/shard_map/ppermute | solution.py:408
  43.2 0.0 collective-permute-start.12
  43.2 3.2 %collective-permute-start.11 = (bf16[1,64,128]{2,1,0:T(8,128)(2,1)S(1)}, bf16[1,64,128]{2,1,0:T(8,128)(2,1)S(1)}, u32[]{:S(2)}, u32[]{:S(2)}) collective-permute-start(bf16[1,64,128]{2,1,0:T(8,128)(2,1)S(1)} %get-tuple-element.22), channel_id=1, source_target_pairs={{0,4},{4,0},{8,12},{12,8},{1,5},{5,1},{9,13},{13,9},{2,6},{6,2},{1... | collective-permute-start | bytes 49160 | tf_op jit(solution)/shard_map/ppermute | solution.py:408
  46.5 1.4 %collective-permute-done.13.refs_3_ = bf16[1,64,128]{2,1,0:T(8,128)(2,1)S(1)} collective-permute-done((bf16[1,64,128]{2,1,0:T(8,128)(2,1)S(1)}, bf16[1,64,128]{2,1,0:T(8,128)(2,1)S(1)}, u32[]{:S(2)}, u32[]{:S(2)}) %collective-permute-start.13) | collective-permute-done | bytes 16416 | tf_op jit(solution)/shard_map/ppermute | solution.py:408
  47.9 0.3 collective-permute-done.12.refs_2_
  48.2 0.0 collective-permute-done.11.refs_1_
  48.2 0.7 %finish.1 = bf16[1,8192]{1,0:T(2,128)(2,1)} custom-call(bf16[1,64,128]{2,1,0:T(8,128)(2,1)S(1)} %get-tuple-element.23.refs_0_, bf16[1,64,128]{2,1,0:T(8,128)(2,1)S(1)} %collective-permute-done.11.refs_1_, bf16[1,64,128]{2,1,0:T(8,128)(2,1)S(1)} %collective-permute-done.12.refs_2_, bf16[1,64,128]{2,1,0:T(8,128)(2,1)S(1)} %collective-permute-done.13.refs_3_, ...), custom_call_target="tpu_custom_call" | custom-call | tf_op jit(solution)/shard_map/finish/pallas_call | solution.py:396
  (3 shorter events, 0.1 us)
Async XLA Ops:
  0.0 8.9 %collective-permute-start.1 = (bf16[1,8192]{1,0:T(2,128)(2,1)}, bf16[1,8192]{1,0:T(2,128)(2,1)S(1)}, u32[]{:S(2)}, u32[]{:S(2)}) collective-permute-start(bf16[1,8192]{1,0:T(2,128)(2,1)} %refs_0_.1), channel_id=1, source_target_pairs={{0,8},{4,12},{8,0},{12,4},{1,9},{5,13},{9,1},{13,5},{2,10},{6,14},... | collective-permute-start | bytes 49160 | tf_op jit(solution)/shard_map/ppermute | solution.py:408
  4.0 4.8 %collective-permute-start = (bf16[1,8192]{1,0:T(2,128)(2,1)}, bf16[1,8192]{1,0:T(2,128)(2,1)S(1)}, u32[]{:S(2)}, u32[]{:S(2)}) collective-permute-start(bf16[1,8192]{1,0:T(2,128)(2,1)} %refs_0_.1), channel_id=1, source_target_pairs={{0,4},{4,0},{8,12},{12,8},{1,5},{5,1},{9,13},{13,9},{2,6},{6,2},{1... | collective-permute-start | bytes 49160 | tf_op jit(solution)/shard_map/ppermute | solution.py:408
  5.6 5.9 %collective-permute-start.2 = (bf16[1,8192]{1,0:T(2,128)(2,1)}, bf16[1,8192]{1,0:T(2,128)(2,1)S(1)}, u32[]{:S(2)}, u32[]{:S(2)}) collective-permute-start(bf16[1,8192]{1,0:T(2,128)(2,1)} %refs_0_.1), channel_id=1, source_target_pairs={{0,12},{4,8},{8,4},{12,0},{1,13},{5,9},{9,5},{13,1},{2,14},{6,10},... | collective-permute-start | bytes 49160 | tf_op jit(solution)/shard_map/ppermute | solution.py:408
  5.6 5.9 %copy-start = (bf16[1,8192]{1,0:T(2,128)(2,1)S(1)}, bf16[1,8192]{1,0:T(2,128)(2,1)}, u32[]{:S(2)}) copy-start(bf16[1,8192]{1,0:T(2,128)(2,1)} %refs_0_.1) | copy-start | bytes 49156
  11.6 6.8 %collective-permute-start.5 = (bf16[4,64,128]{2,1,0:T(8,128)(2,1)S(1)}, bf16[4,64,128]{2,1,0:T(8,128)(2,1)S(1)}, u32[]{:S(2)}, u32[]{:S(2)}) collective-permute-start(bf16[4,64,128]{2,1,0:T(8,128)(2,1)S(1)} %stack.1.refs_0_), channel_id=1, source_target_pairs={{0,16},{2,18},{16,0},{18,2},{1,17},{3,19},{17,1},{19,3},{4,20},{6,... | collective-permute-start | bytes 196616 | tf_op jit(solution)/shard_map/ppermute | solution.py:408
  13.2 5.2 %collective-permute-start.4 = (bf16[4,64,128]{2,1,0:T(8,128)(2,1)S(1)}, bf16[4,64,128]{2,1,0:T(8,128)(2,1)S(1)}, u32[]{:S(2)}, u32[]{:S(2)}) collective-permute-start(bf16[4,64,128]{2,1,0:T(8,128)(2,1)S(1)} %stack.1.refs_0_), channel_id=1, source_target_pairs={{0,2},{2,0},{16,18},{18,16},{1,3},{3,1},{17,19},{19,17},{4,6},{6,4... | collective-permute-start | bytes 196616 | tf_op jit(solution)/shard_map/ppermute | solution.py:408
  14.7 5.2 %collective-permute-start.3 = (bf16[4,64,128]{2,1,0:T(8,128)(2,1)S(1)}, bf16[4,64,128]{2,1,0:T(8,128)(2,1)S(1)}, u32[]{:S(2)}, u32[]{:S(2)}) collective-permute-start(bf16[4,64,128]{2,1,0:T(8,128)(2,1)S(1)} %stack.1.refs_0_), channel_id=1, source_target_pairs={{0,18},{2,16},{16,2},{18,0},{1,19},{3,17},{17,3},{19,1},{4,22},{6,... | collective-permute-start | bytes 196616 | tf_op jit(solution)/shard_map/ppermute | solution.py:408
  20.1 1.6 %collective-permute-start.6 = (bf16[16,8192]{1,0:T(8,128)(2,1)S(1)}, bf16[16,8192]{1,0:T(8,128)(2,1)S(1)}, u32[]{:S(2)}, u32[]{:S(2)}) collective-permute-start(bf16[16,8192]{1,0:T(8,128)(2,1)S(1)} %pack.1.near_ref), channel_id=1, source_target_pairs={{0,1},{1,0},{2,3},{3,2},{4,5},{5,4},{6,7},{7,6},{8,9},{9,8},{10,11... | collective-permute-start | bytes 786440 | tf_op jit(solution)/shard_map/ppermute | solution.py:408
  33.9 1.6 %collective-permute-start.7 = (bf16[16,64,128]{2,1,0:T(8,128)(2,1)S(1)}, bf16[16,64,128]{2,1,0:T(8,128)(2,1)S(1)}, u32[]{:S(2)}, u32[]{:S(2)}) collective-permute-start(bf16[16,64,128]{2,1,0:T(8,128)(2,1)S(1)} %get-tuple-element.16), channel_id=1, source_target_pairs={{0,1},{1,0},{2,3},{3,2},{4,5},{5,4},{6,7},{7,6},{8,9},{9,8},{10,11... | collective-permute-start | bytes 786440 | tf_op jit(solution)/shard_map/ppermute | solution.py:408
  35.6 5.8 %collective-permute-start.8 = (bf16[4,64,128]{2,1,0:T(8,128)(2,1)S(1)}, bf16[4,64,128]{2,1,0:T(8,128)(2,1)S(1)}, u32[]{:S(2)}, u32[]{:S(2)}) collective-permute-start(bf16[4,64,128]{2,1,0:T(8,128)(2,1)S(1)} %get-tuple-element.17), channel_id=1, source_target_pairs={{0,18},{2,16},{16,2},{18,0},{1,19},{3,17},{17,3},{19,1},{4,22},{6,... | collective-permute-start | bytes 196616 | tf_op jit(solution)/shard_map/ppermute | solution.py:408
  36.7 5.3 %collective-permute-start.10 = (bf16[4,64,128]{2,1,0:T(8,128)(2,1)S(1)}, bf16[4,64,128]{2,1,0:T(8,128)(2,1)S(1)}, u32[]{:S(2)}, u32[]{:S(2)}) collective-permute-start(bf16[4,64,128]{2,1,0:T(8,128)(2,1)S(1)} %get-tuple-element.18), channel_id=1, source_target_pairs={{0,16},{2,18},{16,0},{18,2},{1,17},{3,19},{17,1},{19,3},{4,20},{6,... | collective-permute-start | bytes 196616 | tf_op jit(solution)/shard_map/ppermute | solution.py:408
  37.7 4.3 %collective-permute-start.9 = (bf16[4,64,128]{2,1,0:T(8,128)(2,1)S(1)}, bf16[4,64,128]{2,1,0:T(8,128)(2,1)S(1)}, u32[]{:S(2)}, u32[]{:S(2)}) collective-permute-start(bf16[4,64,128]{2,1,0:T(8,128)(2,1)S(1)} %get-tuple-element.19), channel_id=1, source_target_pairs={{0,2},{2,0},{16,18},{18,16},{1,3},{3,1},{17,19},{19,17},{4,6},{6,4... | collective-permute-start | bytes 196616 | tf_op jit(solution)/shard_map/ppermute | solution.py:408
  42.0 5.9 %collective-permute-start.13 = (bf16[1,64,128]{2,1,0:T(8,128)(2,1)S(1)}, bf16[1,64,128]{2,1,0:T(8,128)(2,1)S(1)}, u32[]{:S(2)}, u32[]{:S(2)}) collective-permute-start(bf16[1,64,128]{2,1,0:T(8,128)(2,1)S(1)} %get-tuple-element.20), channel_id=1, source_target_pairs={{0,12},{4,8},{8,4},{12,0},{1,13},{5,9},{9,5},{13,1},{2,14},{6,10},... | collective-permute-start | bytes 49160 | tf_op jit(solution)/shard_map/ppermute | solution.py:408
  43.2 5.0 %collective-permute-start.12 = (bf16[1,64,128]{2,1,0:T(8,128)(2,1)S(1)}, bf16[1,64,128]{2,1,0:T(8,128)(2,1)S(1)}, u32[]{:S(2)}, u32[]{:S(2)}) collective-permute-start(bf16[1,64,128]{2,1,0:T(8,128)(2,1)S(1)} %get-tuple-element.21), channel_id=1, source_target_pairs={{0,8},{4,12},{8,0},{12,4},{1,9},{5,13},{9,1},{13,5},{2,10},{6,14},... | collective-permute-start | bytes 49160 | tf_op jit(solution)/shard_map/ppermute | solution.py:408
  43.2 5.0 %collective-permute-start.11 = (bf16[1,64,128]{2,1,0:T(8,128)(2,1)S(1)}, bf16[1,64,128]{2,1,0:T(8,128)(2,1)S(1)}, u32[]{:S(2)}, u32[]{:S(2)}) collective-permute-start(bf16[1,64,128]{2,1,0:T(8,128)(2,1)S(1)} %get-tuple-element.22), channel_id=1, source_target_pairs={{0,4},{4,0},{8,12},{12,8},{1,5},{5,1},{9,13},{13,9},{2,6},{6,2},{1... | collective-permute-start | bytes 49160 | tf_op jit(solution)/shard_map/ppermute | solution.py:408

commit v7 on v6

--- a/solution.py
+++ b/solution.py
@@ -408,6 +408,23 @@
     return lax.ppermute(value, axes, [(place, place ^ offset) for place in places])
 
 
+def sum_direct(column, deep):
+    pieces = jnp.split(column.astype(jnp.bfloat16), deep, axis=0)
+    return pieces[:1] + [swap(piece, "z", at + 1) for at, piece in enumerate(pieces[1:])]
+
+
+def sum_line(column):
+    inward = lax.ppermute(column[1:].astype(jnp.bfloat16), "z", [(0, 1), (3, 2)]).astype(
+        jnp.float32
+    )
+    own = column[:1] + inward[:1]
+    crossing = jnp.concatenate([column[3:] + inward[1:2], column[2:3] + inward[2:]], axis=0)
+    crossed = lax.ppermute(crossing.astype(jnp.bfloat16), "z", [(1, 2), (2, 1)])
+    outer = column[1:2] + crossed[1:].astype(jnp.float32)
+    outward = lax.ppermute(outer.astype(jnp.bfloat16), "z", [(1, 0), (2, 3)])
+    return [own, crossed[:1], outward]
+
+
 def shared(tokens, norm_gain, w_gate, w_up, w_down, lengths, hit_lengths, start_positions):
     square = ("groups", "x")
     half = w_gate.shape[1] // lax.axis_size("groups")
@@ -431,7 +448,7 @@
     first, gain = load_first(w_gate, w_up, norm_gain.reshape(-1, LANES), half, 2 * CHUNK)
     column = stack(column, gain)
     plane = [column] + [swap(column, square, at) for at in far_first]
-    second, live = load_second(w_gate, w_up, half, 2 * CHUNK, 2 * CHUNK, requests, place)
+    second, live = load_second(w_gate, w_up, half, 2 * CHUNK, 3 * CHUNK, requests, place)
     near = pack(plane, gain, live)
     far = swap(near, "core", 1)
     kept, sent = block(near, far, (first, second), w_gate, w_up, w_down, half)
@@ -441,11 +458,7 @@
     column = pieces[0].astype(jnp.float32)
     for piece in arrived:
         column = column + piece.astype(jnp.float32)
-    column = column.astype(jnp.bfloat16)
-    pieces = jnp.split(column, deep, axis=0)
-    return finish(
-        pieces[:1] + [swap(piece, "z", at + 1) for at, piece in enumerate(pieces[1:])], live
-    )
+    return finish(sum_line(column) if deep == 4 else sum_direct(column, deep), live)
 
 
 def solution(mesh):

time: 49 us -> 57.3 us (1.17)
  waiting for transfers between devices: 11.6 us -> 20.2 us
  starting transfers between devices: 17.4 us -> 16.2 us
  Pallas kernels: 19.6 us -> 20.3 us
    ppermute x0 -> x3, waiting for transfers between devices: none -> 10.9 us  [the longest x1 9.14 us: sum_line(): outward = lax.ppermute(outer.astype(jnp.bfloat16), 'z', [(1, 0), (2, 3)])]
    ppermute x14 -> x11, starting transfers between devices: 17.4 us -> 13 us  [swap(): lax.ppermute(value, axes, [(place, place ^ offset) for place in places])]
    ppermute x0 -> x3, starting transfers between devices: none -> 3.25 us  [the longest x1 1.29 us: sum_line(): lax.ppermute(column[1:].astype(jnp.bfloat16), 'z', [(0, 1), (3, 2)])]
    ppermute x14 -> x11, waiting for transfers between devices: 11.6 us -> 9.34 us  [swap(): lax.ppermute(value, axes, [(place, place ^ offset) for place in places])]
    pallas_call x1, Pallas kernels: 3.2 us -> 4.34 us  [load_second(): pl.pallas_call(functools.partial(load_second_kernel, half, row, place), o...]
  transfers between devices with their start and end apart: 14 -> 14, of which waited for: 8 -> 9; matrix products, arithmetic and copies ran while one was open for 0% -> 0% of each run, Pallas kernels for 13% -> 13%
where the time goes in v7:
time: 57.3 us; the launch traced here: 57.1 us
  Pallas kernels  20.3 us (35%)
  waiting for transfers between devices  20.2 us (35%)
  starting transfers between devices  16.2 us (28%)
    ppermute x11, starting transfers between devices, swap(): lax.ppermute(value, axes, [(place, place ^ offset) for place in places])  13 us
    pallas_call x1, Pallas kernels, block(): pl.pallas_call(body, out_shape=(jax.ShapeDtypeStruct((rows, lines, LANES)...  11.8 us
    ppermute x11, waiting for transfers between devices, swap(): lax.ppermute(value, axes, [(place, place ^ offset) for place in places])  9.34 us
    ppermute x1, waiting for transfers between devices, sum_line(): outward = lax.ppermute(outer.astype(jnp.bfloat16), 'z', [(1, 0), (2, 3)])  9.14 us
    pallas_call x1, Pallas kernels, load_second(): pl.pallas_call(functools.partial(load_second_kernel, half, row, place), o...  4.34 us
    pallas_call x1, Pallas kernels, load_first(): pl.pallas_call(functools.partial(load_gain_kernel, half), out_shape=(pltp...  3.22 us
    ppermute x1, waiting for transfers between devices, sum_line(): lax.ppermute(column[1:].astype(jnp.bfloat16), 'z', [(0, 1), (3, 2)])  1.73 us
    ppermute x1, starting transfers between devices, sum_line(): lax.ppermute(column[1:].astype(jnp.bfloat16), 'z', [(0, 1), (3, 2)])  1.29 us
  transfers between devices with their start and end apart: 14, of which 9 were waited for; matrix products, arithmetic and copies ran while one was open for 0% of the time, Pallas kernels for 13%

profile of v7, /device:TPU:0, one launch (start us, length us, event | category | flops | bytes accessed | tf_op | source)
XLA Modules:
  0.0 57.1 jit_solution(3733404529644718476)
XLA Ops:
  0.0 4.0 %collective-permute-start.1 = (bf16[1,8192]{1,0:T(2,128)(2,1)}, bf16[1,8192]{1,0:T(2,128)(2,1)S(1)}, u32[]{:S(2)}, u32[]{:S(2)}) collective-permute-start(bf16[1,8192]{1,0:T(2,128)(2,1)} %refs_0_.1), channel_id=1, source_target_pairs={{0,8},{4,12},{8,0},{12,4},{1,9},{5,13},{9,1},{13,5},{2,10},{6,14},... | collective-permute-start | bytes 49160 | tf_op jit(solution)/shard_map/ppermute | solution.py:408
  4.0 1.6 %collective-permute-start = (bf16[1,8192]{1,0:T(2,128)(2,1)}, bf16[1,8192]{1,0:T(2,128)(2,1)S(1)}, u32[]{:S(2)}, u32[]{:S(2)}) collective-permute-start(bf16[1,8192]{1,0:T(2,128)(2,1)} %refs_0_.1), channel_id=1, source_target_pairs={{0,4},{4,0},{8,12},{12,8},{1,5},{5,1},{9,13},{13,9},{2,6},{6,2},{1... | collective-permute-start | bytes 49160 | tf_op jit(solution)/shard_map/ppermute | solution.py:408
  5.6 0.0 collective-permute-start.2
  5.6 0.0 copy-start
  5.6 3.2 %load_first.1 = (bf16[2048,1792]{1,0:T(8,128)(2,1)S(1)}, bf16[64,128]{1,0:T(8,128)(2,1)S(1)}) custom-call(bf16[8192,1792]{1,0:T(8,128)(2,1)} %refs_2_.1, bf16[8192,1792]{1,0:T(8,128)(2,1)} %refs_3_.1, bf16[64,128]{1,0:T(8,128)(2,1)} %bitcast.1), custom_call_target="tpu_custom_call" | custom-call | bytes 7340032 | tf_op jit(solution)/shard_map/load_first/pallas_call | solution.py:110
  8.8 0.0 collective-permute-done.1.refs_2_
  8.9 0.0 collective-permute-done.refs_1_
  8.9 2.7 %collective-permute-done.2.refs_3_ = bf16[1,8192]{1,0:T(2,128)(2,1)S(1)} collective-permute-done((bf16[1,8192]{1,0:T(2,128)(2,1)}, bf16[1,8192]{1,0:T(2,128)(2,1)S(1)}, u32[]{:S(2)}, u32[]{:S(2)}) %collective-permute-start.2) | collective-permute-done | bytes 16416 | tf_op jit(solution)/shard_map/ppermute | solution.py:408
  11.5 0.0 copy-done
  11.5 0.1 stack.1.refs_0_
  11.6 1.6 %collective-permute-start.5 = (bf16[4,64,128]{2,1,0:T(8,128)(2,1)S(1)}, bf16[4,64,128]{2,1,0:T(8,128)(2,1)S(1)}, u32[]{:S(2)}, u32[]{:S(2)}) collective-permute-start(bf16[4,64,128]{2,1,0:T(8,128)(2,1)S(1)} %stack.1.refs_0_), channel_id=1, source_target_pairs={{0,16},{2,18},{16,0},{18,2},{1,17},{3,19},{17,1},{19,3},{4,20},{6,... | collective-permute-start | bytes 196616 | tf_op jit(solution)/shard_map/ppermute | solution.py:408
  13.2 1.5 %collective-permute-start.4 = (bf16[4,64,128]{2,1,0:T(8,128)(2,1)S(1)}, bf16[4,64,128]{2,1,0:T(8,128)(2,1)S(1)}, u32[]{:S(2)}, u32[]{:S(2)}) collective-permute-start(bf16[4,64,128]{2,1,0:T(8,128)(2,1)S(1)} %stack.1.refs_0_), channel_id=1, source_target_pairs={{0,2},{2,0},{16,18},{18,16},{1,3},{3,1},{17,19},{19,17},{4,6},{6,4... | collective-permute-start | bytes 196616 | tf_op jit(solution)/shard_map/ppermute | solution.py:408
  14.7 0.5 collective-permute-start.3
  15.2 4.3 %load_second.1 = (bf16[3072,1792]{1,0:T(8,128)(2,1)S(1)}, f32[8,128]{1,0:T(8,128)S(1)}) custom-call(s32[8]{0:T(128)} %lengths.1, s32[8]{0:T(128)} %hit_lengths.1, s32[8]{0:T(128)} %start_positions.1, bf16[8192,1792]{1,0:T(8,128)(2,1)} %refs_2_.1, bf16[8192,1792]{1,0:T(8,128)(2,1)} %refs_3_.1), custom_call_target="tpu_custom_call" | custom-call | bytes 11010048 | tf_op jit(solution)/shard_map/load_second/pallas_call | solution.py:169
  19.5 0.0 collective-permute-done.5.refs_3_
  19.5 0.0 collective-permute-done.4.refs_2_
  19.5 0.3 collective-permute-done.3.refs_1_
  19.9 0.2 pack.1.near_ref
  20.1 0.1 collective-permute-start.6
  20.2 1.5 %collective-permute-done.6.far_ref = bf16[16,8192]{1,0:T(8,128)(2,1)S(1)} collective-permute-done((bf16[16,8192]{1,0:T(8,128)(2,1)S(1)}, bf16[16,8192]{1,0:T(8,128)(2,1)S(1)}, u32[]{:S(2)}, u32[]{:S(2)}) %collective-permute-start.6) | collective-permute-done | bytes 262176 | tf_op jit(solution)/shard_map/ppermute | solution.py:408
  21.7 11.8 %block.1 = (f32[16,64,128]{2,1,0:T(8,128)S(1)}, bf16[16,64,128]{2,1,0:T(8,128)(2,1)S(1)}) custom-call(bf16[16,8192]{1,0:T(8,128)(2,1)S(1)} %pack.1.near_ref, bf16[16,8192]{1,0:T(8,128)(2,1)S(1)} %collective-permute-done.6.far_ref, bf16[2048,1792]{1,0:T(8,128)(2,1)S(1)} %get-tuple-element.13.refs_0_, bf16[3072,1792]{1,0:T(8,128)(2,1)S(1)} %get-tuple-element.14.refs_1_, ...), custom_call_target="tpu_custom_call" | custom-call | flops 1409286144 | bytes 25690112 | tf_op jit(solution)/shard_map/block/pallas_call | solution.py:347
  33.5 0.2 collective-permute-start.7
  33.7 1.4 %collective-permute-done.7 = bf16[16,64,128]{2,1,0:T(8,128)(2,1)S(1)} collective-permute-done((bf16[16,64,128]{2,1,0:T(8,128)(2,1)S(1)}, bf16[16,64,128]{2,1,0:T(8,128)(2,1)S(1)}, u32[]{:S(2)}, u32[]{:S(2)}) %collective-permute-start.7) | collective-permute-done | bytes 262176 | tf_op jit(solution)/shard_map/ppermute | solution.py:408
  35.1 0.1 add_convert_fusion
  35.2 2.1 %collective-permute-start.8 = (bf16[4,64,128]{2,1,0:T(8,128)(2,1)S(1)}, bf16[4,64,128]{2,1,0:T(8,128)(2,1)S(1)}, u32[]{:S(2)}, u32[]{:S(2)}) collective-permute-start(bf16[4,64,128]{2,1,0:T(8,128)(2,1)S(1)} %get-tuple-element.17), channel_id=1, source_target_pairs={{0,18},{2,16},{16,2},{18,0},{1,19},{3,17},{17,3},{19,1},{4,22},{6,... | collective-permute-start | bytes 196616 | tf_op jit(solution)/shard_map/ppermute | solution.py:408
  37.3 0.6 %collective-permute-start.10 = (bf16[4,64,128]{2,1,0:T(8,128)(2,1)S(1)}, bf16[4,64,128]{2,1,0:T(8,128)(2,1)S(1)}, u32[]{:S(2)}, u32[]{:S(2)}) collective-permute-start(bf16[4,64,128]{2,1,0:T(8,128)(2,1)S(1)} %get-tuple-element.18), channel_id=1, source_target_pairs={{0,16},{2,18},{16,0},{18,2},{1,17},{3,19},{17,1},{19,3},{4,20},{6,... | collective-permute-start | bytes 196616 | tf_op jit(solution)/shard_map/ppermute | solution.py:408
  37.9 0.8 %collective-permute-start.9 = (bf16[4,64,128]{2,1,0:T(8,128)(2,1)S(1)}, bf16[4,64,128]{2,1,0:T(8,128)(2,1)S(1)}, u32[]{:S(2)}, u32[]{:S(2)}) collective-permute-start(bf16[4,64,128]{2,1,0:T(8,128)(2,1)S(1)} %get-tuple-element.19), channel_id=1, source_target_pairs={{0,2},{2,0},{16,18},{18,16},{1,3},{3,1},{17,19},{19,17},{4,6},{6,4... | collective-permute-start | bytes 196616 | tf_op jit(solution)/shard_map/ppermute | solution.py:408
  38.7 1.7 %collective-permute-done.8 = bf16[4,64,128]{2,1,0:T(8,128)(2,1)S(1)} collective-permute-done((bf16[4,64,128]{2,1,0:T(8,128)(2,1)S(1)}, bf16[4,64,128]{2,1,0:T(8,128)(2,1)S(1)}, u32[]{:S(2)}, u32[]{:S(2)}) %collective-permute-start.8) | collective-permute-done | bytes 65568 | tf_op jit(solution)/shard_map/ppermute | solution.py:408
  40.5 1.3 %collective-permute-done.10 = bf16[4,64,128]{2,1,0:T(8,128)(2,1)S(1)} collective-permute-done((bf16[4,64,128]{2,1,0:T(8,128)(2,1)S(1)}, bf16[4,64,128]{2,1,0:T(8,128)(2,1)S(1)}, u32[]{:S(2)}, u32[]{:S(2)}) %collective-permute-start.10) | collective-permute-done | bytes 65568 | tf_op jit(solution)/shard_map/ppermute | solution.py:408
  41.8 0.3 collective-permute-done.9
  42.2 1.3 %collective-permute-start.11 = (bf16[3,64,128]{2,1,0:T(8,128)(2,1)S(1)}, bf16[3,64,128]{2,1,0:T(8,128)(2,1)S(1)}, u32[]{:S(2)}, u32[]{:S(2)}) collective-permute-start(bf16[3,64,128]{2,1,0:T(8,128)(2,1)S(1)} %slice.66), channel_id=1, source_target_pairs={{0,4},{12,8},{1,5},{13,9},{2,6},{14,10},{3,7},{15,11},{16,20},{28,... | collective-permute-start | bytes 147464 | tf_op jit(solution)/shard_map/ppermute | solution.py:417
  43.5 1.7 %collective-permute-done.11 = bf16[3,64,128]{2,1,0:T(8,128)(2,1)S(1)} collective-permute-done((bf16[3,64,128]{2,1,0:T(8,128)(2,1)S(1)}, bf16[3,64,128]{2,1,0:T(8,128)(2,1)S(1)}, u32[]{:S(2)}, u32[]{:S(2)}) %collective-permute-start.11) | collective-permute-done | bytes 49184 | tf_op jit(solution)/shard_map/ppermute | solution.py:417
  45.3 0.7 %collective-permute-start.12 = (bf16[2,64,128]{2,1,0:T(8,128)(2,1)S(1)}, bf16[2,64,128]{2,1,0:T(8,128)(2,1)S(1)}, u32[]{:S(2)}, u32[]{:S(2)}) collective-permute-start(bf16[2,64,128]{2,1,0:T(8,128)(2,1)S(1)} %pad_maximum_fusion), channel_id=1, source_target_pairs={{4,8},{8,4},{5,9},{9,5},{6,10},{10,6},{7,11},{11,7},{20,24},{24,20... | collective-permute-start | bytes 98312 | tf_op jit(solution)/shard_map/ppermute | solution.py:422
  46.0 0.0 collective-permute-done.12
  46.0 1.3 %collective-permute-start.13 = (bf16[1,64,128]{2,1,0:T(8,128)(2,1)S(1)}, bf16[1,64,128]{2,1,0:T(8,128)(2,1)S(1)}, u32[]{:S(2)}, u32[]{:S(2)}) collective-permute-start(bf16[1,64,128]{2,1,0:T(8,128)(2,1)S(1)} %fusion), channel_id=1, source_target_pairs={{4,0},{8,12},{5,1},{9,13},{6,2},{10,14},{7,3},{11,15},{20,16},{24,... | collective-permute-start | bytes 49160 | tf_op jit(solution)/shard_map/ppermute | solution.py:424
  47.3 9.1 %collective-permute-done.13.refs_2_ = bf16[1,64,128]{2,1,0:T(8,128)(2,1)S(1)} collective-permute-done((bf16[1,64,128]{2,1,0:T(8,128)(2,1)S(1)}, bf16[1,64,128]{2,1,0:T(8,128)(2,1)S(1)}, u32[]{:S(2)}, u32[]{:S(2)}) %collective-permute-start.13) | collective-permute-done | bytes 16416 | tf_op jit(solution)/shard_map/ppermute | solution.py:424
  56.5 0.7 %finish.1 = bf16[1,8192]{1,0:T(2,128)(2,1)} custom-call(f32[1,64,128]{2,1,0:T(8,128)S(1)} %get-tuple-element.22.refs_0_, bf16[1,64,128]{2,1,0:T(8,128)(2,1)S(1)} %slice.48.refs_1_, bf16[1,64,128]{2,1,0:T(8,128)(2,1)S(1)} %collective-permute-done.13.refs_2_, f32[8,128]{1,0:T(8,128)S(1)} %get-tuple-element.12.refs_5_.refs_3_), custom_call_target="tpu_custom_call" | custom-call | tf_op jit(solution)/shard_map/finish/pallas_call | solution.py:396
  (8 shorter events, 0.1 us)
Async XLA Ops:
  0.0 8.9 %collective-permute-start.1 = (bf16[1,8192]{1,0:T(2,128)(2,1)}, bf16[1,8192]{1,0:T(2,128)(2,1)S(1)}, u32[]{:S(2)}, u32[]{:S(2)}) collective-permute-start(bf16[1,8192]{1,0:T(2,128)(2,1)} %refs_0_.1), channel_id=1, source_target_pairs={{0,8},{4,12},{8,0},{12,4},{1,9},{5,13},{9,1},{13,5},{2,10},{6,14},... | collective-permute-start | bytes 49160 | tf_op jit(solution)/shard_map/ppermute | solution.py:408
  4.0 4.8 %collective-permute-start = (bf16[1,8192]{1,0:T(2,128)(2,1)}, bf16[1,8192]{1,0:T(2,128)(2,1)S(1)}, u32[]{:S(2)}, u32[]{:S(2)}) collective-permute-start(bf16[1,8192]{1,0:T(2,128)(2,1)} %refs_0_.1), channel_id=1, source_target_pairs={{0,4},{4,0},{8,12},{12,8},{1,5},{5,1},{9,13},{13,9},{2,6},{6,2},{1... | collective-permute-start | bytes 49160 | tf_op jit(solution)/shard_map/ppermute | solution.py:408
  5.6 5.9 %collective-permute-start.2 = (bf16[1,8192]{1,0:T(2,128)(2,1)}, bf16[1,8192]{1,0:T(2,128)(2,1)S(1)}, u32[]{:S(2)}, u32[]{:S(2)}) collective-permute-start(bf16[1,8192]{1,0:T(2,128)(2,1)} %refs_0_.1), channel_id=1, source_target_pairs={{0,12},{4,8},{8,4},{12,0},{1,13},{5,9},{9,5},{13,1},{2,14},{6,10},... | collective-permute-start | bytes 49160 | tf_op jit(solution)/shard_map/ppermute | solution.py:408
  5.6 5.9 %copy-start = (bf16[1,8192]{1,0:T(2,128)(2,1)S(1)}, bf16[1,8192]{1,0:T(2,128)(2,1)}, u32[]{:S(2)}) copy-start(bf16[1,8192]{1,0:T(2,128)(2,1)} %refs_0_.1) | copy-start | bytes 49156
  11.6 7.9 %collective-permute-start.5 = (bf16[4,64,128]{2,1,0:T(8,128)(2,1)S(1)}, bf16[4,64,128]{2,1,0:T(8,128)(2,1)S(1)}, u32[]{:S(2)}, u32[]{:S(2)}) collective-permute-start(bf16[4,64,128]{2,1,0:T(8,128)(2,1)S(1)} %stack.1.refs_0_), channel_id=1, source_target_pairs={{0,16},{2,18},{16,0},{18,2},{1,17},{3,19},{17,1},{19,3},{4,20},{6,... | collective-permute-start | bytes 196616 | tf_op jit(solution)/shard_map/ppermute | solution.py:408
  13.2 6.3 %collective-permute-start.4 = (bf16[4,64,128]{2,1,0:T(8,128)(2,1)S(1)}, bf16[4,64,128]{2,1,0:T(8,128)(2,1)S(1)}, u32[]{:S(2)}, u32[]{:S(2)}) collective-permute-start(bf16[4,64,128]{2,1,0:T(8,128)(2,1)S(1)} %stack.1.refs_0_), channel_id=1, source_target_pairs={{0,2},{2,0},{16,18},{18,16},{1,3},{3,1},{17,19},{19,17},{4,6},{6,4... | collective-permute-start | bytes 196616 | tf_op jit(solution)/shard_map/ppermute | solution.py:408
  14.7 5.2 %collective-permute-start.3 = (bf16[4,64,128]{2,1,0:T(8,128)(2,1)S(1)}, bf16[4,64,128]{2,1,0:T(8,128)(2,1)S(1)}, u32[]{:S(2)}, u32[]{:S(2)}) collective-permute-start(bf16[4,64,128]{2,1,0:T(8,128)(2,1)S(1)} %stack.1.refs_0_), channel_id=1, source_target_pairs={{0,18},{2,16},{16,2},{18,0},{1,19},{3,17},{17,3},{19,1},{4,22},{6,... | collective-permute-start | bytes 196616 | tf_op jit(solution)/shard_map/ppermute | solution.py:408
  20.1 1.6 %collective-permute-start.6 = (bf16[16,8192]{1,0:T(8,128)(2,1)S(1)}, bf16[16,8192]{1,0:T(8,128)(2,1)S(1)}, u32[]{:S(2)}, u32[]{:S(2)}) collective-permute-start(bf16[16,8192]{1,0:T(8,128)(2,1)S(1)} %pack.1.near_ref), channel_id=1, source_target_pairs={{0,1},{1,0},{2,3},{3,2},{4,5},{5,4},{6,7},{7,6},{8,9},{9,8},{10,11... | collective-permute-start | bytes 786440 | tf_op jit(solution)/shard_map/ppermute | solution.py:408
  33.5 1.6 %collective-permute-start.7 = (bf16[16,64,128]{2,1,0:T(8,128)(2,1)S(1)}, bf16[16,64,128]{2,1,0:T(8,128)(2,1)S(1)}, u32[]{:S(2)}, u32[]{:S(2)}) collective-permute-start(bf16[16,64,128]{2,1,0:T(8,128)(2,1)S(1)} %get-tuple-element.16), channel_id=1, source_target_pairs={{0,1},{1,0},{2,3},{3,2},{4,5},{5,4},{6,7},{7,6},{8,9},{9,8},{10,11... | collective-permute-start | bytes 786440 | tf_op jit(solution)/shard_map/ppermute | solution.py:408
  35.2 5.3 %collective-permute-start.8 = (bf16[4,64,128]{2,1,0:T(8,128)(2,1)S(1)}, bf16[4,64,128]{2,1,0:T(8,128)(2,1)S(1)}, u32[]{:S(2)}, u32[]{:S(2)}) collective-permute-start(bf16[4,64,128]{2,1,0:T(8,128)(2,1)S(1)} %get-tuple-element.17), channel_id=1, source_target_pairs={{0,18},{2,16},{16,2},{18,0},{1,19},{3,17},{17,3},{19,1},{4,22},{6,... | collective-permute-start | bytes 196616 | tf_op jit(solution)/shard_map/ppermute | solution.py:408
  37.3 4.5 %collective-permute-start.10 = (bf16[4,64,128]{2,1,0:T(8,128)(2,1)S(1)}, bf16[4,64,128]{2,1,0:T(8,128)(2,1)S(1)}, u32[]{:S(2)}, u32[]{:S(2)}) collective-permute-start(bf16[4,64,128]{2,1,0:T(8,128)(2,1)S(1)} %get-tuple-element.18), channel_id=1, source_target_pairs={{0,16},{2,18},{16,0},{18,2},{1,17},{3,19},{17,1},{19,3},{4,20},{6,... | collective-permute-start | bytes 196616 | tf_op jit(solution)/shard_map/ppermute | solution.py:408
  37.9 4.3 %collective-permute-start.9 = (bf16[4,64,128]{2,1,0:T(8,128)(2,1)S(1)}, bf16[4,64,128]{2,1,0:T(8,128)(2,1)S(1)}, u32[]{:S(2)}, u32[]{:S(2)}) collective-permute-start(bf16[4,64,128]{2,1,0:T(8,128)(2,1)S(1)} %get-tuple-element.19), channel_id=1, source_target_pairs={{0,2},{2,0},{16,18},{18,16},{1,3},{3,1},{17,19},{19,17},{4,6},{6,4... | collective-permute-start | bytes 196616 | tf_op jit(solution)/shard_map/ppermute | solution.py:408
  42.2 3.0 %collective-permute-start.11 = (bf16[3,64,128]{2,1,0:T(8,128)(2,1)S(1)}, bf16[3,64,128]{2,1,0:T(8,128)(2,1)S(1)}, u32[]{:S(2)}, u32[]{:S(2)}) collective-permute-start(bf16[3,64,128]{2,1,0:T(8,128)(2,1)S(1)} %slice.66), channel_id=1, source_target_pairs={{0,4},{12,8},{1,5},{13,9},{2,6},{14,10},{3,7},{15,11},{16,20},{28,... | collective-permute-start | bytes 147464 | tf_op jit(solution)/shard_map/ppermute | solution.py:417
  45.3 0.7 %collective-permute-start.12 = (bf16[2,64,128]{2,1,0:T(8,128)(2,1)S(1)}, bf16[2,64,128]{2,1,0:T(8,128)(2,1)S(1)}, u32[]{:S(2)}, u32[]{:S(2)}) collective-permute-start(bf16[2,64,128]{2,1,0:T(8,128)(2,1)S(1)} %pad_maximum_fusion), channel_id=1, source_target_pairs={{4,8},{8,4},{5,9},{9,5},{6,10},{10,6},{7,11},{11,7},{20,24},{24,20... | collective-permute-start | bytes 98312 | tf_op jit(solution)/shard_map/ppermute | solution.py:422
  46.0 10.5 %collective-permute-start.13 = (bf16[1,64,128]{2,1,0:T(8,128)(2,1)S(1)}, bf16[1,64,128]{2,1,0:T(8,128)(2,1)S(1)}, u32[]{:S(2)}, u32[]{:S(2)}) collective-permute-start(bf16[1,64,128]{2,1,0:T(8,128)(2,1)S(1)} %fusion), channel_id=1, source_target_pairs={{4,0},{8,12},{5,1},{9,13},{6,2},{10,14},{7,3},{11,15},{20,16},{24,... | collective-permute-start | bytes 49160 | tf_op jit(solution)/shard_map/ppermute | solution.py:424

commit v8 on v6

--- a/solution.py
+++ b/solution.py
@@ -67,20 +67,20 @@
     return live
 
 
-def stack_kernel(*refs):
+def stack_kernel(rows, *refs):
     pieces, out_ref, wide_ref = refs[:-3], refs[-2], refs[-1]
     lines = out_ref.shape[1]
-    for at, piece in enumerate(pieces):
+    for at, piece in zip(rows, pieces):
         values = piece[...].astype(jnp.float32)
         for line in range(lines):
             wide_ref[at, line : line + 1] = values[:, line * LANES : (line + 1) * LANES]
     out_ref[...] = wide_ref[...].astype(out_ref.dtype)
 
 
-def stack(pieces, gain):
+def stack(rows, pieces, gain):
     shape = (len(pieces), pieces[0].shape[1] // LANES, LANES)
     return pl.pallas_call(
-        stack_kernel,
+        functools.partial(stack_kernel, rows),
         out_shape=jax.ShapeDtypeStruct(shape, pieces[0].dtype),
         in_specs=[VMEM] * len(pieces) + [pl.BlockSpec(memory_space=pl.ANY)],
         out_specs=VMEM,
@@ -246,12 +246,13 @@
     loaded = sum(ref.shape[0] for ref in first_refs)
     own = pl.multiple_of(lax.axis_index("groups") * half, LANES)
     loads = []
-    for step, at in enumerate(range(0, depth - loaded, chunk)):
+    deal = rest_ref.shape[0] // both_sems.shape[0]
+    for step, at in enumerate(range(0, depth - loaded, deal)):
         loads.append(
             [
                 pltpu.make_async_copy(
-                    weight.at[pl.ds(loaded + at, chunk), pl.ds(own, half)],
-                    rest_ref.at[pl.ds(at, chunk), pl.ds(side * half, half)],
+                    weight.at[pl.ds(loaded + at, deal), pl.ds(own, half)],
+                    rest_ref.at[pl.ds(at, deal), pl.ds(side * half, half)],
                     both_sems.at[step, side],
                 )
                 for side, weight in enumerate((gate_hbm, up_hbm))
@@ -269,8 +270,8 @@
             ]
         )
 
-    def start(numbers):
-        for number in numbers:
+    def start(first, last):
+        for number in range(first, min(last, len(loads))):
             for copy in loads[number]:
                 copy.start()
 
@@ -278,18 +279,8 @@
         for copy in loads[number]:
             copy.wait()
 
-    waiting = list(range(len(loads)))
-
-    def start_next(count):
-        start(waiting[:count])
-        del waiting[:count]
-
-    start_next(1)
-    rows_ref[: rows // 2] = near_ref[...]
-    rows_ref[rows // 2 :] = far_ref[...]
-
-    def multiply(at, count, ref, row, paced):
-        for number, column in enumerate(range(0, 2 * half, tile)):
+    def multiply(at, count, ref, row):
+        for column in range(0, 2 * half, tile):
             columns = pl.ds(column, tile)
             value = jnp.dot(
                 rows_ref[:, at : at + count],
@@ -300,21 +291,23 @@
                 product_ref[:, columns] = value
             else:
                 product_ref[:, columns] += value
-            if number in paced:
-                start_next(1)
-
+
+    start(0, pairs)
+    rows_ref[: rows // 2] = near_ref[...]
+    rows_ref[rows // 2 :] = far_ref[...]
     at = 0
     for ref in first_refs:
-        multiply(at, ref.shape[0], ref, 0, (1, 6) if at == 0 else (3, 5, 6))
+        multiply(at, ref.shape[0], ref, 0)
         at += ref.shape[0]
+    start(pairs, pairs + 2)
     for step in range(pairs):
         wait(step)
-        multiply(at, chunk, rest_ref, step * chunk, (3, 6))
-        at += chunk
+        multiply(at, deal, rest_ref, step * deal)
+        start(pairs + 2 + step, len(loads) if step == pairs - 1 else pairs + 3 + step)
+        at += deal
     gate_out = product_ref[:, :half]
     up_out = product_ref[:, half:]
     hidden_ref[...] = (gate_out / (1.0 + jnp.exp(-gate_out)) * up_out).astype(jnp.bfloat16)
-    start_next(len(waiting))
     for step in range(depth // chunk):
         wait(pairs + step)
         for at in range(step * chunk, (step + 1) * chunk, tile):
@@ -342,7 +335,7 @@
 
     def body(near_ref, far_ref, *refs):
         count = len(firsts)
-        block_kernel(half, CHUNK, near_ref, far_ref, refs[:count], *refs[count:])
+        block_kernel(half, 2 * CHUNK, near_ref, far_ref, refs[:count], *refs[count:])
 
     return pl.pallas_call(
         body,
@@ -359,8 +352,8 @@
             pltpu.VMEM((2 * rows, half), jnp.bfloat16),
             pltpu.VMEM((rest, 2 * half), jnp.bfloat16),
             pltpu.VMEM((half, depth), jnp.bfloat16),
-            pltpu.SemaphoreType.DMA((rest // CHUNK, 2)),
-            pltpu.SemaphoreType.DMA((depth // CHUNK,)),
+            pltpu.SemaphoreType.DMA((2, 2)),
+            pltpu.SemaphoreType.DMA((depth // (2 * CHUNK),)),
         ],
         compiler_params=pltpu.CompilerParams(
             vmem_limit_bytes=(rest * 2 + depth) * half * 2 + (6 << 20)
@@ -425,24 +418,22 @@
         ) + lax.axis_index("core")
 
     deep = lax.axis_size("z")
-    far_first = [3, 1, 2]
-    rest = [0] + far_first
-    column = [tokens] + [swap(tokens, "z", at) for at in range(1, deep)]
+    others = range(1, lax.axis_size(square))
+    rows = [0] + list(range(2, deep)) + [1]
+    column = [swap(tokens, "z", at) if at else tokens for at in rows]
     first, gain = load_first(w_gate, w_up, norm_gain.reshape(-1, LANES), half, 2 * CHUNK)
-    column = stack(column, gain)
-    plane = [column] + [swap(column, square, at) for at in far_first]
-    second, live = load_second(w_gate, w_up, half, 2 * CHUNK, 2 * CHUNK, requests, place)
+    column = stack(rows, column, gain)
+    plane = [column] + [swap(column, square, at) for at in others]
+    second, live = load_second(w_gate, w_up, half, 2 * CHUNK, 3 * CHUNK, requests, place)
     near = pack(plane, gain, live)
     far = swap(near, "core", 1)
     kept, sent = block(near, far, (first, second), w_gate, w_up, w_down, half)
     plane = (kept + swap(sent, "core", 1).astype(jnp.float32)).astype(jnp.bfloat16)
-    pieces = jnp.split(plane, len(rest), axis=0)
-    arrived = [swap(piece, square, at) for at, piece in zip(far_first, pieces[1:])]
+    pieces = jnp.split(plane, lax.axis_size(square), axis=0)
     column = pieces[0].astype(jnp.float32)
-    for piece in arrived:
+    for piece in [swap(pieces[at], square, at) for at in reversed(others)]:
         column = column + piece.astype(jnp.float32)
-    column = column.astype(jnp.bfloat16)
-    pieces = jnp.split(column, deep, axis=0)
+    pieces = jnp.split(column.astype(jnp.bfloat16), deep, axis=0)
     return finish(
         pieces[:1] + [swap(piece, "z", at + 1) for at, piece in enumerate(pieces[1:])], live
     )

time: 49 us -> 48.2 us (0.984)
  waiting for transfers between devices: 11.6 us -> 10.7 us
    pallas_call x1, Pallas kernels: 3.2 us -> 4.34 us  [load_second(): pl.pallas_call(functools.partial(load_second_kernel, half, row, place), o...]
    pallas_call x1, Pallas kernels: 12.2 us -> 11.2 us  [block(): pl.pallas_call(body, out_shape=(jax.ShapeDtypeStruct((rows, lines, LANES)...]
    ppermute x14, waiting for transfers between devices: 11.6 us -> 10.7 us  [swap(): lax.ppermute(value, axes, [(place, place ^ offset) for place in places])]
  transfers between devices with their start and end apart: 14 -> 14, of which waited for: 8 -> 8; matrix products, arithmetic and copies ran while one was open for 0% -> 0% of each run, Pallas kernels for 13% -> 16%
where the time goes in v8:
time: 48.2 us; the launch traced here: 48 us
  Pallas kernels  19.7 us (41%)
  starting transfers between devices  17.5 us (36%)
  waiting for transfers between devices  10.7 us (22%)
    ppermute x14, starting transfers between devices, swap(): lax.ppermute(value, axes, [(place, place ^ offset) for place in places])  17.5 us
    pallas_call x1, Pallas kernels, block(): pl.pallas_call(body, out_shape=(jax.ShapeDtypeStruct((rows, lines, LANES)...  11.2 us
    ppermute x14, waiting for transfers between devices, swap(): lax.ppermute(value, axes, [(place, place ^ offset) for place in places])  10.7 us
    pallas_call x1, Pallas kernels, load_second(): pl.pallas_call(functools.partial(load_second_kernel, half, row, place), o...  4.34 us
    pallas_call x1, Pallas kernels, load_first(): pl.pallas_call(functools.partial(load_gain_kernel, half), out_shape=(pltp...  3.22 us
  transfers between devices with their start and end apart: 14, of which 8 were waited for; matrix products, arithmetic and copies ran while one was open for 0% of the time, Pallas kernels for 16%

profile of v8, /device:TPU:0, one launch (start us, length us, event | category | flops | bytes accessed | tf_op | source)
XLA Modules:
  0.0 48.0 jit_solution(1702649174128842279)
XLA Ops:
  0.0 5.0 %collective-permute-start.1 = (bf16[1,8192]{1,0:T(2,128)(2,1)}, bf16[1,8192]{1,0:T(2,128)(2,1)S(1)}, u32[]{:S(2)}, u32[]{:S(2)}) collective-permute-start(bf16[1,8192]{1,0:T(2,128)(2,1)} %refs_0_.1), channel_id=1, source_target_pairs={{0,12},{4,8},{8,4},{12,0},{1,13},{5,9},{9,5},{13,1},{2,14},{6,10},... | collective-permute-start | bytes 49160 | tf_op jit(solution)/shard_map/ppermute | solution.py:401
  5.0 0.0 collective-permute-start
  5.1 0.6 %collective-permute-start.2 = (bf16[1,8192]{1,0:T(2,128)(2,1)}, bf16[1,8192]{1,0:T(2,128)(2,1)S(1)}, u32[]{:S(2)}, u32[]{:S(2)}) collective-permute-start(bf16[1,8192]{1,0:T(2,128)(2,1)} %refs_0_.1), channel_id=1, source_target_pairs={{0,4},{4,0},{8,12},{12,8},{1,5},{5,1},{9,13},{13,9},{2,6},{6,2},{1... | collective-permute-start | bytes 49160 | tf_op jit(solution)/shard_map/ppermute | solution.py:401
  5.6 0.0 copy-start
  5.6 3.2 %load_first.1 = (bf16[2048,1792]{1,0:T(8,128)(2,1)S(1)}, bf16[64,128]{1,0:T(8,128)(2,1)S(1)}) custom-call(bf16[8192,1792]{1,0:T(8,128)(2,1)} %refs_2_.1, bf16[8192,1792]{1,0:T(8,128)(2,1)} %refs_3_.1, bf16[64,128]{1,0:T(8,128)(2,1)} %bitcast.1), custom_call_target="tpu_custom_call" | custom-call | bytes 7340032 | tf_op jit(solution)/shard_map/load_first/pallas_call | solution.py:110
  8.8 0.0 collective-permute-done.1.refs_2_
  8.9 1.2 %collective-permute-done.refs_1_ = bf16[1,8192]{1,0:T(2,128)(2,1)S(1)} collective-permute-done((bf16[1,8192]{1,0:T(2,128)(2,1)}, bf16[1,8192]{1,0:T(2,128)(2,1)S(1)}, u32[]{:S(2)}, u32[]{:S(2)}) %collective-permute-start) | collective-permute-done | bytes 16416 | tf_op jit(solution)/shard_map/ppermute | solution.py:401
  10.1 0.0 collective-permute-done.2.refs_3_
  10.1 0.0 copy-done
  10.1 0.1 stack.1.refs_0_
  10.2 2.5 %collective-permute-start.5 = (bf16[4,64,128]{2,1,0:T(8,128)(2,1)S(1)}, bf16[4,64,128]{2,1,0:T(8,128)(2,1)S(1)}, u32[]{:S(2)}, u32[]{:S(2)}) collective-permute-start(bf16[4,64,128]{2,1,0:T(8,128)(2,1)S(1)} %stack.1.refs_0_), channel_id=1, source_target_pairs={{0,18},{2,16},{16,2},{18,0},{1,19},{3,17},{17,3},{19,1},{4,22},{6,... | collective-permute-start | bytes 196616 | tf_op jit(solution)/shard_map/ppermute | solution.py:401
  12.7 0.5 %collective-permute-start.4 = (bf16[4,64,128]{2,1,0:T(8,128)(2,1)S(1)}, bf16[4,64,128]{2,1,0:T(8,128)(2,1)S(1)}, u32[]{:S(2)}, u32[]{:S(2)}) collective-permute-start(bf16[4,64,128]{2,1,0:T(8,128)(2,1)S(1)} %stack.1.refs_0_), channel_id=1, source_target_pairs={{0,16},{2,18},{16,0},{18,2},{1,17},{3,19},{17,1},{19,3},{4,20},{6,... | collective-permute-start | bytes 196616 | tf_op jit(solution)/shard_map/ppermute | solution.py:401
  13.2 0.5 %collective-permute-start.3 = (bf16[4,64,128]{2,1,0:T(8,128)(2,1)S(1)}, bf16[4,64,128]{2,1,0:T(8,128)(2,1)S(1)}, u32[]{:S(2)}, u32[]{:S(2)}) collective-permute-start(bf16[4,64,128]{2,1,0:T(8,128)(2,1)S(1)} %stack.1.refs_0_), channel_id=1, source_target_pairs={{0,2},{2,0},{16,18},{18,16},{1,3},{3,1},{17,19},{19,17},{4,6},{6,4... | collective-permute-start | bytes 196616 | tf_op jit(solution)/shard_map/ppermute | solution.py:401
  13.7 4.3 %load_second.1 = (bf16[3072,1792]{1,0:T(8,128)(2,1)S(1)}, f32[8,128]{1,0:T(8,128)S(1)}) custom-call(s32[8]{0:T(128)} %lengths.1, s32[8]{0:T(128)} %hit_lengths.1, s32[8]{0:T(128)} %start_positions.1, bf16[8192,1792]{1,0:T(8,128)(2,1)} %refs_2_.1, bf16[8192,1792]{1,0:T(8,128)(2,1)} %refs_3_.1), custom_call_target="tpu_custom_call" | custom-call | bytes 11010048 | tf_op jit(solution)/shard_map/load_second/pallas_call | solution.py:169
  18.1 0.0 collective-permute-done.5.refs_3_
  18.1 0.0 collective-permute-done.4.refs_2_
  18.1 0.0 collective-permute-done.3.refs_1_
  18.1 0.2 pack.1.near_ref
  18.3 0.1 collective-permute-start.6
  18.4 1.5 %collective-permute-done.6.far_ref = bf16[16,8192]{1,0:T(8,128)(2,1)S(1)} collective-permute-done((bf16[16,8192]{1,0:T(8,128)(2,1)S(1)}, bf16[16,8192]{1,0:T(8,128)(2,1)S(1)}, u32[]{:S(2)}, u32[]{:S(2)}) %collective-permute-start.6) | collective-permute-done | bytes 262176 | tf_op jit(solution)/shard_map/ppermute | solution.py:401
  19.9 11.2 %block.1 = (f32[16,64,128]{2,1,0:T(8,128)S(1)}, bf16[16,64,128]{2,1,0:T(8,128)(2,1)S(1)}) custom-call(bf16[16,8192]{1,0:T(8,128)(2,1)S(1)} %pack.1.near_ref, bf16[16,8192]{1,0:T(8,128)(2,1)S(1)} %collective-permute-done.6.far_ref, bf16[2048,1792]{1,0:T(8,128)(2,1)S(1)} %get-tuple-element.13.refs_0_, bf16[3072,1792]{1,0:T(8,128)(2,1)S(1)} %get-tuple-element.14.refs_1_, ...), custom_call_target="tpu_custom_call" | custom-call | flops 1409286144 | bytes 25690112 | tf_op jit(solution)/shard_map/block/pallas_call | solution.py:340
  31.1 0.2 collective-permute-start.7
  31.3 1.4 %collective-permute-done.7 = bf16[16,64,128]{2,1,0:T(8,128)(2,1)S(1)} collective-permute-done((bf16[16,64,128]{2,1,0:T(8,128)(2,1)S(1)}, bf16[16,64,128]{2,1,0:T(8,128)(2,1)S(1)}, u32[]{:S(2)}, u32[]{:S(2)}) %collective-permute-start.7) | collective-permute-done | bytes 262176 | tf_op jit(solution)/shard_map/ppermute | solution.py:401
  32.7 0.1 add_convert_fusion
  32.8 2.4 %collective-permute-start.8 = (bf16[4,64,128]{2,1,0:T(8,128)(2,1)S(1)}, bf16[4,64,128]{2,1,0:T(8,128)(2,1)S(1)}, u32[]{:S(2)}, u32[]{:S(2)}) collective-permute-start(bf16[4,64,128]{2,1,0:T(8,128)(2,1)S(1)} %get-tuple-element.17), channel_id=1, source_target_pairs={{0,18},{2,16},{16,2},{18,0},{1,19},{3,17},{17,3},{19,1},{4,22},{6,... | collective-permute-start | bytes 196616 | tf_op jit(solution)/shard_map/ppermute | solution.py:401
  35.2 0.5 %collective-permute-start.10 = (bf16[4,64,128]{2,1,0:T(8,128)(2,1)S(1)}, bf16[4,64,128]{2,1,0:T(8,128)(2,1)S(1)}, u32[]{:S(2)}, u32[]{:S(2)}) collective-permute-start(bf16[4,64,128]{2,1,0:T(8,128)(2,1)S(1)} %get-tuple-element.18), channel_id=1, source_target_pairs={{0,2},{2,0},{16,18},{18,16},{1,3},{3,1},{17,19},{19,17},{4,6},{6,4... | collective-permute-start | bytes 196616 | tf_op jit(solution)/shard_map/ppermute | solution.py:401
  35.7 0.6 %collective-permute-start.9 = (bf16[4,64,128]{2,1,0:T(8,128)(2,1)S(1)}, bf16[4,64,128]{2,1,0:T(8,128)(2,1)S(1)}, u32[]{:S(2)}, u32[]{:S(2)}) collective-permute-start(bf16[4,64,128]{2,1,0:T(8,128)(2,1)S(1)} %get-tuple-element.19), channel_id=1, source_target_pairs={{0,16},{2,18},{16,0},{18,2},{1,17},{3,19},{17,1},{19,3},{4,20},{6,... | collective-permute-start | bytes 196616 | tf_op jit(solution)/shard_map/ppermute | solution.py:401
  36.3 2.1 %collective-permute-done.8 = bf16[4,64,128]{2,1,0:T(8,128)(2,1)S(1)} collective-permute-done((bf16[4,64,128]{2,1,0:T(8,128)(2,1)S(1)}, bf16[4,64,128]{2,1,0:T(8,128)(2,1)S(1)}, u32[]{:S(2)}, u32[]{:S(2)}) %collective-permute-start.8) | collective-permute-done | bytes 65568 | tf_op jit(solution)/shard_map/ppermute | solution.py:401
  38.4 1.0 %collective-permute-done.10 = bf16[4,64,128]{2,1,0:T(8,128)(2,1)S(1)} collective-permute-done((bf16[4,64,128]{2,1,0:T(8,128)(2,1)S(1)}, bf16[4,64,128]{2,1,0:T(8,128)(2,1)S(1)}, u32[]{:S(2)}, u32[]{:S(2)}) %collective-permute-start.10) | collective-permute-done | bytes 65568 | tf_op jit(solution)/shard_map/ppermute | solution.py:401
  39.5 0.5 %collective-permute-done.9 = bf16[4,64,128]{2,1,0:T(8,128)(2,1)S(1)} collective-permute-done((bf16[4,64,128]{2,1,0:T(8,128)(2,1)S(1)}, bf16[4,64,128]{2,1,0:T(8,128)(2,1)S(1)}, u32[]{:S(2)}, u32[]{:S(2)}) %collective-permute-start.9) | collective-permute-done | bytes 65568 | tf_op jit(solution)/shard_map/ppermute | solution.py:401
  40.0 2.7 %collective-permute-start.13 = (bf16[1,64,128]{2,1,0:T(8,128)(2,1)S(1)}, bf16[1,64,128]{2,1,0:T(8,128)(2,1)S(1)}, u32[]{:S(2)}, u32[]{:S(2)}) collective-permute-start(bf16[1,64,128]{2,1,0:T(8,128)(2,1)S(1)} %get-tuple-element.20), channel_id=1, source_target_pairs={{0,12},{4,8},{8,4},{12,0},{1,13},{5,9},{9,5},{13,1},{2,14},{6,10},... | collective-permute-start | bytes 49160 | tf_op jit(solution)/shard_map/ppermute | solution.py:401
  42.7 0.0 collective-permute-start.12
  42.7 1.8 %collective-permute-start.11 = (bf16[1,64,128]{2,1,0:T(8,128)(2,1)S(1)}, bf16[1,64,128]{2,1,0:T(8,128)(2,1)S(1)}, u32[]{:S(2)}, u32[]{:S(2)}) collective-permute-start(bf16[1,64,128]{2,1,0:T(8,128)(2,1)S(1)} %get-tuple-element.22), channel_id=1, source_target_pairs={{0,4},{4,0},{8,12},{12,8},{1,5},{5,1},{9,13},{13,9},{2,6},{6,2},{1... | collective-permute-start | bytes 49160 | tf_op jit(solution)/shard_map/ppermute | solution.py:401
  44.5 1.1 %collective-permute-done.13.refs_3_ = bf16[1,64,128]{2,1,0:T(8,128)(2,1)S(1)} collective-permute-done((bf16[1,64,128]{2,1,0:T(8,128)(2,1)S(1)}, bf16[1,64,128]{2,1,0:T(8,128)(2,1)S(1)}, u32[]{:S(2)}, u32[]{:S(2)}) %collective-permute-start.13) | collective-permute-done | bytes 16416 | tf_op jit(solution)/shard_map/ppermute | solution.py:401
  45.7 1.7 %collective-permute-done.12.refs_2_ = bf16[1,64,128]{2,1,0:T(8,128)(2,1)S(1)} collective-permute-done((bf16[1,64,128]{2,1,0:T(8,128)(2,1)S(1)}, bf16[1,64,128]{2,1,0:T(8,128)(2,1)S(1)}, u32[]{:S(2)}, u32[]{:S(2)}) %collective-permute-start.12) | collective-permute-done | bytes 16416 | tf_op jit(solution)/shard_map/ppermute | solution.py:401
  47.4 0.0 collective-permute-done.11.refs_1_
  47.4 0.7 %finish.1 = bf16[1,8192]{1,0:T(2,128)(2,1)} custom-call(bf16[1,64,128]{2,1,0:T(8,128)(2,1)S(1)} %get-tuple-element.23.refs_0_, bf16[1,64,128]{2,1,0:T(8,128)(2,1)S(1)} %collective-permute-done.11.refs_1_, bf16[1,64,128]{2,1,0:T(8,128)(2,1)S(1)} %collective-permute-done.12.refs_2_, bf16[1,64,128]{2,1,0:T(8,128)(2,1)S(1)} %collective-permute-done.13.refs_3_, ...), custom_call_target="tpu_custom_call" | custom-call | tf_op jit(solution)/shard_map/finish/pallas_call | solution.py:389
  (3 shorter events, 0.1 us)
Async XLA Ops:
  0.0 8.9 %collective-permute-start.1 = (bf16[1,8192]{1,0:T(2,128)(2,1)}, bf16[1,8192]{1,0:T(2,128)(2,1)S(1)}, u32[]{:S(2)}, u32[]{:S(2)}) collective-permute-start(bf16[1,8192]{1,0:T(2,128)(2,1)} %refs_0_.1), channel_id=1, source_target_pairs={{0,12},{4,8},{8,4},{12,0},{1,13},{5,9},{9,5},{13,1},{2,14},{6,10},... | collective-permute-start | bytes 49160 | tf_op jit(solution)/shard_map/ppermute | solution.py:401
  5.0 5.0 %collective-permute-start = (bf16[1,8192]{1,0:T(2,128)(2,1)}, bf16[1,8192]{1,0:T(2,128)(2,1)S(1)}, u32[]{:S(2)}, u32[]{:S(2)}) collective-permute-start(bf16[1,8192]{1,0:T(2,128)(2,1)} %refs_0_.1), channel_id=1, source_target_pairs={{0,8},{4,12},{8,0},{12,4},{1,9},{5,13},{9,1},{13,5},{2,10},{6,14},... | collective-permute-start | bytes 49160 | tf_op jit(solution)/shard_map/ppermute | solution.py:401
  5.1 5.0 %collective-permute-start.2 = (bf16[1,8192]{1,0:T(2,128)(2,1)}, bf16[1,8192]{1,0:T(2,128)(2,1)S(1)}, u32[]{:S(2)}, u32[]{:S(2)}) collective-permute-start(bf16[1,8192]{1,0:T(2,128)(2,1)} %refs_0_.1), channel_id=1, source_target_pairs={{0,4},{4,0},{8,12},{12,8},{1,5},{5,1},{9,13},{13,9},{2,6},{6,2},{1... | collective-permute-start | bytes 49160 | tf_op jit(solution)/shard_map/ppermute | solution.py:401
  5.6 4.5 %copy-start = (bf16[1,8192]{1,0:T(2,128)(2,1)S(1)}, bf16[1,8192]{1,0:T(2,128)(2,1)}, u32[]{:S(2)}) copy-start(bf16[1,8192]{1,0:T(2,128)(2,1)} %refs_0_.1) | copy-start | bytes 49156
  10.2 7.9 %collective-permute-start.5 = (bf16[4,64,128]{2,1,0:T(8,128)(2,1)S(1)}, bf16[4,64,128]{2,1,0:T(8,128)(2,1)S(1)}, u32[]{:S(2)}, u32[]{:S(2)}) collective-permute-start(bf16[4,64,128]{2,1,0:T(8,128)(2,1)S(1)} %stack.1.refs_0_), channel_id=1, source_target_pairs={{0,18},{2,16},{16,2},{18,0},{1,19},{3,17},{17,3},{19,1},{4,22},{6,... | collective-permute-start | bytes 196616 | tf_op jit(solution)/shard_map/ppermute | solution.py:401
  12.7 5.4 %collective-permute-start.4 = (bf16[4,64,128]{2,1,0:T(8,128)(2,1)S(1)}, bf16[4,64,128]{2,1,0:T(8,128)(2,1)S(1)}, u32[]{:S(2)}, u32[]{:S(2)}) collective-permute-start(bf16[4,64,128]{2,1,0:T(8,128)(2,1)S(1)} %stack.1.refs_0_), channel_id=1, source_target_pairs={{0,16},{2,18},{16,0},{18,2},{1,17},{3,19},{17,1},{19,3},{4,20},{6,... | collective-permute-start | bytes 196616 | tf_op jit(solution)/shard_map/ppermute | solution.py:401
  13.2 4.9 %collective-permute-start.3 = (bf16[4,64,128]{2,1,0:T(8,128)(2,1)S(1)}, bf16[4,64,128]{2,1,0:T(8,128)(2,1)S(1)}, u32[]{:S(2)}, u32[]{:S(2)}) collective-permute-start(bf16[4,64,128]{2,1,0:T(8,128)(2,1)S(1)} %stack.1.refs_0_), channel_id=1, source_target_pairs={{0,2},{2,0},{16,18},{18,16},{1,3},{3,1},{17,19},{19,17},{4,6},{6,4... | collective-permute-start | bytes 196616 | tf_op jit(solution)/shard_map/ppermute | solution.py:401
  18.3 1.6 %collective-permute-start.6 = (bf16[16,8192]{1,0:T(8,128)(2,1)S(1)}, bf16[16,8192]{1,0:T(8,128)(2,1)S(1)}, u32[]{:S(2)}, u32[]{:S(2)}) collective-permute-start(bf16[16,8192]{1,0:T(8,128)(2,1)S(1)} %pack.1.near_ref), channel_id=1, source_target_pairs={{0,1},{1,0},{2,3},{3,2},{4,5},{5,4},{6,7},{7,6},{8,9},{9,8},{10,11... | collective-permute-start | bytes 786440 | tf_op jit(solution)/shard_map/ppermute | solution.py:401
  31.1 1.6 %collective-permute-start.7 = (bf16[16,64,128]{2,1,0:T(8,128)(2,1)S(1)}, bf16[16,64,128]{2,1,0:T(8,128)(2,1)S(1)}, u32[]{:S(2)}, u32[]{:S(2)}) collective-permute-start(bf16[16,64,128]{2,1,0:T(8,128)(2,1)S(1)} %get-tuple-element.16), channel_id=1, source_target_pairs={{0,1},{1,0},{2,3},{3,2},{4,5},{5,4},{6,7},{7,6},{8,9},{9,8},{10,11... | collective-permute-start | bytes 786440 | tf_op jit(solution)/shard_map/ppermute | solution.py:401
  32.8 5.6 %collective-permute-start.8 = (bf16[4,64,128]{2,1,0:T(8,128)(2,1)S(1)}, bf16[4,64,128]{2,1,0:T(8,128)(2,1)S(1)}, u32[]{:S(2)}, u32[]{:S(2)}) collective-permute-start(bf16[4,64,128]{2,1,0:T(8,128)(2,1)S(1)} %get-tuple-element.17), channel_id=1, source_target_pairs={{0,18},{2,16},{16,2},{18,0},{1,19},{3,17},{17,3},{19,1},{4,22},{6,... | collective-permute-start | bytes 196616 | tf_op jit(solution)/shard_map/ppermute | solution.py:401
  35.2 4.3 %collective-permute-start.10 = (bf16[4,64,128]{2,1,0:T(8,128)(2,1)S(1)}, bf16[4,64,128]{2,1,0:T(8,128)(2,1)S(1)}, u32[]{:S(2)}, u32[]{:S(2)}) collective-permute-start(bf16[4,64,128]{2,1,0:T(8,128)(2,1)S(1)} %get-tuple-element.18), channel_id=1, source_target_pairs={{0,2},{2,0},{16,18},{18,16},{1,3},{3,1},{17,19},{19,17},{4,6},{6,4... | collective-permute-start | bytes 196616 | tf_op jit(solution)/shard_map/ppermute | solution.py:401
  35.7 4.3 %collective-permute-start.9 = (bf16[4,64,128]{2,1,0:T(8,128)(2,1)S(1)}, bf16[4,64,128]{2,1,0:T(8,128)(2,1)S(1)}, u32[]{:S(2)}, u32[]{:S(2)}) collective-permute-start(bf16[4,64,128]{2,1,0:T(8,128)(2,1)S(1)} %get-tuple-element.19), channel_id=1, source_target_pairs={{0,16},{2,18},{16,0},{18,2},{1,17},{3,19},{17,1},{19,3},{4,20},{6,... | collective-permute-start | bytes 196616 | tf_op jit(solution)/shard_map/ppermute | solution.py:401
  40.0 5.6 %collective-permute-start.13 = (bf16[1,64,128]{2,1,0:T(8,128)(2,1)S(1)}, bf16[1,64,128]{2,1,0:T(8,128)(2,1)S(1)}, u32[]{:S(2)}, u32[]{:S(2)}) collective-permute-start(bf16[1,64,128]{2,1,0:T(8,128)(2,1)S(1)} %get-tuple-element.20), channel_id=1, source_target_pairs={{0,12},{4,8},{8,4},{12,0},{1,13},{5,9},{9,5},{13,1},{2,14},{6,10},... | collective-permute-start | bytes 49160 | tf_op jit(solution)/shard_map/ppermute | solution.py:401
  42.7 4.6 %collective-permute-start.12 = (bf16[1,64,128]{2,1,0:T(8,128)(2,1)S(1)}, bf16[1,64,128]{2,1,0:T(8,128)(2,1)S(1)}, u32[]{:S(2)}, u32[]{:S(2)}) collective-permute-start(bf16[1,64,128]{2,1,0:T(8,128)(2,1)S(1)} %get-tuple-element.21), channel_id=1, source_target_pairs={{0,8},{4,12},{8,0},{12,4},{1,9},{5,13},{9,1},{13,5},{2,10},{6,14},... | collective-permute-start | bytes 49160 | tf_op jit(solution)/shard_map/ppermute | solution.py:401
  42.7 4.6 %collective-permute-start.11 = (bf16[1,64,128]{2,1,0:T(8,128)(2,1)S(1)}, bf16[1,64,128]{2,1,0:T(8,128)(2,1)S(1)}, u32[]{:S(2)}, u32[]{:S(2)}) collective-permute-start(bf16[1,64,128]{2,1,0:T(8,128)(2,1)S(1)} %get-tuple-element.22), channel_id=1, source_target_pairs={{0,4},{4,0},{8,12},{12,8},{1,5},{5,1},{9,13},{13,9},{2,6},{6,2},{1... | collective-permute-start | bytes 49160 | tf_op jit(solution)/shard_map/ppermute | solution.py:401

commit v9 on v8

--- a/solution.py
+++ b/solution.py
@@ -221,6 +221,7 @@
 def block_kernel(
     half,
     chunk,
+    deals,
     near_ref,
     far_ref,
     first_refs,
@@ -238,7 +239,7 @@
     both_sems,
     down_sems,
 ):
-    tile = 256
+    tile = 512
     rows, depth = rows_ref.shape
     lanes = LANES
     lines = depth // lanes
@@ -246,8 +247,8 @@
     loaded = sum(ref.shape[0] for ref in first_refs)
     own = pl.multiple_of(lax.axis_index("groups") * half, LANES)
     loads = []
-    deal = rest_ref.shape[0] // both_sems.shape[0]
-    for step, at in enumerate(range(0, depth - loaded, deal)):
+    at = 0
+    for step, deal in enumerate(deals):
         loads.append(
             [
                 pltpu.make_async_copy(
@@ -258,6 +259,7 @@
                 for side, weight in enumerate((gate_hbm, up_hbm))
             ]
         )
+        at += deal
     pairs = len(loads)
     for step, at in enumerate(range(0, depth, chunk)):
         loads.append(
@@ -270,18 +272,20 @@
             ]
         )
 
-    def start(first, last):
-        for number in range(first, min(last, len(loads))):
-            for copy in loads[number]:
+    waiting = list(loads)
+
+    def start():
+        if waiting:
+            for copy in waiting.pop(0):
                 copy.start()
 
     def wait(number):
         for copy in loads[number]:
             copy.wait()
 
-    def multiply(at, count, ref, row):
+    def multiply(at, count, ref, row, halfway):
         for column in range(0, 2 * half, tile):
-            columns = pl.ds(column, tile)
+            columns = pl.ds(column, min(tile, 2 * half - column))
             value = jnp.dot(
                 rows_ref[:, at : at + count],
                 ref[row : row + count, columns],
@@ -291,20 +295,27 @@
                 product_ref[:, columns] = value
             else:
                 product_ref[:, columns] += value
-
-    start(0, pairs)
+            if halfway and column == tile:
+                start()
+
+    start()
     rows_ref[: rows // 2] = near_ref[...]
     rows_ref[rows // 2 :] = far_ref[...]
     at = 0
     for ref in first_refs:
-        multiply(at, ref.shape[0], ref, 0)
+        multiply(at, ref.shape[0], ref, 0, False)
+        if at == 0:
+            start()
         at += ref.shape[0]
-    start(pairs, pairs + 2)
-    for step in range(pairs):
+    row = 0
+    for step, deal in enumerate(deals):
         wait(step)
-        multiply(at, deal, rest_ref, step * deal)
-        start(pairs + 2 + step, len(loads) if step == pairs - 1 else pairs + 3 + step)
+        multiply(at, deal, rest_ref, row, True)
+        start()
         at += deal
+        row += deal
+    while waiting:
+        start()
     gate_out = product_ref[:, :half]
     up_out = product_ref[:, half:]
     hidden_ref[...] = (gate_out / (1.0 + jnp.exp(-gate_out)) * up_out).astype(jnp.bfloat16)
@@ -332,10 +343,11 @@
     rows, depth = near.shape
     lines = depth // LANES
     rest = depth - sum(first.shape[0] for first in firsts)
+    deals = (rest * 3 // 7, rest - rest * 3 // 7)
 
     def body(near_ref, far_ref, *refs):
         count = len(firsts)
-        block_kernel(half, 2 * CHUNK, near_ref, far_ref, refs[:count], *refs[count:])
+        block_kernel(half, 2 * CHUNK, deals, near_ref, far_ref, refs[:count], *refs[count:])
 
     return pl.pallas_call(
         body,
@@ -424,7 +436,7 @@
     first, gain = load_first(w_gate, w_up, norm_gain.reshape(-1, LANES), half, 2 * CHUNK)
     column = stack(rows, column, gain)
     plane = [column] + [swap(column, square, at) for at in others]
-    second, live = load_second(w_gate, w_up, half, 2 * CHUNK, 3 * CHUNK, requests, place)
+    second, live = load_second(w_gate, w_up, half, 2 * CHUNK, 5 * CHUNK // 2, requests, place)
     near = pack(plane, gain, live)
     far = swap(near, "core", 1)
     kept, sent = block(near, far, (first, second), w_gate, w_up, w_down, half)

time: 48.2 us -> 47.2 us (0.979)
  Pallas kernels: 19.7 us -> 18.6 us
    pallas_call x1, Pallas kernels: 4.34 us -> 3.74 us  [load_second(): pl.pallas_call(functools.partial(load_second_kernel, half, row, place), o...]
  transfers between devices with their start and end apart: 14 -> 14, of which waited for: 8 -> 8; matrix products, arithmetic and copies ran while one was open for 0% -> 0% of each run, Pallas kernels for 16% -> 15%
where the time goes in v9:
time: 47.2 us; the launch traced here: 47.1 us
  Pallas kernels  18.6 us (39%)
  starting transfers between devices  17.5 us (37%)
  waiting for transfers between devices  10.8 us (23%)
    ppermute x14, starting transfers between devices, swap(): lax.ppermute(value, axes, [(place, place ^ offset) for place in places])  17.5 us
    ppermute x14, waiting for transfers between devices, swap(): lax.ppermute(value, axes, [(place, place ^ offset) for place in places])  10.8 us
    pallas_call x1, Pallas kernels, block(): pl.pallas_call(body, out_shape=(jax.ShapeDtypeStruct((rows, lines, LANES)...  10.7 us
    pallas_call x1, Pallas kernels, load_second(): pl.pallas_call(functools.partial(load_second_kernel, half, row, place), o...  3.74 us
    pallas_call x1, Pallas kernels, load_first(): pl.pallas_call(functools.partial(load_gain_kernel, half), out_shape=(pltp...  3.22 us
  transfers between devices with their start and end apart: 14, of which 8 were waited for; matrix products, arithmetic and copies ran while one was open for 0% of the time, Pallas kernels for 15%

profile of v9, /device:TPU:0, one launch (start us, length us, event | category | flops | bytes accessed | tf_op | source)
XLA Modules:
  0.0 47.1 jit_solution(13313201724074988007)
XLA Ops:
  0.0 5.0 %collective-permute-start.1 = (bf16[1,8192]{1,0:T(2,128)(2,1)}, bf16[1,8192]{1,0:T(2,128)(2,1)S(1)}, u32[]{:S(2)}, u32[]{:S(2)}) collective-permute-start(bf16[1,8192]{1,0:T(2,128)(2,1)} %refs_0_.1), channel_id=1, source_target_pairs={{0,12},{4,8},{8,4},{12,0},{1,13},{5,9},{9,5},{13,1},{2,14},{6,10},... | collective-permute-start | bytes 49160 | tf_op jit(solution)/shard_map/ppermute | solution.py:413
  5.0 0.0 collective-permute-start
  5.1 0.6 %collective-permute-start.2 = (bf16[1,8192]{1,0:T(2,128)(2,1)}, bf16[1,8192]{1,0:T(2,128)(2,1)S(1)}, u32[]{:S(2)}, u32[]{:S(2)}) collective-permute-start(bf16[1,8192]{1,0:T(2,128)(2,1)} %refs_0_.1), channel_id=1, source_target_pairs={{0,4},{4,0},{8,12},{12,8},{1,5},{5,1},{9,13},{13,9},{2,6},{6,2},{1... | collective-permute-start | bytes 49160 | tf_op jit(solution)/shard_map/ppermute | solution.py:413
  5.6 0.0 copy-start
  5.6 3.2 %load_first.1 = (bf16[2048,1792]{1,0:T(8,128)(2,1)S(1)}, bf16[64,128]{1,0:T(8,128)(2,1)S(1)}) custom-call(bf16[8192,1792]{1,0:T(8,128)(2,1)} %refs_2_.1, bf16[8192,1792]{1,0:T(8,128)(2,1)} %refs_3_.1, bf16[64,128]{1,0:T(8,128)(2,1)} %bitcast.1), custom_call_target="tpu_custom_call" | custom-call | bytes 7340032 | tf_op jit(solution)/shard_map/load_first/pallas_call | solution.py:110
  8.8 0.0 collective-permute-done.1.refs_2_
  8.9 1.2 %collective-permute-done.refs_1_ = bf16[1,8192]{1,0:T(2,128)(2,1)S(1)} collective-permute-done((bf16[1,8192]{1,0:T(2,128)(2,1)}, bf16[1,8192]{1,0:T(2,128)(2,1)S(1)}, u32[]{:S(2)}, u32[]{:S(2)}) %collective-permute-start) | collective-permute-done | bytes 16416 | tf_op jit(solution)/shard_map/ppermute | solution.py:413
  10.1 0.0 collective-permute-done.2.refs_3_
  10.1 0.0 copy-done
  10.1 0.1 stack.1.refs_0_
  10.2 2.5 %collective-permute-start.5 = (bf16[4,64,128]{2,1,0:T(8,128)(2,1)S(1)}, bf16[4,64,128]{2,1,0:T(8,128)(2,1)S(1)}, u32[]{:S(2)}, u32[]{:S(2)}) collective-permute-start(bf16[4,64,128]{2,1,0:T(8,128)(2,1)S(1)} %stack.1.refs_0_), channel_id=1, source_target_pairs={{0,18},{2,16},{16,2},{18,0},{1,19},{3,17},{17,3},{19,1},{4,22},{6,... | collective-permute-start | bytes 196616 | tf_op jit(solution)/shard_map/ppermute | solution.py:413
  12.7 0.5 %collective-permute-start.4 = (bf16[4,64,128]{2,1,0:T(8,128)(2,1)S(1)}, bf16[4,64,128]{2,1,0:T(8,128)(2,1)S(1)}, u32[]{:S(2)}, u32[]{:S(2)}) collective-permute-start(bf16[4,64,128]{2,1,0:T(8,128)(2,1)S(1)} %stack.1.refs_0_), channel_id=1, source_target_pairs={{0,16},{2,18},{16,0},{18,2},{1,17},{3,19},{17,1},{19,3},{4,20},{6,... | collective-permute-start | bytes 196616 | tf_op jit(solution)/shard_map/ppermute | solution.py:413
  13.2 0.5 %collective-permute-start.3 = (bf16[4,64,128]{2,1,0:T(8,128)(2,1)S(1)}, bf16[4,64,128]{2,1,0:T(8,128)(2,1)S(1)}, u32[]{:S(2)}, u32[]{:S(2)}) collective-permute-start(bf16[4,64,128]{2,1,0:T(8,128)(2,1)S(1)} %stack.1.refs_0_), channel_id=1, source_target_pairs={{0,2},{2,0},{16,18},{18,16},{1,3},{3,1},{17,19},{19,17},{4,6},{6,4... | collective-permute-start | bytes 196616 | tf_op jit(solution)/shard_map/ppermute | solution.py:413
  13.7 3.7 %load_second.1 = (bf16[2560,1792]{1,0:T(8,128)(2,1)S(1)}, f32[8,128]{1,0:T(8,128)S(1)}) custom-call(s32[8]{0:T(128)} %lengths.1, s32[8]{0:T(128)} %hit_lengths.1, s32[8]{0:T(128)} %start_positions.1, bf16[8192,1792]{1,0:T(8,128)(2,1)} %refs_2_.1, bf16[8192,1792]{1,0:T(8,128)(2,1)} %refs_3_.1), custom_call_target="tpu_custom_call" | custom-call | bytes 9175040 | tf_op jit(solution)/shard_map/load_second/pallas_call | solution.py:169
  17.5 0.0 collective-permute-done.5.refs_3_
  17.5 0.0 collective-permute-done.4.refs_2_
  17.5 0.0 collective-permute-done.3.refs_1_
  17.5 0.2 pack.1.near_ref
  17.7 0.1 collective-permute-start.6
  17.8 1.5 %collective-permute-done.6.far_ref = bf16[16,8192]{1,0:T(8,128)(2,1)S(1)} collective-permute-done((bf16[16,8192]{1,0:T(8,128)(2,1)S(1)}, bf16[16,8192]{1,0:T(8,128)(2,1)S(1)}, u32[]{:S(2)}, u32[]{:S(2)}) %collective-permute-start.6) | collective-permute-done | bytes 262176 | tf_op jit(solution)/shard_map/ppermute | solution.py:413
  19.3 10.7 %block.1 = (f32[16,64,128]{2,1,0:T(8,128)S(1)}, bf16[16,64,128]{2,1,0:T(8,128)(2,1)S(1)}) custom-call(bf16[16,8192]{1,0:T(8,128)(2,1)S(1)} %pack.1.near_ref, bf16[16,8192]{1,0:T(8,128)(2,1)S(1)} %collective-permute-done.6.far_ref, bf16[2048,1792]{1,0:T(8,128)(2,1)S(1)} %get-tuple-element.13.refs_0_, bf16[2560,1792]{1,0:T(8,128)(2,1)S(1)} %get-tuple-element.14.refs_1_, ...), custom_call_target="tpu_custom_call" | custom-call | flops 1409286144 | bytes 27525120 | tf_op jit(solution)/shard_map/block/pallas_call | solution.py:352
  30.0 0.2 collective-permute-start.7
  30.2 1.4 %collective-permute-done.7 = bf16[16,64,128]{2,1,0:T(8,128)(2,1)S(1)} collective-permute-done((bf16[16,64,128]{2,1,0:T(8,128)(2,1)S(1)}, bf16[16,64,128]{2,1,0:T(8,128)(2,1)S(1)}, u32[]{:S(2)}, u32[]{:S(2)}) %collective-permute-start.7) | collective-permute-done | bytes 262176 | tf_op jit(solution)/shard_map/ppermute | solution.py:413
  31.6 0.1 add_convert_fusion
  31.7 2.5 %collective-permute-start.8 = (bf16[4,64,128]{2,1,0:T(8,128)(2,1)S(1)}, bf16[4,64,128]{2,1,0:T(8,128)(2,1)S(1)}, u32[]{:S(2)}, u32[]{:S(2)}) collective-permute-start(bf16[4,64,128]{2,1,0:T(8,128)(2,1)S(1)} %get-tuple-element.17), channel_id=1, source_target_pairs={{0,18},{2,16},{16,2},{18,0},{1,19},{3,17},{17,3},{19,1},{4,22},{6,... | collective-permute-start | bytes 196616 | tf_op jit(solution)/shard_map/ppermute | solution.py:413
  34.2 0.5 %collective-permute-start.10 = (bf16[4,64,128]{2,1,0:T(8,128)(2,1)S(1)}, bf16[4,64,128]{2,1,0:T(8,128)(2,1)S(1)}, u32[]{:S(2)}, u32[]{:S(2)}) collective-permute-start(bf16[4,64,128]{2,1,0:T(8,128)(2,1)S(1)} %get-tuple-element.18), channel_id=1, source_target_pairs={{0,2},{2,0},{16,18},{18,16},{1,3},{3,1},{17,19},{19,17},{4,6},{6,4... | collective-permute-start | bytes 196616 | tf_op jit(solution)/shard_map/ppermute | solution.py:413
  34.8 0.5 %collective-permute-start.9 = (bf16[4,64,128]{2,1,0:T(8,128)(2,1)S(1)}, bf16[4,64,128]{2,1,0:T(8,128)(2,1)S(1)}, u32[]{:S(2)}, u32[]{:S(2)}) collective-permute-start(bf16[4,64,128]{2,1,0:T(8,128)(2,1)S(1)} %get-tuple-element.19), channel_id=1, source_target_pairs={{0,16},{2,18},{16,0},{18,2},{1,17},{3,19},{17,1},{19,3},{4,20},{6,... | collective-permute-start | bytes 196616 | tf_op jit(solution)/shard_map/ppermute | solution.py:413
  35.3 2.1 %collective-permute-done.8 = bf16[4,64,128]{2,1,0:T(8,128)(2,1)S(1)} collective-permute-done((bf16[4,64,128]{2,1,0:T(8,128)(2,1)S(1)}, bf16[4,64,128]{2,1,0:T(8,128)(2,1)S(1)}, u32[]{:S(2)}, u32[]{:S(2)}) %collective-permute-start.8) | collective-permute-done | bytes 65568 | tf_op jit(solution)/shard_map/ppermute | solution.py:413
  37.4 1.1 %collective-permute-done.10 = bf16[4,64,128]{2,1,0:T(8,128)(2,1)S(1)} collective-permute-done((bf16[4,64,128]{2,1,0:T(8,128)(2,1)S(1)}, bf16[4,64,128]{2,1,0:T(8,128)(2,1)S(1)}, u32[]{:S(2)}, u32[]{:S(2)}) %collective-permute-start.10) | collective-permute-done | bytes 65568 | tf_op jit(solution)/shard_map/ppermute | solution.py:413
  38.5 0.5 %collective-permute-done.9 = bf16[4,64,128]{2,1,0:T(8,128)(2,1)S(1)} collective-permute-done((bf16[4,64,128]{2,1,0:T(8,128)(2,1)S(1)}, bf16[4,64,128]{2,1,0:T(8,128)(2,1)S(1)}, u32[]{:S(2)}, u32[]{:S(2)}) %collective-permute-start.9) | collective-permute-done | bytes 65568 | tf_op jit(solution)/shard_map/ppermute | solution.py:413
  39.1 2.7 %collective-permute-start.13 = (bf16[1,64,128]{2,1,0:T(8,128)(2,1)S(1)}, bf16[1,64,128]{2,1,0:T(8,128)(2,1)S(1)}, u32[]{:S(2)}, u32[]{:S(2)}) collective-permute-start(bf16[1,64,128]{2,1,0:T(8,128)(2,1)S(1)} %get-tuple-element.20), channel_id=1, source_target_pairs={{0,12},{4,8},{8,4},{12,0},{1,13},{5,9},{9,5},{13,1},{2,14},{6,10},... | collective-permute-start | bytes 49160 | tf_op jit(solution)/shard_map/ppermute | solution.py:413
  41.8 0.0 collective-permute-start.12
  41.8 1.8 %collective-permute-start.11 = (bf16[1,64,128]{2,1,0:T(8,128)(2,1)S(1)}, bf16[1,64,128]{2,1,0:T(8,128)(2,1)S(1)}, u32[]{:S(2)}, u32[]{:S(2)}) collective-permute-start(bf16[1,64,128]{2,1,0:T(8,128)(2,1)S(1)} %get-tuple-element.22), channel_id=1, source_target_pairs={{0,4},{4,0},{8,12},{12,8},{1,5},{5,1},{9,13},{13,9},{2,6},{6,2},{1... | collective-permute-start | bytes 49160 | tf_op jit(solution)/shard_map/ppermute | solution.py:413
  43.6 1.1 %collective-permute-done.13.refs_3_ = bf16[1,64,128]{2,1,0:T(8,128)(2,1)S(1)} collective-permute-done((bf16[1,64,128]{2,1,0:T(8,128)(2,1)S(1)}, bf16[1,64,128]{2,1,0:T(8,128)(2,1)S(1)}, u32[]{:S(2)}, u32[]{:S(2)}) %collective-permute-start.13) | collective-permute-done | bytes 16416 | tf_op jit(solution)/shard_map/ppermute | solution.py:413
  44.7 1.7 %collective-permute-done.12.refs_2_ = bf16[1,64,128]{2,1,0:T(8,128)(2,1)S(1)} collective-permute-done((bf16[1,64,128]{2,1,0:T(8,128)(2,1)S(1)}, bf16[1,64,128]{2,1,0:T(8,128)(2,1)S(1)}, u32[]{:S(2)}, u32[]{:S(2)}) %collective-permute-start.12) | collective-permute-done | bytes 16416 | tf_op jit(solution)/shard_map/ppermute | solution.py:413
  46.4 0.0 collective-permute-done.11.refs_1_
  46.4 0.7 %finish.1 = bf16[1,8192]{1,0:T(2,128)(2,1)} custom-call(bf16[1,64,128]{2,1,0:T(8,128)(2,1)S(1)} %get-tuple-element.23.refs_0_, bf16[1,64,128]{2,1,0:T(8,128)(2,1)S(1)} %collective-permute-done.11.refs_1_, bf16[1,64,128]{2,1,0:T(8,128)(2,1)S(1)} %collective-permute-done.12.refs_2_, bf16[1,64,128]{2,1,0:T(8,128)(2,1)S(1)} %collective-permute-done.13.refs_3_, ...), custom_call_target="tpu_custom_call" | custom-call | tf_op jit(solution)/shard_map/finish/pallas_call | solution.py:401
  (3 shorter events, 0.1 us)
Async XLA Ops:
  0.0 8.9 %collective-permute-start.1 = (bf16[1,8192]{1,0:T(2,128)(2,1)}, bf16[1,8192]{1,0:T(2,128)(2,1)S(1)}, u32[]{:S(2)}, u32[]{:S(2)}) collective-permute-start(bf16[1,8192]{1,0:T(2,128)(2,1)} %refs_0_.1), channel_id=1, source_target_pairs={{0,12},{4,8},{8,4},{12,0},{1,13},{5,9},{9,5},{13,1},{2,14},{6,10},... | collective-permute-start | bytes 49160 | tf_op jit(solution)/shard_map/ppermute | solution.py:413
  5.0 5.0 %collective-permute-start = (bf16[1,8192]{1,0:T(2,128)(2,1)}, bf16[1,8192]{1,0:T(2,128)(2,1)S(1)}, u32[]{:S(2)}, u32[]{:S(2)}) collective-permute-start(bf16[1,8192]{1,0:T(2,128)(2,1)} %refs_0_.1), channel_id=1, source_target_pairs={{0,8},{4,12},{8,0},{12,4},{1,9},{5,13},{9,1},{13,5},{2,10},{6,14},... | collective-permute-start | bytes 49160 | tf_op jit(solution)/shard_map/ppermute | solution.py:413
  5.1 5.0 %collective-permute-start.2 = (bf16[1,8192]{1,0:T(2,128)(2,1)}, bf16[1,8192]{1,0:T(2,128)(2,1)S(1)}, u32[]{:S(2)}, u32[]{:S(2)}) collective-permute-start(bf16[1,8192]{1,0:T(2,128)(2,1)} %refs_0_.1), channel_id=1, source_target_pairs={{0,4},{4,0},{8,12},{12,8},{1,5},{5,1},{9,13},{13,9},{2,6},{6,2},{1... | collective-permute-start | bytes 49160 | tf_op jit(solution)/shard_map/ppermute | solution.py:413
  5.6 4.5 %copy-start = (bf16[1,8192]{1,0:T(2,128)(2,1)S(1)}, bf16[1,8192]{1,0:T(2,128)(2,1)}, u32[]{:S(2)}) copy-start(bf16[1,8192]{1,0:T(2,128)(2,1)} %refs_0_.1) | copy-start | bytes 49156
  10.2 7.3 %collective-permute-start.5 = (bf16[4,64,128]{2,1,0:T(8,128)(2,1)S(1)}, bf16[4,64,128]{2,1,0:T(8,128)(2,1)S(1)}, u32[]{:S(2)}, u32[]{:S(2)}) collective-permute-start(bf16[4,64,128]{2,1,0:T(8,128)(2,1)S(1)} %stack.1.refs_0_), channel_id=1, source_target_pairs={{0,18},{2,16},{16,2},{18,0},{1,19},{3,17},{17,3},{19,1},{4,22},{6,... | collective-permute-start | bytes 196616 | tf_op jit(solution)/shard_map/ppermute | solution.py:413
  12.7 4.8 %collective-permute-start.4 = (bf16[4,64,128]{2,1,0:T(8,128)(2,1)S(1)}, bf16[4,64,128]{2,1,0:T(8,128)(2,1)S(1)}, u32[]{:S(2)}, u32[]{:S(2)}) collective-permute-start(bf16[4,64,128]{2,1,0:T(8,128)(2,1)S(1)} %stack.1.refs_0_), channel_id=1, source_target_pairs={{0,16},{2,18},{16,0},{18,2},{1,17},{3,19},{17,1},{19,3},{4,20},{6,... | collective-permute-start | bytes 196616 | tf_op jit(solution)/shard_map/ppermute | solution.py:413
  13.2 4.3 %collective-permute-start.3 = (bf16[4,64,128]{2,1,0:T(8,128)(2,1)S(1)}, bf16[4,64,128]{2,1,0:T(8,128)(2,1)S(1)}, u32[]{:S(2)}, u32[]{:S(2)}) collective-permute-start(bf16[4,64,128]{2,1,0:T(8,128)(2,1)S(1)} %stack.1.refs_0_), channel_id=1, source_target_pairs={{0,2},{2,0},{16,18},{18,16},{1,3},{3,1},{17,19},{19,17},{4,6},{6,4... | collective-permute-start | bytes 196616 | tf_op jit(solution)/shard_map/ppermute | solution.py:413
  17.7 1.6 %collective-permute-start.6 = (bf16[16,8192]{1,0:T(8,128)(2,1)S(1)}, bf16[16,8192]{1,0:T(8,128)(2,1)S(1)}, u32[]{:S(2)}, u32[]{:S(2)}) collective-permute-start(bf16[16,8192]{1,0:T(8,128)(2,1)S(1)} %pack.1.near_ref), channel_id=1, source_target_pairs={{0,1},{1,0},{2,3},{3,2},{4,5},{5,4},{6,7},{7,6},{8,9},{9,8},{10,11... | collective-permute-start | bytes 786440 | tf_op jit(solution)/shard_map/ppermute | solution.py:413
  30.0 1.6 %collective-permute-start.7 = (bf16[16,64,128]{2,1,0:T(8,128)(2,1)S(1)}, bf16[16,64,128]{2,1,0:T(8,128)(2,1)S(1)}, u32[]{:S(2)}, u32[]{:S(2)}) collective-permute-start(bf16[16,64,128]{2,1,0:T(8,128)(2,1)S(1)} %get-tuple-element.16), channel_id=1, source_target_pairs={{0,1},{1,0},{2,3},{3,2},{4,5},{5,4},{6,7},{7,6},{8,9},{9,8},{10,11... | collective-permute-start | bytes 786440 | tf_op jit(solution)/shard_map/ppermute | solution.py:413
  31.7 5.6 %collective-permute-start.8 = (bf16[4,64,128]{2,1,0:T(8,128)(2,1)S(1)}, bf16[4,64,128]{2,1,0:T(8,128)(2,1)S(1)}, u32[]{:S(2)}, u32[]{:S(2)}) collective-permute-start(bf16[4,64,128]{2,1,0:T(8,128)(2,1)S(1)} %get-tuple-element.17), channel_id=1, source_target_pairs={{0,18},{2,16},{16,2},{18,0},{1,19},{3,17},{17,3},{19,1},{4,22},{6,... | collective-permute-start | bytes 196616 | tf_op jit(solution)/shard_map/ppermute | solution.py:413
  34.2 4.3 %collective-permute-start.10 = (bf16[4,64,128]{2,1,0:T(8,128)(2,1)S(1)}, bf16[4,64,128]{2,1,0:T(8,128)(2,1)S(1)}, u32[]{:S(2)}, u32[]{:S(2)}) collective-permute-start(bf16[4,64,128]{2,1,0:T(8,128)(2,1)S(1)} %get-tuple-element.18), channel_id=1, source_target_pairs={{0,2},{2,0},{16,18},{18,16},{1,3},{3,1},{17,19},{19,17},{4,6},{6,4... | collective-permute-start | bytes 196616 | tf_op jit(solution)/shard_map/ppermute | solution.py:413
  34.8 4.3 %collective-permute-start.9 = (bf16[4,64,128]{2,1,0:T(8,128)(2,1)S(1)}, bf16[4,64,128]{2,1,0:T(8,128)(2,1)S(1)}, u32[]{:S(2)}, u32[]{:S(2)}) collective-permute-start(bf16[4,64,128]{2,1,0:T(8,128)(2,1)S(1)} %get-tuple-element.19), channel_id=1, source_target_pairs={{0,16},{2,18},{16,0},{18,2},{1,17},{3,19},{17,1},{19,3},{4,20},{6,... | collective-permute-start | bytes 196616 | tf_op jit(solution)/shard_map/ppermute | solution.py:413
  39.1 5.6 %collective-permute-start.13 = (bf16[1,64,128]{2,1,0:T(8,128)(2,1)S(1)}, bf16[1,64,128]{2,1,0:T(8,128)(2,1)S(1)}, u32[]{:S(2)}, u32[]{:S(2)}) collective-permute-start(bf16[1,64,128]{2,1,0:T(8,128)(2,1)S(1)} %get-tuple-element.20), channel_id=1, source_target_pairs={{0,12},{4,8},{8,4},{12,0},{1,13},{5,9},{9,5},{13,1},{2,14},{6,10},... | collective-permute-start | bytes 49160 | tf_op jit(solution)/shard_map/ppermute | solution.py:413
  41.8 4.6 %collective-permute-start.12 = (bf16[1,64,128]{2,1,0:T(8,128)(2,1)S(1)}, bf16[1,64,128]{2,1,0:T(8,128)(2,1)S(1)}, u32[]{:S(2)}, u32[]{:S(2)}) collective-permute-start(bf16[1,64,128]{2,1,0:T(8,128)(2,1)S(1)} %get-tuple-element.21), channel_id=1, source_target_pairs={{0,8},{4,12},{8,0},{12,4},{1,9},{5,13},{9,1},{13,5},{2,10},{6,14},... | collective-permute-start | bytes 49160 | tf_op jit(solution)/shard_map/ppermute | solution.py:413
  41.8 4.6 %collective-permute-start.11 = (bf16[1,64,128]{2,1,0:T(8,128)(2,1)S(1)}, bf16[1,64,128]{2,1,0:T(8,128)(2,1)S(1)}, u32[]{:S(2)}, u32[]{:S(2)}) collective-permute-start(bf16[1,64,128]{2,1,0:T(8,128)(2,1)S(1)} %get-tuple-element.22), channel_id=1, source_target_pairs={{0,4},{4,0},{8,12},{12,8},{1,5},{5,1},{9,13},{13,9},{2,6},{6,2},{1... | collective-permute-start | bytes 49160 | tf_op jit(solution)/shard_map/ppermute | solution.py:413

commit v10 on v9

--- a/solution.py
+++ b/solution.py
@@ -9,6 +9,7 @@
 
 LANES = 128
 ROW_LINES = ("groups", "z", "x", "core")
+LAYER = ("groups", "x", "z")
 
 
 def normalize(tokens, norm_gain):
@@ -319,6 +320,7 @@
     gate_out = product_ref[:, :half]
     up_out = product_ref[:, half:]
     hidden_ref[...] = (gate_out / (1.0 + jnp.exp(-gate_out)) * up_out).astype(jnp.bfloat16)
+    place = lax.axis_index(LAYER)
     for step in range(depth // chunk):
         wait(pairs + step)
         for at in range(step * chunk, (step + 1) * chunk, tile):
@@ -331,12 +333,13 @@
                 ]
         done = step * chunk // lanes
         count = chunk // lanes
-        for row in range(rows):
-            ready = wide_ref[row * stride + done : row * stride + done + count]
-            if row < rows // 2:
-                keep_ref[row, done : done + count] = ready
-            else:
-                send_ref[row - rows // 2, done : done + count] = ready.astype(jnp.bfloat16)
+        for row in range(rows // 2):
+            owner = lax.bitwise_xor(place, row)
+            keep_ref[owner, done : done + count] = wide_ref[
+                row * stride + done : row * stride + done + count
+            ]
+            at = (row + rows // 2) * stride + done
+            send_ref[owner, done : done + count] = wide_ref[at : at + count].astype(jnp.bfloat16)
 
 
 def block(near, far, firsts, w_gate, w_up, w_down, half):
@@ -386,26 +389,22 @@
     )
 
 
-def finish_kernel(*refs):
-    pieces, live_ref, out_ref = refs[:-2], refs[-2], refs[-1]
-    totals = pieces[0][...].astype(jnp.float32)
-    for piece in pieces[1:]:
-        totals = totals + piece[...].astype(jnp.float32)
-    totals = jnp.where(live_ref[:1] > 0, totals[0], jnp.zeros_like(totals[0]))
+def finish_kernel(pieces_ref, live_ref, out_ref):
+    totals = jnp.sum(pieces_ref[...].astype(jnp.float32), axis=0)
+    totals = jnp.where(live_ref[:1] > 0, totals, jnp.zeros_like(totals))
     for line in range(totals.shape[0]):
         out_ref[:, line * LANES : (line + 1) * LANES] = totals[line : line + 1].astype(jnp.bfloat16)
 
 
 def finish(pieces, live):
-    lines = pieces[0].shape[1]
     return pl.pallas_call(
         finish_kernel,
-        out_shape=jax.ShapeDtypeStruct((1, lines * LANES), jnp.bfloat16),
-        in_specs=[VMEM] * (len(pieces) + 1),
+        out_shape=jax.ShapeDtypeStruct((1, pieces.shape[1] * LANES), jnp.bfloat16),
+        in_specs=[VMEM] * 2,
         out_specs=VMEM,
-        compiler_params=pltpu.CompilerParams(vmem_limit_bytes=1 << 20),
+        compiler_params=pltpu.CompilerParams(vmem_limit_bytes=4 << 20),
         name="finish",
-    )(*pieces, live)
+    )(pieces, live)
 
 
 def swap(value, axes, offset):
@@ -441,14 +440,7 @@
     far = swap(near, "core", 1)
     kept, sent = block(near, far, (first, second), w_gate, w_up, w_down, half)
     plane = (kept + swap(sent, "core", 1).astype(jnp.float32)).astype(jnp.bfloat16)
-    pieces = jnp.split(plane, lax.axis_size(square), axis=0)
-    column = pieces[0].astype(jnp.float32)
-    for piece in [swap(pieces[at], square, at) for at in reversed(others)]:
-        column = column + piece.astype(jnp.float32)
-    pieces = jnp.split(column.astype(jnp.bfloat16), deep, axis=0)
-    return finish(
-        pieces[:1] + [swap(piece, "z", at + 1) for at, piece in enumerate(pieces[1:])], live
-    )
+    return finish(lax.all_to_all(plane, LAYER, split_axis=0, concat_axis=0, tiled=True), live)
 
 
 def solution(mesh):

time: 47.2 us -> 48.4 us (1.025)
  blocking collectives: 0 us -> 16.6 us
  starting transfers between devices: 17.5 us -> 9.44 us
  waiting for transfers between devices: 10.8 us -> 4.15 us
  Pallas kernels: 18.6 us -> 18 us
    all_to_all x0 -> x1, blocking collectives: none -> 16.6 us  [shared(): lax.all_to_all(plane, LAYER, split_axis=0, concat_axis=0, tiled=True)]
    ppermute x14 -> x8, starting transfers between devices: 17.5 us -> 9.44 us  [swap(): lax.ppermute(value, axes, [(place, place ^ offset) for place in places])]
    ppermute x14 -> x8, waiting for transfers between devices: 10.8 us -> 4.15 us  [swap(): lax.ppermute(value, axes, [(place, place ^ offset) for place in places])]
    pallas_call x1, Pallas kernels: 10.7 us -> 10 us  [block(): pl.pallas_call(body, out_shape=(jax.ShapeDtypeStruct((rows, lines, LANES)...]
  transfers between devices with their start and end apart: 14 -> 8, of which waited for: 8 -> 3; matrix products, arithmetic and copies ran while one was open for 0% -> 0% of each run, Pallas kernels for 15% -> 14%
where the time goes in v10:
time: 48.4 us; the launch traced here: 48.3 us
  Pallas kernels  18 us (37%)
  blocking collectives  16.6 us (34%)
  starting transfers between devices  9.44 us (20%)
  waiting for transfers between devices  4.15 us (9%)
    all_to_all x1, blocking collectives, shared(): lax.all_to_all(plane, LAYER, split_axis=0, concat_axis=0, tiled=True)  16.6 us
    pallas_call x1, Pallas kernels, block(): pl.pallas_call(body, out_shape=(jax.ShapeDtypeStruct((rows, lines, LANES)...  10 us
    ppermute x8, starting transfers between devices, swap(): lax.ppermute(value, axes, [(place, place ^ offset) for place in places])  9.44 us
    ppermute x8, waiting for transfers between devices, swap(): lax.ppermute(value, axes, [(place, place ^ offset) for place in places])  4.15 us
    pallas_call x1, Pallas kernels, load_second(): pl.pallas_call(functools.partial(load_second_kernel, half, row, place), o...  3.74 us
    pallas_call x1, Pallas kernels, load_first(): pl.pallas_call(functools.partial(load_gain_kernel, half), out_shape=(pltp...  3.22 us
  transfers between devices with their start and end apart: 8, of which 3 were waited for; matrix products, arithmetic and copies ran while one was open for 0% of the time, Pallas kernels for 14%

profile of v10, /device:TPU:0, one launch (start us, length us, event | category | flops | bytes accessed | tf_op | source)
XLA Modules:
  0.0 48.3 jit_solution(13782890489316263608)
XLA Ops:
  0.0 5.0 %collective-permute-start.1 = (bf16[1,8192]{1,0:T(2,128)(2,1)}, bf16[1,8192]{1,0:T(2,128)(2,1)S(1)}, u32[]{:S(2)}, u32[]{:S(2)}) collective-permute-start(bf16[1,8192]{1,0:T(2,128)(2,1)} %refs_0_.1), channel_id=1, source_target_pairs={{0,12},{4,8},{8,4},{12,0},{1,13},{5,9},{9,5},{13,1},{2,14},{6,10},... | collective-permute-start | bytes 49160 | tf_op jit(solution)/shard_map/ppermute | solution.py:412
  5.0 0.0 collective-permute-start
  5.1 0.6 %collective-permute-start.2 = (bf16[1,8192]{1,0:T(2,128)(2,1)}, bf16[1,8192]{1,0:T(2,128)(2,1)S(1)}, u32[]{:S(2)}, u32[]{:S(2)}) collective-permute-start(bf16[1,8192]{1,0:T(2,128)(2,1)} %refs_0_.1), channel_id=1, source_target_pairs={{0,4},{4,0},{8,12},{12,8},{1,5},{5,1},{9,13},{13,9},{2,6},{6,2},{1... | collective-permute-start | bytes 49160 | tf_op jit(solution)/shard_map/ppermute | solution.py:412
  5.6 0.0 copy-start
  5.6 3.2 %load_first.1 = (bf16[2048,1792]{1,0:T(8,128)(2,1)S(1)}, bf16[64,128]{1,0:T(8,128)(2,1)S(1)}) custom-call(bf16[8192,1792]{1,0:T(8,128)(2,1)} %refs_2_.1, bf16[8192,1792]{1,0:T(8,128)(2,1)} %refs_3_.1, bf16[64,128]{1,0:T(8,128)(2,1)} %bitcast.1), custom_call_target="tpu_custom_call" | custom-call | bytes 7340032 | tf_op jit(solution)/shard_map/load_first/pallas_call | solution.py:111
  8.8 0.0 collective-permute-done.1.refs_2_
  8.9 1.2 %collective-permute-done.refs_1_ = bf16[1,8192]{1,0:T(2,128)(2,1)S(1)} collective-permute-done((bf16[1,8192]{1,0:T(2,128)(2,1)}, bf16[1,8192]{1,0:T(2,128)(2,1)S(1)}, u32[]{:S(2)}, u32[]{:S(2)}) %collective-permute-start) | collective-permute-done | bytes 16416 | tf_op jit(solution)/shard_map/ppermute | solution.py:412
  10.1 0.0 collective-permute-done.2.refs_3_
  10.1 0.0 copy-done
  10.1 0.1 stack.1.refs_0_
  10.2 2.5 %collective-permute-start.5 = (bf16[4,64,128]{2,1,0:T(8,128)(2,1)S(1)}, bf16[4,64,128]{2,1,0:T(8,128)(2,1)S(1)}, u32[]{:S(2)}, u32[]{:S(2)}) collective-permute-start(bf16[4,64,128]{2,1,0:T(8,128)(2,1)S(1)} %stack.1.refs_0_), channel_id=1, source_target_pairs={{0,18},{2,16},{16,2},{18,0},{1,19},{3,17},{17,3},{19,1},{4,22},{6,... | collective-permute-start | bytes 196616 | tf_op jit(solution)/shard_map/ppermute | solution.py:412
  12.7 0.5 %collective-permute-start.4 = (bf16[4,64,128]{2,1,0:T(8,128)(2,1)S(1)}, bf16[4,64,128]{2,1,0:T(8,128)(2,1)S(1)}, u32[]{:S(2)}, u32[]{:S(2)}) collective-permute-start(bf16[4,64,128]{2,1,0:T(8,128)(2,1)S(1)} %stack.1.refs_0_), channel_id=1, source_target_pairs={{0,16},{2,18},{16,0},{18,2},{1,17},{3,19},{17,1},{19,3},{4,20},{6,... | collective-permute-start | bytes 196616 | tf_op jit(solution)/shard_map/ppermute | solution.py:412
  13.2 0.5 %collective-permute-start.3 = (bf16[4,64,128]{2,1,0:T(8,128)(2,1)S(1)}, bf16[4,64,128]{2,1,0:T(8,128)(2,1)S(1)}, u32[]{:S(2)}, u32[]{:S(2)}) collective-permute-start(bf16[4,64,128]{2,1,0:T(8,128)(2,1)S(1)} %stack.1.refs_0_), channel_id=1, source_target_pairs={{0,2},{2,0},{16,18},{18,16},{1,3},{3,1},{17,19},{19,17},{4,6},{6,4... | collective-permute-start | bytes 196616 | tf_op jit(solution)/shard_map/ppermute | solution.py:412
  13.7 3.7 %load_second.1 = (bf16[2560,1792]{1,0:T(8,128)(2,1)S(1)}, f32[8,128]{1,0:T(8,128)S(1)}) custom-call(s32[8]{0:T(128)} %lengths.1, s32[8]{0:T(128)} %hit_lengths.1, s32[8]{0:T(128)} %start_positions.1, bf16[8192,1792]{1,0:T(8,128)(2,1)} %refs_2_.1, bf16[8192,1792]{1,0:T(8,128)(2,1)} %refs_3_.1), custom_call_target="tpu_custom_call" | custom-call | bytes 9175040 | tf_op jit(solution)/shard_map/load_second/pallas_call | solution.py:170
  17.5 0.0 collective-permute-done.5.refs_3_
  17.5 0.0 collective-permute-done.4.refs_2_
  17.5 0.0 collective-permute-done.3.refs_1_
  17.5 0.2 pack.1.near_ref
  17.7 0.1 collective-permute-start.6
  17.8 1.5 %collective-permute-done.6.far_ref = bf16[16,8192]{1,0:T(8,128)(2,1)S(1)} collective-permute-done((bf16[16,8192]{1,0:T(8,128)(2,1)S(1)}, bf16[16,8192]{1,0:T(8,128)(2,1)S(1)}, u32[]{:S(2)}, u32[]{:S(2)}) %collective-permute-start.6) | collective-permute-done | bytes 262176 | tf_op jit(solution)/shard_map/ppermute | solution.py:412
  19.3 10.0 %block.1 = (f32[16,64,128]{2,1,0:T(8,128)S(1)}, bf16[16,64,128]{2,1,0:T(8,128)(2,1)S(1)}) custom-call(bf16[16,8192]{1,0:T(8,128)(2,1)S(1)} %pack.1.near_ref, bf16[16,8192]{1,0:T(8,128)(2,1)S(1)} %collective-permute-done.6.far_ref, bf16[2048,1792]{1,0:T(8,128)(2,1)S(1)} %get-tuple-element.13.refs_0_, bf16[2560,1792]{1,0:T(8,128)(2,1)S(1)} %get-tuple-element.14.refs_1_, ...), custom_call_target="tpu_custom_call" | custom-call | flops 1409286144 | bytes 27525120 | tf_op jit(solution)/shard_map/block/pallas_call | solution.py:355
  29.3 0.2 collective-permute-start.7
  29.5 1.4 %collective-permute-done.7 = bf16[16,64,128]{2,1,0:T(8,128)(2,1)S(1)} collective-permute-done((bf16[16,64,128]{2,1,0:T(8,128)(2,1)S(1)}, bf16[16,64,128]{2,1,0:T(8,128)(2,1)S(1)}, u32[]{:S(2)}, u32[]{:S(2)}) %collective-permute-start.7) | collective-permute-done | bytes 262176 | tf_op jit(solution)/shard_map/ppermute | solution.py:412
  30.9 0.1 add_convert_fusion
  31.0 16.6 %all_to_all.5.pieces_ref = bf16[16,64,128]{2,1,0:T(8,128)(2,1)S(1)} all-to-all(bf16[16,64,128]{2,1,0:T(8,128)(2,1)S(1)} %add_convert_fusion), channel_id=1, replica_groups=mesh['groups'=2,'z'=4,'x'=2,'core'=2] {'groups','x','z'}, dimensions={0} | all-to-all | bytes 524288 | tf_op jit(solution)/shard_map/all_to_all | solution.py:443
  47.6 0.7 %finish.1 = bf16[1,8192]{1,0:T(2,128)(2,1)} custom-call(bf16[16,64,128]{2,1,0:T(8,128)(2,1)S(1)} %all_to_all.5.pieces_ref, f32[8,128]{1,0:T(8,128)S(1)} %get-tuple-element.12.refs_5_.live_ref), custom_call_target="tpu_custom_call" | custom-call | tf_op jit(solution)/shard_map/finish/pallas_call | solution.py:400
Async XLA Ops:
  0.0 8.9 %collective-permute-start.1 = (bf16[1,8192]{1,0:T(2,128)(2,1)}, bf16[1,8192]{1,0:T(2,128)(2,1)S(1)}, u32[]{:S(2)}, u32[]{:S(2)}) collective-permute-start(bf16[1,8192]{1,0:T(2,128)(2,1)} %refs_0_.1), channel_id=1, source_target_pairs={{0,12},{4,8},{8,4},{12,0},{1,13},{5,9},{9,5},{13,1},{2,14},{6,10},... | collective-permute-start | bytes 49160 | tf_op jit(solution)/shard_map/ppermute | solution.py:412
  5.0 5.0 %collective-permute-start = (bf16[1,8192]{1,0:T(2,128)(2,1)}, bf16[1,8192]{1,0:T(2,128)(2,1)S(1)}, u32[]{:S(2)}, u32[]{:S(2)}) collective-permute-start(bf16[1,8192]{1,0:T(2,128)(2,1)} %refs_0_.1), channel_id=1, source_target_pairs={{0,8},{4,12},{8,0},{12,4},{1,9},{5,13},{9,1},{13,5},{2,10},{6,14},... | collective-permute-start | bytes 49160 | tf_op jit(solution)/shard_map/ppermute | solution.py:412
  5.1 5.0 %collective-permute-start.2 = (bf16[1,8192]{1,0:T(2,128)(2,1)}, bf16[1,8192]{1,0:T(2,128)(2,1)S(1)}, u32[]{:S(2)}, u32[]{:S(2)}) collective-permute-start(bf16[1,8192]{1,0:T(2,128)(2,1)} %refs_0_.1), channel_id=1, source_target_pairs={{0,4},{4,0},{8,12},{12,8},{1,5},{5,1},{9,13},{13,9},{2,6},{6,2},{1... | collective-permute-start | bytes 49160 | tf_op jit(solution)/shard_map/ppermute | solution.py:412
  5.6 4.5 %copy-start = (bf16[1,8192]{1,0:T(2,128)(2,1)S(1)}, bf16[1,8192]{1,0:T(2,128)(2,1)}, u32[]{:S(2)}) copy-start(bf16[1,8192]{1,0:T(2,128)(2,1)} %refs_0_.1) | copy-start | bytes 49156
  10.2 7.3 %collective-permute-start.5 = (bf16[4,64,128]{2,1,0:T(8,128)(2,1)S(1)}, bf16[4,64,128]{2,1,0:T(8,128)(2,1)S(1)}, u32[]{:S(2)}, u32[]{:S(2)}) collective-permute-start(bf16[4,64,128]{2,1,0:T(8,128)(2,1)S(1)} %stack.1.refs_0_), channel_id=1, source_target_pairs={{0,18},{2,16},{16,2},{18,0},{1,19},{3,17},{17,3},{19,1},{4,22},{6,... | collective-permute-start | bytes 196616 | tf_op jit(solution)/shard_map/ppermute | solution.py:412
  12.7 4.8 %collective-permute-start.4 = (bf16[4,64,128]{2,1,0:T(8,128)(2,1)S(1)}, bf16[4,64,128]{2,1,0:T(8,128)(2,1)S(1)}, u32[]{:S(2)}, u32[]{:S(2)}) collective-permute-start(bf16[4,64,128]{2,1,0:T(8,128)(2,1)S(1)} %stack.1.refs_0_), channel_id=1, source_target_pairs={{0,16},{2,18},{16,0},{18,2},{1,17},{3,19},{17,1},{19,3},{4,20},{6,... | collective-permute-start | bytes 196616 | tf_op jit(solution)/shard_map/ppermute | solution.py:412
  13.2 4.3 %collective-permute-start.3 = (bf16[4,64,128]{2,1,0:T(8,128)(2,1)S(1)}, bf16[4,64,128]{2,1,0:T(8,128)(2,1)S(1)}, u32[]{:S(2)}, u32[]{:S(2)}) collective-permute-start(bf16[4,64,128]{2,1,0:T(8,128)(2,1)S(1)} %stack.1.refs_0_), channel_id=1, source_target_pairs={{0,2},{2,0},{16,18},{18,16},{1,3},{3,1},{17,19},{19,17},{4,6},{6,4... | collective-permute-start | bytes 196616 | tf_op jit(solution)/shard_map/ppermute | solution.py:412
  17.7 1.6 %collective-permute-start.6 = (bf16[16,8192]{1,0:T(8,128)(2,1)S(1)}, bf16[16,8192]{1,0:T(8,128)(2,1)S(1)}, u32[]{:S(2)}, u32[]{:S(2)}) collective-permute-start(bf16[16,8192]{1,0:T(8,128)(2,1)S(1)} %pack.1.near_ref), channel_id=1, source_target_pairs={{0,1},{1,0},{2,3},{3,2},{4,5},{5,4},{6,7},{7,6},{8,9},{9,8},{10,11... | collective-permute-start | bytes 786440 | tf_op jit(solution)/shard_map/ppermute | solution.py:412
  29.3 1.6 %collective-permute-start.7 = (bf16[16,64,128]{2,1,0:T(8,128)(2,1)S(1)}, bf16[16,64,128]{2,1,0:T(8,128)(2,1)S(1)}, u32[]{:S(2)}, u32[]{:S(2)}) collective-permute-start(bf16[16,64,128]{2,1,0:T(8,128)(2,1)S(1)} %get-tuple-element.16), channel_id=1, source_target_pairs={{0,1},{1,0},{2,3},{3,2},{4,5},{5,4},{6,7},{7,6},{8,9},{9,8},{10,11... | collective-permute-start | bytes 786440 | tf_op jit(solution)/shard_map/ppermute | solution.py:412

commit v11 on v9

--- a/solution.py
+++ b/solution.py
@@ -182,6 +182,37 @@
         ),
         name="load_second",
     )(*requests, w_gate, w_up)
+
+
+def load_third_kernel(half, row, gate_hbm, up_hbm, near_ref, both_vmem, sems):
+    own = pl.multiple_of(lax.axis_index("groups") * half, LANES)
+    copies = [
+        pltpu.make_async_copy(
+            weight.at[pl.ds(row, both_vmem.shape[0]), pl.ds(own, half)],
+            both_vmem.at[:, pl.ds(at * half, half)],
+            sems.at[at],
+        )
+        for at, weight in enumerate((gate_hbm, up_hbm))
+    ]
+    for copy in copies:
+        copy.start()
+    for copy in copies:
+        copy.wait()
+
+
+def load_third(w_gate, w_up, near, half, row, count):
+    return pl.pallas_call(
+        functools.partial(load_third_kernel, half, row),
+        out_shape=pltpu.VMEM((count, 2 * half), w_gate.dtype),
+        in_specs=[HBM] * 2 + [pl.BlockSpec(memory_space=pl.ANY)],
+        out_specs=VMEM,
+        scratch_shapes=[pltpu.SemaphoreType.DMA((2,))],
+        compiler_params=pltpu.CompilerParams(vmem_limit_bytes=1 << 20),
+        cost_estimate=pl.CostEstimate(
+            flops=0, bytes_accessed=2 * count * half * 2, transcendentals=0
+        ),
+        name="load_third",
+    )(w_gate, w_up, near)
 
 
 def pack_kernel(*refs):
@@ -319,6 +350,7 @@
     gate_out = product_ref[:, :half]
     up_out = product_ref[:, half:]
     hidden_ref[...] = (gate_out / (1.0 + jnp.exp(-gate_out)) * up_out).astype(jnp.bfloat16)
+    zero = jnp.minimum(lax.axis_index("core"), 0)
     for step in range(depth // chunk):
         wait(pairs + step)
         for at in range(step * chunk, (step + 1) * chunk, tile):
@@ -331,19 +363,22 @@
                 ]
         done = step * chunk // lanes
         count = chunk // lanes
-        for row in range(rows):
-            ready = wide_ref[row * stride + done : row * stride + done + count]
-            if row < rows // 2:
-                keep_ref[row, done : done + count] = ready
-            else:
-                send_ref[row - rows // 2, done : done + count] = ready.astype(jnp.bfloat16)
+        for row in range(rows // 2):
+            keep_ref[row + zero, done : done + count] = wide_ref[
+                row * stride + done : row * stride + done + count
+            ]
+            at = (row + rows // 2) * stride + done
+            send_ref[row + zero, done : done + count] = wide_ref[at : at + count].astype(
+                jnp.bfloat16
+            )
 
 
 def block(near, far, firsts, w_gate, w_up, w_down, half):
     rows, depth = near.shape
     lines = depth // LANES
     rest = depth - sum(first.shape[0] for first in firsts)
-    deals = (rest * 3 // 7, rest - rest * 3 // 7)
+    early = rest * 3 // 7 // 256 * 256
+    deals = (early, rest - early)
 
     def body(near_ref, far_ref, *refs):
         count = len(firsts)
@@ -439,7 +474,8 @@
     second, live = load_second(w_gate, w_up, half, 2 * CHUNK, 5 * CHUNK // 2, requests, place)
     near = pack(plane, gain, live)
     far = swap(near, "core", 1)
-    kept, sent = block(near, far, (first, second), w_gate, w_up, w_down, half)
+    third = load_third(w_gate, w_up, near, half, 9 * CHUNK // 2, CHUNK // 2)
+    kept, sent = block(near, far, (first, second, third), w_gate, w_up, w_down, half)
     plane = (kept + swap(sent, "core", 1).astype(jnp.float32)).astype(jnp.bfloat16)
     pieces = jnp.split(plane, lax.axis_size(square), axis=0)
     column = pieces[0].astype(jnp.float32)

time: 47.2 us -> 49 us (1.038)
  Pallas kernels: 18.6 us -> 21.8 us
  waiting for transfers between devices: 10.8 us -> 9.05 us
    ppermute x14, waiting for transfers between devices: 10.8 us -> 9.05 us  [swap(): lax.ppermute(value, axes, [(place, place ^ offset) for place in places])]
    pallas_call x1, Pallas kernels: 10.7 us -> 12.4 us  [block(): pl.pallas_call(body, out_shape=(jax.ShapeDtypeStruct((rows, lines, LANES)...]
    pallas_call x0 -> x1, Pallas kernels: none -> 1.49 us  [load_third(): pl.pallas_call(functools.partial(load_third_kernel, half, row), out_shape...]
  transfers between devices with their start and end apart: 14 -> 14, of which waited for: 8 -> 7; matrix products, arithmetic and copies ran while one was open for 0% -> 0% of each run, Pallas kernels for 15% -> 17%
where the time goes in v11:
time: 49 us; the launch traced here: 48.9 us
  Pallas kernels  21.8 us (44%)
  starting transfers between devices  17.8 us (36%)
  waiting for transfers between devices  9.05 us (18%)
    ppermute x14, starting transfers between devices, swap(): lax.ppermute(value, axes, [(place, place ^ offset) for place in places])  17.8 us
    pallas_call x1, Pallas kernels, block(): pl.pallas_call(body, out_shape=(jax.ShapeDtypeStruct((rows, lines, LANES)...  12.4 us
    ppermute x14, waiting for transfers between devices, swap(): lax.ppermute(value, axes, [(place, place ^ offset) for place in places])  9.05 us
    pallas_call x1, Pallas kernels, load_second(): pl.pallas_call(functools.partial(load_second_kernel, half, row, place), o...  3.74 us
    pallas_call x1, Pallas kernels, load_first(): pl.pallas_call(functools.partial(load_gain_kernel, half), out_shape=(pltp...  3.22 us
    pallas_call x1, Pallas kernels, load_third(): pl.pallas_call(functools.partial(load_third_kernel, half, row), out_shape...  1.49 us
  transfers between devices with their start and end apart: 14, of which 7 were waited for; matrix products, arithmetic and copies ran while one was open for 0% of the time, Pallas kernels for 17%

profile of v11, /device:TPU:0, one launch (start us, length us, event | category | flops | bytes accessed | tf_op | source)
XLA Modules:
  0.0 48.9 jit_solution(12802174177222579773)
XLA Ops:
  0.0 5.0 %collective-permute-start.1 = (bf16[1,8192]{1,0:T(2,128)(2,1)}, bf16[1,8192]{1,0:T(2,128)(2,1)S(1)}, u32[]{:S(2)}, u32[]{:S(2)}) collective-permute-start(bf16[1,8192]{1,0:T(2,128)(2,1)} %refs_0_.1), channel_id=1, source_target_pairs={{0,12},{4,8},{8,4},{12,0},{1,13},{5,9},{9,5},{13,1},{2,14},{6,10},... | collective-permute-start | bytes 49160 | tf_op jit(solution)/shard_map/ppermute | solution.py:448
  5.0 0.0 collective-permute-start
  5.1 0.6 %collective-permute-start.2 = (bf16[1,8192]{1,0:T(2,128)(2,1)}, bf16[1,8192]{1,0:T(2,128)(2,1)S(1)}, u32[]{:S(2)}, u32[]{:S(2)}) collective-permute-start(bf16[1,8192]{1,0:T(2,128)(2,1)} %refs_0_.1), channel_id=1, source_target_pairs={{0,4},{4,0},{8,12},{12,8},{1,5},{5,1},{9,13},{13,9},{2,6},{6,2},{1... | collective-permute-start | bytes 49160 | tf_op jit(solution)/shard_map/ppermute | solution.py:448
  5.6 0.0 copy-start
  5.6 3.2 %load_first.1 = (bf16[2048,1792]{1,0:T(8,128)(2,1)S(1)}, bf16[64,128]{1,0:T(8,128)(2,1)S(1)}) custom-call(bf16[8192,1792]{1,0:T(8,128)(2,1)} %refs_3_.1, bf16[8192,1792]{1,0:T(8,128)(2,1)} %refs_4_.1, bf16[64,128]{1,0:T(8,128)(2,1)} %bitcast.1), custom_call_target="tpu_custom_call" | custom-call | bytes 7340032 | tf_op jit(solution)/shard_map/load_first/pallas_call | solution.py:110
  8.8 0.0 collective-permute-done.1.refs_2_
  8.9 1.2 %collective-permute-done.refs_1_ = bf16[1,8192]{1,0:T(2,128)(2,1)S(1)} collective-permute-done((bf16[1,8192]{1,0:T(2,128)(2,1)}, bf16[1,8192]{1,0:T(2,128)(2,1)S(1)}, u32[]{:S(2)}, u32[]{:S(2)}) %collective-permute-start) | collective-permute-done | bytes 16416 | tf_op jit(solution)/shard_map/ppermute | solution.py:448
  10.1 0.0 collective-permute-done.2.refs_3_
  10.1 0.0 copy-done
  10.1 0.1 stack.1.refs_0_
  10.2 2.5 %collective-permute-start.5 = (bf16[4,64,128]{2,1,0:T(8,128)(2,1)S(1)}, bf16[4,64,128]{2,1,0:T(8,128)(2,1)S(1)}, u32[]{:S(2)}, u32[]{:S(2)}) collective-permute-start(bf16[4,64,128]{2,1,0:T(8,128)(2,1)S(1)} %stack.1.refs_0_), channel_id=1, source_target_pairs={{0,18},{2,16},{16,2},{18,0},{1,19},{3,17},{17,3},{19,1},{4,22},{6,... | collective-permute-start | bytes 196616 | tf_op jit(solution)/shard_map/ppermute | solution.py:448
  12.7 0.5 %collective-permute-start.4 = (bf16[4,64,128]{2,1,0:T(8,128)(2,1)S(1)}, bf16[4,64,128]{2,1,0:T(8,128)(2,1)S(1)}, u32[]{:S(2)}, u32[]{:S(2)}) collective-permute-start(bf16[4,64,128]{2,1,0:T(8,128)(2,1)S(1)} %stack.1.refs_0_), channel_id=1, source_target_pairs={{0,16},{2,18},{16,0},{18,2},{1,17},{3,19},{17,1},{19,3},{4,20},{6,... | collective-permute-start | bytes 196616 | tf_op jit(solution)/shard_map/ppermute | solution.py:448
  13.2 0.5 %collective-permute-start.3 = (bf16[4,64,128]{2,1,0:T(8,128)(2,1)S(1)}, bf16[4,64,128]{2,1,0:T(8,128)(2,1)S(1)}, u32[]{:S(2)}, u32[]{:S(2)}) collective-permute-start(bf16[4,64,128]{2,1,0:T(8,128)(2,1)S(1)} %stack.1.refs_0_), channel_id=1, source_target_pairs={{0,2},{2,0},{16,18},{18,16},{1,3},{3,1},{17,19},{19,17},{4,6},{6,4... | collective-permute-start | bytes 196616 | tf_op jit(solution)/shard_map/ppermute | solution.py:448
  13.7 3.7 %load_second.1 = (bf16[2560,1792]{1,0:T(8,128)(2,1)S(1)}, f32[8,128]{1,0:T(8,128)S(1)}) custom-call(s32[8]{0:T(128)} %lengths.1, s32[8]{0:T(128)} %hit_lengths.1, s32[8]{0:T(128)} %start_positions.1, bf16[8192,1792]{1,0:T(8,128)(2,1)} %refs_3_.1, bf16[8192,1792]{1,0:T(8,128)(2,1)} %refs_4_.1), custom_call_target="tpu_custom_call" | custom-call | bytes 9175040 | tf_op jit(solution)/shard_map/load_second/pallas_call | solution.py:169
  17.5 0.0 collective-permute-done.5.refs_3_
  17.5 0.0 collective-permute-done.4.refs_2_
  17.5 0.0 collective-permute-done.3.refs_1_
  17.5 0.2 pack.1.near_ref
  17.7 0.1 collective-permute-start.6
  17.8 1.5 %load_third.1.refs_2_ = bf16[512,1792]{1,0:T(8,128)(2,1)S(1)} custom-call(bf16[8192,1792]{1,0:T(8,128)(2,1)} %refs_3_.1, bf16[8192,1792]{1,0:T(8,128)(2,1)} %refs_4_.1, bf16[16,8192]{1,0:T(8,128)(2,1)S(1)} %pack.1.near_ref), custom_call_target="tpu_custom_call" | custom-call | bytes 1835008 | tf_op jit(solution)/shard_map/load_third/pallas_call | solution.py:204
  19.3 0.0 collective-permute-done.6.far_ref
  19.3 12.4 %block.1 = (f32[16,64,128]{2,1,0:T(8,128)S(1)}, bf16[16,64,128]{2,1,0:T(8,128)(2,1)S(1)}) custom-call(bf16[16,8192]{1,0:T(8,128)(2,1)S(1)} %pack.1.near_ref, bf16[16,8192]{1,0:T(8,128)(2,1)S(1)} %collective-permute-done.6.far_ref, bf16[2048,1792]{1,0:T(8,128)(2,1)S(1)} %get-tuple-element.13.refs_0_, bf16[2560,1792]{1,0:T(8,128)(2,1)S(1)} %get-tuple-element.14.refs_1_, ...), custom_call_target="tpu_custom_call" | custom-call | flops 1409286144 | bytes 25690112 | tf_op jit(solution)/shard_map/block/pallas_call | solution.py:387
  31.7 0.5 %collective-permute-start.7 = (bf16[16,64,128]{2,1,0:T(8,128)(2,1)S(1)}, bf16[16,64,128]{2,1,0:T(8,128)(2,1)S(1)}, u32[]{:S(2)}, u32[]{:S(2)}) collective-permute-start(bf16[16,64,128]{2,1,0:T(8,128)(2,1)S(1)} %get-tuple-element.16), channel_id=1, source_target_pairs={{0,1},{1,0},{2,3},{3,2},{4,5},{5,4},{6,7},{7,6},{8,9},{9,8},{10,11... | collective-permute-start | bytes 786440 | tf_op jit(solution)/shard_map/ppermute | solution.py:448
  32.3 1.2 %collective-permute-done.7 = bf16[16,64,128]{2,1,0:T(8,128)(2,1)S(1)} collective-permute-done((bf16[16,64,128]{2,1,0:T(8,128)(2,1)S(1)}, bf16[16,64,128]{2,1,0:T(8,128)(2,1)S(1)}, u32[]{:S(2)}, u32[]{:S(2)}) %collective-permute-start.7) | collective-permute-done | bytes 262176 | tf_op jit(solution)/shard_map/ppermute | solution.py:448
  33.4 0.1 add_convert_fusion
  33.5 2.5 %collective-permute-start.8 = (bf16[4,64,128]{2,1,0:T(8,128)(2,1)S(1)}, bf16[4,64,128]{2,1,0:T(8,128)(2,1)S(1)}, u32[]{:S(2)}, u32[]{:S(2)}) collective-permute-start(bf16[4,64,128]{2,1,0:T(8,128)(2,1)S(1)} %get-tuple-element.17), channel_id=1, source_target_pairs={{0,18},{2,16},{16,2},{18,0},{1,19},{3,17},{17,3},{19,1},{4,22},{6,... | collective-permute-start | bytes 196616 | tf_op jit(solution)/shard_map/ppermute | solution.py:448
  36.0 0.5 %collective-permute-start.10 = (bf16[4,64,128]{2,1,0:T(8,128)(2,1)S(1)}, bf16[4,64,128]{2,1,0:T(8,128)(2,1)S(1)}, u32[]{:S(2)}, u32[]{:S(2)}) collective-permute-start(bf16[4,64,128]{2,1,0:T(8,128)(2,1)S(1)} %get-tuple-element.18), channel_id=1, source_target_pairs={{0,2},{2,0},{16,18},{18,16},{1,3},{3,1},{17,19},{19,17},{4,6},{6,4... | collective-permute-start | bytes 196616 | tf_op jit(solution)/shard_map/ppermute | solution.py:448
  36.6 0.5 %collective-permute-start.9 = (bf16[4,64,128]{2,1,0:T(8,128)(2,1)S(1)}, bf16[4,64,128]{2,1,0:T(8,128)(2,1)S(1)}, u32[]{:S(2)}, u32[]{:S(2)}) collective-permute-start(bf16[4,64,128]{2,1,0:T(8,128)(2,1)S(1)} %get-tuple-element.19), channel_id=1, source_target_pairs={{0,16},{2,18},{16,0},{18,2},{1,17},{3,19},{17,1},{19,3},{4,20},{6,... | collective-permute-start | bytes 196616 | tf_op jit(solution)/shard_map/ppermute | solution.py:448
  37.1 2.0 %collective-permute-done.8 = bf16[4,64,128]{2,1,0:T(8,128)(2,1)S(1)} collective-permute-done((bf16[4,64,128]{2,1,0:T(8,128)(2,1)S(1)}, bf16[4,64,128]{2,1,0:T(8,128)(2,1)S(1)}, u32[]{:S(2)}, u32[]{:S(2)}) %collective-permute-start.8) | collective-permute-done | bytes 65568 | tf_op jit(solution)/shard_map/ppermute | solution.py:448
  39.1 1.2 %collective-permute-done.10 = bf16[4,64,128]{2,1,0:T(8,128)(2,1)S(1)} collective-permute-done((bf16[4,64,128]{2,1,0:T(8,128)(2,1)S(1)}, bf16[4,64,128]{2,1,0:T(8,128)(2,1)S(1)}, u32[]{:S(2)}, u32[]{:S(2)}) %collective-permute-start.10) | collective-permute-done | bytes 65568 | tf_op jit(solution)/shard_map/ppermute | solution.py:448
  40.3 0.5 %collective-permute-done.9 = bf16[4,64,128]{2,1,0:T(8,128)(2,1)S(1)} collective-permute-done((bf16[4,64,128]{2,1,0:T(8,128)(2,1)S(1)}, bf16[4,64,128]{2,1,0:T(8,128)(2,1)S(1)}, u32[]{:S(2)}, u32[]{:S(2)}) %collective-permute-start.9) | collective-permute-done | bytes 65568 | tf_op jit(solution)/shard_map/ppermute | solution.py:448
  40.9 2.7 %collective-permute-start.13 = (bf16[1,64,128]{2,1,0:T(8,128)(2,1)S(1)}, bf16[1,64,128]{2,1,0:T(8,128)(2,1)S(1)}, u32[]{:S(2)}, u32[]{:S(2)}) collective-permute-start(bf16[1,64,128]{2,1,0:T(8,128)(2,1)S(1)} %get-tuple-element.20), channel_id=1, source_target_pairs={{0,12},{4,8},{8,4},{12,0},{1,13},{5,9},{9,5},{13,1},{2,14},{6,10},... | collective-permute-start | bytes 49160 | tf_op jit(solution)/shard_map/ppermute | solution.py:448
  43.6 0.0 collective-permute-start.12
  43.6 1.8 %collective-permute-start.11 = (bf16[1,64,128]{2,1,0:T(8,128)(2,1)S(1)}, bf16[1,64,128]{2,1,0:T(8,128)(2,1)S(1)}, u32[]{:S(2)}, u32[]{:S(2)}) collective-permute-start(bf16[1,64,128]{2,1,0:T(8,128)(2,1)S(1)} %get-tuple-element.22), channel_id=1, source_target_pairs={{0,4},{4,0},{8,12},{12,8},{1,5},{5,1},{9,13},{13,9},{2,6},{6,2},{1... | collective-permute-start | bytes 49160 | tf_op jit(solution)/shard_map/ppermute | solution.py:448
  45.4 1.1 %collective-permute-done.13.refs_3_ = bf16[1,64,128]{2,1,0:T(8,128)(2,1)S(1)} collective-permute-done((bf16[1,64,128]{2,1,0:T(8,128)(2,1)S(1)}, bf16[1,64,128]{2,1,0:T(8,128)(2,1)S(1)}, u32[]{:S(2)}, u32[]{:S(2)}) %collective-permute-start.13) | collective-permute-done | bytes 16416 | tf_op jit(solution)/shard_map/ppermute | solution.py:448
  46.5 1.7 %collective-permute-done.12.refs_2_ = bf16[1,64,128]{2,1,0:T(8,128)(2,1)S(1)} collective-permute-done((bf16[1,64,128]{2,1,0:T(8,128)(2,1)S(1)}, bf16[1,64,128]{2,1,0:T(8,128)(2,1)S(1)}, u32[]{:S(2)}, u32[]{:S(2)}) %collective-permute-start.12) | collective-permute-done | bytes 16416 | tf_op jit(solution)/shard_map/ppermute | solution.py:448
  48.2 0.0 collective-permute-done.11.refs_1_
  48.2 0.7 %finish.1 = bf16[1,8192]{1,0:T(2,128)(2,1)} custom-call(bf16[1,64,128]{2,1,0:T(8,128)(2,1)S(1)} %get-tuple-element.23.refs_0_, bf16[1,64,128]{2,1,0:T(8,128)(2,1)S(1)} %collective-permute-done.11.refs_1_, bf16[1,64,128]{2,1,0:T(8,128)(2,1)S(1)} %collective-permute-done.12.refs_2_, bf16[1,64,128]{2,1,0:T(8,128)(2,1)S(1)} %collective-permute-done.13.refs_3_, ...), custom_call_target="tpu_custom_call" | custom-call | tf_op jit(solution)/shard_map/finish/pallas_call | solution.py:436
  (3 shorter events, 0.1 us)
Async XLA Ops:
  0.0 8.9 %collective-permute-start.1 = (bf16[1,8192]{1,0:T(2,128)(2,1)}, bf16[1,8192]{1,0:T(2,128)(2,1)S(1)}, u32[]{:S(2)}, u32[]{:S(2)}) collective-permute-start(bf16[1,8192]{1,0:T(2,128)(2,1)} %refs_0_.1), channel_id=1, source_target_pairs={{0,12},{4,8},{8,4},{12,0},{1,13},{5,9},{9,5},{13,1},{2,14},{6,10},... | collective-permute-start | bytes 49160 | tf_op jit(solution)/shard_map/ppermute | solution.py:448
  5.0 5.0 %collective-permute-start = (bf16[1,8192]{1,0:T(2,128)(2,1)}, bf16[1,8192]{1,0:T(2,128)(2,1)S(1)}, u32[]{:S(2)}, u32[]{:S(2)}) collective-permute-start(bf16[1,8192]{1,0:T(2,128)(2,1)} %refs_0_.1), channel_id=1, source_target_pairs={{0,8},{4,12},{8,0},{12,4},{1,9},{5,13},{9,1},{13,5},{2,10},{6,14},... | collective-permute-start | bytes 49160 | tf_op jit(solution)/shard_map/ppermute | solution.py:448
  5.1 5.0 %collective-permute-start.2 = (bf16[1,8192]{1,0:T(2,128)(2,1)}, bf16[1,8192]{1,0:T(2,128)(2,1)S(1)}, u32[]{:S(2)}, u32[]{:S(2)}) collective-permute-start(bf16[1,8192]{1,0:T(2,128)(2,1)} %refs_0_.1), channel_id=1, source_target_pairs={{0,4},{4,0},{8,12},{12,8},{1,5},{5,1},{9,13},{13,9},{2,6},{6,2},{1... | collective-permute-start | bytes 49160 | tf_op jit(solution)/shard_map/ppermute | solution.py:448
  5.6 4.5 %copy-start = (bf16[1,8192]{1,0:T(2,128)(2,1)S(1)}, bf16[1,8192]{1,0:T(2,128)(2,1)}, u32[]{:S(2)}) copy-start(bf16[1,8192]{1,0:T(2,128)(2,1)} %refs_0_.1) | copy-start | bytes 49156
  10.2 7.3 %collective-permute-start.5 = (bf16[4,64,128]{2,1,0:T(8,128)(2,1)S(1)}, bf16[4,64,128]{2,1,0:T(8,128)(2,1)S(1)}, u32[]{:S(2)}, u32[]{:S(2)}) collective-permute-start(bf16[4,64,128]{2,1,0:T(8,128)(2,1)S(1)} %stack.1.refs_0_), channel_id=1, source_target_pairs={{0,18},{2,16},{16,2},{18,0},{1,19},{3,17},{17,3},{19,1},{4,22},{6,... | collective-permute-start | bytes 196616 | tf_op jit(solution)/shard_map/ppermute | solution.py:448
  12.7 4.8 %collective-permute-start.4 = (bf16[4,64,128]{2,1,0:T(8,128)(2,1)S(1)}, bf16[4,64,128]{2,1,0:T(8,128)(2,1)S(1)}, u32[]{:S(2)}, u32[]{:S(2)}) collective-permute-start(bf16[4,64,128]{2,1,0:T(8,128)(2,1)S(1)} %stack.1.refs_0_), channel_id=1, source_target_pairs={{0,16},{2,18},{16,0},{18,2},{1,17},{3,19},{17,1},{19,3},{4,20},{6,... | collective-permute-start | bytes 196616 | tf_op jit(solution)/shard_map/ppermute | solution.py:448
  13.2 4.3 %collective-permute-start.3 = (bf16[4,64,128]{2,1,0:T(8,128)(2,1)S(1)}, bf16[4,64,128]{2,1,0:T(8,128)(2,1)S(1)}, u32[]{:S(2)}, u32[]{:S(2)}) collective-permute-start(bf16[4,64,128]{2,1,0:T(8,128)(2,1)S(1)} %stack.1.refs_0_), channel_id=1, source_target_pairs={{0,2},{2,0},{16,18},{18,16},{1,3},{3,1},{17,19},{19,17},{4,6},{6,4... | collective-permute-start | bytes 196616 | tf_op jit(solution)/shard_map/ppermute | solution.py:448
  17.7 1.6 %collective-permute-start.6 = (bf16[16,8192]{1,0:T(8,128)(2,1)S(1)}, bf16[16,8192]{1,0:T(8,128)(2,1)S(1)}, u32[]{:S(2)}, u32[]{:S(2)}) collective-permute-start(bf16[16,8192]{1,0:T(8,128)(2,1)S(1)} %pack.1.near_ref), channel_id=1, source_target_pairs={{0,1},{1,0},{2,3},{3,2},{4,5},{5,4},{6,7},{7,6},{8,9},{9,8},{10,11... | collective-permute-start | bytes 786440 | tf_op jit(solution)/shard_map/ppermute | solution.py:448
  31.7 1.7 %collective-permute-start.7 = (bf16[16,64,128]{2,1,0:T(8,128)(2,1)S(1)}, bf16[16,64,128]{2,1,0:T(8,128)(2,1)S(1)}, u32[]{:S(2)}, u32[]{:S(2)}) collective-permute-start(bf16[16,64,128]{2,1,0:T(8,128)(2,1)S(1)} %get-tuple-element.16), channel_id=1, source_target_pairs={{0,1},{1,0},{2,3},{3,2},{4,5},{5,4},{6,7},{7,6},{8,9},{9,8},{10,11... | collective-permute-start | bytes 786440 | tf_op jit(solution)/shard_map/ppermute | solution.py:448
  33.5 5.6 %collective-permute-start.8 = (bf16[4,64,128]{2,1,0:T(8,128)(2,1)S(1)}, bf16[4,64,128]{2,1,0:T(8,128)(2,1)S(1)}, u32[]{:S(2)}, u32[]{:S(2)}) collective-permute-start(bf16[4,64,128]{2,1,0:T(8,128)(2,1)S(1)} %get-tuple-element.17), channel_id=1, source_target_pairs={{0,18},{2,16},{16,2},{18,0},{1,19},{3,17},{17,3},{19,1},{4,22},{6,... | collective-permute-start | bytes 196616 | tf_op jit(solution)/shard_map/ppermute | solution.py:448
  36.0 4.3 %collective-permute-start.10 = (bf16[4,64,128]{2,1,0:T(8,128)(2,1)S(1)}, bf16[4,64,128]{2,1,0:T(8,128)(2,1)S(1)}, u32[]{:S(2)}, u32[]{:S(2)}) collective-permute-start(bf16[4,64,128]{2,1,0:T(8,128)(2,1)S(1)} %get-tuple-element.18), channel_id=1, source_target_pairs={{0,2},{2,0},{16,18},{18,16},{1,3},{3,1},{17,19},{19,17},{4,6},{6,4... | collective-permute-start | bytes 196616 | tf_op jit(solution)/shard_map/ppermute | solution.py:448
  36.6 4.3 %collective-permute-start.9 = (bf16[4,64,128]{2,1,0:T(8,128)(2,1)S(1)}, bf16[4,64,128]{2,1,0:T(8,128)(2,1)S(1)}, u32[]{:S(2)}, u32[]{:S(2)}) collective-permute-start(bf16[4,64,128]{2,1,0:T(8,128)(2,1)S(1)} %get-tuple-element.19), channel_id=1, source_target_pairs={{0,16},{2,18},{16,0},{18,2},{1,17},{3,19},{17,1},{19,3},{4,20},{6,... | collective-permute-start | bytes 196616 | tf_op jit(solution)/shard_map/ppermute | solution.py:448
  40.9 5.6 %collective-permute-start.13 = (bf16[1,64,128]{2,1,0:T(8,128)(2,1)S(1)}, bf16[1,64,128]{2,1,0:T(8,128)(2,1)S(1)}, u32[]{:S(2)}, u32[]{:S(2)}) collective-permute-start(bf16[1,64,128]{2,1,0:T(8,128)(2,1)S(1)} %get-tuple-element.20), channel_id=1, source_target_pairs={{0,12},{4,8},{8,4},{12,0},{1,13},{5,9},{9,5},{13,1},{2,14},{6,10},... | collective-permute-start | bytes 49160 | tf_op jit(solution)/shard_map/ppermute | solution.py:448
  43.6 4.6 %collective-permute-start.12 = (bf16[1,64,128]{2,1,0:T(8,128)(2,1)S(1)}, bf16[1,64,128]{2,1,0:T(8,128)(2,1)S(1)}, u32[]{:S(2)}, u32[]{:S(2)}) collective-permute-start(bf16[1,64,128]{2,1,0:T(8,128)(2,1)S(1)} %get-tuple-element.21), channel_id=1, source_target_pairs={{0,8},{4,12},{8,0},{12,4},{1,9},{5,13},{9,1},{13,5},{2,10},{6,14},... | collective-permute-start | bytes 49160 | tf_op jit(solution)/shard_map/ppermute | solution.py:448
  43.6 4.6 %collective-permute-start.11 = (bf16[1,64,128]{2,1,0:T(8,128)(2,1)S(1)}, bf16[1,64,128]{2,1,0:T(8,128)(2,1)S(1)}, u32[]{:S(2)}, u32[]{:S(2)}) collective-permute-start(bf16[1,64,128]{2,1,0:T(8,128)(2,1)S(1)} %get-tuple-element.22), channel_id=1, source_target_pairs={{0,4},{4,0},{8,12},{12,8},{1,5},{5,1},{9,13},{13,9},{2,6},{6,2},{1... | collective-permute-start | bytes 49160 | tf_op jit(solution)/shard_map/ppermute | solution.py:448

commit v12 on v11

--- a/solution.py
+++ b/solution.py
@@ -297,7 +297,7 @@
             [
                 pltpu.make_async_copy(
                     down_hbm.at[pl.ds(own, half), pl.ds(at, chunk)],
-                    down_ref.at[:, pl.ds(at, chunk)],
+                    down_ref.at[pl.ds(0, half), pl.ds(at, chunk)],
                     down_sems.at[step],
                 )
             ]
@@ -330,18 +330,21 @@
                 start()
 
     start()
+    padded = down_ref.shape[0]
+    if padded > half:
+        down_ref[half:] = jnp.zeros((padded - half, depth), down_ref.dtype)
+        hidden_ref[:, half:] = jnp.zeros((rows, padded - half), hidden_ref.dtype)
     rows_ref[: rows // 2] = near_ref[...]
     rows_ref[rows // 2 :] = far_ref[...]
     at = 0
     for ref in first_refs:
         multiply(at, ref.shape[0], ref, 0, False)
-        if at == 0:
-            start()
+        start()
         at += ref.shape[0]
     row = 0
     for step, deal in enumerate(deals):
         wait(step)
-        multiply(at, deal, rest_ref, row, True)
+        multiply(at, deal, rest_ref, row, step > 0)
         start()
         at += deal
         row += deal
@@ -349,7 +352,7 @@
         start()
     gate_out = product_ref[:, :half]
     up_out = product_ref[:, half:]
-    hidden_ref[...] = (gate_out / (1.0 + jnp.exp(-gate_out)) * up_out).astype(jnp.bfloat16)
+    hidden_ref[:, :half] = (gate_out / (1.0 + jnp.exp(-gate_out)) * up_out).astype(jnp.bfloat16)
     zero = jnp.minimum(lax.axis_index("core"), 0)
     for step in range(depth // chunk):
         wait(pairs + step)
@@ -377,8 +380,8 @@
     rows, depth = near.shape
     lines = depth // LANES
     rest = depth - sum(first.shape[0] for first in firsts)
-    early = rest * 3 // 7 // 256 * 256
-    deals = (early, rest - early)
+    deals = (CHUNK, rest - CHUNK)
+    padded = -(-half // 256) * 256
 
     def body(near_ref, far_ref, *refs):
         count = len(firsts)
@@ -396,14 +399,14 @@
             pltpu.VMEM((2 * rows * (lines + 1), LANES), jnp.float32),
             pltpu.VMEM((2 * rows, depth), jnp.bfloat16),
             pltpu.VMEM((2 * rows, 2 * half), jnp.float32),
-            pltpu.VMEM((2 * rows, half), jnp.bfloat16),
+            pltpu.VMEM((2 * rows, padded), jnp.bfloat16),
             pltpu.VMEM((rest, 2 * half), jnp.bfloat16),
-            pltpu.VMEM((half, depth), jnp.bfloat16),
+            pltpu.VMEM((padded, depth), jnp.bfloat16),
             pltpu.SemaphoreType.DMA((2, 2)),
             pltpu.SemaphoreType.DMA((depth // (2 * CHUNK),)),
         ],
         compiler_params=pltpu.CompilerParams(
-            vmem_limit_bytes=(rest * 2 + depth) * half * 2 + (6 << 20)
+            vmem_limit_bytes=(rest * 2 * half + depth * padded) * 2 + (6 << 20)
         ),
         cost_estimate=pl.CostEstimate(
             flops=12 * rows * depth * half,

time: 49 us -> 49.1 us (level)
  no operation moved by 1% of the time
where the time goes in v12:
time: 49.1 us; the launch traced here: 49 us
  Pallas kernels  21.9 us (45%)
  starting transfers between devices  17.8 us (36%)
  waiting for transfers between devices  9.05 us (18%)
    ppermute x14, starting transfers between devices, swap(): lax.ppermute(value, axes, [(place, place ^ offset) for place in places])  17.8 us
    pallas_call x1, Pallas kernels, block(): pl.pallas_call(body, out_shape=(jax.ShapeDtypeStruct((rows, lines, LANES)...  12.5 us
    ppermute x14, waiting for transfers between devices, swap(): lax.ppermute(value, axes, [(place, place ^ offset) for place in places])  9.05 us
    pallas_call x1, Pallas kernels, load_second(): pl.pallas_call(functools.partial(load_second_kernel, half, row, place), o...  3.74 us
    pallas_call x1, Pallas kernels, load_first(): pl.pallas_call(functools.partial(load_gain_kernel, half), out_shape=(pltp...  3.22 us
    pallas_call x1, Pallas kernels, load_third(): pl.pallas_call(functools.partial(load_third_kernel, half, row), out_shape...  1.49 us
  transfers between devices with their start and end apart: 14, of which 7 were waited for; matrix products, arithmetic and copies ran while one was open for 0% of the time, Pallas kernels for 17%

profile of v12, /device:TPU:0, one launch (start us, length us, event | category | flops | bytes accessed | tf_op | source)
XLA Modules:
  0.0 49.0 jit_solution(18269680987000003529)
XLA Ops:
  0.0 5.0 %collective-permute-start.1 = (bf16[1,8192]{1,0:T(2,128)(2,1)}, bf16[1,8192]{1,0:T(2,128)(2,1)S(1)}, u32[]{:S(2)}, u32[]{:S(2)}) collective-permute-start(bf16[1,8192]{1,0:T(2,128)(2,1)} %refs_0_.1), channel_id=1, source_target_pairs={{0,12},{4,8},{8,4},{12,0},{1,13},{5,9},{9,5},{13,1},{2,14},{6,10},... | collective-permute-start | bytes 49160 | tf_op jit(solution)/shard_map/ppermute | solution.py:451
  5.0 0.0 collective-permute-start
  5.1 0.6 %collective-permute-start.2 = (bf16[1,8192]{1,0:T(2,128)(2,1)}, bf16[1,8192]{1,0:T(2,128)(2,1)S(1)}, u32[]{:S(2)}, u32[]{:S(2)}) collective-permute-start(bf16[1,8192]{1,0:T(2,128)(2,1)} %refs_0_.1), channel_id=1, source_target_pairs={{0,4},{4,0},{8,12},{12,8},{1,5},{5,1},{9,13},{13,9},{2,6},{6,2},{1... | collective-permute-start | bytes 49160 | tf_op jit(solution)/shard_map/ppermute | solution.py:451
  5.6 0.0 copy-start
  5.6 3.2 %load_first.1 = (bf16[2048,1792]{1,0:T(8,128)(2,1)S(1)}, bf16[64,128]{1,0:T(8,128)(2,1)S(1)}) custom-call(bf16[8192,1792]{1,0:T(8,128)(2,1)} %refs_3_.1, bf16[8192,1792]{1,0:T(8,128)(2,1)} %refs_4_.1, bf16[64,128]{1,0:T(8,128)(2,1)} %bitcast.1), custom_call_target="tpu_custom_call" | custom-call | bytes 7340032 | tf_op jit(solution)/shard_map/load_first/pallas_call | solution.py:110
  8.8 0.0 collective-permute-done.1.refs_2_
  8.9 1.2 %collective-permute-done.refs_1_ = bf16[1,8192]{1,0:T(2,128)(2,1)S(1)} collective-permute-done((bf16[1,8192]{1,0:T(2,128)(2,1)}, bf16[1,8192]{1,0:T(2,128)(2,1)S(1)}, u32[]{:S(2)}, u32[]{:S(2)}) %collective-permute-start) | collective-permute-done | bytes 16416 | tf_op jit(solution)/shard_map/ppermute | solution.py:451
  10.1 0.0 collective-permute-done.2.refs_3_
  10.1 0.0 copy-done
  10.1 0.1 stack.1.refs_0_
  10.2 2.5 %collective-permute-start.5 = (bf16[4,64,128]{2,1,0:T(8,128)(2,1)S(1)}, bf16[4,64,128]{2,1,0:T(8,128)(2,1)S(1)}, u32[]{:S(2)}, u32[]{:S(2)}) collective-permute-start(bf16[4,64,128]{2,1,0:T(8,128)(2,1)S(1)} %stack.1.refs_0_), channel_id=1, source_target_pairs={{0,18},{2,16},{16,2},{18,0},{1,19},{3,17},{17,3},{19,1},{4,22},{6,... | collective-permute-start | bytes 196616 | tf_op jit(solution)/shard_map/ppermute | solution.py:451
  12.7 0.5 %collective-permute-start.4 = (bf16[4,64,128]{2,1,0:T(8,128)(2,1)S(1)}, bf16[4,64,128]{2,1,0:T(8,128)(2,1)S(1)}, u32[]{:S(2)}, u32[]{:S(2)}) collective-permute-start(bf16[4,64,128]{2,1,0:T(8,128)(2,1)S(1)} %stack.1.refs_0_), channel_id=1, source_target_pairs={{0,16},{2,18},{16,0},{18,2},{1,17},{3,19},{17,1},{19,3},{4,20},{6,... | collective-permute-start | bytes 196616 | tf_op jit(solution)/shard_map/ppermute | solution.py:451
  13.2 0.5 %collective-permute-start.3 = (bf16[4,64,128]{2,1,0:T(8,128)(2,1)S(1)}, bf16[4,64,128]{2,1,0:T(8,128)(2,1)S(1)}, u32[]{:S(2)}, u32[]{:S(2)}) collective-permute-start(bf16[4,64,128]{2,1,0:T(8,128)(2,1)S(1)} %stack.1.refs_0_), channel_id=1, source_target_pairs={{0,2},{2,0},{16,18},{18,16},{1,3},{3,1},{17,19},{19,17},{4,6},{6,4... | collective-permute-start | bytes 196616 | tf_op jit(solution)/shard_map/ppermute | solution.py:451
  13.7 3.7 %load_second.1 = (bf16[2560,1792]{1,0:T(8,128)(2,1)S(1)}, f32[8,128]{1,0:T(8,128)S(1)}) custom-call(s32[8]{0:T(128)} %lengths.1, s32[8]{0:T(128)} %hit_lengths.1, s32[8]{0:T(128)} %start_positions.1, bf16[8192,1792]{1,0:T(8,128)(2,1)} %refs_3_.1, bf16[8192,1792]{1,0:T(8,128)(2,1)} %refs_4_.1), custom_call_target="tpu_custom_call" | custom-call | bytes 9175040 | tf_op jit(solution)/shard_map/load_second/pallas_call | solution.py:169
  17.5 0.0 collective-permute-done.5.refs_3_
  17.5 0.0 collective-permute-done.4.refs_2_
  17.5 0.0 collective-permute-done.3.refs_1_
  17.5 0.2 pack.1.near_ref
  17.7 0.1 collective-permute-start.6
  17.8 1.5 %load_third.1.refs_2_ = bf16[512,1792]{1,0:T(8,128)(2,1)S(1)} custom-call(bf16[8192,1792]{1,0:T(8,128)(2,1)} %refs_3_.1, bf16[8192,1792]{1,0:T(8,128)(2,1)} %refs_4_.1, bf16[16,8192]{1,0:T(8,128)(2,1)S(1)} %pack.1.near_ref), custom_call_target="tpu_custom_call" | custom-call | bytes 1835008 | tf_op jit(solution)/shard_map/load_third/pallas_call | solution.py:204
  19.3 0.0 collective-permute-done.6.far_ref
  19.3 12.5 %block.1 = (f32[16,64,128]{2,1,0:T(8,128)S(1)}, bf16[16,64,128]{2,1,0:T(8,128)(2,1)S(1)}) custom-call(bf16[16,8192]{1,0:T(8,128)(2,1)S(1)} %pack.1.near_ref, bf16[16,8192]{1,0:T(8,128)(2,1)S(1)} %collective-permute-done.6.far_ref, bf16[2048,1792]{1,0:T(8,128)(2,1)S(1)} %get-tuple-element.13.refs_0_, bf16[2560,1792]{1,0:T(8,128)(2,1)S(1)} %get-tuple-element.14.refs_1_, ...), custom_call_target="tpu_custom_call" | custom-call | flops 1409286144 | bytes 25690112 | tf_op jit(solution)/shard_map/block/pallas_call | solution.py:390
  31.8 0.5 %collective-permute-start.7 = (bf16[16,64,128]{2,1,0:T(8,128)(2,1)S(1)}, bf16[16,64,128]{2,1,0:T(8,128)(2,1)S(1)}, u32[]{:S(2)}, u32[]{:S(2)}) collective-permute-start(bf16[16,64,128]{2,1,0:T(8,128)(2,1)S(1)} %get-tuple-element.16), channel_id=1, source_target_pairs={{0,1},{1,0},{2,3},{3,2},{4,5},{5,4},{6,7},{7,6},{8,9},{9,8},{10,11... | collective-permute-start | bytes 786440 | tf_op jit(solution)/shard_map/ppermute | solution.py:451
  32.3 1.2 %collective-permute-done.7 = bf16[16,64,128]{2,1,0:T(8,128)(2,1)S(1)} collective-permute-done((bf16[16,64,128]{2,1,0:T(8,128)(2,1)S(1)}, bf16[16,64,128]{2,1,0:T(8,128)(2,1)S(1)}, u32[]{:S(2)}, u32[]{:S(2)}) %collective-permute-start.7) | collective-permute-done | bytes 262176 | tf_op jit(solution)/shard_map/ppermute | solution.py:451
  33.5 0.1 add_convert_fusion
  33.6 2.5 %collective-permute-start.8 = (bf16[4,64,128]{2,1,0:T(8,128)(2,1)S(1)}, bf16[4,64,128]{2,1,0:T(8,128)(2,1)S(1)}, u32[]{:S(2)}, u32[]{:S(2)}) collective-permute-start(bf16[4,64,128]{2,1,0:T(8,128)(2,1)S(1)} %get-tuple-element.17), channel_id=1, source_target_pairs={{0,18},{2,16},{16,2},{18,0},{1,19},{3,17},{17,3},{19,1},{4,22},{6,... | collective-permute-start | bytes 196616 | tf_op jit(solution)/shard_map/ppermute | solution.py:451
  36.1 0.5 %collective-permute-start.10 = (bf16[4,64,128]{2,1,0:T(8,128)(2,1)S(1)}, bf16[4,64,128]{2,1,0:T(8,128)(2,1)S(1)}, u32[]{:S(2)}, u32[]{:S(2)}) collective-permute-start(bf16[4,64,128]{2,1,0:T(8,128)(2,1)S(1)} %get-tuple-element.18), channel_id=1, source_target_pairs={{0,2},{2,0},{16,18},{18,16},{1,3},{3,1},{17,19},{19,17},{4,6},{6,4... | collective-permute-start | bytes 196616 | tf_op jit(solution)/shard_map/ppermute | solution.py:451
  36.7 0.5 %collective-permute-start.9 = (bf16[4,64,128]{2,1,0:T(8,128)(2,1)S(1)}, bf16[4,64,128]{2,1,0:T(8,128)(2,1)S(1)}, u32[]{:S(2)}, u32[]{:S(2)}) collective-permute-start(bf16[4,64,128]{2,1,0:T(8,128)(2,1)S(1)} %get-tuple-element.19), channel_id=1, source_target_pairs={{0,16},{2,18},{16,0},{18,2},{1,17},{3,19},{17,1},{19,3},{4,20},{6,... | collective-permute-start | bytes 196616 | tf_op jit(solution)/shard_map/ppermute | solution.py:451
  37.2 2.0 %collective-permute-done.8 = bf16[4,64,128]{2,1,0:T(8,128)(2,1)S(1)} collective-permute-done((bf16[4,64,128]{2,1,0:T(8,128)(2,1)S(1)}, bf16[4,64,128]{2,1,0:T(8,128)(2,1)S(1)}, u32[]{:S(2)}, u32[]{:S(2)}) %collective-permute-start.8) | collective-permute-done | bytes 65568 | tf_op jit(solution)/shard_map/ppermute | solution.py:451
  39.2 1.2 %collective-permute-done.10 = bf16[4,64,128]{2,1,0:T(8,128)(2,1)S(1)} collective-permute-done((bf16[4,64,128]{2,1,0:T(8,128)(2,1)S(1)}, bf16[4,64,128]{2,1,0:T(8,128)(2,1)S(1)}, u32[]{:S(2)}, u32[]{:S(2)}) %collective-permute-start.10) | collective-permute-done | bytes 65568 | tf_op jit(solution)/shard_map/ppermute | solution.py:451
  40.4 0.5 %collective-permute-done.9 = bf16[4,64,128]{2,1,0:T(8,128)(2,1)S(1)} collective-permute-done((bf16[4,64,128]{2,1,0:T(8,128)(2,1)S(1)}, bf16[4,64,128]{2,1,0:T(8,128)(2,1)S(1)}, u32[]{:S(2)}, u32[]{:S(2)}) %collective-permute-start.9) | collective-permute-done | bytes 65568 | tf_op jit(solution)/shard_map/ppermute | solution.py:451
  41.0 2.7 %collective-permute-start.13 = (bf16[1,64,128]{2,1,0:T(8,128)(2,1)S(1)}, bf16[1,64,128]{2,1,0:T(8,128)(2,1)S(1)}, u32[]{:S(2)}, u32[]{:S(2)}) collective-permute-start(bf16[1,64,128]{2,1,0:T(8,128)(2,1)S(1)} %get-tuple-element.20), channel_id=1, source_target_pairs={{0,12},{4,8},{8,4},{12,0},{1,13},{5,9},{9,5},{13,1},{2,14},{6,10},... | collective-permute-start | bytes 49160 | tf_op jit(solution)/shard_map/ppermute | solution.py:451
  43.7 0.0 collective-permute-start.12
  43.7 1.8 %collective-permute-start.11 = (bf16[1,64,128]{2,1,0:T(8,128)(2,1)S(1)}, bf16[1,64,128]{2,1,0:T(8,128)(2,1)S(1)}, u32[]{:S(2)}, u32[]{:S(2)}) collective-permute-start(bf16[1,64,128]{2,1,0:T(8,128)(2,1)S(1)} %get-tuple-element.22), channel_id=1, source_target_pairs={{0,4},{4,0},{8,12},{12,8},{1,5},{5,1},{9,13},{13,9},{2,6},{6,2},{1... | collective-permute-start | bytes 49160 | tf_op jit(solution)/shard_map/ppermute | solution.py:451
  45.4 1.1 %collective-permute-done.13.refs_3_ = bf16[1,64,128]{2,1,0:T(8,128)(2,1)S(1)} collective-permute-done((bf16[1,64,128]{2,1,0:T(8,128)(2,1)S(1)}, bf16[1,64,128]{2,1,0:T(8,128)(2,1)S(1)}, u32[]{:S(2)}, u32[]{:S(2)}) %collective-permute-start.13) | collective-permute-done | bytes 16416 | tf_op jit(solution)/shard_map/ppermute | solution.py:451
  46.6 1.7 %collective-permute-done.12.refs_2_ = bf16[1,64,128]{2,1,0:T(8,128)(2,1)S(1)} collective-permute-done((bf16[1,64,128]{2,1,0:T(8,128)(2,1)S(1)}, bf16[1,64,128]{2,1,0:T(8,128)(2,1)S(1)}, u32[]{:S(2)}, u32[]{:S(2)}) %collective-permute-start.12) | collective-permute-done | bytes 16416 | tf_op jit(solution)/shard_map/ppermute | solution.py:451
  48.3 0.0 collective-permute-done.11.refs_1_
  48.3 0.7 %finish.1 = bf16[1,8192]{1,0:T(2,128)(2,1)} custom-call(bf16[1,64,128]{2,1,0:T(8,128)(2,1)S(1)} %get-tuple-element.23.refs_0_, bf16[1,64,128]{2,1,0:T(8,128)(2,1)S(1)} %collective-permute-done.11.refs_1_, bf16[1,64,128]{2,1,0:T(8,128)(2,1)S(1)} %collective-permute-done.12.refs_2_, bf16[1,64,128]{2,1,0:T(8,128)(2,1)S(1)} %collective-permute-done.13.refs_3_, ...), custom_call_target="tpu_custom_call" | custom-call | tf_op jit(solution)/shard_map/finish/pallas_call | solution.py:439
  (3 shorter events, 0.1 us)
Async XLA Ops:
  0.0 8.9 %collective-permute-start.1 = (bf16[1,8192]{1,0:T(2,128)(2,1)}, bf16[1,8192]{1,0:T(2,128)(2,1)S(1)}, u32[]{:S(2)}, u32[]{:S(2)}) collective-permute-start(bf16[1,8192]{1,0:T(2,128)(2,1)} %refs_0_.1), channel_id=1, source_target_pairs={{0,12},{4,8},{8,4},{12,0},{1,13},{5,9},{9,5},{13,1},{2,14},{6,10},... | collective-permute-start | bytes 49160 | tf_op jit(solution)/shard_map/ppermute | solution.py:451
  5.0 5.0 %collective-permute-start = (bf16[1,8192]{1,0:T(2,128)(2,1)}, bf16[1,8192]{1,0:T(2,128)(2,1)S(1)}, u32[]{:S(2)}, u32[]{:S(2)}) collective-permute-start(bf16[1,8192]{1,0:T(2,128)(2,1)} %refs_0_.1), channel_id=1, source_target_pairs={{0,8},{4,12},{8,0},{12,4},{1,9},{5,13},{9,1},{13,5},{2,10},{6,14},... | collective-permute-start | bytes 49160 | tf_op jit(solution)/shard_map/ppermute | solution.py:451
  5.1 5.0 %collective-permute-start.2 = (bf16[1,8192]{1,0:T(2,128)(2,1)}, bf16[1,8192]{1,0:T(2,128)(2,1)S(1)}, u32[]{:S(2)}, u32[]{:S(2)}) collective-permute-start(bf16[1,8192]{1,0:T(2,128)(2,1)} %refs_0_.1), channel_id=1, source_target_pairs={{0,4},{4,0},{8,12},{12,8},{1,5},{5,1},{9,13},{13,9},{2,6},{6,2},{1... | collective-permute-start | bytes 49160 | tf_op jit(solution)/shard_map/ppermute | solution.py:451
  5.6 4.5 %copy-start = (bf16[1,8192]{1,0:T(2,128)(2,1)S(1)}, bf16[1,8192]{1,0:T(2,128)(2,1)}, u32[]{:S(2)}) copy-start(bf16[1,8192]{1,0:T(2,128)(2,1)} %refs_0_.1) | copy-start | bytes 49156
  10.2 7.3 %collective-permute-start.5 = (bf16[4,64,128]{2,1,0:T(8,128)(2,1)S(1)}, bf16[4,64,128]{2,1,0:T(8,128)(2,1)S(1)}, u32[]{:S(2)}, u32[]{:S(2)}) collective-permute-start(bf16[4,64,128]{2,1,0:T(8,128)(2,1)S(1)} %stack.1.refs_0_), channel_id=1, source_target_pairs={{0,18},{2,16},{16,2},{18,0},{1,19},{3,17},{17,3},{19,1},{4,22},{6,... | collective-permute-start | bytes 196616 | tf_op jit(solution)/shard_map/ppermute | solution.py:451
  12.7 4.8 %collective-permute-start.4 = (bf16[4,64,128]{2,1,0:T(8,128)(2,1)S(1)}, bf16[4,64,128]{2,1,0:T(8,128)(2,1)S(1)}, u32[]{:S(2)}, u32[]{:S(2)}) collective-permute-start(bf16[4,64,128]{2,1,0:T(8,128)(2,1)S(1)} %stack.1.refs_0_), channel_id=1, source_target_pairs={{0,16},{2,18},{16,0},{18,2},{1,17},{3,19},{17,1},{19,3},{4,20},{6,... | collective-permute-start | bytes 196616 | tf_op jit(solution)/shard_map/ppermute | solution.py:451
  13.2 4.3 %collective-permute-start.3 = (bf16[4,64,128]{2,1,0:T(8,128)(2,1)S(1)}, bf16[4,64,128]{2,1,0:T(8,128)(2,1)S(1)}, u32[]{:S(2)}, u32[]{:S(2)}) collective-permute-start(bf16[4,64,128]{2,1,0:T(8,128)(2,1)S(1)} %stack.1.refs_0_), channel_id=1, source_target_pairs={{0,2},{2,0},{16,18},{18,16},{1,3},{3,1},{17,19},{19,17},{4,6},{6,4... | collective-permute-start | bytes 196616 | tf_op jit(solution)/shard_map/ppermute | solution.py:451
  17.7 1.6 %collective-permute-start.6 = (bf16[16,8192]{1,0:T(8,128)(2,1)S(1)}, bf16[16,8192]{1,0:T(8,128)(2,1)S(1)}, u32[]{:S(2)}, u32[]{:S(2)}) collective-permute-start(bf16[16,8192]{1,0:T(8,128)(2,1)S(1)} %pack.1.near_ref), channel_id=1, source_target_pairs={{0,1},{1,0},{2,3},{3,2},{4,5},{5,4},{6,7},{7,6},{8,9},{9,8},{10,11... | collective-permute-start | bytes 786440 | tf_op jit(solution)/shard_map/ppermute | solution.py:451
  31.8 1.7 %collective-permute-start.7 = (bf16[16,64,128]{2,1,0:T(8,128)(2,1)S(1)}, bf16[16,64,128]{2,1,0:T(8,128)(2,1)S(1)}, u32[]{:S(2)}, u32[]{:S(2)}) collective-permute-start(bf16[16,64,128]{2,1,0:T(8,128)(2,1)S(1)} %get-tuple-element.16), channel_id=1, source_target_pairs={{0,1},{1,0},{2,3},{3,2},{4,5},{5,4},{6,7},{7,6},{8,9},{9,8},{10,11... | collective-permute-start | bytes 786440 | tf_op jit(solution)/shard_map/ppermute | solution.py:451
  33.6 5.6 %collective-permute-start.8 = (bf16[4,64,128]{2,1,0:T(8,128)(2,1)S(1)}, bf16[4,64,128]{2,1,0:T(8,128)(2,1)S(1)}, u32[]{:S(2)}, u32[]{:S(2)}) collective-permute-start(bf16[4,64,128]{2,1,0:T(8,128)(2,1)S(1)} %get-tuple-element.17), channel_id=1, source_target_pairs={{0,18},{2,16},{16,2},{18,0},{1,19},{3,17},{17,3},{19,1},{4,22},{6,... | collective-permute-start | bytes 196616 | tf_op jit(solution)/shard_map/ppermute | solution.py:451
  36.1 4.3 %collective-permute-start.10 = (bf16[4,64,128]{2,1,0:T(8,128)(2,1)S(1)}, bf16[4,64,128]{2,1,0:T(8,128)(2,1)S(1)}, u32[]{:S(2)}, u32[]{:S(2)}) collective-permute-start(bf16[4,64,128]{2,1,0:T(8,128)(2,1)S(1)} %get-tuple-element.18), channel_id=1, source_target_pairs={{0,2},{2,0},{16,18},{18,16},{1,3},{3,1},{17,19},{19,17},{4,6},{6,4... | collective-permute-start | bytes 196616 | tf_op jit(solution)/shard_map/ppermute | solution.py:451
  36.7 4.3 %collective-permute-start.9 = (bf16[4,64,128]{2,1,0:T(8,128)(2,1)S(1)}, bf16[4,64,128]{2,1,0:T(8,128)(2,1)S(1)}, u32[]{:S(2)}, u32[]{:S(2)}) collective-permute-start(bf16[4,64,128]{2,1,0:T(8,128)(2,1)S(1)} %get-tuple-element.19), channel_id=1, source_target_pairs={{0,16},{2,18},{16,0},{18,2},{1,17},{3,19},{17,1},{19,3},{4,20},{6,... | collective-permute-start | bytes 196616 | tf_op jit(solution)/shard_map/ppermute | solution.py:451
  41.0 5.6 %collective-permute-start.13 = (bf16[1,64,128]{2,1,0:T(8,128)(2,1)S(1)}, bf16[1,64,128]{2,1,0:T(8,128)(2,1)S(1)}, u32[]{:S(2)}, u32[]{:S(2)}) collective-permute-start(bf16[1,64,128]{2,1,0:T(8,128)(2,1)S(1)} %get-tuple-element.20), channel_id=1, source_target_pairs={{0,12},{4,8},{8,4},{12,0},{1,13},{5,9},{9,5},{13,1},{2,14},{6,10},... | collective-permute-start | bytes 49160 | tf_op jit(solution)/shard_map/ppermute | solution.py:451
  43.7 4.6 %collective-permute-start.12 = (bf16[1,64,128]{2,1,0:T(8,128)(2,1)S(1)}, bf16[1,64,128]{2,1,0:T(8,128)(2,1)S(1)}, u32[]{:S(2)}, u32[]{:S(2)}) collective-permute-start(bf16[1,64,128]{2,1,0:T(8,128)(2,1)S(1)} %get-tuple-element.21), channel_id=1, source_target_pairs={{0,8},{4,12},{8,0},{12,4},{1,9},{5,13},{9,1},{13,5},{2,10},{6,14},... | collective-permute-start | bytes 49160 | tf_op jit(solution)/shard_map/ppermute | solution.py:451
  43.7 4.6 %collective-permute-start.11 = (bf16[1,64,128]{2,1,0:T(8,128)(2,1)S(1)}, bf16[1,64,128]{2,1,0:T(8,128)(2,1)S(1)}, u32[]{:S(2)}, u32[]{:S(2)}) collective-permute-start(bf16[1,64,128]{2,1,0:T(8,128)(2,1)S(1)} %get-tuple-element.22), channel_id=1, source_target_pairs={{0,4},{4,0},{8,12},{12,8},{1,5},{5,1},{9,13},{13,9},{2,6},{6,2},{1... | collective-permute-start | bytes 49160 | tf_op jit(solution)/shard_map/ppermute | solution.py:451

commit v13 on v9

--- a/solution.py
+++ b/solution.py
@@ -319,6 +319,7 @@
     gate_out = product_ref[:, :half]
     up_out = product_ref[:, half:]
     hidden_ref[...] = (gate_out / (1.0 + jnp.exp(-gate_out)) * up_out).astype(jnp.bfloat16)
+    zero = jnp.minimum(lax.axis_index("core"), 0)
     for step in range(depth // chunk):
         wait(pairs + step)
         for at in range(step * chunk, (step + 1) * chunk, tile):
@@ -331,12 +332,14 @@
                 ]
         done = step * chunk // lanes
         count = chunk // lanes
-        for row in range(rows):
-            ready = wide_ref[row * stride + done : row * stride + done + count]
-            if row < rows // 2:
-                keep_ref[row, done : done + count] = ready
-            else:
-                send_ref[row - rows // 2, done : done + count] = ready.astype(jnp.bfloat16)
+        for row in range(rows // 2):
+            keep_ref[row + zero, done : done + count] = wide_ref[
+                row * stride + done : row * stride + done + count
+            ]
+            at = (row + rows // 2) * stride + done
+            send_ref[row + zero, done : done + count] = wide_ref[at : at + count].astype(
+                jnp.bfloat16
+            )
 
 
 def block(near, far, firsts, w_gate, w_up, w_down, half):

time: 47.2 us -> 46.6 us (0.987)
  Pallas kernels: 18.6 us -> 17.9 us
    pallas_call x1, Pallas kernels: 10.7 us -> 10 us  [block(): pl.pallas_call(body, out_shape=(jax.ShapeDtypeStruct((rows, lines, LANES)...]
where the time goes in v13:
time: 46.6 us; the launch traced here: 46.4 us
  Pallas kernels  17.9 us (38%)
  starting transfers between devices  17.4 us (37%)
  waiting for transfers between devices  10.8 us (23%)
    ppermute x14, starting transfers between devices, swap(): lax.ppermute(value, axes, [(place, place ^ offset) for place in places])  17.4 us
    ppermute x14, waiting for transfers between devices, swap(): lax.ppermute(value, axes, [(place, place ^ offset) for place in places])  10.8 us
    pallas_call x1, Pallas kernels, block(): pl.pallas_call(body, out_shape=(jax.ShapeDtypeStruct((rows, lines, LANES)...  10 us
    pallas_call x1, Pallas kernels, load_second(): pl.pallas_call(functools.partial(load_second_kernel, half, row, place), o...  3.74 us
    pallas_call x1, Pallas kernels, load_first(): pl.pallas_call(functools.partial(load_gain_kernel, half), out_shape=(pltp...  3.22 us
  transfers between devices with their start and end apart: 14, of which 8 were waited for; matrix products, arithmetic and copies ran while one was open for 0% of the time, Pallas kernels for 15%

profile of v13, /device:TPU:0, one launch (start us, length us, event | category | flops | bytes accessed | tf_op | source)
XLA Modules:
  0.0 46.4 jit_solution(11614843826443157779)
XLA Ops:
  0.0 5.0 %collective-permute-start.1 = (bf16[1,8192]{1,0:T(2,128)(2,1)}, bf16[1,8192]{1,0:T(2,128)(2,1)S(1)}, u32[]{:S(2)}, u32[]{:S(2)}) collective-permute-start(bf16[1,8192]{1,0:T(2,128)(2,1)} %refs_0_.1), channel_id=1, source_target_pairs={{0,12},{4,8},{8,4},{12,0},{1,13},{5,9},{9,5},{13,1},{2,14},{6,10},... | collective-permute-start | bytes 49160 | tf_op jit(solution)/shard_map/ppermute | solution.py:416
  5.0 0.0 collective-permute-start
  5.1 0.6 %collective-permute-start.2 = (bf16[1,8192]{1,0:T(2,128)(2,1)}, bf16[1,8192]{1,0:T(2,128)(2,1)S(1)}, u32[]{:S(2)}, u32[]{:S(2)}) collective-permute-start(bf16[1,8192]{1,0:T(2,128)(2,1)} %refs_0_.1), channel_id=1, source_target_pairs={{0,4},{4,0},{8,12},{12,8},{1,5},{5,1},{9,13},{13,9},{2,6},{6,2},{1... | collective-permute-start | bytes 49160 | tf_op jit(solution)/shard_map/ppermute | solution.py:416
  5.6 0.0 copy-start
  5.6 3.2 %load_first.1 = (bf16[2048,1792]{1,0:T(8,128)(2,1)S(1)}, bf16[64,128]{1,0:T(8,128)(2,1)S(1)}) custom-call(bf16[8192,1792]{1,0:T(8,128)(2,1)} %refs_2_.1, bf16[8192,1792]{1,0:T(8,128)(2,1)} %refs_3_.1, bf16[64,128]{1,0:T(8,128)(2,1)} %bitcast.1), custom_call_target="tpu_custom_call" | custom-call | bytes 7340032 | tf_op jit(solution)/shard_map/load_first/pallas_call | solution.py:110
  8.8 0.0 collective-permute-done.1.refs_2_
  8.9 1.2 %collective-permute-done.refs_1_ = bf16[1,8192]{1,0:T(2,128)(2,1)S(1)} collective-permute-done((bf16[1,8192]{1,0:T(2,128)(2,1)}, bf16[1,8192]{1,0:T(2,128)(2,1)S(1)}, u32[]{:S(2)}, u32[]{:S(2)}) %collective-permute-start) | collective-permute-done | bytes 16416 | tf_op jit(solution)/shard_map/ppermute | solution.py:416
  10.1 0.0 collective-permute-done.2.refs_3_
  10.1 0.0 copy-done
  10.1 0.1 stack.1.refs_0_
  10.2 2.5 %collective-permute-start.5 = (bf16[4,64,128]{2,1,0:T(8,128)(2,1)S(1)}, bf16[4,64,128]{2,1,0:T(8,128)(2,1)S(1)}, u32[]{:S(2)}, u32[]{:S(2)}) collective-permute-start(bf16[4,64,128]{2,1,0:T(8,128)(2,1)S(1)} %stack.1.refs_0_), channel_id=1, source_target_pairs={{0,18},{2,16},{16,2},{18,0},{1,19},{3,17},{17,3},{19,1},{4,22},{6,... | collective-permute-start | bytes 196616 | tf_op jit(solution)/shard_map/ppermute | solution.py:416
  12.7 0.5 %collective-permute-start.4 = (bf16[4,64,128]{2,1,0:T(8,128)(2,1)S(1)}, bf16[4,64,128]{2,1,0:T(8,128)(2,1)S(1)}, u32[]{:S(2)}, u32[]{:S(2)}) collective-permute-start(bf16[4,64,128]{2,1,0:T(8,128)(2,1)S(1)} %stack.1.refs_0_), channel_id=1, source_target_pairs={{0,16},{2,18},{16,0},{18,2},{1,17},{3,19},{17,1},{19,3},{4,20},{6,... | collective-permute-start | bytes 196616 | tf_op jit(solution)/shard_map/ppermute | solution.py:416
  13.2 0.5 %collective-permute-start.3 = (bf16[4,64,128]{2,1,0:T(8,128)(2,1)S(1)}, bf16[4,64,128]{2,1,0:T(8,128)(2,1)S(1)}, u32[]{:S(2)}, u32[]{:S(2)}) collective-permute-start(bf16[4,64,128]{2,1,0:T(8,128)(2,1)S(1)} %stack.1.refs_0_), channel_id=1, source_target_pairs={{0,2},{2,0},{16,18},{18,16},{1,3},{3,1},{17,19},{19,17},{4,6},{6,4... | collective-permute-start | bytes 196616 | tf_op jit(solution)/shard_map/ppermute | solution.py:416
  13.7 3.7 %load_second.1 = (bf16[2560,1792]{1,0:T(8,128)(2,1)S(1)}, f32[8,128]{1,0:T(8,128)S(1)}) custom-call(s32[8]{0:T(128)} %lengths.1, s32[8]{0:T(128)} %hit_lengths.1, s32[8]{0:T(128)} %start_positions.1, bf16[8192,1792]{1,0:T(8,128)(2,1)} %refs_2_.1, bf16[8192,1792]{1,0:T(8,128)(2,1)} %refs_3_.1), custom_call_target="tpu_custom_call" | custom-call | bytes 9175040 | tf_op jit(solution)/shard_map/load_second/pallas_call | solution.py:169
  17.5 0.0 collective-permute-done.5.refs_3_
  17.5 0.0 collective-permute-done.4.refs_2_
  17.5 0.0 collective-permute-done.3.refs_1_
  17.5 0.2 pack.1.near_ref
  17.7 0.1 collective-permute-start.6
  17.8 1.5 %collective-permute-done.6.far_ref = bf16[16,8192]{1,0:T(8,128)(2,1)S(1)} collective-permute-done((bf16[16,8192]{1,0:T(8,128)(2,1)S(1)}, bf16[16,8192]{1,0:T(8,128)(2,1)S(1)}, u32[]{:S(2)}, u32[]{:S(2)}) %collective-permute-start.6) | collective-permute-done | bytes 262176 | tf_op jit(solution)/shard_map/ppermute | solution.py:416
  19.3 10.0 %block.1 = (f32[16,64,128]{2,1,0:T(8,128)S(1)}, bf16[16,64,128]{2,1,0:T(8,128)(2,1)S(1)}) custom-call(bf16[16,8192]{1,0:T(8,128)(2,1)S(1)} %pack.1.near_ref, bf16[16,8192]{1,0:T(8,128)(2,1)S(1)} %collective-permute-done.6.far_ref, bf16[2048,1792]{1,0:T(8,128)(2,1)S(1)} %get-tuple-element.13.refs_0_, bf16[2560,1792]{1,0:T(8,128)(2,1)S(1)} %get-tuple-element.14.refs_1_, ...), custom_call_target="tpu_custom_call" | custom-call | flops 1409286144 | bytes 27525120 | tf_op jit(solution)/shard_map/block/pallas_call | solution.py:355
  29.3 0.2 collective-permute-start.7
  29.6 1.4 %collective-permute-done.7 = bf16[16,64,128]{2,1,0:T(8,128)(2,1)S(1)} collective-permute-done((bf16[16,64,128]{2,1,0:T(8,128)(2,1)S(1)}, bf16[16,64,128]{2,1,0:T(8,128)(2,1)S(1)}, u32[]{:S(2)}, u32[]{:S(2)}) %collective-permute-start.7) | collective-permute-done | bytes 262176 | tf_op jit(solution)/shard_map/ppermute | solution.py:416
  30.9 0.1 add_convert_fusion
  31.1 2.5 %collective-permute-start.8 = (bf16[4,64,128]{2,1,0:T(8,128)(2,1)S(1)}, bf16[4,64,128]{2,1,0:T(8,128)(2,1)S(1)}, u32[]{:S(2)}, u32[]{:S(2)}) collective-permute-start(bf16[4,64,128]{2,1,0:T(8,128)(2,1)S(1)} %get-tuple-element.17), channel_id=1, source_target_pairs={{0,18},{2,16},{16,2},{18,0},{1,19},{3,17},{17,3},{19,1},{4,22},{6,... | collective-permute-start | bytes 196616 | tf_op jit(solution)/shard_map/ppermute | solution.py:416
  33.6 0.5 %collective-permute-start.10 = (bf16[4,64,128]{2,1,0:T(8,128)(2,1)S(1)}, bf16[4,64,128]{2,1,0:T(8,128)(2,1)S(1)}, u32[]{:S(2)}, u32[]{:S(2)}) collective-permute-start(bf16[4,64,128]{2,1,0:T(8,128)(2,1)S(1)} %get-tuple-element.18), channel_id=1, source_target_pairs={{0,2},{2,0},{16,18},{18,16},{1,3},{3,1},{17,19},{19,17},{4,6},{6,4... | collective-permute-start | bytes 196616 | tf_op jit(solution)/shard_map/ppermute | solution.py:416
  34.1 0.5 %collective-permute-start.9 = (bf16[4,64,128]{2,1,0:T(8,128)(2,1)S(1)}, bf16[4,64,128]{2,1,0:T(8,128)(2,1)S(1)}, u32[]{:S(2)}, u32[]{:S(2)}) collective-permute-start(bf16[4,64,128]{2,1,0:T(8,128)(2,1)S(1)} %get-tuple-element.19), channel_id=1, source_target_pairs={{0,16},{2,18},{16,0},{18,2},{1,17},{3,19},{17,1},{19,3},{4,20},{6,... | collective-permute-start | bytes 196616 | tf_op jit(solution)/shard_map/ppermute | solution.py:416
  34.6 2.1 %collective-permute-done.8 = bf16[4,64,128]{2,1,0:T(8,128)(2,1)S(1)} collective-permute-done((bf16[4,64,128]{2,1,0:T(8,128)(2,1)S(1)}, bf16[4,64,128]{2,1,0:T(8,128)(2,1)S(1)}, u32[]{:S(2)}, u32[]{:S(2)}) %collective-permute-start.8) | collective-permute-done | bytes 65568 | tf_op jit(solution)/shard_map/ppermute | solution.py:416
  36.7 1.1 %collective-permute-done.10 = bf16[4,64,128]{2,1,0:T(8,128)(2,1)S(1)} collective-permute-done((bf16[4,64,128]{2,1,0:T(8,128)(2,1)S(1)}, bf16[4,64,128]{2,1,0:T(8,128)(2,1)S(1)}, u32[]{:S(2)}, u32[]{:S(2)}) %collective-permute-start.10) | collective-permute-done | bytes 65568 | tf_op jit(solution)/shard_map/ppermute | solution.py:416
  37.8 0.5 %collective-permute-done.9 = bf16[4,64,128]{2,1,0:T(8,128)(2,1)S(1)} collective-permute-done((bf16[4,64,128]{2,1,0:T(8,128)(2,1)S(1)}, bf16[4,64,128]{2,1,0:T(8,128)(2,1)S(1)}, u32[]{:S(2)}, u32[]{:S(2)}) %collective-permute-start.9) | collective-permute-done | bytes 65568 | tf_op jit(solution)/shard_map/ppermute | solution.py:416
  38.4 2.7 %collective-permute-start.13 = (bf16[1,64,128]{2,1,0:T(8,128)(2,1)S(1)}, bf16[1,64,128]{2,1,0:T(8,128)(2,1)S(1)}, u32[]{:S(2)}, u32[]{:S(2)}) collective-permute-start(bf16[1,64,128]{2,1,0:T(8,128)(2,1)S(1)} %get-tuple-element.20), channel_id=1, source_target_pairs={{0,12},{4,8},{8,4},{12,0},{1,13},{5,9},{9,5},{13,1},{2,14},{6,10},... | collective-permute-start | bytes 49160 | tf_op jit(solution)/shard_map/ppermute | solution.py:416
  41.1 0.0 collective-permute-start.12
  41.1 1.8 %collective-permute-start.11 = (bf16[1,64,128]{2,1,0:T(8,128)(2,1)S(1)}, bf16[1,64,128]{2,1,0:T(8,128)(2,1)S(1)}, u32[]{:S(2)}, u32[]{:S(2)}) collective-permute-start(bf16[1,64,128]{2,1,0:T(8,128)(2,1)S(1)} %get-tuple-element.22), channel_id=1, source_target_pairs={{0,4},{4,0},{8,12},{12,8},{1,5},{5,1},{9,13},{13,9},{2,6},{6,2},{1... | collective-permute-start | bytes 49160 | tf_op jit(solution)/shard_map/ppermute | solution.py:416
  42.9 1.1 %collective-permute-done.13.refs_3_ = bf16[1,64,128]{2,1,0:T(8,128)(2,1)S(1)} collective-permute-done((bf16[1,64,128]{2,1,0:T(8,128)(2,1)S(1)}, bf16[1,64,128]{2,1,0:T(8,128)(2,1)S(1)}, u32[]{:S(2)}, u32[]{:S(2)}) %collective-permute-start.13) | collective-permute-done | bytes 16416 | tf_op jit(solution)/shard_map/ppermute | solution.py:416
  44.0 1.7 %collective-permute-done.12.refs_2_ = bf16[1,64,128]{2,1,0:T(8,128)(2,1)S(1)} collective-permute-done((bf16[1,64,128]{2,1,0:T(8,128)(2,1)S(1)}, bf16[1,64,128]{2,1,0:T(8,128)(2,1)S(1)}, u32[]{:S(2)}, u32[]{:S(2)}) %collective-permute-start.12) | collective-permute-done | bytes 16416 | tf_op jit(solution)/shard_map/ppermute | solution.py:416
  45.7 0.0 collective-permute-done.11.refs_1_
  45.7 0.7 %finish.1 = bf16[1,8192]{1,0:T(2,128)(2,1)} custom-call(bf16[1,64,128]{2,1,0:T(8,128)(2,1)S(1)} %get-tuple-element.23.refs_0_, bf16[1,64,128]{2,1,0:T(8,128)(2,1)S(1)} %collective-permute-done.11.refs_1_, bf16[1,64,128]{2,1,0:T(8,128)(2,1)S(1)} %collective-permute-done.12.refs_2_, bf16[1,64,128]{2,1,0:T(8,128)(2,1)S(1)} %collective-permute-done.13.refs_3_, ...), custom_call_target="tpu_custom_call" | custom-call | tf_op jit(solution)/shard_map/finish/pallas_call | solution.py:404
  (3 shorter events, 0.1 us)
Async XLA Ops:
  0.0 8.9 %collective-permute-start.1 = (bf16[1,8192]{1,0:T(2,128)(2,1)}, bf16[1,8192]{1,0:T(2,128)(2,1)S(1)}, u32[]{:S(2)}, u32[]{:S(2)}) collective-permute-start(bf16[1,8192]{1,0:T(2,128)(2,1)} %refs_0_.1), channel_id=1, source_target_pairs={{0,12},{4,8},{8,4},{12,0},{1,13},{5,9},{9,5},{13,1},{2,14},{6,10},... | collective-permute-start | bytes 49160 | tf_op jit(solution)/shard_map/ppermute | solution.py:416
  5.0 5.0 %collective-permute-start = (bf16[1,8192]{1,0:T(2,128)(2,1)}, bf16[1,8192]{1,0:T(2,128)(2,1)S(1)}, u32[]{:S(2)}, u32[]{:S(2)}) collective-permute-start(bf16[1,8192]{1,0:T(2,128)(2,1)} %refs_0_.1), channel_id=1, source_target_pairs={{0,8},{4,12},{8,0},{12,4},{1,9},{5,13},{9,1},{13,5},{2,10},{6,14},... | collective-permute-start | bytes 49160 | tf_op jit(solution)/shard_map/ppermute | solution.py:416
  5.1 5.0 %collective-permute-start.2 = (bf16[1,8192]{1,0:T(2,128)(2,1)}, bf16[1,8192]{1,0:T(2,128)(2,1)S(1)}, u32[]{:S(2)}, u32[]{:S(2)}) collective-permute-start(bf16[1,8192]{1,0:T(2,128)(2,1)} %refs_0_.1), channel_id=1, source_target_pairs={{0,4},{4,0},{8,12},{12,8},{1,5},{5,1},{9,13},{13,9},{2,6},{6,2},{1... | collective-permute-start | bytes 49160 | tf_op jit(solution)/shard_map/ppermute | solution.py:416
  5.6 4.5 %copy-start = (bf16[1,8192]{1,0:T(2,128)(2,1)S(1)}, bf16[1,8192]{1,0:T(2,128)(2,1)}, u32[]{:S(2)}) copy-start(bf16[1,8192]{1,0:T(2,128)(2,1)} %refs_0_.1) | copy-start | bytes 49156
  10.2 7.3 %collective-permute-start.5 = (bf16[4,64,128]{2,1,0:T(8,128)(2,1)S(1)}, bf16[4,64,128]{2,1,0:T(8,128)(2,1)S(1)}, u32[]{:S(2)}, u32[]{:S(2)}) collective-permute-start(bf16[4,64,128]{2,1,0:T(8,128)(2,1)S(1)} %stack.1.refs_0_), channel_id=1, source_target_pairs={{0,18},{2,16},{16,2},{18,0},{1,19},{3,17},{17,3},{19,1},{4,22},{6,... | collective-permute-start | bytes 196616 | tf_op jit(solution)/shard_map/ppermute | solution.py:416
  12.7 4.8 %collective-permute-start.4 = (bf16[4,64,128]{2,1,0:T(8,128)(2,1)S(1)}, bf16[4,64,128]{2,1,0:T(8,128)(2,1)S(1)}, u32[]{:S(2)}, u32[]{:S(2)}) collective-permute-start(bf16[4,64,128]{2,1,0:T(8,128)(2,1)S(1)} %stack.1.refs_0_), channel_id=1, source_target_pairs={{0,16},{2,18},{16,0},{18,2},{1,17},{3,19},{17,1},{19,3},{4,20},{6,... | collective-permute-start | bytes 196616 | tf_op jit(solution)/shard_map/ppermute | solution.py:416
  13.2 4.3 %collective-permute-start.3 = (bf16[4,64,128]{2,1,0:T(8,128)(2,1)S(1)}, bf16[4,64,128]{2,1,0:T(8,128)(2,1)S(1)}, u32[]{:S(2)}, u32[]{:S(2)}) collective-permute-start(bf16[4,64,128]{2,1,0:T(8,128)(2,1)S(1)} %stack.1.refs_0_), channel_id=1, source_target_pairs={{0,2},{2,0},{16,18},{18,16},{1,3},{3,1},{17,19},{19,17},{4,6},{6,4... | collective-permute-start | bytes 196616 | tf_op jit(solution)/shard_map/ppermute | solution.py:416
  17.7 1.6 %collective-permute-start.6 = (bf16[16,8192]{1,0:T(8,128)(2,1)S(1)}, bf16[16,8192]{1,0:T(8,128)(2,1)S(1)}, u32[]{:S(2)}, u32[]{:S(2)}) collective-permute-start(bf16[16,8192]{1,0:T(8,128)(2,1)S(1)} %pack.1.near_ref), channel_id=1, source_target_pairs={{0,1},{1,0},{2,3},{3,2},{4,5},{5,4},{6,7},{7,6},{8,9},{9,8},{10,11... | collective-permute-start | bytes 786440 | tf_op jit(solution)/shard_map/ppermute | solution.py:416
  29.3 1.6 %collective-permute-start.7 = (bf16[16,64,128]{2,1,0:T(8,128)(2,1)S(1)}, bf16[16,64,128]{2,1,0:T(8,128)(2,1)S(1)}, u32[]{:S(2)}, u32[]{:S(2)}) collective-permute-start(bf16[16,64,128]{2,1,0:T(8,128)(2,1)S(1)} %get-tuple-element.16), channel_id=1, source_target_pairs={{0,1},{1,0},{2,3},{3,2},{4,5},{5,4},{6,7},{7,6},{8,9},{9,8},{10,11... | collective-permute-start | bytes 786440 | tf_op jit(solution)/shard_map/ppermute | solution.py:416
  31.1 5.6 %collective-permute-start.8 = (bf16[4,64,128]{2,1,0:T(8,128)(2,1)S(1)}, bf16[4,64,128]{2,1,0:T(8,128)(2,1)S(1)}, u32[]{:S(2)}, u32[]{:S(2)}) collective-permute-start(bf16[4,64,128]{2,1,0:T(8,128)(2,1)S(1)} %get-tuple-element.17), channel_id=1, source_target_pairs={{0,18},{2,16},{16,2},{18,0},{1,19},{3,17},{17,3},{19,1},{4,22},{6,... | collective-permute-start | bytes 196616 | tf_op jit(solution)/shard_map/ppermute | solution.py:416
  33.6 4.3 %collective-permute-start.10 = (bf16[4,64,128]{2,1,0:T(8,128)(2,1)S(1)}, bf16[4,64,128]{2,1,0:T(8,128)(2,1)S(1)}, u32[]{:S(2)}, u32[]{:S(2)}) collective-permute-start(bf16[4,64,128]{2,1,0:T(8,128)(2,1)S(1)} %get-tuple-element.18), channel_id=1, source_target_pairs={{0,2},{2,0},{16,18},{18,16},{1,3},{3,1},{17,19},{19,17},{4,6},{6,4... | collective-permute-start | bytes 196616 | tf_op jit(solution)/shard_map/ppermute | solution.py:416
  34.1 4.3 %collective-permute-start.9 = (bf16[4,64,128]{2,1,0:T(8,128)(2,1)S(1)}, bf16[4,64,128]{2,1,0:T(8,128)(2,1)S(1)}, u32[]{:S(2)}, u32[]{:S(2)}) collective-permute-start(bf16[4,64,128]{2,1,0:T(8,128)(2,1)S(1)} %get-tuple-element.19), channel_id=1, source_target_pairs={{0,16},{2,18},{16,0},{18,2},{1,17},{3,19},{17,1},{19,3},{4,20},{6,... | collective-permute-start | bytes 196616 | tf_op jit(solution)/shard_map/ppermute | solution.py:416
  38.4 5.6 %collective-permute-start.13 = (bf16[1,64,128]{2,1,0:T(8,128)(2,1)S(1)}, bf16[1,64,128]{2,1,0:T(8,128)(2,1)S(1)}, u32[]{:S(2)}, u32[]{:S(2)}) collective-permute-start(bf16[1,64,128]{2,1,0:T(8,128)(2,1)S(1)} %get-tuple-element.20), channel_id=1, source_target_pairs={{0,12},{4,8},{8,4},{12,0},{1,13},{5,9},{9,5},{13,1},{2,14},{6,10},... | collective-permute-start | bytes 49160 | tf_op jit(solution)/shard_map/ppermute | solution.py:416
  41.1 4.6 %collective-permute-start.12 = (bf16[1,64,128]{2,1,0:T(8,128)(2,1)S(1)}, bf16[1,64,128]{2,1,0:T(8,128)(2,1)S(1)}, u32[]{:S(2)}, u32[]{:S(2)}) collective-permute-start(bf16[1,64,128]{2,1,0:T(8,128)(2,1)S(1)} %get-tuple-element.21), channel_id=1, source_target_pairs={{0,8},{4,12},{8,0},{12,4},{1,9},{5,13},{9,1},{13,5},{2,10},{6,14},... | collective-permute-start | bytes 49160 | tf_op jit(solution)/shard_map/ppermute | solution.py:416
  41.1 4.6 %collective-permute-start.11 = (bf16[1,64,128]{2,1,0:T(8,128)(2,1)S(1)}, bf16[1,64,128]{2,1,0:T(8,128)(2,1)S(1)}, u32[]{:S(2)}, u32[]{:S(2)}) collective-permute-start(bf16[1,64,128]{2,1,0:T(8,128)(2,1)S(1)} %get-tuple-element.22), channel_id=1, source_target_pairs={{0,4},{4,0},{8,12},{12,8},{1,5},{5,1},{9,13},{13,9},{2,6},{6,2},{1... | collective-permute-start | bytes 49160 | tf_op jit(solution)/shard_map/ppermute | solution.py:416

commit v14 on v13

--- a/solution.py
+++ b/solution.py
@@ -261,12 +261,16 @@
         )
         at += deal
     pairs = len(loads)
-    for step, at in enumerate(range(0, depth, chunk)):
+    spans = []
+    while sum(width for _, width in spans) < depth:
+        at = sum(width for _, width in spans)
+        spans.append((at, chunk if depth - at > chunk else chunk // 2))
+    for step, (at, width) in enumerate(spans):
         loads.append(
             [
                 pltpu.make_async_copy(
-                    down_hbm.at[pl.ds(own, half), pl.ds(at, chunk)],
-                    down_ref.at[:, pl.ds(at, chunk)],
+                    down_hbm.at[pl.ds(own, half), pl.ds(at, width)],
+                    down_ref.at[:, pl.ds(at, width)],
                     down_sems.at[step],
                 )
             ]
@@ -304,8 +308,7 @@
     at = 0
     for ref in first_refs:
         multiply(at, ref.shape[0], ref, 0, False)
-        if at == 0:
-            start()
+        start()
         at += ref.shape[0]
     row = 0
     for step, deal in enumerate(deals):
@@ -320,9 +323,9 @@
     up_out = product_ref[:, half:]
     hidden_ref[...] = (gate_out / (1.0 + jnp.exp(-gate_out)) * up_out).astype(jnp.bfloat16)
     zero = jnp.minimum(lax.axis_index("core"), 0)
-    for step in range(depth // chunk):
+    for step, (begin, width) in enumerate(spans):
         wait(pairs + step)
-        for at in range(step * chunk, (step + 1) * chunk, tile):
+        for at in range(begin, begin + width, tile):
             result = jnp.dot(
                 hidden_ref[...], down_ref[:, pl.ds(at, tile)], preferred_element_type=jnp.float32
             )
@@ -330,8 +333,8 @@
                 wide_ref[pl.ds(at // lanes + line, rows, stride=stride), :] = result[
                     :, line * lanes : (line + 1) * lanes
                 ]
-        done = step * chunk // lanes
-        count = chunk // lanes
+        done = begin // lanes
+        count = width // lanes
         for row in range(rows // 2):
             keep_ref[row + zero, done : done + count] = wide_ref[
                 row * stride + done : row * stride + done + count
@@ -368,7 +371,7 @@
             pltpu.VMEM((rest, 2 * half), jnp.bfloat16),
             pltpu.VMEM((half, depth), jnp.bfloat16),
             pltpu.SemaphoreType.DMA((2, 2)),
-            pltpu.SemaphoreType.DMA((depth // (2 * CHUNK),)),
+            pltpu.SemaphoreType.DMA((depth // (2 * CHUNK) + 1,)),
         ],
         compiler_params=pltpu.CompilerParams(
             vmem_limit_bytes=(rest * 2 + depth) * half * 2 + (6 << 20)

time: 46.6 us -> 46.4 us (level)
  no operation moved by 1% of the time
where the time goes in v14:
time: 46.4 us; the launch traced here: 46.3 us
  Pallas kernels  17.8 us (38%)
  starting transfers between devices  17.4 us (37%)
  waiting for transfers between devices  10.8 us (23%)
    ppermute x14, starting transfers between devices, swap(): lax.ppermute(value, axes, [(place, place ^ offset) for place in places])  17.4 us
    ppermute x14, waiting for transfers between devices, swap(): lax.ppermute(value, axes, [(place, place ^ offset) for place in places])  10.8 us
    pallas_call x1, Pallas kernels, block(): pl.pallas_call(body, out_shape=(jax.ShapeDtypeStruct((rows, lines, LANES)...  9.88 us
    pallas_call x1, Pallas kernels, load_second(): pl.pallas_call(functools.partial(load_second_kernel, half, row, place), o...  3.74 us
    pallas_call x1, Pallas kernels, load_first(): pl.pallas_call(functools.partial(load_gain_kernel, half), out_shape=(pltp...  3.22 us
  transfers between devices with their start and end apart: 14, of which 8 were waited for; matrix products, arithmetic and copies ran while one was open for 0% of the time, Pallas kernels for 15%

profile of v14, /device:TPU:0, one launch (start us, length us, event | category | flops | bytes accessed | tf_op | source)
XLA Modules:
  0.0 46.3 jit_solution(10384838494576362460)
XLA Ops:
  0.0 5.0 %collective-permute-start.1 = (bf16[1,8192]{1,0:T(2,128)(2,1)}, bf16[1,8192]{1,0:T(2,128)(2,1)S(1)}, u32[]{:S(2)}, u32[]{:S(2)}) collective-permute-start(bf16[1,8192]{1,0:T(2,128)(2,1)} %refs_0_.1), channel_id=1, source_target_pairs={{0,12},{4,8},{8,4},{12,0},{1,13},{5,9},{9,5},{13,1},{2,14},{6,10},... | collective-permute-start | bytes 49160 | tf_op jit(solution)/shard_map/ppermute | solution.py:419
  5.0 0.0 collective-permute-start
  5.1 0.6 %collective-permute-start.2 = (bf16[1,8192]{1,0:T(2,128)(2,1)}, bf16[1,8192]{1,0:T(2,128)(2,1)S(1)}, u32[]{:S(2)}, u32[]{:S(2)}) collective-permute-start(bf16[1,8192]{1,0:T(2,128)(2,1)} %refs_0_.1), channel_id=1, source_target_pairs={{0,4},{4,0},{8,12},{12,8},{1,5},{5,1},{9,13},{13,9},{2,6},{6,2},{1... | collective-permute-start | bytes 49160 | tf_op jit(solution)/shard_map/ppermute | solution.py:419
  5.6 0.0 copy-start
  5.6 3.2 %load_first.1 = (bf16[2048,1792]{1,0:T(8,128)(2,1)S(1)}, bf16[64,128]{1,0:T(8,128)(2,1)S(1)}) custom-call(bf16[8192,1792]{1,0:T(8,128)(2,1)} %refs_2_.1, bf16[8192,1792]{1,0:T(8,128)(2,1)} %refs_3_.1, bf16[64,128]{1,0:T(8,128)(2,1)} %bitcast.1), custom_call_target="tpu_custom_call" | custom-call | bytes 7340032 | tf_op jit(solution)/shard_map/load_first/pallas_call | solution.py:110
  8.8 0.0 collective-permute-done.1.refs_2_
  8.9 1.2 %collective-permute-done.refs_1_ = bf16[1,8192]{1,0:T(2,128)(2,1)S(1)} collective-permute-done((bf16[1,8192]{1,0:T(2,128)(2,1)}, bf16[1,8192]{1,0:T(2,128)(2,1)S(1)}, u32[]{:S(2)}, u32[]{:S(2)}) %collective-permute-start) | collective-permute-done | bytes 16416 | tf_op jit(solution)/shard_map/ppermute | solution.py:419
  10.1 0.0 collective-permute-done.2.refs_3_
  10.1 0.0 copy-done
  10.1 0.1 stack.1.refs_0_
  10.2 2.5 %collective-permute-start.5 = (bf16[4,64,128]{2,1,0:T(8,128)(2,1)S(1)}, bf16[4,64,128]{2,1,0:T(8,128)(2,1)S(1)}, u32[]{:S(2)}, u32[]{:S(2)}) collective-permute-start(bf16[4,64,128]{2,1,0:T(8,128)(2,1)S(1)} %stack.1.refs_0_), channel_id=1, source_target_pairs={{0,18},{2,16},{16,2},{18,0},{1,19},{3,17},{17,3},{19,1},{4,22},{6,... | collective-permute-start | bytes 196616 | tf_op jit(solution)/shard_map/ppermute | solution.py:419
  12.7 0.5 %collective-permute-start.4 = (bf16[4,64,128]{2,1,0:T(8,128)(2,1)S(1)}, bf16[4,64,128]{2,1,0:T(8,128)(2,1)S(1)}, u32[]{:S(2)}, u32[]{:S(2)}) collective-permute-start(bf16[4,64,128]{2,1,0:T(8,128)(2,1)S(1)} %stack.1.refs_0_), channel_id=1, source_target_pairs={{0,16},{2,18},{16,0},{18,2},{1,17},{3,19},{17,1},{19,3},{4,20},{6,... | collective-permute-start | bytes 196616 | tf_op jit(solution)/shard_map/ppermute | solution.py:419
  13.2 0.5 %collective-permute-start.3 = (bf16[4,64,128]{2,1,0:T(8,128)(2,1)S(1)}, bf16[4,64,128]{2,1,0:T(8,128)(2,1)S(1)}, u32[]{:S(2)}, u32[]{:S(2)}) collective-permute-start(bf16[4,64,128]{2,1,0:T(8,128)(2,1)S(1)} %stack.1.refs_0_), channel_id=1, source_target_pairs={{0,2},{2,0},{16,18},{18,16},{1,3},{3,1},{17,19},{19,17},{4,6},{6,4... | collective-permute-start | bytes 196616 | tf_op jit(solution)/shard_map/ppermute | solution.py:419
  13.7 3.7 %load_second.1 = (bf16[2560,1792]{1,0:T(8,128)(2,1)S(1)}, f32[8,128]{1,0:T(8,128)S(1)}) custom-call(s32[8]{0:T(128)} %lengths.1, s32[8]{0:T(128)} %hit_lengths.1, s32[8]{0:T(128)} %start_positions.1, bf16[8192,1792]{1,0:T(8,128)(2,1)} %refs_2_.1, bf16[8192,1792]{1,0:T(8,128)(2,1)} %refs_3_.1), custom_call_target="tpu_custom_call" | custom-call | bytes 9175040 | tf_op jit(solution)/shard_map/load_second/pallas_call | solution.py:169
  17.5 0.0 collective-permute-done.5.refs_3_
  17.5 0.0 collective-permute-done.4.refs_2_
  17.5 0.0 collective-permute-done.3.refs_1_
  17.5 0.2 pack.1.near_ref
  17.7 0.1 collective-permute-start.6
  17.8 1.5 %collective-permute-done.6.far_ref = bf16[16,8192]{1,0:T(8,128)(2,1)S(1)} collective-permute-done((bf16[16,8192]{1,0:T(8,128)(2,1)S(1)}, bf16[16,8192]{1,0:T(8,128)(2,1)S(1)}, u32[]{:S(2)}, u32[]{:S(2)}) %collective-permute-start.6) | collective-permute-done | bytes 262176 | tf_op jit(solution)/shard_map/ppermute | solution.py:419
  19.3 9.9 %block.1 = (f32[16,64,128]{2,1,0:T(8,128)S(1)}, bf16[16,64,128]{2,1,0:T(8,128)(2,1)S(1)}) custom-call(bf16[16,8192]{1,0:T(8,128)(2,1)S(1)} %pack.1.near_ref, bf16[16,8192]{1,0:T(8,128)(2,1)S(1)} %collective-permute-done.6.far_ref, bf16[2048,1792]{1,0:T(8,128)(2,1)S(1)} %get-tuple-element.13.refs_0_, bf16[2560,1792]{1,0:T(8,128)(2,1)S(1)} %get-tuple-element.14.refs_1_, ...), custom_call_target="tpu_custom_call" | custom-call | flops 1409286144 | bytes 27525120 | tf_op jit(solution)/shard_map/block/pallas_call | solution.py:358
  29.2 0.2 collective-permute-start.7
  29.4 1.4 %collective-permute-done.7 = bf16[16,64,128]{2,1,0:T(8,128)(2,1)S(1)} collective-permute-done((bf16[16,64,128]{2,1,0:T(8,128)(2,1)S(1)}, bf16[16,64,128]{2,1,0:T(8,128)(2,1)S(1)}, u32[]{:S(2)}, u32[]{:S(2)}) %collective-permute-start.7) | collective-permute-done | bytes 262176 | tf_op jit(solution)/shard_map/ppermute | solution.py:419
  30.8 0.1 add_convert_fusion
  30.9 2.5 %collective-permute-start.8 = (bf16[4,64,128]{2,1,0:T(8,128)(2,1)S(1)}, bf16[4,64,128]{2,1,0:T(8,128)(2,1)S(1)}, u32[]{:S(2)}, u32[]{:S(2)}) collective-permute-start(bf16[4,64,128]{2,1,0:T(8,128)(2,1)S(1)} %get-tuple-element.17), channel_id=1, source_target_pairs={{0,18},{2,16},{16,2},{18,0},{1,19},{3,17},{17,3},{19,1},{4,22},{6,... | collective-permute-start | bytes 196616 | tf_op jit(solution)/shard_map/ppermute | solution.py:419
  33.4 0.5 %collective-permute-start.10 = (bf16[4,64,128]{2,1,0:T(8,128)(2,1)S(1)}, bf16[4,64,128]{2,1,0:T(8,128)(2,1)S(1)}, u32[]{:S(2)}, u32[]{:S(2)}) collective-permute-start(bf16[4,64,128]{2,1,0:T(8,128)(2,1)S(1)} %get-tuple-element.18), channel_id=1, source_target_pairs={{0,2},{2,0},{16,18},{18,16},{1,3},{3,1},{17,19},{19,17},{4,6},{6,4... | collective-permute-start | bytes 196616 | tf_op jit(solution)/shard_map/ppermute | solution.py:419
  34.0 0.5 %collective-permute-start.9 = (bf16[4,64,128]{2,1,0:T(8,128)(2,1)S(1)}, bf16[4,64,128]{2,1,0:T(8,128)(2,1)S(1)}, u32[]{:S(2)}, u32[]{:S(2)}) collective-permute-start(bf16[4,64,128]{2,1,0:T(8,128)(2,1)S(1)} %get-tuple-element.19), channel_id=1, source_target_pairs={{0,16},{2,18},{16,0},{18,2},{1,17},{3,19},{17,1},{19,3},{4,20},{6,... | collective-permute-start | bytes 196616 | tf_op jit(solution)/shard_map/ppermute | solution.py:419
  34.5 2.1 %collective-permute-done.8 = bf16[4,64,128]{2,1,0:T(8,128)(2,1)S(1)} collective-permute-done((bf16[4,64,128]{2,1,0:T(8,128)(2,1)S(1)}, bf16[4,64,128]{2,1,0:T(8,128)(2,1)S(1)}, u32[]{:S(2)}, u32[]{:S(2)}) %collective-permute-start.8) | collective-permute-done | bytes 65568 | tf_op jit(solution)/shard_map/ppermute | solution.py:419
  36.6 1.1 %collective-permute-done.10 = bf16[4,64,128]{2,1,0:T(8,128)(2,1)S(1)} collective-permute-done((bf16[4,64,128]{2,1,0:T(8,128)(2,1)S(1)}, bf16[4,64,128]{2,1,0:T(8,128)(2,1)S(1)}, u32[]{:S(2)}, u32[]{:S(2)}) %collective-permute-start.10) | collective-permute-done | bytes 65568 | tf_op jit(solution)/shard_map/ppermute | solution.py:419
  37.7 0.5 %collective-permute-done.9 = bf16[4,64,128]{2,1,0:T(8,128)(2,1)S(1)} collective-permute-done((bf16[4,64,128]{2,1,0:T(8,128)(2,1)S(1)}, bf16[4,64,128]{2,1,0:T(8,128)(2,1)S(1)}, u32[]{:S(2)}, u32[]{:S(2)}) %collective-permute-start.9) | collective-permute-done | bytes 65568 | tf_op jit(solution)/shard_map/ppermute | solution.py:419
  38.3 2.7 %collective-permute-start.13 = (bf16[1,64,128]{2,1,0:T(8,128)(2,1)S(1)}, bf16[1,64,128]{2,1,0:T(8,128)(2,1)S(1)}, u32[]{:S(2)}, u32[]{:S(2)}) collective-permute-start(bf16[1,64,128]{2,1,0:T(8,128)(2,1)S(1)} %get-tuple-element.20), channel_id=1, source_target_pairs={{0,12},{4,8},{8,4},{12,0},{1,13},{5,9},{9,5},{13,1},{2,14},{6,10},... | collective-permute-start | bytes 49160 | tf_op jit(solution)/shard_map/ppermute | solution.py:419
  41.0 0.0 collective-permute-start.12
  41.0 1.8 %collective-permute-start.11 = (bf16[1,64,128]{2,1,0:T(8,128)(2,1)S(1)}, bf16[1,64,128]{2,1,0:T(8,128)(2,1)S(1)}, u32[]{:S(2)}, u32[]{:S(2)}) collective-permute-start(bf16[1,64,128]{2,1,0:T(8,128)(2,1)S(1)} %get-tuple-element.22), channel_id=1, source_target_pairs={{0,4},{4,0},{8,12},{12,8},{1,5},{5,1},{9,13},{13,9},{2,6},{6,2},{1... | collective-permute-start | bytes 49160 | tf_op jit(solution)/shard_map/ppermute | solution.py:419
  42.7 1.1 %collective-permute-done.13.refs_3_ = bf16[1,64,128]{2,1,0:T(8,128)(2,1)S(1)} collective-permute-done((bf16[1,64,128]{2,1,0:T(8,128)(2,1)S(1)}, bf16[1,64,128]{2,1,0:T(8,128)(2,1)S(1)}, u32[]{:S(2)}, u32[]{:S(2)}) %collective-permute-start.13) | collective-permute-done | bytes 16416 | tf_op jit(solution)/shard_map/ppermute | solution.py:419
  43.9 1.7 %collective-permute-done.12.refs_2_ = bf16[1,64,128]{2,1,0:T(8,128)(2,1)S(1)} collective-permute-done((bf16[1,64,128]{2,1,0:T(8,128)(2,1)S(1)}, bf16[1,64,128]{2,1,0:T(8,128)(2,1)S(1)}, u32[]{:S(2)}, u32[]{:S(2)}) %collective-permute-start.12) | collective-permute-done | bytes 16416 | tf_op jit(solution)/shard_map/ppermute | solution.py:419
  45.6 0.0 collective-permute-done.11.refs_1_
  45.6 0.7 %finish.1 = bf16[1,8192]{1,0:T(2,128)(2,1)} custom-call(bf16[1,64,128]{2,1,0:T(8,128)(2,1)S(1)} %get-tuple-element.23.refs_0_, bf16[1,64,128]{2,1,0:T(8,128)(2,1)S(1)} %collective-permute-done.11.refs_1_, bf16[1,64,128]{2,1,0:T(8,128)(2,1)S(1)} %collective-permute-done.12.refs_2_, bf16[1,64,128]{2,1,0:T(8,128)(2,1)S(1)} %collective-permute-done.13.refs_3_, ...), custom_call_target="tpu_custom_call" | custom-call | tf_op jit(solution)/shard_map/finish/pallas_call | solution.py:407
  (3 shorter events, 0.1 us)
Async XLA Ops:
  0.0 8.9 %collective-permute-start.1 = (bf16[1,8192]{1,0:T(2,128)(2,1)}, bf16[1,8192]{1,0:T(2,128)(2,1)S(1)}, u32[]{:S(2)}, u32[]{:S(2)}) collective-permute-start(bf16[1,8192]{1,0:T(2,128)(2,1)} %refs_0_.1), channel_id=1, source_target_pairs={{0,12},{4,8},{8,4},{12,0},{1,13},{5,9},{9,5},{13,1},{2,14},{6,10},... | collective-permute-start | bytes 49160 | tf_op jit(solution)/shard_map/ppermute | solution.py:419
  5.0 5.0 %collective-permute-start = (bf16[1,8192]{1,0:T(2,128)(2,1)}, bf16[1,8192]{1,0:T(2,128)(2,1)S(1)}, u32[]{:S(2)}, u32[]{:S(2)}) collective-permute-start(bf16[1,8192]{1,0:T(2,128)(2,1)} %refs_0_.1), channel_id=1, source_target_pairs={{0,8},{4,12},{8,0},{12,4},{1,9},{5,13},{9,1},{13,5},{2,10},{6,14},... | collective-permute-start | bytes 49160 | tf_op jit(solution)/shard_map/ppermute | solution.py:419
  5.1 5.0 %collective-permute-start.2 = (bf16[1,8192]{1,0:T(2,128)(2,1)}, bf16[1,8192]{1,0:T(2,128)(2,1)S(1)}, u32[]{:S(2)}, u32[]{:S(2)}) collective-permute-start(bf16[1,8192]{1,0:T(2,128)(2,1)} %refs_0_.1), channel_id=1, source_target_pairs={{0,4},{4,0},{8,12},{12,8},{1,5},{5,1},{9,13},{13,9},{2,6},{6,2},{1... | collective-permute-start | bytes 49160 | tf_op jit(solution)/shard_map/ppermute | solution.py:419
  5.6 4.5 %copy-start = (bf16[1,8192]{1,0:T(2,128)(2,1)S(1)}, bf16[1,8192]{1,0:T(2,128)(2,1)}, u32[]{:S(2)}) copy-start(bf16[1,8192]{1,0:T(2,128)(2,1)} %refs_0_.1) | copy-start | bytes 49156
  10.2 7.3 %collective-permute-start.5 = (bf16[4,64,128]{2,1,0:T(8,128)(2,1)S(1)}, bf16[4,64,128]{2,1,0:T(8,128)(2,1)S(1)}, u32[]{:S(2)}, u32[]{:S(2)}) collective-permute-start(bf16[4,64,128]{2,1,0:T(8,128)(2,1)S(1)} %stack.1.refs_0_), channel_id=1, source_target_pairs={{0,18},{2,16},{16,2},{18,0},{1,19},{3,17},{17,3},{19,1},{4,22},{6,... | collective-permute-start | bytes 196616 | tf_op jit(solution)/shard_map/ppermute | solution.py:419
  12.7 4.8 %collective-permute-start.4 = (bf16[4,64,128]{2,1,0:T(8,128)(2,1)S(1)}, bf16[4,64,128]{2,1,0:T(8,128)(2,1)S(1)}, u32[]{:S(2)}, u32[]{:S(2)}) collective-permute-start(bf16[4,64,128]{2,1,0:T(8,128)(2,1)S(1)} %stack.1.refs_0_), channel_id=1, source_target_pairs={{0,16},{2,18},{16,0},{18,2},{1,17},{3,19},{17,1},{19,3},{4,20},{6,... | collective-permute-start | bytes 196616 | tf_op jit(solution)/shard_map/ppermute | solution.py:419
  13.2 4.3 %collective-permute-start.3 = (bf16[4,64,128]{2,1,0:T(8,128)(2,1)S(1)}, bf16[4,64,128]{2,1,0:T(8,128)(2,1)S(1)}, u32[]{:S(2)}, u32[]{:S(2)}) collective-permute-start(bf16[4,64,128]{2,1,0:T(8,128)(2,1)S(1)} %stack.1.refs_0_), channel_id=1, source_target_pairs={{0,2},{2,0},{16,18},{18,16},{1,3},{3,1},{17,19},{19,17},{4,6},{6,4... | collective-permute-start | bytes 196616 | tf_op jit(solution)/shard_map/ppermute | solution.py:419
  17.7 1.6 %collective-permute-start.6 = (bf16[16,8192]{1,0:T(8,128)(2,1)S(1)}, bf16[16,8192]{1,0:T(8,128)(2,1)S(1)}, u32[]{:S(2)}, u32[]{:S(2)}) collective-permute-start(bf16[16,8192]{1,0:T(8,128)(2,1)S(1)} %pack.1.near_ref), channel_id=1, source_target_pairs={{0,1},{1,0},{2,3},{3,2},{4,5},{5,4},{6,7},{7,6},{8,9},{9,8},{10,11... | collective-permute-start | bytes 786440 | tf_op jit(solution)/shard_map/ppermute | solution.py:419
  29.2 1.6 %collective-permute-start.7 = (bf16[16,64,128]{2,1,0:T(8,128)(2,1)S(1)}, bf16[16,64,128]{2,1,0:T(8,128)(2,1)S(1)}, u32[]{:S(2)}, u32[]{:S(2)}) collective-permute-start(bf16[16,64,128]{2,1,0:T(8,128)(2,1)S(1)} %get-tuple-element.16), channel_id=1, source_target_pairs={{0,1},{1,0},{2,3},{3,2},{4,5},{5,4},{6,7},{7,6},{8,9},{9,8},{10,11... | collective-permute-start | bytes 786440 | tf_op jit(solution)/shard_map/ppermute | solution.py:419
  30.9 5.6 %collective-permute-start.8 = (bf16[4,64,128]{2,1,0:T(8,128)(2,1)S(1)}, bf16[4,64,128]{2,1,0:T(8,128)(2,1)S(1)}, u32[]{:S(2)}, u32[]{:S(2)}) collective-permute-start(bf16[4,64,128]{2,1,0:T(8,128)(2,1)S(1)} %get-tuple-element.17), channel_id=1, source_target_pairs={{0,18},{2,16},{16,2},{18,0},{1,19},{3,17},{17,3},{19,1},{4,22},{6,... | collective-permute-start | bytes 196616 | tf_op jit(solution)/shard_map/ppermute | solution.py:419
  33.4 4.3 %collective-permute-start.10 = (bf16[4,64,128]{2,1,0:T(8,128)(2,1)S(1)}, bf16[4,64,128]{2,1,0:T(8,128)(2,1)S(1)}, u32[]{:S(2)}, u32[]{:S(2)}) collective-permute-start(bf16[4,64,128]{2,1,0:T(8,128)(2,1)S(1)} %get-tuple-element.18), channel_id=1, source_target_pairs={{0,2},{2,0},{16,18},{18,16},{1,3},{3,1},{17,19},{19,17},{4,6},{6,4... | collective-permute-start | bytes 196616 | tf_op jit(solution)/shard_map/ppermute | solution.py:419
  34.0 4.3 %collective-permute-start.9 = (bf16[4,64,128]{2,1,0:T(8,128)(2,1)S(1)}, bf16[4,64,128]{2,1,0:T(8,128)(2,1)S(1)}, u32[]{:S(2)}, u32[]{:S(2)}) collective-permute-start(bf16[4,64,128]{2,1,0:T(8,128)(2,1)S(1)} %get-tuple-element.19), channel_id=1, source_target_pairs={{0,16},{2,18},{16,0},{18,2},{1,17},{3,19},{17,1},{19,3},{4,20},{6,... | collective-permute-start | bytes 196616 | tf_op jit(solution)/shard_map/ppermute | solution.py:419
  38.3 5.6 %collective-permute-start.13 = (bf16[1,64,128]{2,1,0:T(8,128)(2,1)S(1)}, bf16[1,64,128]{2,1,0:T(8,128)(2,1)S(1)}, u32[]{:S(2)}, u32[]{:S(2)}) collective-permute-start(bf16[1,64,128]{2,1,0:T(8,128)(2,1)S(1)} %get-tuple-element.20), channel_id=1, source_target_pairs={{0,12},{4,8},{8,4},{12,0},{1,13},{5,9},{9,5},{13,1},{2,14},{6,10},... | collective-permute-start | bytes 49160 | tf_op jit(solution)/shard_map/ppermute | solution.py:419
  41.0 4.6 %collective-permute-start.12 = (bf16[1,64,128]{2,1,0:T(8,128)(2,1)S(1)}, bf16[1,64,128]{2,1,0:T(8,128)(2,1)S(1)}, u32[]{:S(2)}, u32[]{:S(2)}) collective-permute-start(bf16[1,64,128]{2,1,0:T(8,128)(2,1)S(1)} %get-tuple-element.21), channel_id=1, source_target_pairs={{0,8},{4,12},{8,0},{12,4},{1,9},{5,13},{9,1},{13,5},{2,10},{6,14},... | collective-permute-start | bytes 49160 | tf_op jit(solution)/shard_map/ppermute | solution.py:419
  41.0 4.6 %collective-permute-start.11 = (bf16[1,64,128]{2,1,0:T(8,128)(2,1)S(1)}, bf16[1,64,128]{2,1,0:T(8,128)(2,1)S(1)}, u32[]{:S(2)}, u32[]{:S(2)}) collective-permute-start(bf16[1,64,128]{2,1,0:T(8,128)(2,1)S(1)} %get-tuple-element.22), channel_id=1, source_target_pairs={{0,4},{4,0},{8,12},{12,8},{1,5},{5,1},{9,13},{13,9},{2,6},{6,2},{1... | collective-permute-start | bytes 49160 | tf_op jit(solution)/shard_map/ppermute | solution.py:419

commit v15 on v14

--- a/solution.py
+++ b/solution.py
@@ -313,7 +313,7 @@
     row = 0
     for step, deal in enumerate(deals):
         wait(step)
-        multiply(at, deal, rest_ref, row, True)
+        multiply(at, deal, rest_ref, row, step < pairs - 1)
         start()
         at += deal
         row += deal
@@ -349,7 +349,7 @@
     rows, depth = near.shape
     lines = depth // LANES
     rest = depth - sum(first.shape[0] for first in firsts)
-    deals = (rest * 3 // 7, rest - rest * 3 // 7)
+    deals = (rest * 3 // 8, rest * 3 // 8, rest // 4)
 
     def body(near_ref, far_ref, *refs):
         count = len(firsts)
@@ -370,7 +370,7 @@
             pltpu.VMEM((2 * rows, half), jnp.bfloat16),
             pltpu.VMEM((rest, 2 * half), jnp.bfloat16),
             pltpu.VMEM((half, depth), jnp.bfloat16),
-            pltpu.SemaphoreType.DMA((2, 2)),
+            pltpu.SemaphoreType.DMA((len(deals), 2)),
             pltpu.SemaphoreType.DMA((depth // (2 * CHUNK) + 1,)),
         ],
         compiler_params=pltpu.CompilerParams(
@@ -439,10 +439,10 @@
     others = range(1, lax.axis_size(square))
     rows = [0] + list(range(2, deep)) + [1]
     column = [swap(tokens, "z", at) if at else tokens for at in rows]
-    first, gain = load_first(w_gate, w_up, norm_gain.reshape(-1, LANES), half, 2 * CHUNK)
+    first, gain = load_first(w_gate, w_up, norm_gain.reshape(-1, LANES), half, 3 * CHUNK // 2)
     column = stack(rows, column, gain)
     plane = [column] + [swap(column, square, at) for at in others]
-    second, live = load_second(w_gate, w_up, half, 2 * CHUNK, 5 * CHUNK // 2, requests, place)
+    second, live = load_second(w_gate, w_up, half, 3 * CHUNK // 2, 5 * CHUNK // 2, requests, place)
     near = pack(plane, gain, live)
     far = swap(near, "core", 1)
     kept, sent = block(near, far, (first, second), w_gate, w_up, w_down, half)

time: 46.4 us -> 47.8 us (1.030)
  Pallas kernels: 17.8 us -> 19.1 us
    pallas_call x1, Pallas kernels: 9.88 us -> 11.7 us  [block(): pl.pallas_call(body, out_shape=(jax.ShapeDtypeStruct((rows, lines, LANES)...]
    pallas_call x1, Pallas kernels: 3.22 us -> 2.65 us  [load_first(): pl.pallas_call(functools.partial(load_gain_kernel, half), out_shape=(pltp...]
  transfers between devices with their start and end apart: 14 -> 14, of which waited for: 8 -> 8; matrix products, arithmetic and copies ran while one was open for 0% -> 0% of each run, Pallas kernels for 15% -> 13%
where the time goes in v15:
time: 47.8 us; the launch traced here: 47.7 us
  Pallas kernels  19.1 us (40%)
  starting transfers between devices  17.5 us (37%)
  waiting for transfers between devices  10.9 us (23%)
    ppermute x14, starting transfers between devices, swap(): lax.ppermute(value, axes, [(place, place ^ offset) for place in places])  17.5 us
    pallas_call x1, Pallas kernels, block(): pl.pallas_call(body, out_shape=(jax.ShapeDtypeStruct((rows, lines, LANES)...  11.7 us
    ppermute x14, waiting for transfers between devices, swap(): lax.ppermute(value, axes, [(place, place ^ offset) for place in places])  10.9 us
    pallas_call x1, Pallas kernels, load_second(): pl.pallas_call(functools.partial(load_second_kernel, half, row, place), o...  3.78 us
    pallas_call x1, Pallas kernels, load_first(): pl.pallas_call(functools.partial(load_gain_kernel, half), out_shape=(pltp...  2.65 us
  transfers between devices with their start and end apart: 14, of which 8 were waited for; matrix products, arithmetic and copies ran while one was open for 0% of the time, Pallas kernels for 13%

profile of v15, /device:TPU:0, one launch (start us, length us, event | category | flops | bytes accessed | tf_op | source)
XLA Modules:
  0.0 47.7 jit_solution(4513902529788661160)
XLA Ops:
  0.0 5.0 %collective-permute-start.1 = (bf16[1,8192]{1,0:T(2,128)(2,1)}, bf16[1,8192]{1,0:T(2,128)(2,1)S(1)}, u32[]{:S(2)}, u32[]{:S(2)}) collective-permute-start(bf16[1,8192]{1,0:T(2,128)(2,1)} %refs_0_.1), channel_id=1, source_target_pairs={{0,12},{4,8},{8,4},{12,0},{1,13},{5,9},{9,5},{13,1},{2,14},{6,10},... | collective-permute-start | bytes 49160 | tf_op jit(solution)/shard_map/ppermute | solution.py:419
  5.0 0.0 collective-permute-start
  5.1 0.6 %collective-permute-start.2 = (bf16[1,8192]{1,0:T(2,128)(2,1)}, bf16[1,8192]{1,0:T(2,128)(2,1)S(1)}, u32[]{:S(2)}, u32[]{:S(2)}) collective-permute-start(bf16[1,8192]{1,0:T(2,128)(2,1)} %refs_0_.1), channel_id=1, source_target_pairs={{0,4},{4,0},{8,12},{12,8},{1,5},{5,1},{9,13},{13,9},{2,6},{6,2},{1... | collective-permute-start | bytes 49160 | tf_op jit(solution)/shard_map/ppermute | solution.py:419
  5.6 0.0 copy-start
  5.6 2.7 %load_first.1 = (bf16[1536,1792]{1,0:T(8,128)(2,1)S(1)}, bf16[64,128]{1,0:T(8,128)(2,1)S(1)}) custom-call(bf16[8192,1792]{1,0:T(8,128)(2,1)} %refs_2_.1, bf16[8192,1792]{1,0:T(8,128)(2,1)} %refs_3_.1, bf16[64,128]{1,0:T(8,128)(2,1)} %bitcast.1), custom_call_target="tpu_custom_call" | custom-call | bytes 5505024 | tf_op jit(solution)/shard_map/load_first/pallas_call | solution.py:110
  8.3 0.0 collective-permute-done.1.refs_2_
  8.3 1.8 %collective-permute-done.refs_1_ = bf16[1,8192]{1,0:T(2,128)(2,1)S(1)} collective-permute-done((bf16[1,8192]{1,0:T(2,128)(2,1)}, bf16[1,8192]{1,0:T(2,128)(2,1)S(1)}, u32[]{:S(2)}, u32[]{:S(2)}) %collective-permute-start) | collective-permute-done | bytes 16416 | tf_op jit(solution)/shard_map/ppermute | solution.py:419
  10.1 0.0 collective-permute-done.2.refs_3_
  10.1 0.0 copy-done
  10.1 0.1 stack.1.refs_0_
  10.2 2.5 %collective-permute-start.5 = (bf16[4,64,128]{2,1,0:T(8,128)(2,1)S(1)}, bf16[4,64,128]{2,1,0:T(8,128)(2,1)S(1)}, u32[]{:S(2)}, u32[]{:S(2)}) collective-permute-start(bf16[4,64,128]{2,1,0:T(8,128)(2,1)S(1)} %stack.1.refs_0_), channel_id=1, source_target_pairs={{0,18},{2,16},{16,2},{18,0},{1,19},{3,17},{17,3},{19,1},{4,22},{6,... | collective-permute-start | bytes 196616 | tf_op jit(solution)/shard_map/ppermute | solution.py:419
  12.7 0.5 %collective-permute-start.4 = (bf16[4,64,128]{2,1,0:T(8,128)(2,1)S(1)}, bf16[4,64,128]{2,1,0:T(8,128)(2,1)S(1)}, u32[]{:S(2)}, u32[]{:S(2)}) collective-permute-start(bf16[4,64,128]{2,1,0:T(8,128)(2,1)S(1)} %stack.1.refs_0_), channel_id=1, source_target_pairs={{0,16},{2,18},{16,0},{18,2},{1,17},{3,19},{17,1},{19,3},{4,20},{6,... | collective-permute-start | bytes 196616 | tf_op jit(solution)/shard_map/ppermute | solution.py:419
  13.2 0.5 %collective-permute-start.3 = (bf16[4,64,128]{2,1,0:T(8,128)(2,1)S(1)}, bf16[4,64,128]{2,1,0:T(8,128)(2,1)S(1)}, u32[]{:S(2)}, u32[]{:S(2)}) collective-permute-start(bf16[4,64,128]{2,1,0:T(8,128)(2,1)S(1)} %stack.1.refs_0_), channel_id=1, source_target_pairs={{0,2},{2,0},{16,18},{18,16},{1,3},{3,1},{17,19},{19,17},{4,6},{6,4... | collective-permute-start | bytes 196616 | tf_op jit(solution)/shard_map/ppermute | solution.py:419
  13.7 3.8 %load_second.1 = (bf16[2560,1792]{1,0:T(8,128)(2,1)S(1)}, f32[8,128]{1,0:T(8,128)S(1)}) custom-call(s32[8]{0:T(128)} %lengths.1, s32[8]{0:T(128)} %hit_lengths.1, s32[8]{0:T(128)} %start_positions.1, bf16[8192,1792]{1,0:T(8,128)(2,1)} %refs_2_.1, bf16[8192,1792]{1,0:T(8,128)(2,1)} %refs_3_.1), custom_call_target="tpu_custom_call" | custom-call | bytes 9175040 | tf_op jit(solution)/shard_map/load_second/pallas_call | solution.py:169
  17.5 0.0 collective-permute-done.5.refs_3_
  17.5 0.0 collective-permute-done.4.refs_2_
  17.5 0.0 collective-permute-done.3.refs_1_
  17.5 0.2 pack.1.near_ref
  17.7 0.1 collective-permute-start.6
  17.8 1.5 %collective-permute-done.6.far_ref = bf16[16,8192]{1,0:T(8,128)(2,1)S(1)} collective-permute-done((bf16[16,8192]{1,0:T(8,128)(2,1)S(1)}, bf16[16,8192]{1,0:T(8,128)(2,1)S(1)}, u32[]{:S(2)}, u32[]{:S(2)}) %collective-permute-start.6) | collective-permute-done | bytes 262176 | tf_op jit(solution)/shard_map/ppermute | solution.py:419
  19.3 11.7 %block.1 = (f32[16,64,128]{2,1,0:T(8,128)S(1)}, bf16[16,64,128]{2,1,0:T(8,128)(2,1)S(1)}) custom-call(bf16[16,8192]{1,0:T(8,128)(2,1)S(1)} %pack.1.near_ref, bf16[16,8192]{1,0:T(8,128)(2,1)S(1)} %collective-permute-done.6.far_ref, bf16[1536,1792]{1,0:T(8,128)(2,1)S(1)} %get-tuple-element.13.refs_0_, bf16[2560,1792]{1,0:T(8,128)(2,1)S(1)} %get-tuple-element.14.refs_1_, ...), custom_call_target="tpu_custom_call" | custom-call | flops 1409286144 | bytes 29360128 | tf_op jit(solution)/shard_map/block/pallas_call | solution.py:358
  31.1 0.2 collective-permute-start.7
  31.3 1.4 %collective-permute-done.7 = bf16[16,64,128]{2,1,0:T(8,128)(2,1)S(1)} collective-permute-done((bf16[16,64,128]{2,1,0:T(8,128)(2,1)S(1)}, bf16[16,64,128]{2,1,0:T(8,128)(2,1)S(1)}, u32[]{:S(2)}, u32[]{:S(2)}) %collective-permute-start.7) | collective-permute-done | bytes 262176 | tf_op jit(solution)/shard_map/ppermute | solution.py:419
  32.7 0.1 add_convert_fusion
  32.8 2.5 %collective-permute-start.8 = (bf16[4,64,128]{2,1,0:T(8,128)(2,1)S(1)}, bf16[4,64,128]{2,1,0:T(8,128)(2,1)S(1)}, u32[]{:S(2)}, u32[]{:S(2)}) collective-permute-start(bf16[4,64,128]{2,1,0:T(8,128)(2,1)S(1)} %get-tuple-element.17), channel_id=1, source_target_pairs={{0,18},{2,16},{16,2},{18,0},{1,19},{3,17},{17,3},{19,1},{4,22},{6,... | collective-permute-start | bytes 196616 | tf_op jit(solution)/shard_map/ppermute | solution.py:419
  35.3 0.5 %collective-permute-start.10 = (bf16[4,64,128]{2,1,0:T(8,128)(2,1)S(1)}, bf16[4,64,128]{2,1,0:T(8,128)(2,1)S(1)}, u32[]{:S(2)}, u32[]{:S(2)}) collective-permute-start(bf16[4,64,128]{2,1,0:T(8,128)(2,1)S(1)} %get-tuple-element.18), channel_id=1, source_target_pairs={{0,2},{2,0},{16,18},{18,16},{1,3},{3,1},{17,19},{19,17},{4,6},{6,4... | collective-permute-start | bytes 196616 | tf_op jit(solution)/shard_map/ppermute | solution.py:419
  35.8 0.5 %collective-permute-start.9 = (bf16[4,64,128]{2,1,0:T(8,128)(2,1)S(1)}, bf16[4,64,128]{2,1,0:T(8,128)(2,1)S(1)}, u32[]{:S(2)}, u32[]{:S(2)}) collective-permute-start(bf16[4,64,128]{2,1,0:T(8,128)(2,1)S(1)} %get-tuple-element.19), channel_id=1, source_target_pairs={{0,16},{2,18},{16,0},{18,2},{1,17},{3,19},{17,1},{19,3},{4,20},{6,... | collective-permute-start | bytes 196616 | tf_op jit(solution)/shard_map/ppermute | solution.py:419
  36.4 2.1 %collective-permute-done.8 = bf16[4,64,128]{2,1,0:T(8,128)(2,1)S(1)} collective-permute-done((bf16[4,64,128]{2,1,0:T(8,128)(2,1)S(1)}, bf16[4,64,128]{2,1,0:T(8,128)(2,1)S(1)}, u32[]{:S(2)}, u32[]{:S(2)}) %collective-permute-start.8) | collective-permute-done | bytes 65568 | tf_op jit(solution)/shard_map/ppermute | solution.py:419
  38.4 1.1 %collective-permute-done.10 = bf16[4,64,128]{2,1,0:T(8,128)(2,1)S(1)} collective-permute-done((bf16[4,64,128]{2,1,0:T(8,128)(2,1)S(1)}, bf16[4,64,128]{2,1,0:T(8,128)(2,1)S(1)}, u32[]{:S(2)}, u32[]{:S(2)}) %collective-permute-start.10) | collective-permute-done | bytes 65568 | tf_op jit(solution)/shard_map/ppermute | solution.py:419
  39.5 0.5 %collective-permute-done.9 = bf16[4,64,128]{2,1,0:T(8,128)(2,1)S(1)} collective-permute-done((bf16[4,64,128]{2,1,0:T(8,128)(2,1)S(1)}, bf16[4,64,128]{2,1,0:T(8,128)(2,1)S(1)}, u32[]{:S(2)}, u32[]{:S(2)}) %collective-permute-start.9) | collective-permute-done | bytes 65568 | tf_op jit(solution)/shard_map/ppermute | solution.py:419
  40.1 2.1 %collective-permute-start.13 = (bf16[1,64,128]{2,1,0:T(8,128)(2,1)S(1)}, bf16[1,64,128]{2,1,0:T(8,128)(2,1)S(1)}, u32[]{:S(2)}, u32[]{:S(2)}) collective-permute-start(bf16[1,64,128]{2,1,0:T(8,128)(2,1)S(1)} %get-tuple-element.20), channel_id=1, source_target_pairs={{0,12},{4,8},{8,4},{12,0},{1,13},{5,9},{9,5},{13,1},{2,14},{6,10},... | collective-permute-start | bytes 49160 | tf_op jit(solution)/shard_map/ppermute | solution.py:419
  42.3 0.0 collective-permute-start.12
  42.3 2.3 %collective-permute-start.11 = (bf16[1,64,128]{2,1,0:T(8,128)(2,1)S(1)}, bf16[1,64,128]{2,1,0:T(8,128)(2,1)S(1)}, u32[]{:S(2)}, u32[]{:S(2)}) collective-permute-start(bf16[1,64,128]{2,1,0:T(8,128)(2,1)S(1)} %get-tuple-element.22), channel_id=1, source_target_pairs={{0,4},{4,0},{8,12},{12,8},{1,5},{5,1},{9,13},{13,9},{2,6},{6,2},{1... | collective-permute-start | bytes 49160 | tf_op jit(solution)/shard_map/ppermute | solution.py:419
  44.6 1.3 %collective-permute-done.13.refs_3_ = bf16[1,64,128]{2,1,0:T(8,128)(2,1)S(1)} collective-permute-done((bf16[1,64,128]{2,1,0:T(8,128)(2,1)S(1)}, bf16[1,64,128]{2,1,0:T(8,128)(2,1)S(1)}, u32[]{:S(2)}, u32[]{:S(2)}) %collective-permute-start.13) | collective-permute-done | bytes 16416 | tf_op jit(solution)/shard_map/ppermute | solution.py:419
  45.9 1.2 %collective-permute-done.12.refs_2_ = bf16[1,64,128]{2,1,0:T(8,128)(2,1)S(1)} collective-permute-done((bf16[1,64,128]{2,1,0:T(8,128)(2,1)S(1)}, bf16[1,64,128]{2,1,0:T(8,128)(2,1)S(1)}, u32[]{:S(2)}, u32[]{:S(2)}) %collective-permute-start.12) | collective-permute-done | bytes 16416 | tf_op jit(solution)/shard_map/ppermute | solution.py:419
  47.0 0.0 collective-permute-done.11.refs_1_
  47.0 0.7 %finish.1 = bf16[1,8192]{1,0:T(2,128)(2,1)} custom-call(bf16[1,64,128]{2,1,0:T(8,128)(2,1)S(1)} %get-tuple-element.23.refs_0_, bf16[1,64,128]{2,1,0:T(8,128)(2,1)S(1)} %collective-permute-done.11.refs_1_, bf16[1,64,128]{2,1,0:T(8,128)(2,1)S(1)} %collective-permute-done.12.refs_2_, bf16[1,64,128]{2,1,0:T(8,128)(2,1)S(1)} %collective-permute-done.13.refs_3_, ...), custom_call_target="tpu_custom_call" | custom-call | tf_op jit(solution)/shard_map/finish/pallas_call | solution.py:407
  (3 shorter events, 0.1 us)
Async XLA Ops:
  0.0 8.3 %collective-permute-start.1 = (bf16[1,8192]{1,0:T(2,128)(2,1)}, bf16[1,8192]{1,0:T(2,128)(2,1)S(1)}, u32[]{:S(2)}, u32[]{:S(2)}) collective-permute-start(bf16[1,8192]{1,0:T(2,128)(2,1)} %refs_0_.1), channel_id=1, source_target_pairs={{0,12},{4,8},{8,4},{12,0},{1,13},{5,9},{9,5},{13,1},{2,14},{6,10},... | collective-permute-start | bytes 49160 | tf_op jit(solution)/shard_map/ppermute | solution.py:419
  5.0 5.0 %collective-permute-start = (bf16[1,8192]{1,0:T(2,128)(2,1)}, bf16[1,8192]{1,0:T(2,128)(2,1)S(1)}, u32[]{:S(2)}, u32[]{:S(2)}) collective-permute-start(bf16[1,8192]{1,0:T(2,128)(2,1)} %refs_0_.1), channel_id=1, source_target_pairs={{0,8},{4,12},{8,0},{12,4},{1,9},{5,13},{9,1},{13,5},{2,10},{6,14},... | collective-permute-start | bytes 49160 | tf_op jit(solution)/shard_map/ppermute | solution.py:419
  5.1 5.0 %collective-permute-start.2 = (bf16[1,8192]{1,0:T(2,128)(2,1)}, bf16[1,8192]{1,0:T(2,128)(2,1)S(1)}, u32[]{:S(2)}, u32[]{:S(2)}) collective-permute-start(bf16[1,8192]{1,0:T(2,128)(2,1)} %refs_0_.1), channel_id=1, source_target_pairs={{0,4},{4,0},{8,12},{12,8},{1,5},{5,1},{9,13},{13,9},{2,6},{6,2},{1... | collective-permute-start | bytes 49160 | tf_op jit(solution)/shard_map/ppermute | solution.py:419
  5.6 4.5 %copy-start = (bf16[1,8192]{1,0:T(2,128)(2,1)S(1)}, bf16[1,8192]{1,0:T(2,128)(2,1)}, u32[]{:S(2)}) copy-start(bf16[1,8192]{1,0:T(2,128)(2,1)} %refs_0_.1) | copy-start | bytes 49156
  10.2 7.3 %collective-permute-start.5 = (bf16[4,64,128]{2,1,0:T(8,128)(2,1)S(1)}, bf16[4,64,128]{2,1,0:T(8,128)(2,1)S(1)}, u32[]{:S(2)}, u32[]{:S(2)}) collective-permute-start(bf16[4,64,128]{2,1,0:T(8,128)(2,1)S(1)} %stack.1.refs_0_), channel_id=1, source_target_pairs={{0,18},{2,16},{16,2},{18,0},{1,19},{3,17},{17,3},{19,1},{4,22},{6,... | collective-permute-start | bytes 196616 | tf_op jit(solution)/shard_map/ppermute | solution.py:419
  12.7 4.8 %collective-permute-start.4 = (bf16[4,64,128]{2,1,0:T(8,128)(2,1)S(1)}, bf16[4,64,128]{2,1,0:T(8,128)(2,1)S(1)}, u32[]{:S(2)}, u32[]{:S(2)}) collective-permute-start(bf16[4,64,128]{2,1,0:T(8,128)(2,1)S(1)} %stack.1.refs_0_), channel_id=1, source_target_pairs={{0,16},{2,18},{16,0},{18,2},{1,17},{3,19},{17,1},{19,3},{4,20},{6,... | collective-permute-start | bytes 196616 | tf_op jit(solution)/shard_map/ppermute | solution.py:419
  13.2 4.3 %collective-permute-start.3 = (bf16[4,64,128]{2,1,0:T(8,128)(2,1)S(1)}, bf16[4,64,128]{2,1,0:T(8,128)(2,1)S(1)}, u32[]{:S(2)}, u32[]{:S(2)}) collective-permute-start(bf16[4,64,128]{2,1,0:T(8,128)(2,1)S(1)} %stack.1.refs_0_), channel_id=1, source_target_pairs={{0,2},{2,0},{16,18},{18,16},{1,3},{3,1},{17,19},{19,17},{4,6},{6,4... | collective-permute-start | bytes 196616 | tf_op jit(solution)/shard_map/ppermute | solution.py:419
  17.7 1.6 %collective-permute-start.6 = (bf16[16,8192]{1,0:T(8,128)(2,1)S(1)}, bf16[16,8192]{1,0:T(8,128)(2,1)S(1)}, u32[]{:S(2)}, u32[]{:S(2)}) collective-permute-start(bf16[16,8192]{1,0:T(8,128)(2,1)S(1)} %pack.1.near_ref), channel_id=1, source_target_pairs={{0,1},{1,0},{2,3},{3,2},{4,5},{5,4},{6,7},{7,6},{8,9},{9,8},{10,11... | collective-permute-start | bytes 786440 | tf_op jit(solution)/shard_map/ppermute | solution.py:419
  31.1 1.6 %collective-permute-start.7 = (bf16[16,64,128]{2,1,0:T(8,128)(2,1)S(1)}, bf16[16,64,128]{2,1,0:T(8,128)(2,1)S(1)}, u32[]{:S(2)}, u32[]{:S(2)}) collective-permute-start(bf16[16,64,128]{2,1,0:T(8,128)(2,1)S(1)} %get-tuple-element.16), channel_id=1, source_target_pairs={{0,1},{1,0},{2,3},{3,2},{4,5},{5,4},{6,7},{7,6},{8,9},{9,8},{10,11... | collective-permute-start | bytes 786440 | tf_op jit(solution)/shard_map/ppermute | solution.py:419
  32.8 5.6 %collective-permute-start.8 = (bf16[4,64,128]{2,1,0:T(8,128)(2,1)S(1)}, bf16[4,64,128]{2,1,0:T(8,128)(2,1)S(1)}, u32[]{:S(2)}, u32[]{:S(2)}) collective-permute-start(bf16[4,64,128]{2,1,0:T(8,128)(2,1)S(1)} %get-tuple-element.17), channel_id=1, source_target_pairs={{0,18},{2,16},{16,2},{18,0},{1,19},{3,17},{17,3},{19,1},{4,22},{6,... | collective-permute-start | bytes 196616 | tf_op jit(solution)/shard_map/ppermute | solution.py:419
  35.3 4.3 %collective-permute-start.10 = (bf16[4,64,128]{2,1,0:T(8,128)(2,1)S(1)}, bf16[4,64,128]{2,1,0:T(8,128)(2,1)S(1)}, u32[]{:S(2)}, u32[]{:S(2)}) collective-permute-start(bf16[4,64,128]{2,1,0:T(8,128)(2,1)S(1)} %get-tuple-element.18), channel_id=1, source_target_pairs={{0,2},{2,0},{16,18},{18,16},{1,3},{3,1},{17,19},{19,17},{4,6},{6,4... | collective-permute-start | bytes 196616 | tf_op jit(solution)/shard_map/ppermute | solution.py:419
  35.8 4.3 %collective-permute-start.9 = (bf16[4,64,128]{2,1,0:T(8,128)(2,1)S(1)}, bf16[4,64,128]{2,1,0:T(8,128)(2,1)S(1)}, u32[]{:S(2)}, u32[]{:S(2)}) collective-permute-start(bf16[4,64,128]{2,1,0:T(8,128)(2,1)S(1)} %get-tuple-element.19), channel_id=1, source_target_pairs={{0,16},{2,18},{16,0},{18,2},{1,17},{3,19},{17,1},{19,3},{4,20},{6,... | collective-permute-start | bytes 196616 | tf_op jit(solution)/shard_map/ppermute | solution.py:419
  40.1 5.7 %collective-permute-start.13 = (bf16[1,64,128]{2,1,0:T(8,128)(2,1)S(1)}, bf16[1,64,128]{2,1,0:T(8,128)(2,1)S(1)}, u32[]{:S(2)}, u32[]{:S(2)}) collective-permute-start(bf16[1,64,128]{2,1,0:T(8,128)(2,1)S(1)} %get-tuple-element.20), channel_id=1, source_target_pairs={{0,12},{4,8},{8,4},{12,0},{1,13},{5,9},{9,5},{13,1},{2,14},{6,10},... | collective-permute-start | bytes 49160 | tf_op jit(solution)/shard_map/ppermute | solution.py:419
  42.3 4.8 %collective-permute-start.12 = (bf16[1,64,128]{2,1,0:T(8,128)(2,1)S(1)}, bf16[1,64,128]{2,1,0:T(8,128)(2,1)S(1)}, u32[]{:S(2)}, u32[]{:S(2)}) collective-permute-start(bf16[1,64,128]{2,1,0:T(8,128)(2,1)S(1)} %get-tuple-element.21), channel_id=1, source_target_pairs={{0,8},{4,12},{8,0},{12,4},{1,9},{5,13},{9,1},{13,5},{2,10},{6,14},... | collective-permute-start | bytes 49160 | tf_op jit(solution)/shard_map/ppermute | solution.py:419
  42.3 4.7 %collective-permute-start.11 = (bf16[1,64,128]{2,1,0:T(8,128)(2,1)S(1)}, bf16[1,64,128]{2,1,0:T(8,128)(2,1)S(1)}, u32[]{:S(2)}, u32[]{:S(2)}) collective-permute-start(bf16[1,64,128]{2,1,0:T(8,128)(2,1)S(1)} %get-tuple-element.22), channel_id=1, source_target_pairs={{0,4},{4,0},{8,12},{12,8},{1,5},{5,1},{9,13},{13,9},{2,6},{6,2},{1... | collective-permute-start | bytes 49160 | tf_op jit(solution)/shard_map/ppermute | solution.py:419

commit v16 on v14

--- a/solution.py
+++ b/solution.py
@@ -287,15 +287,18 @@
         for copy in loads[number]:
             copy.wait()
 
-    def multiply(at, count, ref, row, halfway):
+    def multiply(terms, first, halfway):
         for column in range(0, 2 * half, tile):
             columns = pl.ds(column, min(tile, 2 * half - column))
-            value = jnp.dot(
-                rows_ref[:, at : at + count],
-                ref[row : row + count, columns],
-                preferred_element_type=jnp.float32,
-            )
-            if at == 0:
+            value = None
+            for at, count, ref, row in terms:
+                term = jnp.dot(
+                    rows_ref[:, at : at + count],
+                    ref[row : row + count, columns],
+                    preferred_element_type=jnp.float32,
+                )
+                value = term if value is None else value + term
+            if first:
                 product_ref[:, columns] = value
             else:
                 product_ref[:, columns] += value
@@ -306,14 +309,16 @@
     rows_ref[: rows // 2] = near_ref[...]
     rows_ref[rows // 2 :] = far_ref[...]
     at = 0
+    held = []
     for ref in first_refs:
-        multiply(at, ref.shape[0], ref, 0, False)
-        start()
+        held.append((at, ref.shape[0], ref, 0))
         at += ref.shape[0]
+    multiply(held, True, True)
+    start()
     row = 0
     for step, deal in enumerate(deals):
         wait(step)
-        multiply(at, deal, rest_ref, row, True)
+        multiply([(at, deal, rest_ref, row)], False, True)
         start()
         at += deal
         row += deal

time: 46.4 us -> 49 us (1.056)
  Pallas kernels: 17.8 us -> 20.4 us
    pallas_call x1, Pallas kernels: 9.88 us -> 12.5 us  [block(): pl.pallas_call(body, out_shape=(jax.ShapeDtypeStruct((rows, lines, LANES)...]
  transfers between devices with their start and end apart: 14 -> 14, of which waited for: 8 -> 8; matrix products, arithmetic and copies ran while one was open for 0% -> 0% of each run, Pallas kernels for 15% -> 14%
where the time goes in v16:
time: 49 us; the launch traced here: 48.9 us
  Pallas kernels  20.4 us (42%)
  starting transfers between devices  17.4 us (36%)
  waiting for transfers between devices  10.8 us (22%)
    ppermute x14, starting transfers between devices, swap(): lax.ppermute(value, axes, [(place, place ^ offset) for place in places])  17.4 us
    pallas_call x1, Pallas kernels, block(): pl.pallas_call(body, out_shape=(jax.ShapeDtypeStruct((rows, lines, LANES)...  12.5 us
    ppermute x14, waiting for transfers between devices, swap(): lax.ppermute(value, axes, [(place, place ^ offset) for place in places])  10.8 us
    pallas_call x1, Pallas kernels, load_second(): pl.pallas_call(functools.partial(load_second_kernel, half, row, place), o...  3.74 us
    pallas_call x1, Pallas kernels, load_first(): pl.pallas_call(functools.partial(load_gain_kernel, half), out_shape=(pltp...  3.22 us
  transfers between devices with their start and end apart: 14, of which 8 were waited for; matrix products, arithmetic and copies ran while one was open for 0% of the time, Pallas kernels for 14%

profile of v16, /device:TPU:0, one launch (start us, length us, event | category | flops | bytes accessed | tf_op | source)
XLA Modules:
  0.0 48.9 jit_solution(9051824718884254648)
XLA Ops:
  0.0 5.0 %collective-permute-start.1 = (bf16[1,8192]{1,0:T(2,128)(2,1)}, bf16[1,8192]{1,0:T(2,128)(2,1)S(1)}, u32[]{:S(2)}, u32[]{:S(2)}) collective-permute-start(bf16[1,8192]{1,0:T(2,128)(2,1)} %refs_0_.1), channel_id=1, source_target_pairs={{0,12},{4,8},{8,4},{12,0},{1,13},{5,9},{9,5},{13,1},{2,14},{6,10},... | collective-permute-start | bytes 49160 | tf_op jit(solution)/shard_map/ppermute | solution.py:424
  5.0 0.0 collective-permute-start
  5.1 0.6 %collective-permute-start.2 = (bf16[1,8192]{1,0:T(2,128)(2,1)}, bf16[1,8192]{1,0:T(2,128)(2,1)S(1)}, u32[]{:S(2)}, u32[]{:S(2)}) collective-permute-start(bf16[1,8192]{1,0:T(2,128)(2,1)} %refs_0_.1), channel_id=1, source_target_pairs={{0,4},{4,0},{8,12},{12,8},{1,5},{5,1},{9,13},{13,9},{2,6},{6,2},{1... | collective-permute-start | bytes 49160 | tf_op jit(solution)/shard_map/ppermute | solution.py:424
  5.6 0.0 copy-start
  5.6 3.2 %load_first.1 = (bf16[2048,1792]{1,0:T(8,128)(2,1)S(1)}, bf16[64,128]{1,0:T(8,128)(2,1)S(1)}) custom-call(bf16[8192,1792]{1,0:T(8,128)(2,1)} %refs_2_.1, bf16[8192,1792]{1,0:T(8,128)(2,1)} %refs_3_.1, bf16[64,128]{1,0:T(8,128)(2,1)} %bitcast.1), custom_call_target="tpu_custom_call" | custom-call | bytes 7340032 | tf_op jit(solution)/shard_map/load_first/pallas_call | solution.py:110
  8.8 0.0 collective-permute-done.1.refs_2_
  8.9 1.2 %collective-permute-done.refs_1_ = bf16[1,8192]{1,0:T(2,128)(2,1)S(1)} collective-permute-done((bf16[1,8192]{1,0:T(2,128)(2,1)}, bf16[1,8192]{1,0:T(2,128)(2,1)S(1)}, u32[]{:S(2)}, u32[]{:S(2)}) %collective-permute-start) | collective-permute-done | bytes 16416 | tf_op jit(solution)/shard_map/ppermute | solution.py:424
  10.1 0.0 collective-permute-done.2.refs_3_
  10.1 0.0 copy-done
  10.1 0.1 stack.1.refs_0_
  10.2 2.5 %collective-permute-start.5 = (bf16[4,64,128]{2,1,0:T(8,128)(2,1)S(1)}, bf16[4,64,128]{2,1,0:T(8,128)(2,1)S(1)}, u32[]{:S(2)}, u32[]{:S(2)}) collective-permute-start(bf16[4,64,128]{2,1,0:T(8,128)(2,1)S(1)} %stack.1.refs_0_), channel_id=1, source_target_pairs={{0,18},{2,16},{16,2},{18,0},{1,19},{3,17},{17,3},{19,1},{4,22},{6,... | collective-permute-start | bytes 196616 | tf_op jit(solution)/shard_map/ppermute | solution.py:424
  12.7 0.5 %collective-permute-start.4 = (bf16[4,64,128]{2,1,0:T(8,128)(2,1)S(1)}, bf16[4,64,128]{2,1,0:T(8,128)(2,1)S(1)}, u32[]{:S(2)}, u32[]{:S(2)}) collective-permute-start(bf16[4,64,128]{2,1,0:T(8,128)(2,1)S(1)} %stack.1.refs_0_), channel_id=1, source_target_pairs={{0,16},{2,18},{16,0},{18,2},{1,17},{3,19},{17,1},{19,3},{4,20},{6,... | collective-permute-start | bytes 196616 | tf_op jit(solution)/shard_map/ppermute | solution.py:424
  13.2 0.5 %collective-permute-start.3 = (bf16[4,64,128]{2,1,0:T(8,128)(2,1)S(1)}, bf16[4,64,128]{2,1,0:T(8,128)(2,1)S(1)}, u32[]{:S(2)}, u32[]{:S(2)}) collective-permute-start(bf16[4,64,128]{2,1,0:T(8,128)(2,1)S(1)} %stack.1.refs_0_), channel_id=1, source_target_pairs={{0,2},{2,0},{16,18},{18,16},{1,3},{3,1},{17,19},{19,17},{4,6},{6,4... | collective-permute-start | bytes 196616 | tf_op jit(solution)/shard_map/ppermute | solution.py:424
  13.7 3.7 %load_second.1 = (bf16[2560,1792]{1,0:T(8,128)(2,1)S(1)}, f32[8,128]{1,0:T(8,128)S(1)}) custom-call(s32[8]{0:T(128)} %lengths.1, s32[8]{0:T(128)} %hit_lengths.1, s32[8]{0:T(128)} %start_positions.1, bf16[8192,1792]{1,0:T(8,128)(2,1)} %refs_2_.1, bf16[8192,1792]{1,0:T(8,128)(2,1)} %refs_3_.1), custom_call_target="tpu_custom_call" | custom-call | bytes 9175040 | tf_op jit(solution)/shard_map/load_second/pallas_call | solution.py:169
  17.5 0.0 collective-permute-done.5.refs_3_
  17.5 0.0 collective-permute-done.4.refs_2_
  17.5 0.0 collective-permute-done.3.refs_1_
  17.5 0.2 pack.1.near_ref
  17.7 0.1 collective-permute-start.6
  17.8 1.5 %collective-permute-done.6.far_ref = bf16[16,8192]{1,0:T(8,128)(2,1)S(1)} collective-permute-done((bf16[16,8192]{1,0:T(8,128)(2,1)S(1)}, bf16[16,8192]{1,0:T(8,128)(2,1)S(1)}, u32[]{:S(2)}, u32[]{:S(2)}) %collective-permute-start.6) | collective-permute-done | bytes 262176 | tf_op jit(solution)/shard_map/ppermute | solution.py:424
  19.3 12.5 %block.1 = (f32[16,64,128]{2,1,0:T(8,128)S(1)}, bf16[16,64,128]{2,1,0:T(8,128)(2,1)S(1)}) custom-call(bf16[16,8192]{1,0:T(8,128)(2,1)S(1)} %pack.1.near_ref, bf16[16,8192]{1,0:T(8,128)(2,1)S(1)} %collective-permute-done.6.far_ref, bf16[2048,1792]{1,0:T(8,128)(2,1)S(1)} %get-tuple-element.13.refs_0_, bf16[2560,1792]{1,0:T(8,128)(2,1)S(1)} %get-tuple-element.14.refs_1_, ...), custom_call_target="tpu_custom_call" | custom-call | flops 1409286144 | bytes 27525120 | tf_op jit(solution)/shard_map/block/pallas_call | solution.py:363
  31.8 0.2 collective-permute-start.7
  32.0 1.4 %collective-permute-done.7 = bf16[16,64,128]{2,1,0:T(8,128)(2,1)S(1)} collective-permute-done((bf16[16,64,128]{2,1,0:T(8,128)(2,1)S(1)}, bf16[16,64,128]{2,1,0:T(8,128)(2,1)S(1)}, u32[]{:S(2)}, u32[]{:S(2)}) %collective-permute-start.7) | collective-permute-done | bytes 262176 | tf_op jit(solution)/shard_map/ppermute | solution.py:424
  33.4 0.1 add_convert_fusion
  33.5 2.5 %collective-permute-start.8 = (bf16[4,64,128]{2,1,0:T(8,128)(2,1)S(1)}, bf16[4,64,128]{2,1,0:T(8,128)(2,1)S(1)}, u32[]{:S(2)}, u32[]{:S(2)}) collective-permute-start(bf16[4,64,128]{2,1,0:T(8,128)(2,1)S(1)} %get-tuple-element.17), channel_id=1, source_target_pairs={{0,18},{2,16},{16,2},{18,0},{1,19},{3,17},{17,3},{19,1},{4,22},{6,... | collective-permute-start | bytes 196616 | tf_op jit(solution)/shard_map/ppermute | solution.py:424
  36.1 0.5 %collective-permute-start.10 = (bf16[4,64,128]{2,1,0:T(8,128)(2,1)S(1)}, bf16[4,64,128]{2,1,0:T(8,128)(2,1)S(1)}, u32[]{:S(2)}, u32[]{:S(2)}) collective-permute-start(bf16[4,64,128]{2,1,0:T(8,128)(2,1)S(1)} %get-tuple-element.18), channel_id=1, source_target_pairs={{0,2},{2,0},{16,18},{18,16},{1,3},{3,1},{17,19},{19,17},{4,6},{6,4... | collective-permute-start | bytes 196616 | tf_op jit(solution)/shard_map/ppermute | solution.py:424
  36.6 0.5 %collective-permute-start.9 = (bf16[4,64,128]{2,1,0:T(8,128)(2,1)S(1)}, bf16[4,64,128]{2,1,0:T(8,128)(2,1)S(1)}, u32[]{:S(2)}, u32[]{:S(2)}) collective-permute-start(bf16[4,64,128]{2,1,0:T(8,128)(2,1)S(1)} %get-tuple-element.19), channel_id=1, source_target_pairs={{0,16},{2,18},{16,0},{18,2},{1,17},{3,19},{17,1},{19,3},{4,20},{6,... | collective-permute-start | bytes 196616 | tf_op jit(solution)/shard_map/ppermute | solution.py:424
  37.1 2.1 %collective-permute-done.8 = bf16[4,64,128]{2,1,0:T(8,128)(2,1)S(1)} collective-permute-done((bf16[4,64,128]{2,1,0:T(8,128)(2,1)S(1)}, bf16[4,64,128]{2,1,0:T(8,128)(2,1)S(1)}, u32[]{:S(2)}, u32[]{:S(2)}) %collective-permute-start.8) | collective-permute-done | bytes 65568 | tf_op jit(solution)/shard_map/ppermute | solution.py:424
  39.2 1.1 %collective-permute-done.10 = bf16[4,64,128]{2,1,0:T(8,128)(2,1)S(1)} collective-permute-done((bf16[4,64,128]{2,1,0:T(8,128)(2,1)S(1)}, bf16[4,64,128]{2,1,0:T(8,128)(2,1)S(1)}, u32[]{:S(2)}, u32[]{:S(2)}) %collective-permute-start.10) | collective-permute-done | bytes 65568 | tf_op jit(solution)/shard_map/ppermute | solution.py:424
  40.3 0.5 %collective-permute-done.9 = bf16[4,64,128]{2,1,0:T(8,128)(2,1)S(1)} collective-permute-done((bf16[4,64,128]{2,1,0:T(8,128)(2,1)S(1)}, bf16[4,64,128]{2,1,0:T(8,128)(2,1)S(1)}, u32[]{:S(2)}, u32[]{:S(2)}) %collective-permute-start.9) | collective-permute-done | bytes 65568 | tf_op jit(solution)/shard_map/ppermute | solution.py:424
  40.9 2.7 %collective-permute-start.13 = (bf16[1,64,128]{2,1,0:T(8,128)(2,1)S(1)}, bf16[1,64,128]{2,1,0:T(8,128)(2,1)S(1)}, u32[]{:S(2)}, u32[]{:S(2)}) collective-permute-start(bf16[1,64,128]{2,1,0:T(8,128)(2,1)S(1)} %get-tuple-element.20), channel_id=1, source_target_pairs={{0,12},{4,8},{8,4},{12,0},{1,13},{5,9},{9,5},{13,1},{2,14},{6,10},... | collective-permute-start | bytes 49160 | tf_op jit(solution)/shard_map/ppermute | solution.py:424
  43.6 0.0 collective-permute-start.12
  43.6 1.8 %collective-permute-start.11 = (bf16[1,64,128]{2,1,0:T(8,128)(2,1)S(1)}, bf16[1,64,128]{2,1,0:T(8,128)(2,1)S(1)}, u32[]{:S(2)}, u32[]{:S(2)}) collective-permute-start(bf16[1,64,128]{2,1,0:T(8,128)(2,1)S(1)} %get-tuple-element.22), channel_id=1, source_target_pairs={{0,4},{4,0},{8,12},{12,8},{1,5},{5,1},{9,13},{13,9},{2,6},{6,2},{1... | collective-permute-start | bytes 49160 | tf_op jit(solution)/shard_map/ppermute | solution.py:424
  45.4 1.1 %collective-permute-done.13.refs_3_ = bf16[1,64,128]{2,1,0:T(8,128)(2,1)S(1)} collective-permute-done((bf16[1,64,128]{2,1,0:T(8,128)(2,1)S(1)}, bf16[1,64,128]{2,1,0:T(8,128)(2,1)S(1)}, u32[]{:S(2)}, u32[]{:S(2)}) %collective-permute-start.13) | collective-permute-done | bytes 16416 | tf_op jit(solution)/shard_map/ppermute | solution.py:424
  46.5 1.7 %collective-permute-done.12.refs_2_ = bf16[1,64,128]{2,1,0:T(8,128)(2,1)S(1)} collective-permute-done((bf16[1,64,128]{2,1,0:T(8,128)(2,1)S(1)}, bf16[1,64,128]{2,1,0:T(8,128)(2,1)S(1)}, u32[]{:S(2)}, u32[]{:S(2)}) %collective-permute-start.12) | collective-permute-done | bytes 16416 | tf_op jit(solution)/shard_map/ppermute | solution.py:424
  48.2 0.0 collective-permute-done.11.refs_1_
  48.2 0.7 %finish.1 = bf16[1,8192]{1,0:T(2,128)(2,1)} custom-call(bf16[1,64,128]{2,1,0:T(8,128)(2,1)S(1)} %get-tuple-element.23.refs_0_, bf16[1,64,128]{2,1,0:T(8,128)(2,1)S(1)} %collective-permute-done.11.refs_1_, bf16[1,64,128]{2,1,0:T(8,128)(2,1)S(1)} %collective-permute-done.12.refs_2_, bf16[1,64,128]{2,1,0:T(8,128)(2,1)S(1)} %collective-permute-done.13.refs_3_, ...), custom_call_target="tpu_custom_call" | custom-call | tf_op jit(solution)/shard_map/finish/pallas_call | solution.py:412
  (3 shorter events, 0.1 us)
Async XLA Ops:
  0.0 8.9 %collective-permute-start.1 = (bf16[1,8192]{1,0:T(2,128)(2,1)}, bf16[1,8192]{1,0:T(2,128)(2,1)S(1)}, u32[]{:S(2)}, u32[]{:S(2)}) collective-permute-start(bf16[1,8192]{1,0:T(2,128)(2,1)} %refs_0_.1), channel_id=1, source_target_pairs={{0,12},{4,8},{8,4},{12,0},{1,13},{5,9},{9,5},{13,1},{2,14},{6,10},... | collective-permute-start | bytes 49160 | tf_op jit(solution)/shard_map/ppermute | solution.py:424
  5.0 5.0 %collective-permute-start = (bf16[1,8192]{1,0:T(2,128)(2,1)}, bf16[1,8192]{1,0:T(2,128)(2,1)S(1)}, u32[]{:S(2)}, u32[]{:S(2)}) collective-permute-start(bf16[1,8192]{1,0:T(2,128)(2,1)} %refs_0_.1), channel_id=1, source_target_pairs={{0,8},{4,12},{8,0},{12,4},{1,9},{5,13},{9,1},{13,5},{2,10},{6,14},... | collective-permute-start | bytes 49160 | tf_op jit(solution)/shard_map/ppermute | solution.py:424
  5.1 5.0 %collective-permute-start.2 = (bf16[1,8192]{1,0:T(2,128)(2,1)}, bf16[1,8192]{1,0:T(2,128)(2,1)S(1)}, u32[]{:S(2)}, u32[]{:S(2)}) collective-permute-start(bf16[1,8192]{1,0:T(2,128)(2,1)} %refs_0_.1), channel_id=1, source_target_pairs={{0,4},{4,0},{8,12},{12,8},{1,5},{5,1},{9,13},{13,9},{2,6},{6,2},{1... | collective-permute-start | bytes 49160 | tf_op jit(solution)/shard_map/ppermute | solution.py:424
  5.6 4.5 %copy-start = (bf16[1,8192]{1,0:T(2,128)(2,1)S(1)}, bf16[1,8192]{1,0:T(2,128)(2,1)}, u32[]{:S(2)}) copy-start(bf16[1,8192]{1,0:T(2,128)(2,1)} %refs_0_.1) | copy-start | bytes 49156
  10.2 7.3 %collective-permute-start.5 = (bf16[4,64,128]{2,1,0:T(8,128)(2,1)S(1)}, bf16[4,64,128]{2,1,0:T(8,128)(2,1)S(1)}, u32[]{:S(2)}, u32[]{:S(2)}) collective-permute-start(bf16[4,64,128]{2,1,0:T(8,128)(2,1)S(1)} %stack.1.refs_0_), channel_id=1, source_target_pairs={{0,18},{2,16},{16,2},{18,0},{1,19},{3,17},{17,3},{19,1},{4,22},{6,... | collective-permute-start | bytes 196616 | tf_op jit(solution)/shard_map/ppermute | solution.py:424
  12.7 4.8 %collective-permute-start.4 = (bf16[4,64,128]{2,1,0:T(8,128)(2,1)S(1)}, bf16[4,64,128]{2,1,0:T(8,128)(2,1)S(1)}, u32[]{:S(2)}, u32[]{:S(2)}) collective-permute-start(bf16[4,64,128]{2,1,0:T(8,128)(2,1)S(1)} %stack.1.refs_0_), channel_id=1, source_target_pairs={{0,16},{2,18},{16,0},{18,2},{1,17},{3,19},{17,1},{19,3},{4,20},{6,... | collective-permute-start | bytes 196616 | tf_op jit(solution)/shard_map/ppermute | solution.py:424
  13.2 4.3 %collective-permute-start.3 = (bf16[4,64,128]{2,1,0:T(8,128)(2,1)S(1)}, bf16[4,64,128]{2,1,0:T(8,128)(2,1)S(1)}, u32[]{:S(2)}, u32[]{:S(2)}) collective-permute-start(bf16[4,64,128]{2,1,0:T(8,128)(2,1)S(1)} %stack.1.refs_0_), channel_id=1, source_target_pairs={{0,2},{2,0},{16,18},{18,16},{1,3},{3,1},{17,19},{19,17},{4,6},{6,4... | collective-permute-start | bytes 196616 | tf_op jit(solution)/shard_map/ppermute | solution.py:424
  17.7 1.6 %collective-permute-start.6 = (bf16[16,8192]{1,0:T(8,128)(2,1)S(1)}, bf16[16,8192]{1,0:T(8,128)(2,1)S(1)}, u32[]{:S(2)}, u32[]{:S(2)}) collective-permute-start(bf16[16,8192]{1,0:T(8,128)(2,1)S(1)} %pack.1.near_ref), channel_id=1, source_target_pairs={{0,1},{1,0},{2,3},{3,2},{4,5},{5,4},{6,7},{7,6},{8,9},{9,8},{10,11... | collective-permute-start | bytes 786440 | tf_op jit(solution)/shard_map/ppermute | solution.py:424
  31.8 1.6 %collective-permute-start.7 = (bf16[16,64,128]{2,1,0:T(8,128)(2,1)S(1)}, bf16[16,64,128]{2,1,0:T(8,128)(2,1)S(1)}, u32[]{:S(2)}, u32[]{:S(2)}) collective-permute-start(bf16[16,64,128]{2,1,0:T(8,128)(2,1)S(1)} %get-tuple-element.16), channel_id=1, source_target_pairs={{0,1},{1,0},{2,3},{3,2},{4,5},{5,4},{6,7},{7,6},{8,9},{9,8},{10,11... | collective-permute-start | bytes 786440 | tf_op jit(solution)/shard_map/ppermute | solution.py:424
  33.5 5.6 %collective-permute-start.8 = (bf16[4,64,128]{2,1,0:T(8,128)(2,1)S(1)}, bf16[4,64,128]{2,1,0:T(8,128)(2,1)S(1)}, u32[]{:S(2)}, u32[]{:S(2)}) collective-permute-start(bf16[4,64,128]{2,1,0:T(8,128)(2,1)S(1)} %get-tuple-element.17), channel_id=1, source_target_pairs={{0,18},{2,16},{16,2},{18,0},{1,19},{3,17},{17,3},{19,1},{4,22},{6,... | collective-permute-start | bytes 196616 | tf_op jit(solution)/shard_map/ppermute | solution.py:424
  36.1 4.3 %collective-permute-start.10 = (bf16[4,64,128]{2,1,0:T(8,128)(2,1)S(1)}, bf16[4,64,128]{2,1,0:T(8,128)(2,1)S(1)}, u32[]{:S(2)}, u32[]{:S(2)}) collective-permute-start(bf16[4,64,128]{2,1,0:T(8,128)(2,1)S(1)} %get-tuple-element.18), channel_id=1, source_target_pairs={{0,2},{2,0},{16,18},{18,16},{1,3},{3,1},{17,19},{19,17},{4,6},{6,4... | collective-permute-start | bytes 196616 | tf_op jit(solution)/shard_map/ppermute | solution.py:424
  36.6 4.3 %collective-permute-start.9 = (bf16[4,64,128]{2,1,0:T(8,128)(2,1)S(1)}, bf16[4,64,128]{2,1,0:T(8,128)(2,1)S(1)}, u32[]{:S(2)}, u32[]{:S(2)}) collective-permute-start(bf16[4,64,128]{2,1,0:T(8,128)(2,1)S(1)} %get-tuple-element.19), channel_id=1, source_target_pairs={{0,16},{2,18},{16,0},{18,2},{1,17},{3,19},{17,1},{19,3},{4,20},{6,... | collective-permute-start | bytes 196616 | tf_op jit(solution)/shard_map/ppermute | solution.py:424
  40.9 5.6 %collective-permute-start.13 = (bf16[1,64,128]{2,1,0:T(8,128)(2,1)S(1)}, bf16[1,64,128]{2,1,0:T(8,128)(2,1)S(1)}, u32[]{:S(2)}, u32[]{:S(2)}) collective-permute-start(bf16[1,64,128]{2,1,0:T(8,128)(2,1)S(1)} %get-tuple-element.20), channel_id=1, source_target_pairs={{0,12},{4,8},{8,4},{12,0},{1,13},{5,9},{9,5},{13,1},{2,14},{6,10},... | collective-permute-start | bytes 49160 | tf_op jit(solution)/shard_map/ppermute | solution.py:424
  43.6 4.6 %collective-permute-start.12 = (bf16[1,64,128]{2,1,0:T(8,128)(2,1)S(1)}, bf16[1,64,128]{2,1,0:T(8,128)(2,1)S(1)}, u32[]{:S(2)}, u32[]{:S(2)}) collective-permute-start(bf16[1,64,128]{2,1,0:T(8,128)(2,1)S(1)} %get-tuple-element.21), channel_id=1, source_target_pairs={{0,8},{4,12},{8,0},{12,4},{1,9},{5,13},{9,1},{13,5},{2,10},{6,14},... | collective-permute-start | bytes 49160 | tf_op jit(solution)/shard_map/ppermute | solution.py:424
  43.6 4.6 %collective-permute-start.11 = (bf16[1,64,128]{2,1,0:T(8,128)(2,1)S(1)}, bf16[1,64,128]{2,1,0:T(8,128)(2,1)S(1)}, u32[]{:S(2)}, u32[]{:S(2)}) collective-permute-start(bf16[1,64,128]{2,1,0:T(8,128)(2,1)S(1)} %get-tuple-element.22), channel_id=1, source_target_pairs={{0,4},{4,0},{8,12},{12,8},{1,5},{5,1},{9,13},{13,9},{2,6},{6,2},{1... | collective-permute-start | bytes 49160 | tf_op jit(solution)/shard_map/ppermute | solution.py:424
